TPU v7x, 32 devices: a whole 2x2x4 slice. The times are simulated.
32 devices in a mesh: node: 4 (over y, core), local: 8 (over z, x).
Axes of the slice: x: 2, y: 2, z: 4, core: 2. Of those that a mesh axis runs over, the one named last changes fastest.
Arguments:
- tokens: bfloat16 [4096, 2048], P(('node', 'local')), may hold values from -6 to 6
- cotangent: bfloat16 [4096, 2048], P(('node', 'local')), may hold values from -6 to 6
- routes: int32 [4096, 1], P('node'), may hold values from 0 to 3; in each aligned block of 1024 rows (0 to 1023, 1024 to 2047, ...) at most 272 rows name the same one
- route_weight: float32 [4096, 1], P('node'), may hold values from 0.2 to 1
- fetch_pick: int32 [4, 4], replicated, may hold values from 0 to 1
- panels: bfloat16 [8, 3, 1408, 2048], P('node', None, 'local'), may hold values from -0.125 to 0.125
Outputs:
- mixed: bfloat16 [4096, 2048], P(('node', 'local'))
- token_grad: bfloat16 [4096, 2048], P(('node', 'local'))
- panel_grad: bfloat16 [8, 3, 1408, 2048], P('node', None, 'local')
Inputs may be any that keep to these rules, and one draw needn't show every extreme that they name: `routes`: each row names 1 different slots; in the 1024 rows of one group no slot is named by more than 272 rows, and in some groups one slot is named by exactly 272 rows.
All inputs are finite; a program needn't handle non-finite values.
Results may differ from a plain program's by a relative error of at most 0.013.
Values may be sent and summed in bfloat16 or wider, within the bound.
No kernel may reach another device: no remote copies, remote signals or barrier semaphores. Data moves between devices by JAX's collectives and lax.ppermute only.
A program may use at most 128 MiB of HBM per device.

v0:
```python
import jax
import jax.numpy as jnp
from jax import lax
from jax.sharding import PartitionSpec as P


def from_behind(block, axis, distance):
    devices = range(lax.axis_size(axis))
    route = [((i - distance) % len(devices), i) for i in devices]
    return lax.ppermute(block, axis, route)


def expert_pass(panel, slot_tokens, slot_cotan, slot_scale):
    contract_last = (((1,), (1,)), ((), ()))
    contract_first = (((0,), (0,)), ((), ()))
    gate_pre = lax.dot_general(
        slot_tokens, panel[0], contract_last, preferred_element_type=jnp.float32
    )
    up_pre = lax.dot_general(
        slot_tokens, panel[1], contract_last, preferred_element_type=jnp.float32
    )
    sigmoid_gate = jax.nn.sigmoid(gate_pre)
    activated = gate_pre * sigmoid_gate
    hidden = (activated * up_pre).astype(jnp.bfloat16)
    expert_out = (
        jnp.dot(hidden, panel[2], preferred_element_type=jnp.float32) * slot_scale[:, None]
    ).astype(jnp.bfloat16)
    d_hidden = lax.dot_general(
        slot_cotan, panel[2], contract_last, preferred_element_type=jnp.float32
    )
    d_gate = (d_hidden * up_pre * sigmoid_gate * (1.0 + gate_pre * (1.0 - sigmoid_gate))).astype(
        jnp.bfloat16
    )
    d_up = (d_hidden * activated).astype(jnp.bfloat16)
    input_grad = (
        jnp.dot(d_gate, panel[0], preferred_element_type=jnp.float32)
        + jnp.dot(d_up, panel[1], preferred_element_type=jnp.float32)
    ).astype(jnp.bfloat16)
    weight_grad = jnp.stack(
        [
            lax.dot_general(
                d_gate, slot_tokens, contract_first, preferred_element_type=jnp.float32
            ),
            lax.dot_general(d_up, slot_tokens, contract_first, preferred_element_type=jnp.float32),
            lax.dot_general(hidden, slot_cotan, contract_first, preferred_element_type=jnp.float32),
        ]
    ).astype(jnp.bfloat16)
    return (expert_out, input_grad, weight_grad)


def body(tokens, cotangent, routes, route_weight, fetch_pick, panels):
    node_count = lax.axis_size("node")
    my_node = lax.axis_index("node")
    slot_count = fetch_pick.shape[1]
    stride = node_count // slot_count
    group_x, group_dy = (
        lax.all_gather(tokens, "local", axis=0, tiled=True),
        lax.all_gather(cotangent, "local", axis=0, tiled=True),
    )
    group_size, model_width = group_x.shape
    route_count = routes.shape[1]
    capacity = group_size * route_count * 17 // (16 * slot_count)
    flat_slot = routes.reshape(-1)
    onehot = (flat_slot[:, None] == jnp.arange(slot_count, dtype=jnp.int32)[None, :]).astype(
        jnp.int32
    )
    position = jnp.sum((jnp.cumsum(onehot, axis=0) - 1) * onehot, axis=1)
    target = flat_slot * capacity + position
    token_ids = jnp.arange(group_size * route_count, dtype=jnp.int32) // route_count
    source = jnp.full((slot_count * capacity,), group_size, jnp.int32).at[target].set(token_ids)
    slot_weight = (
        jnp.zeros((slot_count * capacity,), jnp.float32).at[target].set(route_weight.reshape(-1))
    )
    zero_row = jnp.zeros((1, model_width), group_x.dtype)
    slot_tokens = jnp.concatenate([group_x, zero_row], axis=0)[source].reshape(
        slot_count, capacity, model_width
    )
    slot_dy = jnp.concatenate([group_dy, zero_row], axis=0)[source]
    slot_cotan = (
        (slot_dy.astype(jnp.float32) * slot_weight[:, None])
        .astype(jnp.bfloat16)
        .reshape(slot_count, capacity, model_width)
    )
    slot_scale = slot_weight.reshape(slot_count, capacity)

    def chosen_local(round_index):
        reader = (my_node + round_index * stride) % node_count
        return fetch_pick[reader, round_index]

    expert_outs = []
    input_grads = []
    accumulated = jnp.zeros(panels.shape, jnp.float32)
    for round_index in range(slot_count):
        panel_piece = lax.dynamic_index_in_dim(panels, chosen_local(round_index), 0, keepdims=False)
        if round_index > 0:
            panel_piece = from_behind(panel_piece, "node", round_index * stride)
        expert_out, input_grad, weight_grad = expert_pass(
            panel_piece, slot_tokens[round_index], slot_cotan[round_index], slot_scale[round_index]
        )
        expert_outs.append(expert_out)
        input_grads.append(input_grad)
        if round_index > 0:
            weight_grad = from_behind(weight_grad, "node", node_count - round_index * stride)
        accumulated = accumulated.at[chosen_local(round_index)].add(weight_grad.astype(jnp.float32))
    out_all = jnp.concatenate(expert_outs, axis=0)
    mixed_part = jnp.sum(
        out_all[target].reshape(group_size, route_count, model_width).astype(jnp.float32), axis=1
    )
    grad_all = jnp.concatenate(input_grads, axis=0)
    grad_part = jnp.sum(
        grad_all[target].reshape(group_size, route_count, model_width).astype(jnp.float32), axis=1
    )
    mixed, token_grad = (
        lax.psum_scatter(
            mixed_part.astype(jnp.bfloat16), "local", scatter_dimension=0, tiled=True
        ).astype(jnp.float32),
        lax.psum_scatter(
            grad_part.astype(jnp.bfloat16), "local", scatter_dimension=0, tiled=True
        ).astype(jnp.float32),
    )
    return (
        mixed.astype(jnp.bfloat16),
        token_grad.astype(jnp.bfloat16),
        accumulated.astype(jnp.bfloat16),
    )


def solution(mesh):
    return jax.shard_map(
        body,
        mesh=mesh,
        in_specs=(
            P(("node", "local"), None),
            P(("node", "local"), None),
            P("node", None),
            P("node", None),
            P(),
            P("node", None, "local", None),
        ),
        out_specs=(
            P(("node", "local"), None),
            P(("node", "local"), None),
            P("node", None, "local", None),
        ),
        check_vma=False,
    )
```

profile of v0, /device:TPU:0, one launch (start us, length us, event | category | flops | bytes accessed | tf_op | source)
XLA Modules:
  0.0 406.6 jit_solution(9997400669597941463)
XLA Ops:
  7.2 0.7 all-gather.5.cloned.1.call-update
  7.9 0.7 all-gather.3.cloned.1.call-update
  8.7 1.5 constant_dynamic-slice_fusion
  16.2 6.0 %dynamic-slice_bitcast_fusion.2 = (bf16[3,176,2048]{2,1,0:T(8,128)(2,1)}, bf16[3,176,2048]{2,1,0:T(8,128)(2,1)}, bf16[3,176,2048]{2,1,0:T(8,128)(2,1)S(1)}) fusion(bf16[2,3,176,2048]{3,2,1,0:T(8,128)(2,1)} %param.19, s32[]{:T(128)} %select_n.89, s32[]{:T(128)} %select_n.95, s32[]{:T(128)} %select_n.92), kind=kLoop, calls=%fused_computation.61 | loop fusion | bytes 12976140 | tf_op jit(solution)/shard_map/jit(dynamic_index_in_dim)/squeeze | solution.py:94
  22.2 0.6 collective-permute-start
  22.7 1.9 collective-permute-start.2
  24.6 2.4 collective-permute-start.1
  28.3 1.1 reduce-window.6
  30.6 4.3 %scatter_custom_fusion = s32[1088]{0:T(1024)S(1)} fusion(s32[1024]{0:T(1024)S(1)} %bitcast.157, s32[1024]{0:T(1024)S(1)} %iota.11, s32[]{:T(128)} %constant.155.clone.1), kind=kCustom, calls=%fused_computation.147 | custom fusion | bytes 4356 | tf_op jit(solution)/shard_map/scatter | solution.py:70
  35.0 4.5 %scatter_custom_fusion.1 = f32[1088]{0:T(1024)S(1)} fusion(s32[1024]{0:T(1024)S(1)} %bitcast.158, f32[1024]{0:T(1024)} %bitcast.162, f32[]{:T(128)} %constant.166.clone.1), kind=kCustom, calls=%fused_computation.145 | custom fusion | bytes 4864 | tf_op jit(solution)/shard_map/scatter | solution.py:72
  39.6 46.7 %all-gather.5.cloned.1.call-done = bf16[1024,2048]{1,0:T(8,128)(2,1)} async-done(((bf16[128,2048]{1,0:T(8,128)(2,1)}), bf16[1024,2048]{1,0:T(8,128)(2,1)}) %all-gather.5.cloned.1.call-update) | async-done | bytes 4194320 | tf_op jit(solution)/shard_map/all_gather | solution.py:58
  86.3 4.8 %concatenate.36 = bf16[1025,2048]{1,0:T(8,128)(2,1)} pad(bf16[1024,2048]{1,0:T(8,128)(2,1)} %all-gather.5.cloned.1.call-done, bf16[]{:T(256)} %constant.154.clone.1), padding=0_1x0_0 | pad | bytes 8392706 | tf_op jit(solution)/shard_map/concatenate | solution.py:78
  91.1 13.3 %gather_fusion.2 = bf16[1088,2048]{1,0:T(8,128)(2,1)} fusion(bf16[1025,2048]{1,0:T(8,128)(2,1)} %concatenate.36, s32[2048]{0:T(1024)S(1)} %pad_clamp_fusion), kind=kCustom, calls=%fused_computation.2 | custom fusion | bytes 8917248 | tf_op jit(solution)/shard_map/gather | solution.py:78
  104.4 5.2 %multiply_convert_fusion = bf16[1088,2048]{1,0:T(8,128)(2,1)} fusion(bf16[1088,2048]{1,0:T(8,128)(2,1)} %gather_fusion.2, f32[1088]{0:T(1024)S(1)} %scatter_custom_fusion.1), kind=kLoop, calls=%fused_computation.6 | loop fusion | flops 6684672 | bytes 8917248 | tf_op jit(solution)/shard_map/convert_element_type | solution.py:81
  109.6 50.5 %all-gather.3.cloned.1.call-done = bf16[1024,2048]{1,0:T(8,128)(2,1)} async-done(((bf16[128,2048]{1,0:T(8,128)(2,1)}), bf16[1024,2048]{1,0:T(8,128)(2,1)}) %all-gather.3.cloned.1.call-update) | async-done | bytes 4194320 | tf_op jit(solution)/shard_map/all_gather | solution.py:57
  160.1 4.8 %concatenate.34 = bf16[1025,2048]{1,0:T(8,128)(2,1)} pad(bf16[1024,2048]{1,0:T(8,128)(2,1)} %all-gather.3.cloned.1.call-done, bf16[]{:T(256)} %constant.154.clone.1), padding=0_1x0_0 | pad | bytes 8392706 | tf_op jit(solution)/shard_map/concatenate | solution.py:75
  164.9 13.3 %gather_fusion = bf16[1088,2048]{1,0:T(8,128)(2,1)} fusion(bf16[1025,2048]{1,0:T(8,128)(2,1)} %concatenate.34, s32[2048]{0:T(1024)S(1)} %pad_clamp_fusion), kind=kCustom, calls=%fused_computation | custom fusion | bytes 8917248 | tf_op jit(solution)/shard_map/gather | solution.py:75
  178.2 2.3 fusion.57
  180.5 2.3 fusion.55
  182.8 1.9 multiply_convert_fusion.7
  184.7 1.6 fusion.3
  186.3 1.8 fusion.30
  188.1 1.8 fusion.49
  189.9 1.8 fusion.24
  191.7 1.8 fusion.37
  193.5 1.8 fusion.27
  195.3 1.8 fusion.43
  197.1 1.9 multiply_convert_fusion.6
  199.0 1.6 fusion.4
  200.6 1.9 multiply_convert_fusion.2
  202.5 1.6 fusion.6
  204.1 1.9 multiply_convert_fusion.4
  206.0 1.6 fusion.5
  207.6 2.4 pad_maximum_fusion
  209.9 11.6 %gather_fusion.1 = bf16[1024,2048]{1,0:T(8,128)(2,1)} fusion(bf16[1088,2048]{1,0:T(8,128)(2,1)} %pad_maximum_fusion, s32[1024]{0:T(1024)S(1)} %broadcast_clamp_fusion), kind=kCustom, calls=%fused_computation.1 | custom fusion | bytes 8392704 | tf_op jit(solution)/shard_map/gather | solution.py:107
  221.9 1.6 fusion.62
  223.4 1.6 fusion.59
  225.0 1.6 fusion.61
  226.6 1.7 fusion.60
  228.3 1.6 fusion.7
  229.9 1.6 fusion.8
  231.5 1.6 fusion.10
  233.1 1.6 fusion.9
  234.7 2.4 pad_maximum_fusion.1
  237.1 11.7 %gather_fusion.3 = bf16[1024,2048]{1,0:T(8,128)(2,1)} fusion(bf16[1088,2048]{1,0:T(8,128)(2,1)} %pad_maximum_fusion.1, s32[1024]{0:T(1024)S(1)} %broadcast_clamp_fusion), kind=kCustom, calls=%fused_computation.3 | custom fusion | bytes 8392704 | tf_op jit(solution)/shard_map/gather | solution.py:111
  248.9 0.6 copy-done.2
  249.5 0.8 and_reduce_fusion.2
  250.3 1.8 fusion.14
  252.1 1.8 fusion.15
  253.9 1.9 fusion.16
  256.2 1.8 fusion.19
  259.3 1.6 collective-permute-start.4
  261.5 0.5 fusion.21
  263.4 0.8 and_reduce_fusion
  265.8 1.1 broadcast_in_dim.11
  266.9 1.2 select_dynamic-update-slice_fusion
  268.1 31.1 %collective-permute-done.3 = bf16[3,176,2048]{2,1,0:T(8,128)(2,1)S(1)} collective-permute-done((bf16[3,176,2048]{2,1,0:T(8,128)(2,1)S(1)}, bf16[3,176,2048]{2,1,0:T(8,128)(2,1)S(1)}, u32[]{:S(2)}, u32[]{:S(2)}) %collective-permute-start.3) | collective-permute-done | bytes 2162720 | tf_op jit(solution)/shard_map/ppermute | solution.py:10
  299.2 1.6 fusion
  300.8 47.8 %collective-permute-done.4 = bf16[3,176,2048]{2,1,0:T(8,128)(2,1)S(1)} collective-permute-done((bf16[3,176,2048]{2,1,0:T(8,128)(2,1)S(1)}, bf16[3,176,2048]{2,1,0:T(8,128)(2,1)S(1)}, u32[]{:S(2)}, u32[]{:S(2)}) %collective-permute-start.4) | collective-permute-done | bytes 2162720 | tf_op jit(solution)/shard_map/ppermute | solution.py:10
  348.6 1.6 fusion.1
  350.2 1.7 collective-permute-done.5
  351.9 1.6 fusion.2
  353.6 2.7 convert_element_type.132
  356.3 43.8 %reduce-scatter.5.cloned.1.call-done = bf16[128,2048]{1,0:T(8,128)(2,1)} async-done(((bf16[1024,2048]{1,0:T(8,128)(2,1)}), bf16[128,2048]{1,0:T(8,128)(2,1)}) %reduce-scatter.5.cloned.1.call-update) | async-done | bytes 524304 | tf_op jit(solution)/shard_map/reduce_scatter | solution.py:117
  (53 shorter events, 6.1 us)
Async XLA Ops:
  7.2 79.1 %all-gather.5.cloned.1.call-start = ((), (), s32[]{:S(2)}) async-start(), calls=%async_computation.4 | async-start | bytes 4718592 | tf_op jit(solution)/shard_map/all_gather | solution.py:58
  7.9 152.2 %all-gather.3.cloned.1.call-start = ((), (), s32[]{:S(2)}) async-start(), calls=%async_computation.2 | async-start | bytes 4718592 | tf_op jit(solution)/shard_map/all_gather | solution.py:57
  8.6 347.6 %reduce-scatter.3.cloned.1.call-start = ((), (), s32[]{:S(2)}) async-start(), calls=%async_computation.3 | async-start | bytes 4718592 | tf_op jit(solution)/shard_map/reduce_scatter | solution.py:114
  16.2 12.1 %copy-start.1 = (s32[1024,1]{0,1:T(1,128)S(1)}, s32[1024,1]{0,1:T(1,128)}, u32[]{:S(2)}) copy-start(s32[1024,1]{0,1:T(1,128)} %param.16) | copy-start | bytes 12292
  22.2 164.1 %collective-permute-start = (bf16[3,176,2048]{2,1,0:T(8,128)(2,1)}, bf16[3,176,2048]{2,1,0:T(8,128)(2,1)}, u32[]{:S(2)}, u32[]{:S(2)}) collective-permute-start(bf16[3,176,2048]{2,1,0:T(8,128)(2,1)} %get-tuple-element.55), channel_id=1, source_target_pairs={{24,0},{0,8},{8,16},{16,24},{25,1},{1,9},{9,17},{17,25},{26,2},{2,... | collective-permute-start | bytes 6488072 | tf_op jit(solution)/shard_map/ppermute | solution.py:10
  22.7 167.2 %collective-permute-start.2 = (bf16[3,176,2048]{2,1,0:T(8,128)(2,1)}, bf16[3,176,2048]{2,1,0:T(8,128)(2,1)}, u32[]{:S(2)}, u32[]{:S(2)}) collective-permute-start(bf16[3,176,2048]{2,1,0:T(8,128)(2,1)} %get-tuple-element.56), channel_id=1, source_target_pairs={{8,0},{16,8},{24,16},{0,24},{9,1},{17,9},{25,17},{1,25},{10,2},{18... | collective-permute-start | bytes 6488072 | tf_op jit(solution)/shard_map/ppermute | solution.py:10
  24.6 168.9 %collective-permute-start.1 = (bf16[3,176,2048]{2,1,0:T(8,128)(2,1)S(1)}, bf16[3,176,2048]{2,1,0:T(8,128)(2,1)}, u32[]{:S(2)}, u32[]{:S(2)}) collective-permute-start(bf16[3,176,2048]{2,1,0:T(8,128)(2,1)S(1)} %get-tuple-element.57), channel_id=1, source_target_pairs={{16,0},{24,8},{0,16},{8,24},{17,1},{25,9},{1,17},{9,25},{18,2},{26... | collective-permute-start | bytes 6488072 | tf_op jit(solution)/shard_map/ppermute | solution.py:10
  178.2 4.6 %copy-start = (bf16[1088,2048]{1,0:T(8,128)(2,1)S(1)}, bf16[1088,2048]{1,0:T(8,128)(2,1)}, u32[]{:S(2)}) copy-start(bf16[1088,2048]{1,0:T(8,128)(2,1)} %multiply_convert_fusion) | copy-start | bytes 13369348
  180.5 7.6 %slice-start = ((s8[4456448]{0:T(1024)(128)(4,1)}), s8[4194304]{0:T(1024)(128)(4,1)S(1)}, s32[]{:S(2)}) async-start(s8[4456448]{0:T(1024)(128)(4,1)} %bitcast.149), calls=%async_computation.6 | async-start | bytes 8388608
  182.8 5.3 %slice-start.1 = ((s8[4456448]{0:T(1024)(128)(4,1)}), s8[262144]{0:T(1024)(128)(4,1)S(1)}, s32[]{:S(2)}) async-start(s8[4456448]{0:T(1024)(128)(4,1)} %bitcast.149), calls=%async_computation.7 | async-start | bytes 524288
  221.6 178.5 %reduce-scatter.5.cloned.1.call-start = ((), (), s32[]{:S(2)}) async-start(), calls=%async_computation.5 | async-start | bytes 4718592 | tf_op jit(solution)/shard_map/reduce_scatter | solution.py:117
  248.8 0.7 copy-start.2
  248.8 9.1 %slice-start.2 = ((s8[4456448]{0:T(1024)(128)(4,1)}), s8[262144]{0:T(1024)(128)(4,1)S(1)}, s32[]{:S(2)}) async-start(s8[4456448]{0:T(1024)(128)(4,1)} %bitcast.151), calls=%async_computation.8 | async-start | bytes 524288
  253.9 4.1 %slice-start.3 = ((s8[4456448]{0:T(1024)(128)(4,1)}), s8[4194304]{0:T(1024)(128)(4,1)S(1)}, s32[]{:S(2)}) async-start(s8[4456448]{0:T(1024)(128)(4,1)} %bitcast.151), calls=%async_computation.9 | async-start | bytes 8388608
  256.1 43.1 %collective-permute-start.3 = (bf16[3,176,2048]{2,1,0:T(8,128)(2,1)S(1)}, bf16[3,176,2048]{2,1,0:T(8,128)(2,1)S(1)}, u32[]{:S(2)}, u32[]{:S(2)}) collective-permute-start(bf16[3,176,2048]{2,1,0:T(8,128)(2,1)S(1)} %pad_maximum_fusion.2), channel_id=1, source_target_pairs={{8,0},{16,8},{24,16},{0,24},{9,1},{17,9},{25,17},{1,25},{10,2},{18... | collective-permute-start | bytes 6488072 | tf_op jit(solution)/shard_map/ppermute | solution.py:10
  258.0 4.1 slice-start.4
  259.1 3.0 slice-start.5
  259.3 89.2 %collective-permute-start.4 = (bf16[3,176,2048]{2,1,0:T(8,128)(2,1)S(1)}, bf16[3,176,2048]{2,1,0:T(8,128)(2,1)S(1)}, u32[]{:S(2)}, u32[]{:S(2)}) collective-permute-start(bf16[3,176,2048]{2,1,0:T(8,128)(2,1)S(1)} %pad_maximum_fusion.3), channel_id=1, source_target_pairs={{16,0},{24,8},{0,16},{8,24},{17,1},{25,9},{1,17},{9,25},{18,2},{26... | collective-permute-start | bytes 6488072 | tf_op jit(solution)/shard_map/ppermute | solution.py:10
  262.9 89.1 %collective-permute-start.5 = (bf16[3,176,2048]{2,1,0:T(8,128)(2,1)S(1)}, bf16[3,176,2048]{2,1,0:T(8,128)(2,1)S(1)}, u32[]{:S(2)}, u32[]{:S(2)}) collective-permute-start(bf16[3,176,2048]{2,1,0:T(8,128)(2,1)S(1)} %pad_maximum_fusion.4), channel_id=1, source_target_pairs={{24,0},{0,8},{8,16},{16,24},{25,1},{1,9},{9,17},{17,25},{26,2},{2,... | collective-permute-start | bytes 6488072 | tf_op jit(solution)/shard_map/ppermute | solution.py:10
Sparse Core Ops, SparseCore 0:
  10.1 76.0 all-gather.4
  88.4 71.6 all-gather.2
  221.7 86.1 reduce-scatter.2
  312.4 87.6 reduce-scatter.4
where the time goes:
time: 408 us; the launch traced here: 407 us
  waiting for transfers between devices  223 us (55%)
  local copies, waits for them, and re-layouts  77.9 us (19%)
  matrix products  53.7 us (13%)
  other arithmetic  22.5 us (6%)
  between operations  22.2 us (5%)
  starting transfers between devices  7.35 us (2%)
    ppermute x6, waiting for transfers between devices, from_behind(): return lax.ppermute(block, axis, route)  80.6 us
    all_gather x1, waiting for transfers between devices, body(): lax.all_gather(tokens, 'local', axis=0, tiled=True)  50.5 us
    all_gather x1, waiting for transfers between devices, body(): lax.all_gather(cotangent, 'local', axis=0, tiled=True)  46.7 us
    reduce_scatter x1, waiting for transfers between devices, body(): lax.psum_scatter(grad_part.astype(jnp.bfloat16), 'local', scatter_dimensi...  43.8 us
    gather x1, local copies, waits for them, and re-layouts, body(): slot_dy = jnp.concatenate([group_dy, zero_row], axis=0)[source]  13.3 us
    gather x1, local copies, waits for them, and re-layouts, body(): jnp.concatenate([group_x, zero_row], axis=0)[source]  13.3 us
    gather x1, local copies, waits for them, and re-layouts, body(): grad_all[target].reshape(group_size, route_count, model_width)  11.7 us
    gather x1, local copies, waits for them, and re-layouts, body(): out_all[target].reshape(group_size, route_count, model_width)  11.6 us
  transfers between devices with their start and end apart: 10, of which 6 were waited for; matrix products, arithmetic and copies ran while one was open for 31% of the time, Pallas kernels for 0%

commit v1 on v0

v1 whole, which is shorter than its diff:
```python
import jax
import jax.numpy as jnp
from jax import lax
from jax.experimental import pallas as pl
from jax.experimental.pallas import tpu as pltpu
from jax.sharding import PartitionSpec as P

BF16 = jnp.bfloat16
F32 = jnp.float32
VMEM_LIMIT = 48 * 1024 * 1024
CONTRACT_LAST = (((1,), (1,)), ((), ()))
CONTRACT_FIRST = (((0,), (0,)), ((), ()))


def whole_in_vmem():
    return pl.BlockSpec(memory_space=pltpu.VMEM)


def tile_of(size, most):
    tile = min(size, most)
    while size % tile:
        tile -= 1
    return tile


def from_behind(block, axis, distance):
    size = lax.axis_size(axis)
    return lax.ppermute(block, axis, [((i - distance) % size, i) for i in range(size)])


def ring_order(size):
    return list(range(0, size, 2)) + list(range(1, size, 2))[::-1]


def ring_step(block, order, distance):
    size = len(order)
    return lax.ppermute(
        block, "local", [(order[i], order[(i + distance) % size]) for i in range(size)]
    )


def ring_gather(block, order, up_hops):
    size = len(order)
    blocks = [block] + [None] * (size - 1)
    up, down = block, block
    for hop in range(1, max(up_hops, size - 1 - up_hops) + 1):
        if hop <= up_hops:
            up = ring_step(up, order, 1)
            blocks[size - hop] = up
        if hop <= size - 1 - up_hops:
            down = ring_step(down, order, -1)
            blocks[hop] = down
    return blocks


def plus(a, b):
    return (a.astype(F32) + b.astype(F32)).astype(BF16)


def ring_scatter(chunks, order, up_hops):
    size = len(order)
    down_hops = size - 1 - up_hops
    up, down = chunks[up_hops], chunks[(size - down_hops) % size]
    for hop in range(max(up_hops, down_hops), 0, -1):
        if hop <= up_hops:
            up = ring_step(up, order, 1)
            if hop > 1:
                up = plus(up, chunks[hop - 1])
        if hop <= down_hops:
            down = ring_step(down, order, -1)
            if hop > 1:
                down = plus(down, chunks[size - hop + 1])
    return (up.astype(F32) + down.astype(F32) + chunks[0].astype(F32)).astype(BF16)


def slot_kernel(slot, parts, *refs):
    x_refs, dy_refs = refs[:parts], refs[parts : 2 * parts]
    panel, routes, weight, acts, grads = refs[2 * parts : 2 * parts + 5]
    x_all, dy_all = refs[2 * parts + 5 :]
    units = panel.shape[1]
    part, width = x_refs[0].shape
    for d in range(parts):
        x_all[d * part : (d + 1) * part, :] = x_refs[d][...]
        dy_all[d * part : (d + 1) * part, :] = dy_refs[d][...]
    rows = tile_of(x_all.shape[0], 256)
    columns = tile_of(width, 512)

    @pl.loop(0, x_all.shape[0] // rows)
    def _(step):
        here = pl.ds(pl.multiple_of(step * rows, rows), rows)
        x, dy = x_all[here, :], dy_all[here, :]
        gate = lax.dot_general(panel[0], x, CONTRACT_LAST, preferred_element_type=F32)
        up = lax.dot_general(panel[1], x, CONTRACT_LAST, preferred_element_type=F32)
        d_hidden = lax.dot_general(panel[2], dy, CONTRACT_LAST, preferred_element_type=F32)
        scale = jnp.where(routes[:, here] == slot, weight[:, here], 0.0)
        sigmoid_gate = jax.nn.sigmoid(gate)
        activated = gate * sigmoid_gate
        d_hidden = d_hidden * scale
        d_gate = d_hidden * up * sigmoid_gate * (1.0 + gate * (1.0 - sigmoid_gate))
        acts[0:units, here] = d_gate.astype(BF16)
        acts[units : 2 * units, here] = (d_hidden * activated).astype(BF16)
        acts[2 * units : 3 * units, here] = (activated * up * scale).astype(BF16)

    @pl.loop(0, width // columns)
    def _(step):
        here = pl.ds(pl.multiple_of(step * columns, columns), columns)
        x, dy = x_all[:, here], dy_all[:, here]
        d_both = jnp.dot(acts[0 : 2 * units, :], x, preferred_element_type=F32).astype(BF16)
        grads[0, :, here] = d_both[0:units]
        grads[1, :, here] = d_both[units:]
        grads[2, :, here] = jnp.dot(
            acts[2 * units : 3 * units, :], dy, preferred_element_type=F32
        ).astype(BF16)


def slot_pass(slot, x_parts, dy_parts, panel, routes, weight):
    parts = len(x_parts)
    part, width = x_parts[0].shape
    units = panel.shape[1]
    total = parts * part
    return pl.pallas_call(
        lambda *refs: slot_kernel(slot, parts, *refs),
        out_shape=(
            jax.ShapeDtypeStruct((3 * units, total), BF16),
            jax.ShapeDtypeStruct(panel.shape, BF16),
        ),
        in_specs=[whole_in_vmem()] * (2 * parts + 3),
        out_specs=(whole_in_vmem(), whole_in_vmem()),
        scratch_shapes=[pltpu.VMEM((total, width), BF16), pltpu.VMEM((total, width), BF16)],
        compiler_params=pltpu.CompilerParams(vmem_limit_bytes=VMEM_LIMIT),
        cost_estimate=pl.CostEstimate(
            flops=12 * total * units * width,
            bytes_accessed=4 * total * width + 12 * units * width,
            transcendentals=total * units,
        ),
        name=f"slot_{slot}",
    )(*x_parts, *dy_parts, panel, routes, weight)


def chunk_kernel(wanted, slots, part, *refs):
    acts, panels, outs = refs[:slots], refs[slots : 2 * slots], refs[2 * slots :]
    units, width = panels[0].shape[1:]
    columns = tile_of(width, 512)

    @pl.loop(0, width // columns)
    def _(step):
        here = pl.ds(pl.multiple_of(step * columns, columns), columns)
        for out, (kind, d) in zip(outs, wanted):
            rows = slice(d * part, (d + 1) * part)
            total = jnp.zeros((part, columns), F32)
            for act, panel in zip(acts, panels):
                for which in (2,) if kind == "mixed" else (0, 1):
                    total += lax.dot_general(
                        act[which * units : (which + 1) * units, rows],
                        panel[which, :, here],
                        CONTRACT_FIRST,
                        preferred_element_type=F32,
                    )
            out[:, here] = total.astype(BF16)


def chunk_pass(wanted, acts, panels, part):
    slots = len(acts)
    units, width = panels[0].shape[1:]
    work = sum(1 if kind == "mixed" else 2 for kind, _ in wanted)
    return pl.pallas_call(
        lambda *refs: chunk_kernel(wanted, slots, part, *refs),
        out_shape=tuple(jax.ShapeDtypeStruct((part, width), BF16) for _ in wanted),
        in_specs=[whole_in_vmem()] * (2 * slots),
        out_specs=tuple(whole_in_vmem() for _ in wanted),
        compiler_params=pltpu.CompilerParams(vmem_limit_bytes=VMEM_LIMIT),
        cost_estimate=pl.CostEstimate(
            flops=2 * work * slots * part * units * width,
            bytes_accessed=slots * 6 * units * width + 2 * len(wanted) * part * width,
            transcendentals=0,
        ),
        name=f"chunks_{len(wanted)}",
    )(*acts, *panels)


def body(tokens, cotangent, routes, route_weight, fetch_pick, panels):
    node_count = lax.axis_size("node")
    my_node = lax.axis_index("node")
    my_local = lax.axis_index("local")
    slot_count = fetch_pick.shape[1]
    stride = node_count // slot_count
    part, width = tokens.shape
    order = ring_order(lax.axis_size("local"))
    size = len(order)

    x_parts = ring_gather(tokens, order, size // 2)
    dy_parts = ring_gather(cotangent, order, size - 1 - size // 2)

    place = jnp.asarray([order.index(i) for i in range(size)], jnp.int32)[my_local]
    sources = jnp.asarray(order + order, jnp.int32)
    sources = lax.dynamic_slice(sources, (place,), (size,))
    ring_routes = routes.reshape(size, part)[sources].reshape(1, size * part)
    ring_weight = route_weight.reshape(size, part)[sources].reshape(1, size * part)

    def chosen_local(round_index):
        reader = (my_node + round_index * stride) % node_count
        return fetch_pick[reader, round_index]

    chosen = [chosen_local(r) for r in range(slot_count)]
    read = []
    for r in range(slot_count):
        panel = lax.dynamic_index_in_dim(panels, chosen[r], 0, keepdims=False)
        read.append(from_behind(panel, "node", r * stride) if r else panel)

    acts, grads = [None] * slot_count, [None] * slot_count
    for r in list(range(1, slot_count)) + [0]:
        acts[r], grad = slot_pass(r, x_parts, dy_parts, read[r], ring_routes, ring_weight)
        grads[r] = from_behind(grad, "node", node_count - r * stride) if r else grad

    first = size // 2
    early = [("mixed", first), ("grad", size - 1 - first), ("mixed", first + 1), ("grad", first)]
    late = [
        (kind, d)
        for hop in range(first, -1, -1)
        for d in {hop: 0, size - hop: 0}
        if d < size
        for kind in ("mixed", "grad")
        if (kind, d) not in early
    ]
    done = dict(zip(early, chunk_pass(early, acts, read, part)))
    done.update(zip(late, chunk_pass(late, acts, read, part)))
    mixed = ring_scatter([done["mixed", d] for d in range(size)], order, size // 2)
    token_grad = ring_scatter([done["grad", d] for d in range(size)], order, size - 1 - size // 2)

    panel_grad = jnp.stack(
        [
            sum(jnp.where(chosen[r] == e, grads[r].astype(F32), 0.0) for r in range(slot_count))
            for e in range(panels.shape[0])
        ]
    ).astype(BF16)
    return mixed, token_grad, panel_grad


def solution(mesh):
    return jax.shard_map(
        body,
        mesh=mesh,
        in_specs=(
            P(("node", "local"), None),
            P(("node", "local"), None),
            P("node", None),
            P("node", None),
            P(),
            P("node", None, "local", None),
        ),
        out_specs=(
            P(("node", "local"), None),
            P(("node", "local"), None),
            P("node", None, "local", None),
        ),
        check_vma=False,
    )
```

time: 408 us -> 261 us (0.64)
  waiting for transfers between devices: 223 us -> 104 us
  Pallas kernels: 0 us -> 74.3 us
  local copies, waits for them, and re-layouts: 77.9 us -> 17.8 us
  matrix products: 53.7 us -> 0 us
  starting transfers between devices: 7.35 us -> 35.4 us
  other arithmetic: 22.5 us -> 13.8 us
  between operations: 22.2 us -> 15.4 us
    all_gather x2 -> x0, waiting for transfers between devices: 97.2 us -> none  [the longest x1 50.5 us: body(): lax.all_gather(tokens, 'local', axis=0, tiled=True)]
    pallas_call x0 -> x6, Pallas kernels: none -> 74.3 us  [the longest x4 49.7 us: slot_pass(): pl.pallas_call(lambda *refs: slot_kernel(slot, parts, *refs), out_shape=(...]
    dot_general x36 -> x0, matrix products: 53.7 us -> none  [the longest x4 7.94 us: expert_pass(): lax.dot_general(slot_tokens, panel[0], contract_last, preferred_element_t...]
    gather x4 -> x2, local copies, waits for them, and re-layouts: 50 us -> 1.11 us  [the longest x1 0.56 us: body(): route_weight.reshape(size, part)[sources].reshape(1, size * part)]
    reduce_scatter x2 -> x0, waiting for transfers between devices: 43.8 us -> none  [the longest x1 43.8 us: body(): lax.psum_scatter(grad_part.astype(jnp.bfloat16), 'local', scatter_dimensi...]
    ppermute x6 -> x34, starting transfers between devices: 6.98 us -> 35.4 us  [the longest x28 33.9 us: ring_step(): lax.ppermute(block, 'local', [(order[i], order[(i + distance) % size]) fo...]
    ppermute x6 -> x34, waiting for transfers between devices: 80.6 us -> 104 us  [the longest x28 99.9 us: ring_step(): lax.ppermute(block, 'local', [(order[i], order[(i + distance) % size]) fo...]
    concatenate x2 -> x0, local copies, waits for them, and re-layouts: 9.6 us -> none  [the longest x1 4.8 us: body(): slot_dy = jnp.concatenate([group_dy, zero_row], axis=0)[source]]
  transfers between devices with their start and end apart: 10 -> 34, of which waited for: 6 -> 18; matrix products, arithmetic and copies ran while one was open for 31% -> 7% of each run, Pallas kernels for 0% -> 29%
where the time goes in v1:
time: 261 us
  waiting for transfers between devices  104 us (40%)
  Pallas kernels  74.3 us (28%)
  starting transfers between devices  35.4 us (14%)
  local copies, waits for them, and re-layouts  17.8 us (7%)
  between operations  15.4 us (6%)
  other arithmetic  13.8 us (5%)
    ppermute x28, waiting for transfers between devices, ring_step(): lax.ppermute(block, 'local', [(order[i], order[(i + distance) % size]) fo...  99.9 us
    pallas_call x4, Pallas kernels, slot_pass(): pl.pallas_call(lambda *refs: slot_kernel(slot, parts, *refs), out_shape=(...  49.7 us
    ppermute x28, starting transfers between devices, ring_step(): lax.ppermute(block, 'local', [(order[i], order[(i + distance) % size]) fo...  33.9 us
    pallas_call x2, Pallas kernels, chunk_pass(): pl.pallas_call(lambda *refs: chunk_kernel(wanted, slots, part, *refs), ou...  24.6 us
    squeeze x1, local copies, waits for them, and re-layouts, body(): panel = lax.dynamic_index_in_dim(panels, chosen[r], 0, keepdims=False)  7.76 us
    another operation x2, other arithmetic, body(): jnp.stack([sum((jnp.where(chosen[r] == e, grads[r].astype(F32), 0.0) for...  7.05 us
    unnamed x38, local copies, waits for them, and re-layouts  6.81 us
  transfers between devices with their start and end apart: 34, of which 18 were waited for; matrix products, arithmetic and copies ran while one was open for 7% of the time, Pallas kernels for 29%

profile of v1, /device:TPU:0, one launch (start us, length us, event | category | flops | bytes accessed | tf_op | source)
XLA Modules:
  0.0 260.7 jit_solution(9671066738955290542)
XLA Ops:
  0.6 3.0 %collective-permute-start.7 = (bf16[128,2048]{1,0:T(8,128)(2,1)}, bf16[128,2048]{1,0:T(8,128)(2,1)S(1)}, u32[]{:S(2)}, u32[]{:S(2)}) collective-permute-start(bf16[128,2048]{1,0:T(8,128)(2,1)} %refs_8_.7), channel_id=1, source_target_pairs={{0,1},{2,0},{4,2},{6,4},{7,6},{5,7},{3,5},{1,3},{8,9},{10,8},{12,1... | collective-permute-start | bytes 1572872 | tf_op jit(solution)/shard_map/ppermute | solution.py:37
  3.6 0.2 collective-permute-start.3
  3.8 2.0 collective-permute-start.11
  5.8 1.5 constant_dynamic-slice_fusion.3
  14.9 1.8 collective-permute-done.7.refs_9_
  16.7 2.0 collective-permute-start.8
  18.8 11.2 %collective-permute-done.11.refs_15_ = bf16[128,2048]{1,0:T(8,128)(2,1)} collective-permute-done((bf16[128,2048]{1,0:T(8,128)(2,1)}, bf16[128,2048]{1,0:T(8,128)(2,1)}, u32[]{:S(2)}, u32[]{:S(2)}) %collective-permute-start.11) | collective-permute-done | bytes 524320 | tf_op jit(solution)/shard_map/ppermute | solution.py:37
  30.2 7.8 %dynamic-slice_bitcast_fusion = (bf16[3,176,2048]{2,1,0:T(8,128)(2,1)}, bf16[3,176,2048]{2,1,0:T(8,128)(2,1)}, bf16[3,176,2048]{2,1,0:T(8,128)(2,1)}, bf16[3,176,2048]{2,1,0:T(8,128)(2,1)}) fusion(bf16[2,3,176,2048]{3,2,1,0:T(8,128)(2,1)} %param.13, s32[]{:T(128)S(6)} %select_n.118, s32[]{:T(128)S(6)} %select_n.112, s32[]{:T(128)S(6)} %select_n.106, ...), kind=kLoop, calls=%fused_computation.21 | loop fusion | bytes 17301520 | tf_op jit(solution)/shard_map/jit(dynamic_index_in_dim)/squeeze | solution.py:207
  37.9 2.0 collective-permute-start.1
  39.9 1.6 collective-permute-start.9
  41.5 0.5 collective-permute-start.5
  41.9 0.8 copy-done.7
  42.7 9.7 %collective-permute-done.12.refs_14_ = bf16[128,2048]{1,0:T(8,128)(2,1)S(1)} collective-permute-done((bf16[128,2048]{1,0:T(8,128)(2,1)}, bf16[128,2048]{1,0:T(8,128)(2,1)S(1)}, u32[]{:S(2)}, u32[]{:S(2)}) %collective-permute-start.12) | collective-permute-done | bytes 524320 | tf_op jit(solution)/shard_map/ppermute | solution.py:37
  52.4 1.5 collective-permute-start.15
  53.9 0.8 collective-permute-start.13
  54.7 9.2 %collective-permute-done.9.refs_11_ = bf16[128,2048]{1,0:T(8,128)(2,1)} collective-permute-done((bf16[128,2048]{1,0:T(8,128)(2,1)S(1)}, bf16[128,2048]{1,0:T(8,128)(2,1)}, u32[]{:S(2)}, u32[]{:S(2)}) %collective-permute-start.9) | collective-permute-done | bytes 524320 | tf_op jit(solution)/shard_map/ppermute | solution.py:37
  63.9 1.7 collective-permute-start.2
  65.5 0.8 copy-done.9
  66.3 7.1 %collective-permute-done.13.refs_13_ = bf16[128,2048]{1,0:T(8,128)(2,1)S(1)} collective-permute-done((bf16[128,2048]{1,0:T(8,128)(2,1)S(1)}, bf16[128,2048]{1,0:T(8,128)(2,1)S(1)}, u32[]{:S(2)}, u32[]{:S(2)}) %collective-permute-start.13) | collective-permute-done | bytes 524320 | tf_op jit(solution)/shard_map/ppermute | solution.py:37
  73.4 1.6 collective-permute-start.10
  75.0 3.7 %collective-permute-done.2.refs_3_ = bf16[128,2048]{1,0:T(8,128)(2,1)S(1)} collective-permute-done((bf16[128,2048]{1,0:T(8,128)(2,1)S(1)}, bf16[128,2048]{1,0:T(8,128)(2,1)S(1)}, u32[]{:S(2)}, u32[]{:S(2)}) %collective-permute-start.2) | collective-permute-done | bytes 524320 | tf_op jit(solution)/shard_map/ppermute | solution.py:37
  78.7 0.8 copy-done.11
  79.5 1.8 collective-permute-start.6
  81.2 0.6 dynamic_slice.33
  83.9 0.6 gather_fusion
  84.5 0.6 gather_fusion.1
  85.0 3.9 %collective-permute-done.10.refs_12_ = bf16[128,2048]{1,0:T(8,128)(2,1)} collective-permute-done((bf16[128,2048]{1,0:T(8,128)(2,1)}, bf16[128,2048]{1,0:T(8,128)(2,1)}, u32[]{:S(2)}, u32[]{:S(2)}) %collective-permute-start.10) | collective-permute-done | bytes 524320 | tf_op jit(solution)/shard_map/ppermute | solution.py:37
  88.9 2.6 collective-permute-done.6.refs_4_
  91.5 1.0 copy-done.8
  92.5 1.0 copy-done.10
  93.5 1.0 copy-done.12
  94.6 12.4 %slot_0.1 = (bf16[528,1024]{1,0:T(8,128)(2,1)}, bf16[3,176,2048]{2,1,0:T(8,128)(2,1)}) custom-call(bf16[128,2048]{1,0:T(8,128)(2,1)S(1)} %copy-done.5, bf16[128,2048]{1,0:T(8,128)(2,1)S(1)} %collective-permute-done.refs_1_, bf16[128,2048]{1,0:T(8,128)(2,1)S(1)} %copy-done.10, bf16[128,2048]{1,0:T(8,128)(2,1)S(1)} %copy-done.12, ...), custom_call_target="tpu_custom_call" | custom-call | flops 4429185024 | bytes 12713984 | tf_op jit(solution)/shard_map/slot_0/pallas_call | solution.py:121
  107.0 12.4 %slot_3.1 = (bf16[528,1024]{1,0:T(8,128)(2,1)}, bf16[3,176,2048]{2,1,0:T(8,128)(2,1)}) custom-call(bf16[128,2048]{1,0:T(8,128)(2,1)S(1)} %copy-done.5, bf16[128,2048]{1,0:T(8,128)(2,1)S(1)} %collective-permute-done.refs_1_, bf16[128,2048]{1,0:T(8,128)(2,1)S(1)} %copy-done.10, bf16[128,2048]{1,0:T(8,128)(2,1)S(1)} %copy-done.12, ...), custom_call_target="tpu_custom_call" | custom-call | flops 4429185024 | bytes 12713984 | tf_op jit(solution)/shard_map/slot_3/pallas_call | solution.py:121
  119.4 4.1 %collective-permute-done.15.refs_16_.refs_6_ = bf16[3,176,2048]{2,1,0:T(8,128)(2,1)} collective-permute-done((bf16[3,176,2048]{2,1,0:T(8,128)(2,1)}, bf16[3,176,2048]{2,1,0:T(8,128)(2,1)}, u32[]{:S(2)}, u32[]{:S(2)}) %collective-permute-start.15) | collective-permute-done | bytes 2162720 | tf_op jit(solution)/shard_map/ppermute | solution.py:28
  123.5 12.4 %slot_2.1 = (bf16[528,1024]{1,0:T(8,128)(2,1)}, bf16[3,176,2048]{2,1,0:T(8,128)(2,1)}) custom-call(bf16[128,2048]{1,0:T(8,128)(2,1)S(1)} %copy-done.5, bf16[128,2048]{1,0:T(8,128)(2,1)S(1)} %collective-permute-done.refs_1_, bf16[128,2048]{1,0:T(8,128)(2,1)S(1)} %copy-done.10, bf16[128,2048]{1,0:T(8,128)(2,1)S(1)} %copy-done.12, ...), custom_call_target="tpu_custom_call" | custom-call | flops 4429185024 | bytes 12713984 | tf_op jit(solution)/shard_map/slot_2/pallas_call | solution.py:121
  136.0 12.5 %slot_1.1 = (bf16[528,1024]{1,0:T(8,128)(2,1)}, bf16[3,176,2048]{2,1,0:T(8,128)(2,1)}) custom-call(bf16[128,2048]{1,0:T(8,128)(2,1)S(1)} %copy-done.5, bf16[128,2048]{1,0:T(8,128)(2,1)S(1)} %collective-permute-done.refs_1_, bf16[128,2048]{1,0:T(8,128)(2,1)S(1)} %copy-done.10, bf16[128,2048]{1,0:T(8,128)(2,1)S(1)} %copy-done.12, ...), custom_call_target="tpu_custom_call" | custom-call | flops 4429185024 | bytes 12713984 | tf_op jit(solution)/shard_map/slot_1/pallas_call | solution.py:121
  148.5 1.2 copy-done.4
  149.7 8.0 %chunks_4.1 = (bf16[128,2048]{1,0:T(8,128)(2,1)S(1)}, bf16[128,2048]{1,0:T(8,128)(2,1)S(1)}, bf16[128,2048]{1,0:T(8,128)(2,1)S(1)}, bf16[128,2048]{1,0:T(8,128)(2,1)S(1)}) custom-call(bf16[528,1024]{1,0:T(8,128)(2,1)S(1)} %copy-done.2, bf16[528,1024]{1,0:T(8,128)(2,1)S(1)} %copy-done.4, bf16[528,1024]{1,0:T(8,128)(2,1)S(1)} %copy-done.3, ...), custom_call_target="tpu_custom_call" | custom-call | flops 2214592512 | bytes 10747904 | tf_op jit(solution)/shard_map/chunks_4/pallas_call | solution.py:166
  157.8 2.5 collective-permute-start.24
  160.2 2.0 collective-permute-start.17
  162.3 16.5 %chunks_12.1 = (bf16[128,2048]{1,0:T(8,128)(2,1)S(1)}, bf16[128,2048]{1,0:T(8,128)(2,1)S(1)}, bf16[128,2048]{1,0:T(8,128)(2,1)S(1)}, bf16[128,2048]{1,0:T(8,128)...) custom-call(bf16[528,1024]{1,0:T(8,128)(2,1)} %get-tuple-element.27., ...), custom_call_target="tpu_custom_call" | custom-call | flops 6643777536 | bytes 14942208 | tf_op jit(solution)/shard_map/chunks_12/pallas_call | solution.py:166
  179.0 2.1 collective-permute-start.25
  181.2 2.2 collective-permute-done.17
  183.4 1.2 collective-permute-start.28
  184.7 8.9 %collective-permute-done.21 = bf16[128,2048]{1,0:T(8,128)(2,1)S(1)} collective-permute-done((bf16[128,2048]{1,0:T(8,128)(2,1)S(1)}, bf16[128,2048]{1,0:T(8,128)(2,1)S(1)}, u32[]{:S(2)}, u32[]{:S(2)}) %collective-permute-start.21) | collective-permute-done | bytes 524320 | tf_op jit(solution)/shard_map/ppermute | solution.py:37
  193.7 1.8 collective-permute-start.18
  195.6 6.5 %collective-permute-done.28 = bf16[128,2048]{1,0:T(8,128)(2,1)S(1)} collective-permute-done((bf16[128,2048]{1,0:T(8,128)(2,1)S(1)}, bf16[128,2048]{1,0:T(8,128)(2,1)S(1)}, u32[]{:S(2)}, u32[]{:S(2)}) %collective-permute-start.28) | collective-permute-done | bytes 524320 | tf_op jit(solution)/shard_map/ppermute | solution.py:37
  202.3 1.4 collective-permute-done.18
  203.7 0.7 collective-permute-start.29
  204.5 2.1 collective-permute-start.19
  206.8 15.4 %collective-permute-done.29 = bf16[128,2048]{1,0:T(8,128)(2,1)S(1)} collective-permute-done((bf16[128,2048]{1,0:T(8,128)(2,1)S(1)}, bf16[128,2048]{1,0:T(8,128)(2,1)S(1)}, u32[]{:S(2)}, u32[]{:S(2)}) %collective-permute-start.29) | collective-permute-done | bytes 524320 | tf_op jit(solution)/shard_map/ppermute | solution.py:37
  222.3 1.6 collective-permute-start.26
  223.9 0.4 collective-permute-start.30
  224.4 0.9 add_convert_fusion.7
  225.4 11.3 %collective-permute-done.26 = bf16[128,2048]{1,0:T(8,128)(2,1)} collective-permute-done((bf16[128,2048]{1,0:T(8,128)(2,1)S(1)}, bf16[128,2048]{1,0:T(8,128)(2,1)}, u32[]{:S(2)}, u32[]{:S(2)}) %collective-permute-start.26) | collective-permute-done | bytes 524320 | tf_op jit(solution)/shard_map/ppermute | solution.py:37
  236.8 0.7 collective-permute-start.23
  237.5 0.6 collective-permute-done.30
  238.1 1.6 collective-permute-start.20
  244.7 2.4 add_convert_fusion
  247.1 3.6 %collective-permute-done.23 = bf16[128,2048]{1,0:T(8,128)(2,1)} collective-permute-done((bf16[128,2048]{1,0:T(8,128)(2,1)}, bf16[128,2048]{1,0:T(8,128)(2,1)}, u32[]{:S(2)}, u32[]{:S(2)}) %collective-permute-start.23) | collective-permute-done | bytes 524320 | tf_op jit(solution)/shard_map/ppermute | solution.py:37
  250.6 0.8 collective-permute-done.20
  251.4 2.2 add_convert_fusion.6
  253.7 4.6 %fusion.9 = (bf16[1,3,176,2048]{3,2,1,0:T(8,128)(2,1)S(1)}, bf16[1,3,176,2048]{3,2,1,0:T(8,128)(2,1)S(1)}) fusion(bf16[3,176,2048]{2,1,0:T(8,128)(2,1)} %collective-permute-done.33, bf16[3,176,2048]{2,1,0:T(8,128)(2,1)} %collective-permute-done.32, bf16[3,176,2048]{2,1,0:T(8,128)(2,1)} %collective-permute-done.31, bf16[3,176,2048]{2,1,0:T(8,128)(2,1)S(1)} %copy-done.13, ...), kind=kLoop, calls=%fused_computation.20 | loop fusion | flops 21626880 | bytes 12976136 | tf_op jit(solution)/shard_map/stack | solution.py:230
  258.3 2.4 pad_maximum_fusion
  (69 shorter events, 1.7 us)
Async XLA Ops:
  0.6 83.3 %copy-start = (s32[1024,1]{0,1:T(1,128)S(1)}, s32[1024,1]{0,1:T(1,128)}, u32[]{:S(2)}) copy-start(s32[1024,1]{0,1:T(1,128)} %param.10) | copy-start | bytes 12292
  0.6 16.0 %collective-permute-start.7 = (bf16[128,2048]{1,0:T(8,128)(2,1)}, bf16[128,2048]{1,0:T(8,128)(2,1)S(1)}, u32[]{:S(2)}, u32[]{:S(2)}) collective-permute-start(bf16[128,2048]{1,0:T(8,128)(2,1)} %refs_8_.7), channel_id=1, source_target_pairs={{0,1},{2,0},{4,2},{6,4},{7,6},{5,7},{3,5},{1,3},{8,9},{10,8},{12,1... | collective-permute-start | bytes 1572872 | tf_op jit(solution)/shard_map/ppermute | solution.py:37
  3.6 15.1 %collective-permute-start.3 = (bf16[128,2048]{1,0:T(8,128)(2,1)}, bf16[128,2048]{1,0:T(8,128)(2,1)S(1)}, u32[]{:S(2)}, u32[]{:S(2)}) collective-permute-start(bf16[128,2048]{1,0:T(8,128)(2,1)} %refs_0_.7), channel_id=1, source_target_pairs={{0,2},{2,4},{4,6},{6,7},{7,5},{5,3},{3,1},{1,0},{8,10},{10,12},{12... | collective-permute-start | bytes 1572872 | tf_op jit(solution)/shard_map/ppermute | solution.py:37
  3.8 26.2 %collective-permute-start.11 = (bf16[128,2048]{1,0:T(8,128)(2,1)}, bf16[128,2048]{1,0:T(8,128)(2,1)}, u32[]{:S(2)}, u32[]{:S(2)}) collective-permute-start(bf16[128,2048]{1,0:T(8,128)(2,1)} %refs_8_.7), channel_id=1, source_target_pairs={{0,2},{2,4},{4,6},{6,7},{7,5},{5,3},{3,1},{1,0},{8,10},{10,12},{12... | collective-permute-start | bytes 1572872 | tf_op jit(solution)/shard_map/ppermute | solution.py:37
  5.8 32.2 %collective-permute-start = (bf16[128,2048]{1,0:T(8,128)(2,1)}, bf16[128,2048]{1,0:T(8,128)(2,1)S(1)}, u32[]{:S(2)}, u32[]{:S(2)}) collective-permute-start(bf16[128,2048]{1,0:T(8,128)(2,1)} %refs_0_.7), channel_id=1, source_target_pairs={{0,1},{2,0},{4,2},{6,4},{7,6},{5,7},{3,5},{1,3},{8,9},{10,8},{12,1... | collective-permute-start | bytes 1572872 | tf_op jit(solution)/shard_map/ppermute | solution.py:37
  14.8 66.4 %copy-start.18 = (s32[8]{0:T(128)S(1)}, s32[8]{0:T(128)}, u32[]{:S(2)}) copy-start(s32[8]{0:T(128)} %constant.61.clone) | copy-start | bytes 100
  14.8 69.0 %copy-start.17 = (s32[16]{0:T(128)S(1)}, s32[16]{0:T(128)}, u32[]{:S(2)}) copy-start(s32[16]{0:T(128)} %constant.62.clone) | copy-start | bytes 196
  14.8 69.6 %copy-start.14 = (f32[1024,1]{0,1:T(1,128)S(1)}, f32[1024,1]{0,1:T(1,128)}, u32[]{:S(2)}) copy-start(f32[1024,1]{0,1:T(1,128)} %param.11) | copy-start | bytes 12292
  14.9 76.6 %copy-start.5 = (bf16[128,2048]{1,0:T(8,128)(2,1)S(1)}, bf16[128,2048]{1,0:T(8,128)(2,1)}, u32[]{:S(2)}) copy-start(bf16[128,2048]{1,0:T(8,128)(2,1)} %refs_0_.7) | copy-start | bytes 1572868
  14.9 76.6 %copy-start.6 = (bf16[128,2048]{1,0:T(8,128)(2,1)S(1)}, bf16[128,2048]{1,0:T(8,128)(2,1)}, u32[]{:S(2)}) copy-start(bf16[128,2048]{1,0:T(8,128)(2,1)} %refs_8_.7) | copy-start | bytes 1572868
  16.7 23.2 %collective-permute-start.8 = (bf16[128,2048]{1,0:T(8,128)(2,1)S(1)}, bf16[128,2048]{1,0:T(8,128)(2,1)S(1)}, u32[]{:S(2)}, u32[]{:S(2)}) collective-permute-start(bf16[128,2048]{1,0:T(8,128)(2,1)S(1)} %collective-permute-done.7.refs_9_), channel_id=1, source_target_pairs={{0,1},{2,0},{4,2},{6,4},{7,6},{5,7},{3,5},{1,3},{8,9},{10,8},{12,1... | collective-permute-start | bytes 1572872 | tf_op jit(solution)/shard_map/ppermute | solution.py:37
  18.7 22.8 %collective-permute-start.4 = (bf16[128,2048]{1,0:T(8,128)(2,1)S(1)}, bf16[128,2048]{1,0:T(8,128)(2,1)S(1)}, u32[]{:S(2)}, u32[]{:S(2)}) collective-permute-start(bf16[128,2048]{1,0:T(8,128)(2,1)S(1)} %collective-permute-done.3.refs_7_), channel_id=1, source_target_pairs={{0,2},{2,4},{4,6},{6,7},{7,5},{5,3},{3,1},{1,0},{8,10},{10,12},{12... | collective-permute-start | bytes 1572872 | tf_op jit(solution)/shard_map/ppermute | solution.py:37
  30.0 22.4 %collective-permute-start.12 = (bf16[128,2048]{1,0:T(8,128)(2,1)}, bf16[128,2048]{1,0:T(8,128)(2,1)S(1)}, u32[]{:S(2)}, u32[]{:S(2)}) collective-permute-start(bf16[128,2048]{1,0:T(8,128)(2,1)} %collective-permute-done.11.refs_15_), channel_id=1, source_target_pairs={{0,2},{2,4},{4,6},{6,7},{7,5},{5,3},{3,1},{1,0},{8,10},{10,12},{12... | collective-permute-start | bytes 1572872 | tf_op jit(solution)/shard_map/ppermute | solution.py:37
  37.9 69.1 %collective-permute-start.16 = (bf16[3,176,2048]{2,1,0:T(8,128)(2,1)}, bf16[3,176,2048]{2,1,0:T(8,128)(2,1)}, u32[]{:S(2)}, u32[]{:S(2)}) collective-permute-start(bf16[3,176,2048]{2,1,0:T(8,128)(2,1)} %get-tuple-element.53), channel_id=1, source_target_pairs={{8,0},{16,8},{24,16},{0,24},{9,1},{17,9},{25,17},{1,25},{10,2},{18... | collective-permute-start | bytes 6488072 | tf_op jit(solution)/shard_map/ppermute | solution.py:28
  37.9 16.0 %collective-permute-start.1 = (bf16[128,2048]{1,0:T(8,128)(2,1)S(1)}, bf16[128,2048]{1,0:T(8,128)(2,1)S(1)}, u32[]{:S(2)}, u32[]{:S(2)}) collective-permute-start(bf16[128,2048]{1,0:T(8,128)(2,1)S(1)} %collective-permute-done.refs_1_), channel_id=1, source_target_pairs={{0,1},{2,0},{4,2},{6,4},{7,6},{5,7},{3,5},{1,3},{8,9},{10,8},{12,1... | collective-permute-start | bytes 1572872 | tf_op jit(solution)/shard_map/ppermute | solution.py:37
  39.9 24.0 %collective-permute-start.9 = (bf16[128,2048]{1,0:T(8,128)(2,1)S(1)}, bf16[128,2048]{1,0:T(8,128)(2,1)}, u32[]{:S(2)}, u32[]{:S(2)}) collective-permute-start(bf16[128,2048]{1,0:T(8,128)(2,1)S(1)} %collective-permute-done.8.refs_10_), channel_id=1, source_target_pairs={{0,1},{2,0},{4,2},{6,4},{7,6},{5,7},{3,5},{1,3},{8,9},{10,8},{12,1... | collective-permute-start | bytes 1572872 | tf_op jit(solution)/shard_map/ppermute | solution.py:37
  41.5 24.8 %collective-permute-start.5 = (bf16[128,2048]{1,0:T(8,128)(2,1)S(1)}, bf16[128,2048]{1,0:T(8,128)(2,1)}, u32[]{:S(2)}, u32[]{:S(2)}) collective-permute-start(bf16[128,2048]{1,0:T(8,128)(2,1)S(1)} %collective-permute-done.4.refs_6_), channel_id=1, source_target_pairs={{0,2},{2,4},{4,6},{6,7},{7,5},{5,3},{3,1},{1,0},{8,10},{10,12},{12... | collective-permute-start | bytes 1572872 | tf_op jit(solution)/shard_map/ppermute | solution.py:37
  41.9 0.8 copy-start.7
  52.4 26.3 %copy-start.15 = (bf16[128,2048]{1,0:T(8,128)(2,1)}, bf16[128,2048]{1,0:T(8,128)(2,1)S(1)}, u32[]{:S(2)}) copy-start(bf16[128,2048]{1,0:T(8,128)(2,1)S(1)} %collective-permute-done.12.refs_14_) | copy-start | bytes 1572868
  52.4 71.1 %collective-permute-start.15 = (bf16[3,176,2048]{2,1,0:T(8,128)(2,1)}, bf16[3,176,2048]{2,1,0:T(8,128)(2,1)}, u32[]{:S(2)}, u32[]{:S(2)}) collective-permute-start(bf16[3,176,2048]{2,1,0:T(8,128)(2,1)} %get-tuple-element.56), channel_id=1, source_target_pairs={{16,0},{24,8},{0,16},{8,24},{17,1},{25,9},{1,17},{9,25},{18,2},{26... | collective-permute-start | bytes 6488072 | tf_op jit(solution)/shard_map/ppermute | solution.py:28
  53.9 19.5 %collective-permute-start.13 = (bf16[128,2048]{1,0:T(8,128)(2,1)S(1)}, bf16[128,2048]{1,0:T(8,128)(2,1)S(1)}, u32[]{:S(2)}, u32[]{:S(2)}) collective-permute-start(bf16[128,2048]{1,0:T(8,128)(2,1)S(1)} %collective-permute-done.12.refs_14_), channel_id=1, source_target_pairs={{0,2},{2,4},{4,6},{6,7},{7,5},{5,3},{3,1},{1,0},{8,10},{10,12},{12... | collective-permute-start | bytes 1572872 | tf_op jit(solution)/shard_map/ppermute | solution.py:37
  63.9 14.8 %collective-permute-start.2 = (bf16[128,2048]{1,0:T(8,128)(2,1)S(1)}, bf16[128,2048]{1,0:T(8,128)(2,1)S(1)}, u32[]{:S(2)}, u32[]{:S(2)}) collective-permute-start(bf16[128,2048]{1,0:T(8,128)(2,1)S(1)} %collective-permute-done.1.refs_2_), channel_id=1, source_target_pairs={{0,1},{2,0},{4,2},{6,4},{7,6},{5,7},{3,5},{1,3},{8,9},{10,8},{12,1... | collective-permute-start | bytes 1572872 | tf_op jit(solution)/shard_map/ppermute | solution.py:37
  65.5 0.8 copy-start.9
  66.3 69.7 %collective-permute-start.14 = (bf16[3,176,2048]{2,1,0:T(8,128)(2,1)}, bf16[3,176,2048]{2,1,0:T(8,128)(2,1)}, u32[]{:S(2)}, u32[]{:S(2)}) collective-permute-start(bf16[3,176,2048]{2,1,0:T(8,128)(2,1)} %get-tuple-element.54), channel_id=1, source_target_pairs={{24,0},{0,8},{8,16},{16,24},{25,1},{1,9},{9,17},{17,25},{26,2},{2,... | collective-permute-start | bytes 6488072 | tf_op jit(solution)/shard_map/ppermute | solution.py:28
  73.4 5.3 %copy-start.16 = (bf16[128,2048]{1,0:T(8,128)(2,1)}, bf16[128,2048]{1,0:T(8,128)(2,1)S(1)}, u32[]{:S(2)}) copy-start(bf16[128,2048]{1,0:T(8,128)(2,1)S(1)} %collective-permute-done.13.refs_13_) | copy-start | bytes 1572868
  73.4 15.5 %collective-permute-start.10 = (bf16[128,2048]{1,0:T(8,128)(2,1)}, bf16[128,2048]{1,0:T(8,128)(2,1)}, u32[]{:S(2)}, u32[]{:S(2)}) collective-permute-start(bf16[128,2048]{1,0:T(8,128)(2,1)} %collective-permute-done.9.refs_11_), channel_id=1, source_target_pairs={{0,1},{2,0},{4,2},{6,4},{7,6},{5,7},{3,5},{1,3},{8,9},{10,8},{12,1... | collective-permute-start | bytes 1572872 | tf_op jit(solution)/shard_map/ppermute | solution.py:37
  78.7 0.8 copy-start.11
  79.5 12.0 %collective-permute-start.6 = (bf16[128,2048]{1,0:T(8,128)(2,1)}, bf16[128,2048]{1,0:T(8,128)(2,1)}, u32[]{:S(2)}, u32[]{:S(2)}) collective-permute-start(bf16[128,2048]{1,0:T(8,128)(2,1)} %collective-permute-done.5.refs_5_), channel_id=1, source_target_pairs={{0,2},{2,4},{4,6},{6,7},{7,5},{5,3},{3,1},{1,0},{8,10},{10,12},{12... | collective-permute-start | bytes 1572872 | tf_op jit(solution)/shard_map/ppermute | solution.py:37
  91.5 1.0 copy-start.8
  92.5 1.0 copy-start.10
  93.5 1.0 copy-start.12
  119.4 134.2 %collective-permute-start.33 = (bf16[3,176,2048]{2,1,0:T(8,128)(2,1)}, bf16[3,176,2048]{2,1,0:T(8,128)(2,1)}, u32[]{:S(2)}, u32[]{:S(2)}) collective-permute-start(bf16[3,176,2048]{2,1,0:T(8,128)(2,1)} %get-tuple-element.50), channel_id=1, source_target_pairs={{24,0},{0,8},{8,16},{16,24},{25,1},{1,9},{9,17},{17,25},{26,2},{2,... | collective-permute-start | bytes 6488072 | tf_op jit(solution)/shard_map/ppermute | solution.py:28
  135.9 12.5 %copy-start.2 = (bf16[528,1024]{1,0:T(8,128)(2,1)S(1)}, bf16[528,1024]{1,0:T(8,128)(2,1)}, u32[]{:S(2)}) copy-start(bf16[528,1024]{1,0:T(8,128)(2,1)} %get-tuple-element.27.refs_0_) | copy-start | bytes 3244036
  135.9 12.5 %copy-start.3 = (bf16[528,1024]{1,0:T(8,128)(2,1)S(1)}, bf16[528,1024]{1,0:T(8,128)(2,1)}, u32[]{:S(2)}) copy-start(bf16[528,1024]{1,0:T(8,128)(2,1)} %get-tuple-element.29.refs_2_) | copy-start | bytes 3244036
  135.9 117.7 %collective-permute-start.32 = (bf16[3,176,2048]{2,1,0:T(8,128)(2,1)}, bf16[3,176,2048]{2,1,0:T(8,128)(2,1)}, u32[]{:S(2)}, u32[]{:S(2)}) collective-permute-start(bf16[3,176,2048]{2,1,0:T(8,128)(2,1)} %get-tuple-element.49), channel_id=1, source_target_pairs={{16,0},{24,8},{0,16},{8,24},{17,1},{25,9},{1,17},{9,25},{18,2},{26... | collective-permute-start | bytes 6488072 | tf_op jit(solution)/shard_map/ppermute | solution.py:28
  148.5 1.2 copy-start.4
  157.8 21.0 %collective-permute-start.24 = (bf16[128,2048]{1,0:T(8,128)(2,1)S(1)}, bf16[128,2048]{1,0:T(8,128)(2,1)S(1)}, u32[]{:S(2)}, u32[]{:S(2)}) collective-permute-start(bf16[128,2048]{1,0:T(8,128)(2,1)S(1)} %get-tuple-element.39), channel_id=1, source_target_pairs={{0,2},{2,4},{4,6},{6,7},{7,5},{5,3},{3,1},{1,0},{8,10},{10,12},{12... | collective-permute-start | bytes 1572872 | tf_op jit(solution)/shard_map/ppermute | solution.py:37
  160.2 18.7 %collective-permute-start.27 = (bf16[128,2048]{1,0:T(8,128)(2,1)S(1)}, bf16[128,2048]{1,0:T(8,128)(2,1)S(1)}, u32[]{:S(2)}, u32[]{:S(2)}) collective-permute-start(bf16[128,2048]{1,0:T(8,128)(2,1)S(1)} %get-tuple-element.42), channel_id=1, source_target_pairs={{0,1},{2,0},{4,2},{6,4},{7,6},{5,7},{3,5},{1,3},{8,9},{10,8},{12,1... | collective-permute-start | bytes 1572872 | tf_op jit(solution)/shard_map/ppermute | solution.py:37
  160.2 23.1 %collective-permute-start.17 = (bf16[128,2048]{1,0:T(8,128)(2,1)S(1)}, bf16[128,2048]{1,0:T(8,128)(2,1)S(1)}, u32[]{:S(2)}, u32[]{:S(2)}) collective-permute-start(bf16[128,2048]{1,0:T(8,128)(2,1)S(1)} %get-tuple-element.31), channel_id=1, source_target_pairs={{0,2},{2,4},{4,6},{6,7},{7,5},{5,3},{3,1},{1,0},{8,10},{10,12},{12... | collective-permute-start | bytes 1572872 | tf_op jit(solution)/shard_map/ppermute | solution.py:37
  178.8 14.9 %collective-permute-start.21 = (bf16[128,2048]{1,0:T(8,128)(2,1)S(1)}, bf16[128,2048]{1,0:T(8,128)(2,1)S(1)}, u32[]{:S(2)}, u32[]{:S(2)}) collective-permute-start(bf16[128,2048]{1,0:T(8,128)(2,1)S(1)} %get-tuple-element.35), channel_id=1, source_target_pairs={{0,1},{2,0},{4,2},{6,4},{7,6},{5,7},{3,5},{1,3},{8,9},{10,8},{12,1... | collective-permute-start | bytes 1572872 | tf_op jit(solution)/shard_map/ppermute | solution.py:37
  179.0 25.5 %collective-permute-start.25 = (bf16[128,2048]{1,0:T(8,128)(2,1)S(1)}, bf16[128,2048]{1,0:T(8,128)(2,1)S(1)}, u32[]{:S(2)}, u32[]{:S(2)}) collective-permute-start(bf16[128,2048]{1,0:T(8,128)(2,1)S(1)} %add_convert_fusion.5), channel_id=1, source_target_pairs={{0,2},{2,4},{4,6},{6,7},{7,5},{5,3},{3,1},{1,0},{8,10},{10,12},{12... | collective-permute-start | bytes 1572872 | tf_op jit(solution)/shard_map/ppermute | solution.py:37
  183.4 18.8 %collective-permute-start.28 = (bf16[128,2048]{1,0:T(8,128)(2,1)S(1)}, bf16[128,2048]{1,0:T(8,128)(2,1)S(1)}, u32[]{:S(2)}, u32[]{:S(2)}) collective-permute-start(bf16[128,2048]{1,0:T(8,128)(2,1)S(1)} %add_convert_fusion.3), channel_id=1, source_target_pairs={{0,1},{2,0},{4,2},{6,4},{7,6},{5,7},{3,5},{1,3},{8,9},{10,8},{12,1... | collective-permute-start | bytes 1572872 | tf_op jit(solution)/shard_map/ppermute | solution.py:37
  193.7 10.0 %collective-permute-start.18 = (bf16[128,2048]{1,0:T(8,128)(2,1)S(1)}, bf16[128,2048]{1,0:T(8,128)(2,1)S(1)}, u32[]{:S(2)}, u32[]{:S(2)}) collective-permute-start(bf16[128,2048]{1,0:T(8,128)(2,1)S(1)} %add_convert_fusion.11), channel_id=1, source_target_pairs={{0,2},{2,4},{4,6},{6,7},{7,5},{5,3},{3,1},{1,0},{8,10},{10,12},{12... | collective-permute-start | bytes 1572872 | tf_op jit(solution)/shard_map/ppermute | solution.py:37
  202.1 20.1 %collective-permute-start.22 = (bf16[128,2048]{1,0:T(8,128)(2,1)S(1)}, bf16[128,2048]{1,0:T(8,128)(2,1)S(1)}, u32[]{:S(2)}, u32[]{:S(2)}) collective-permute-start(bf16[128,2048]{1,0:T(8,128)(2,1)S(1)} %add_convert_fusion.8), channel_id=1, source_target_pairs={{0,1},{2,0},{4,2},{6,4},{7,6},{5,7},{3,5},{1,3},{8,9},{10,8},{12,1... | collective-permute-start | bytes 1572872 | tf_op jit(solution)/shard_map/ppermute | solution.py:37
  203.7 18.5 %collective-permute-start.29 = (bf16[128,2048]{1,0:T(8,128)(2,1)S(1)}, bf16[128,2048]{1,0:T(8,128)(2,1)S(1)}, u32[]{:S(2)}, u32[]{:S(2)}) collective-permute-start(bf16[128,2048]{1,0:T(8,128)(2,1)S(1)} %add_convert_fusion.2), channel_id=1, source_target_pairs={{0,1},{2,0},{4,2},{6,4},{7,6},{5,7},{3,5},{1,3},{8,9},{10,8},{12,1... | collective-permute-start | bytes 1572872 | tf_op jit(solution)/shard_map/ppermute | solution.py:37
  204.5 19.4 %collective-permute-start.19 = (bf16[128,2048]{1,0:T(8,128)(2,1)S(1)}, bf16[128,2048]{1,0:T(8,128)(2,1)S(1)}, u32[]{:S(2)}, u32[]{:S(2)}) collective-permute-start(bf16[128,2048]{1,0:T(8,128)(2,1)S(1)} %add_convert_fusion.10), channel_id=1, source_target_pairs={{0,2},{2,4},{4,6},{6,7},{7,5},{5,3},{3,1},{1,0},{8,10},{10,12},{12... | collective-permute-start | bytes 1572872 | tf_op jit(solution)/shard_map/ppermute | solution.py:37
  222.1 31.5 %collective-permute-start.31 = (bf16[3,176,2048]{2,1,0:T(8,128)(2,1)}, bf16[3,176,2048]{2,1,0:T(8,128)(2,1)}, u32[]{:S(2)}, u32[]{:S(2)}) collective-permute-start(bf16[3,176,2048]{2,1,0:T(8,128)(2,1)} %get-tuple-element.48), channel_id=1, source_target_pairs={{8,0},{16,8},{24,16},{0,24},{9,1},{17,9},{25,17},{1,25},{10,2},{18... | collective-permute-start | bytes 6488072 | tf_op jit(solution)/shard_map/ppermute | solution.py:28
  222.3 14.5 %collective-permute-start.26 = (bf16[128,2048]{1,0:T(8,128)(2,1)S(1)}, bf16[128,2048]{1,0:T(8,128)(2,1)}, u32[]{:S(2)}, u32[]{:S(2)}) collective-permute-start(bf16[128,2048]{1,0:T(8,128)(2,1)S(1)} %add_convert_fusion.4), channel_id=1, source_target_pairs={{0,2},{2,4},{4,6},{6,7},{7,5},{5,3},{3,1},{1,0},{8,10},{10,12},{12... | collective-permute-start | bytes 1572872 | tf_op jit(solution)/shard_map/ppermute | solution.py:37
  223.9 14.2 %collective-permute-start.30 = (bf16[128,2048]{1,0:T(8,128)(2,1)S(1)}, bf16[128,2048]{1,0:T(8,128)(2,1)}, u32[]{:S(2)}, u32[]{:S(2)}) collective-permute-start(bf16[128,2048]{1,0:T(8,128)(2,1)S(1)} %add_convert_fusion.1), channel_id=1, source_target_pairs={{0,1},{2,0},{4,2},{6,4},{7,6},{5,7},{3,5},{1,3},{8,9},{10,8},{12,1... | collective-permute-start | bytes 1572872 | tf_op jit(solution)/shard_map/ppermute | solution.py:37
  225.4 28.3 %copy-start.13 = (bf16[3,176,2048]{2,1,0:T(8,128)(2,1)S(1)}, bf16[3,176,2048]{2,1,0:T(8,128)(2,1)}, u32[]{:S(2)}) copy-start(bf16[3,176,2048]{2,1,0:T(8,128)(2,1)} %get-tuple-element.47) | copy-start | bytes 6488068
  236.8 13.9 %collective-permute-start.23 = (bf16[128,2048]{1,0:T(8,128)(2,1)}, bf16[128,2048]{1,0:T(8,128)(2,1)}, u32[]{:S(2)}, u32[]{:S(2)}) collective-permute-start(bf16[128,2048]{1,0:T(8,128)(2,1)} %add_convert_fusion.7), channel_id=1, source_target_pairs={{0,1},{2,0},{4,2},{6,4},{7,6},{5,7},{3,5},{1,3},{8,9},{10,8},{12,1... | collective-permute-start | bytes 1572872 | tf_op jit(solution)/shard_map/ppermute | solution.py:37
  238.1 13.3 %collective-permute-start.20 = (bf16[128,2048]{1,0:T(8,128)(2,1)S(1)}, bf16[128,2048]{1,0:T(8,128)(2,1)}, u32[]{:S(2)}, u32[]{:S(2)}) collective-permute-start(bf16[128,2048]{1,0:T(8,128)(2,1)S(1)} %add_convert_fusion.9), channel_id=1, source_target_pairs={{0,2},{2,4},{4,6},{6,7},{7,5},{5,3},{3,1},{1,0},{8,10},{10,12},{12... | collective-permute-start | bytes 1572872 | tf_op jit(solution)/shard_map/ppermute | solution.py:37
  258.3 2.4 copy-start.1

commit v2 on v1

v2 whole, which is shorter than its diff:
```python
import jax
import jax.numpy as jnp
from jax import lax
from jax.experimental import pallas as pl
from jax.experimental.pallas import tpu as pltpu
from jax.sharding import PartitionSpec as P

BF16 = jnp.bfloat16
F32 = jnp.float32
VMEM_LIMIT = 24 * 1024 * 1024
CONTRACT_LAST = (((1,), (1,)), ((), ()))
CONTRACT_FIRST = (((0,), (0,)), ((), ()))


def whole_in_vmem():
    return pl.BlockSpec(memory_space=pltpu.VMEM)


def untouched():
    return pl.BlockSpec(memory_space=pl.ANY)


def tile_of(size, most):
    tile = min(size, most)
    while size % tile:
        tile -= 1
    return tile


def from_behind(block, axis, distance):
    size = lax.axis_size(axis)
    return lax.ppermute(block, axis, [((i - distance) % size, i) for i in range(size)])


def ring_order(size):
    return list(range(0, size, 2)) + list(range(1, size, 2))[::-1]


def ring_source(size, ahead):
    me = lax.axis_index("local")
    half = lax.div(size + 1, 2)
    place = jnp.where(lax.rem(me, 2) == 0, lax.div(me, 2), size - 1 - lax.div(me, 2))
    there = lax.rem(place + ahead, size)
    return jnp.where(there < half, 2 * there, 2 * (size - 1 - there) + 1)


def chosen_of(fetch_pick, slot, node_count):
    stride = node_count // fetch_pick.shape[1]
    return fetch_pick[lax.rem(lax.axis_index("node") + slot * stride, node_count), slot]


def pick_kernel(slots, node_count, fetch_pick, panels, *refs):
    outs, sems = refs[: len(slots)], refs[len(slots)]
    copies = [
        pltpu.make_async_copy(panels.at[chosen_of(fetch_pick, slot, node_count)], out, sems.at[i])
        for i, (slot, out) in enumerate(zip(slots, outs))
    ]
    for copy in copies:
        copy.start()
    for copy in copies:
        copy.wait()


def pick_pass(slots, node_count, fetch_pick, panels):
    return pl.pallas_call(
        lambda *refs: pick_kernel(slots, node_count, *refs),
        out_shape=tuple(jax.ShapeDtypeStruct(panels.shape[1:], BF16) for _ in slots),
        in_specs=[pl.BlockSpec(memory_space=pltpu.SMEM), untouched()],
        out_specs=tuple(untouched() for _ in slots),
        scratch_shapes=[pltpu.SemaphoreType.DMA((len(slots),))],
        compiler_params=pltpu.CompilerParams(vmem_limit_bytes=VMEM_LIMIT),
        name="pick",
    )(fetch_pick, panels)


def total_kernel(node_count, fetch_pick, *refs):
    grads, out = refs[:-1], refs[-1]
    chosen = [chosen_of(fetch_pick, slot, node_count) for slot in range(len(grads))]
    for e in range(out.shape[0]):
        total = jnp.zeros(grads[0].shape, F32)
        for pick, grad in zip(chosen, grads):
            total += jnp.where(pick == e, grad[...].astype(F32), 0.0)
        out[e] = total.astype(BF16)


def total_pass(node_count, fetch_pick, grads, shape):
    kinds, units, width = grads[0].shape
    block = pl.BlockSpec((1, units, width), lambda i: (i, 0, 0))
    return pl.pallas_call(
        lambda *refs: total_kernel(node_count, *refs),
        out_shape=jax.ShapeDtypeStruct(shape, BF16),
        grid=(kinds,),
        in_specs=[pl.BlockSpec(memory_space=pltpu.SMEM)] + [block] * len(grads),
        out_specs=pl.BlockSpec((shape[0], 1, units, width), lambda i: (0, i, 0, 0)),
        compiler_params=pltpu.CompilerParams(vmem_limit_bytes=VMEM_LIMIT),
        name="total",
    )(fetch_pick, *grads)


def ring_step(block, order, distance):
    size = len(order)
    return lax.ppermute(
        block, "local", [(order[i], order[(i + distance) % size]) for i in range(size)]
    )


def ring_gather(block, order, up_hops):
    size = len(order)
    blocks = [block] + [None] * (size - 1)
    up, down = block, block
    for hop in range(1, max(up_hops, size - 1 - up_hops) + 1):
        if hop <= up_hops:
            up = ring_step(up, order, 1)
            blocks[size - hop] = up
        if hop <= size - 1 - up_hops:
            down = ring_step(down, order, -1)
            blocks[hop] = down
    return blocks


def plus(a, b):
    return (a.astype(F32) + b.astype(F32)).astype(BF16)


def ring_scatter(chunks, order, up_hops):
    size = len(order)
    down_hops = size - 1 - up_hops
    up, down = chunks[up_hops], chunks[(size - down_hops) % size]
    for hop in range(max(up_hops, down_hops), 0, -1):
        if hop <= up_hops:
            up = ring_step(up, order, 1)
            if hop > 1:
                up = plus(up, chunks[hop - 1])
        if hop <= down_hops:
            down = ring_step(down, order, -1)
            if hop > 1:
                down = plus(down, chunks[size - hop + 1])
    return (up.astype(F32) + down.astype(F32) + chunks[0].astype(F32)).astype(BF16)


def acts_kernel(slot, size, offsets, *refs):
    parts = len(offsets)
    x_refs, dy_refs = refs[:parts], refs[parts : 2 * parts]
    panel, routes, weight, acts = *refs[2 * parts : 2 * parts + 3], refs[-1]
    units, width = panel.shape[1:]
    part = x_refs[0].shape[0]
    at_once = 2 if parts % 2 == 0 else 1
    for d in range(0, parts, at_once):
        here = slice(d * part, (d + at_once) * part)
        x = jnp.concatenate([ref[...] for ref in x_refs[d : d + at_once]], axis=0)
        dy = jnp.concatenate([ref[...] for ref in dy_refs[d : d + at_once]], axis=0)
        both = lax.dot_general(
            panel[0:2].reshape(2 * units, width), x, CONTRACT_LAST, preferred_element_type=F32
        )
        gate, up = both[:units], both[units:]
        d_hidden = lax.dot_general(panel[2], dy, CONTRACT_LAST, preferred_element_type=F32)
        sources = [ring_source(size, ahead) for ahead in offsets[d : d + at_once]]
        scale = jnp.concatenate(
            [
                jnp.where(routes[pl.ds(i, 1), :] == slot, weight[pl.ds(i, 1), :], 0.0)
                for i in sources
            ],
            axis=1,
        )
        sigmoid_gate = jax.nn.sigmoid(gate)
        activated = gate * sigmoid_gate
        d_hidden = d_hidden * scale
        d_gate = d_hidden * up * sigmoid_gate * (1.0 + gate * (1.0 - sigmoid_gate))
        acts[0:units, here] = d_gate.astype(BF16)
        acts[units : 2 * units, here] = (d_hidden * activated).astype(BF16)
        acts[2 * units : 3 * units, here] = (activated * up * scale).astype(BF16)


def acts_pass(name, slot, offsets, x_parts, dy_parts, panel, routes, weight, after=()):
    parts = len(x_parts)
    part = x_parts[0].shape[0]
    return pl.pallas_call(
        lambda *refs: acts_kernel(slot, routes.shape[0], offsets, *refs),
        out_shape=jax.ShapeDtypeStruct((3 * panel.shape[1], parts * part), BF16),
        in_specs=[whole_in_vmem()] * (2 * parts + 3) + [untouched()] * len(after),
        out_specs=whole_in_vmem(),
        compiler_params=pltpu.CompilerParams(vmem_limit_bytes=VMEM_LIMIT),
        name=f"acts_{slot}_{name}",
    )(*x_parts, *dy_parts, panel, routes, weight, *after)


def grads_kernel(parts, groups, *refs):
    x_refs, dy_refs = refs[:parts], refs[parts : 2 * parts]
    acts, grads = refs[2 * parts : 2 * parts + groups], refs[-1]
    units, width = grads.shape[1:]
    columns = tile_of(width, 512)
    for start in range(0, width, columns):
        here = slice(start, start + columns)
        x = jnp.concatenate([ref[:, here] for ref in x_refs], axis=0)
        dy = jnp.concatenate([ref[:, here] for ref in dy_refs], axis=0)
        d_both = jnp.concatenate([act[0 : 2 * units, :] for act in acts], axis=1)
        d_both = jnp.dot(d_both, x, preferred_element_type=F32).astype(BF16)
        grads[0, :, here] = d_both[0:units]
        grads[1, :, here] = d_both[units:]
        hidden = jnp.concatenate([act[2 * units : 3 * units, :] for act in acts], axis=1)
        grads[2, :, here] = jnp.dot(hidden, dy, preferred_element_type=F32).astype(BF16)


def grads_pass(slot, x_parts, dy_parts, acts, shape, after=()):
    parts = len(x_parts)
    return pl.pallas_call(
        lambda *refs: grads_kernel(parts, len(acts), *refs),
        out_shape=jax.ShapeDtypeStruct(shape, BF16),
        in_specs=[whole_in_vmem()] * (2 * parts + len(acts)) + [untouched()] * len(after),
        out_specs=whole_in_vmem(),
        compiler_params=pltpu.CompilerParams(vmem_limit_bytes=VMEM_LIMIT),
        name=f"grads_{slot}",
    )(*x_parts, *dy_parts, *acts, *after)


def chunk_kernel(wanted, slots, part, acts, panels, outs):
    units, width = panels[0].shape[1:]
    columns = tile_of(width, 512)

    @pl.loop(0, width // columns)
    def _(step):
        here = pl.ds(pl.multiple_of(step * columns, columns), columns)
        kinds = {"mixed": (2, 3), "grad": (0, 2)}
        sides = {
            kind: jnp.concatenate(
                [panel[which, :, here] for panel in panels for which in range(*span)], axis=0
            )
            for kind, span in kinds.items()
        }
        for out, (kind, group, row) in zip(outs, wanted):
            low, high = (units * which for which in kinds[kind])
            act = jnp.concatenate(
                [act[group][low:high, row * part : (row + 1) * part] for act in acts], axis=0
            )
            total = lax.dot_general(act, sides[kind], CONTRACT_FIRST, preferred_element_type=F32)
            out[:, here] = total.astype(BF16)


def chunk_pass(wanted, acts, panels, groups, part, after=()):
    slots = len(panels)
    width = panels[0].shape[2]
    named = [
        (kind, g, group.index(d)) for kind, d in wanted for g, group in enumerate(groups) if d in group
    ]

    def kernel(*refs):
        act_refs = [refs[s * len(groups) : (s + 1) * len(groups)] for s in range(slots)]
        rest = refs[slots * len(groups) :]
        chunk_kernel(named, slots, part, act_refs, rest[:slots], rest[slots + len(after) :])

    return pl.pallas_call(
        kernel,
        out_shape=tuple(jax.ShapeDtypeStruct((part, width), BF16) for _ in wanted),
        in_specs=[whole_in_vmem()] * (slots * len(groups) + slots) + [untouched()] * len(after),
        out_specs=tuple(whole_in_vmem() for _ in wanted),
        compiler_params=pltpu.CompilerParams(vmem_limit_bytes=VMEM_LIMIT),
        name=f"chunks_{len(wanted)}",
    )(*[act for slot_acts in acts for act in slot_acts], *panels, *after)


def body(tokens, cotangent, routes, route_weight, fetch_pick, panels):
    node_count = lax.axis_size("node")
    slot_count = fetch_pick.shape[1]
    stride = node_count // slot_count
    part, width = tokens.shape
    order = ring_order(lax.axis_size("local"))
    size = len(order)

    picked = pick_pass(list(range(slot_count)), node_count, fetch_pick, panels)
    read = [from_behind(picked[r], "node", r * stride) if r else picked[r] for r in range(slot_count)]

    x_parts = ring_gather(tokens, order, size // 2)
    dy_parts = ring_gather(cotangent, order, size - 1 - size // 2)

    ring_routes = routes.reshape(size, part)
    ring_weight = route_weight.reshape(size, part)

    near = [d for d in range(size) if min(d, size - d) <= size // 4 and d != size // 4]
    groups = [near, [d for d in range(size) if d not in near]]

    def make_acts(r, g, after=()):
        take = groups[g]
        return acts_pass(
            "nf"[g],
            r,
            take,
            [x_parts[d] for d in take],
            [dy_parts[d] for d in take],
            read[r],
            ring_routes,
            ring_weight,
            after,
        )

    rows = [d for group in groups for d in group]

    def make_grads(r, after=()):
        return grads_pass(
            r,
            [x_parts[d] for d in rows],
            [dy_parts[d] for d in rows],
            acts[r],
            read[r].shape,
            after,
        )

    acts, grads = [None] * slot_count, [None] * slot_count
    last = slot_count // 2
    turn = [r for r in range(1, slot_count) if r != last] + [0]
    acts_near = {r: make_acts(r, 0) for r in turn}
    done = ()
    for r in turn:
        acts[r] = (acts_near[r], make_acts(r, 1, done))
        done = (acts[r][1],)
        if r == turn[0]:
            grads[r] = make_grads(r)
            done = (grads[r],)
    acts[last] = (make_acts(last, 0, done), make_acts(last, 1))

    first = size // 2
    early = [("mixed", first), ("grad", size - 1 - first), ("mixed", first + 1), ("grad", first)]
    late = [
        (kind, d)
        for hop in range(first, -1, -1)
        for d in {hop: 0, size - hop: 0}
        if d < size
        for kind in ("mixed", "grad")
        if (kind, d) not in early
    ]
    chunks = dict(zip(early, chunk_pass(early, acts, read, groups, part)))
    done = (chunks[early[0]],)
    for r in turn[1:-1] + [last]:
        grads[r] = make_grads(r, done)
        done = (grads[r],)
    chunks.update(zip(late, chunk_pass(late, acts, read, groups, part, done)))
    grads[0] = make_grads(0, (chunks[late[0]],))
    mixed = ring_scatter([chunks["mixed", d] for d in range(size)], order, size // 2)
    token_grad = ring_scatter([chunks["grad", d] for d in range(size)], order, size - 1 - size // 2)

    grads = [
        from_behind(grads[r], "node", node_count - r * stride) if r else grads[r]
        for r in range(slot_count)
    ]
    panel_grad = total_pass(node_count, fetch_pick, grads, panels.shape)
    return mixed, token_grad, panel_grad


def solution(mesh):
    return jax.shard_map(
        body,
        mesh=mesh,
        in_specs=(
            P(("node", "local"), None),
            P(("node", "local"), None),
            P("node", None),
            P("node", None),
            P(),
            P("node", None, "local", None),
        ),
        out_specs=(
            P(("node", "local"), None),
            P(("node", "local"), None),
            P("node", None, "local", None),
        ),
        check_vma=False,
    )
```

time: 261 us -> 215 us (0.82)
  Pallas kernels: 74.3 us -> 41.5 us
  waiting for transfers between devices: 104 us -> 129 us
  local copies, waits for them, and re-layouts: 17.8 us -> 2.92 us
  between operations: 15.4 us -> 0.92 us
  other arithmetic: 13.8 us -> 3.31 us
    pallas_call x6 -> x16, Pallas kernels: 74.3 us -> 41.5 us  [the longest x8 12.6 us: acts_pass(): pl.pallas_call(lambda *refs: acts_kernel(slot, routes.shape[0], offsets,...]
    ppermute x28, waiting for transfers between devices: 99.9 us -> 129 us  [ring_step(): lax.ppermute(block, 'local', [(order[i], order[(i + distance) % size]) fo...]
    squeeze x1 -> x0, local copies, waits for them, and re-layouts: 7.76 us -> none  [body(): panel = lax.dynamic_index_in_dim(panels, chosen[r], 0, keepdims=False)]
    another operation x2 -> x0, other arithmetic: 7.05 us -> none  [body(): jnp.stack([sum((jnp.where(chosen[r] == e, grads[r].astype(F32), 0.0) for...]
    ppermute x6, waiting for transfers between devices: 4.13 us -> 0.02 us  [from_behind(): lax.ppermute(block, axis, [((i - distance) % size, i) for i in range(size)])]
    unnamed x38 -> x12, local copies, waits for them, and re-layouts: 6.81 us -> 2.92 us
  transfers between devices with their start and end apart: 34 -> 34, of which waited for: 18 -> 22; matrix products, arithmetic and copies ran while one was open for 7% -> 2% of each run, Pallas kernels for 29% -> 13%
where the time goes in v2:
time: 215 us; the launch traced here: 214 us
  waiting for transfers between devices  129 us (60%)
  Pallas kernels  41.5 us (19%)
  starting transfers between devices  37 us (17%)
  other arithmetic  3.31 us (2%)
  local copies, waits for them, and re-layouts  2.92 us (1%)
    ppermute x28, waiting for transfers between devices, ring_step(): lax.ppermute(block, 'local', [(order[i], order[(i + distance) % size]) fo...  129 us
    ppermute x28, starting transfers between devices, ring_step(): lax.ppermute(block, 'local', [(order[i], order[(i + distance) % size]) fo...  33.6 us
    pallas_call x8, Pallas kernels, acts_pass(): pl.pallas_call(lambda *refs: acts_kernel(slot, routes.shape[0], offsets,...  12.6 us
    pallas_call x2, Pallas kernels, chunk_pass(): pl.pallas_call(kernel, out_shape=tuple((jax.ShapeDtypeStruct((part, width...  11.6 us
    pallas_call x4, Pallas kernels, grads_pass(): pl.pallas_call(lambda *refs: grads_kernel(parts, len(acts), *refs), out_s...  9.6 us
    pallas_call x1, Pallas kernels, total_pass(): pl.pallas_call(lambda *refs: total_kernel(node_count, *refs), out_shape=j...  6.07 us
  transfers between devices with their start and end apart: 34, of which 22 were waited for; matrix products, arithmetic and copies ran while one was open for 2% of the time, Pallas kernels for 13%

profile of v2, /device:TPU:0, one launch (start us, length us, event | category | flops | bytes accessed | tf_op | source)
XLA Modules:
  0.0 214.3 jit_solution(4490127154917205888)
XLA Ops:
  0.7 3.1 %collective-permute-start.1 = (bf16[128,2048]{1,0:T(8,128)(2,1)}, bf16[128,2048]{1,0:T(8,128)(2,1)S(1)}, u32[]{:S(2)}, u32[]{:S(2)}) collective-permute-start(bf16[128,2048]{1,0:T(8,128)(2,1)} %refs_0_.18), channel_id=1, source_target_pairs={{0,2},{2,4},{4,6},{6,7},{7,5},{5,3},{3,1},{1,0},{8,10},{10,12},{12... | collective-permute-start | bytes 1572872 | tf_op jit(solution)/shard_map/ppermute | solution.py:102
  3.7 2.2 %copy-done.2 = bf16[2,3,176,2048]{3,2,1,0:T(8,128)(2,1)S(1)} copy-done((bf16[2,3,176,2048]{3,2,1,0:T(8,128)(2,1)S(1)}, bf16[2,3,176,2048]{3,2,1,0:T(8,128)(2,1)}, u32[]{:S(2)}) %copy-start.2) | copy-done | bytes 4325400
  6.0 0.7 copy-done.5
  6.6 1.5 pick.1
  8.2 0.7 collective-permute-start.14
  9.4 1.6 collective-permute-start.4
  11.0 5.6 %collective-permute-done.1.refs_3_ = bf16[128,2048]{1,0:T(8,128)(2,1)S(1)} collective-permute-done((bf16[128,2048]{1,0:T(8,128)(2,1)}, bf16[128,2048]{1,0:T(8,128)(2,1)S(1)}, u32[]{:S(2)}, u32[]{:S(2)}) %collective-permute-start.1) | collective-permute-done | bytes 524320 | tf_op jit(solution)/shard_map/ppermute | solution.py:102
  16.6 2.1 collective-permute-start.3
  18.7 5.0 %collective-permute-done.refs_1_ = bf16[128,2048]{1,0:T(8,128)(2,1)S(1)} collective-permute-done((bf16[128,2048]{1,0:T(8,128)(2,1)S(1)}, bf16[128,2048]{1,0:T(8,128)(2,1)S(1)}, u32[]{:S(2)}, u32[]{:S(2)}) %collective-permute-start) | collective-permute-done | bytes 524320 | tf_op jit(solution)/shard_map/ppermute | solution.py:102
  23.7 1.4 collective-permute-start.16
  25.1 1.9 collective-permute-done.4.refs_7_.refs_11_
  27.0 1.8 collective-permute-start.2
  28.8 6.1 %collective-permute-done.3.refs_5_.refs_9_ = bf16[128,2048]{1,0:T(8,128)(2,1)S(1)} collective-permute-done((bf16[128,2048]{1,0:T(8,128)(2,1)S(1)}, bf16[128,2048]{1,0:T(8,128)(2,1)S(1)}, u32[]{:S(2)}, u32[]{:S(2)}) %collective-permute-start.3) | collective-permute-done | bytes 524320 | tf_op jit(solution)/shard_map/ppermute | solution.py:102
  35.4 4.8 %collective-permute-done.2.refs_2_ = bf16[128,2048]{1,0:T(8,128)(2,1)S(1)} collective-permute-done((bf16[128,2048]{1,0:T(8,128)(2,1)S(1)}, bf16[128,2048]{1,0:T(8,128)(2,1)S(1)}, u32[]{:S(2)}, u32[]{:S(2)}) %collective-permute-start.2) | collective-permute-done | bytes 524320 | tf_op jit(solution)/shard_map/ppermute | solution.py:102
  40.1 1.5 collective-permute-start.5
  41.6 7.3 %collective-permute-done.6.refs_0_.refs_4_ = bf16[128,2048]{1,0:T(8,128)(2,1)S(1)} collective-permute-done((bf16[128,2048]{1,0:T(8,128)(2,1)S(1)}, bf16[128,2048]{1,0:T(8,128)(2,1)S(1)}, u32[]{:S(2)}, u32[]{:S(2)}) %collective-permute-start.6) | collective-permute-done | bytes 524320 | tf_op jit(solution)/shard_map/ppermute | solution.py:102
  49.4 3.0 %collective-permute-done.5.refs_6_.refs_10_ = bf16[128,2048]{1,0:T(8,128)(2,1)S(1)} collective-permute-done((bf16[128,2048]{1,0:T(8,128)(2,1)S(1)}, bf16[128,2048]{1,0:T(8,128)(2,1)S(1)}, u32[]{:S(2)}, u32[]{:S(2)}) %collective-permute-start.5) | collective-permute-done | bytes 524320 | tf_op jit(solution)/shard_map/ppermute | solution.py:102
  52.3 1.4 collective-permute-start.8
  53.7 8.3 %collective-permute-done.10.refs_4_.refs_12_ = bf16[128,2048]{1,0:T(8,128)(2,1)S(1)} collective-permute-done((bf16[128,2048]{1,0:T(8,128)(2,1)S(1)}, bf16[128,2048]{1,0:T(8,128)(2,1)S(1)}, u32[]{:S(2)}, u32[]{:S(2)}) %collective-permute-start.10) | collective-permute-done | bytes 524320 | tf_op jit(solution)/shard_map/ppermute | solution.py:102
  62.5 1.1 collective-permute-done.8.refs_3_.refs_7_
  63.6 1.1 collective-permute-start.7
  64.7 12.3 %collective-permute-done.11.refs_5_.refs_13_ = bf16[128,2048]{1,0:T(8,128)(2,1)S(1)} collective-permute-done((bf16[128,2048]{1,0:T(8,128)(2,1)S(1)}, bf16[128,2048]{1,0:T(8,128)(2,1)S(1)}, u32[]{:S(2)}, u32[]{:S(2)}) %collective-permute-start.11) | collective-permute-done | bytes 524320 | tf_op jit(solution)/shard_map/ppermute | solution.py:102
  76.9 1.6 collective-permute-start.13
  78.5 1.6 collective-permute-start.9
  80.5 1.6 acts_0_n.1.refs_0_.refs_16_
  82.1 1.6 acts_3_n.1.refs_6_.refs_16_
  83.7 1.6 acts_1_n.1.refs_16_.refs_2_
  85.3 2.8 %collective-permute-done.7.refs_1_.refs_5_ = bf16[128,2048]{1,0:T(8,128)(2,1)S(1)} collective-permute-done((bf16[128,2048]{1,0:T(8,128)(2,1)S(1)}, bf16[128,2048]{1,0:T(8,128)(2,1)S(1)}, u32[]{:S(2)}, u32[]{:S(2)}) %collective-permute-start.7) | collective-permute-done | bytes 524320 | tf_op jit(solution)/shard_map/ppermute | solution.py:102
  88.2 3.1 %collective-permute-done.13.refs_7_.refs_15_ = bf16[128,2048]{1,0:T(8,128)(2,1)S(1)} collective-permute-done((bf16[128,2048]{1,0:T(8,128)(2,1)S(1)}, bf16[128,2048]{1,0:T(8,128)(2,1)S(1)}, u32[]{:S(2)}, u32[]{:S(2)}) %collective-permute-start.13) | collective-permute-done | bytes 524320 | tf_op jit(solution)/shard_map/ppermute | solution.py:102
  91.3 5.6 %collective-permute-done.9.refs_2_.refs_6_ = bf16[128,2048]{1,0:T(8,128)(2,1)S(1)} collective-permute-done((bf16[128,2048]{1,0:T(8,128)(2,1)S(1)}, bf16[128,2048]{1,0:T(8,128)(2,1)S(1)}, u32[]{:S(2)}, u32[]{:S(2)}) %collective-permute-start.9) | collective-permute-done | bytes 524320 | tf_op jit(solution)/shard_map/ppermute | solution.py:102
  96.9 1.6 acts_1_f.1.refs_17_.refs_3_
  98.5 2.4 %grads_1.1.refs_11_ = bf16[3,176,2048]{2,1,0:T(8,128)(2,1)S(1)} custom-call(bf16[128,2048]{1,0:T(8,128)(2,1)S(1)} %copy-done, bf16[128,2048]{1,0:T(8,128)(2,1)S(1)} %collective-permute-done.refs_1_, bf16[128,2048]{1,0:T(8,128)(2,1)S(1)} %collective-permute-done.2.refs_2_, bf16[128,2048]{1,0:T(8,128)(2,1)S(1)} %collective-permute-done.1.refs_3_, ...), custom_call_target="tpu_custom_call" | custom-call | tf_op jit(solution)/shard_map/grads_1/pallas_call | solution.py:206
  100.9 1.6 acts_3_f.1.refs_11_.refs_7_.refs_17_
  102.5 1.6 acts_0_f.1.refs_11_.refs_1_.refs_17_
  104.0 1.6 acts_2_f.1.refs_5_.refs_17_
  105.6 1.6 acts_2_n.1.refs_4_.refs_16_
  107.2 3.4 %chunks_4.1 = (bf16[128,2048]{1,0:T(8,128)(2,1)S(1)}, bf16[128,2048]{1,0:T(8,128)(2,1)S(1)}, bf16[128,2048]{1,0:T(8,128)(2,1)S(1)}, bf16[128,2048]{1,0:T(8,128)(2,1)S(1)}) custom-call(bf16[528,512]{1,0:T(8,128)(2,1)S(1)} %acts_0_n.1.refs_0_.refs_16_, bf16[528,512]{1,0:T(8,128)(2,1)S(1)} %acts_0_f.1.refs_11_.refs_1_.refs_17_, ...), custom_call_target="tpu_custom_call" | custom-call | tf_op jit(solution)/shard_map/chunks_4/pallas_call | solution.py:251
  110.7 0.5 collective-permute-start.21
  111.2 1.2 collective-permute-start.27
  113.2 2.4 %grads_3.1.refs_18_ = bf16[3,176,2048]{2,1,0:T(8,128)(2,1)S(1)} custom-call(bf16[128,2048]{1,0:T(8,128)(2,1)S(1)} %copy-done, bf16[128,2048]{1,0:T(8,128)(2,1)S(1)} %collective-permute-done.refs_1_, bf16[128,2048]{1,0:T(8,128)(2,1)S(1)} %collective-permute-done.2.refs_2_, bf16[128,2048]{1,0:T(8,128)(2,1)S(1)} %collective-permute-done.1.refs_3_, ...), custom_call_target="tpu_custom_call" | custom-call | tf_op jit(solution)/shard_map/grads_3/pallas_call | solution.py:206
  115.6 2.4 %grads_2.1.refs_12_ = bf16[3,176,2048]{2,1,0:T(8,128)(2,1)S(1)} custom-call(bf16[128,2048]{1,0:T(8,128)(2,1)S(1)} %copy-done, bf16[128,2048]{1,0:T(8,128)(2,1)S(1)} %collective-permute-done.refs_1_, bf16[128,2048]{1,0:T(8,128)(2,1)S(1)} %collective-permute-done.2.refs_2_, bf16[128,2048]{1,0:T(8,128)(2,1)S(1)} %collective-permute-done.1.refs_3_, ...), custom_call_target="tpu_custom_call" | custom-call | tf_op jit(solution)/shard_map/grads_2/pallas_call | solution.py:206
  118.0 0.9 collective-permute-start.32
  118.9 8.2 %chunks_12.1 = (bf16[128,2048]{1,0:T(8,128)(2,1)S(1)}, bf16[128,2048]{1,0:T(8,128)(2,1)S(1)}, bf16[128,2048]{1,0:T(8,128)(2,1)S(1)}, bf16[128,2048]{1,0:T(8,128)...) custom-call(bf16[528,512]{1,0:T(8,128)(2,1)S(1)} %acts_0_n.1.refs_0_, ...), custom_call_target="tpu_custom_call" | custom-call | tf_op jit(solution)/shard_map/chunks_12/pallas_call | solution.py:251
  127.1 1.6 collective-permute-start.24
  128.9 6.7 %collective-permute-done.27 = bf16[128,2048]{1,0:T(8,128)(2,1)S(1)} collective-permute-done((bf16[128,2048]{1,0:T(8,128)(2,1)S(1)}, bf16[128,2048]{1,0:T(8,128)(2,1)S(1)}, u32[]{:S(2)}, u32[]{:S(2)}) %collective-permute-start.27) | collective-permute-done | bytes 524320 | tf_op jit(solution)/shard_map/ppermute | solution.py:102
  136.2 1.5 collective-permute-start.28
  137.8 3.1 %collective-permute-done.24 = bf16[128,2048]{1,0:T(8,128)(2,1)S(1)} collective-permute-done((bf16[128,2048]{1,0:T(8,128)(2,1)S(1)}, bf16[128,2048]{1,0:T(8,128)(2,1)S(1)}, u32[]{:S(2)}, u32[]{:S(2)}) %collective-permute-start.24) | collective-permute-done | bytes 524320 | tf_op jit(solution)/shard_map/ppermute | solution.py:102
  140.9 1.6 collective-permute-start.18
  142.6 16.9 %collective-permute-done.28 = bf16[128,2048]{1,0:T(8,128)(2,1)S(1)} collective-permute-done((bf16[128,2048]{1,0:T(8,128)(2,1)S(1)}, bf16[128,2048]{1,0:T(8,128)(2,1)S(1)}, u32[]{:S(2)}, u32[]{:S(2)}) %collective-permute-start.28) | collective-permute-done | bytes 524320 | tf_op jit(solution)/shard_map/ppermute | solution.py:102
  159.5 1.6 collective-permute-start.25
  161.9 9.6 %collective-permute-done.25 = bf16[128,2048]{1,0:T(8,128)(2,1)S(1)} collective-permute-done((bf16[128,2048]{1,0:T(8,128)(2,1)S(1)}, bf16[128,2048]{1,0:T(8,128)(2,1)S(1)}, u32[]{:S(2)}, u32[]{:S(2)}) %collective-permute-start.25) | collective-permute-done | bytes 524320 | tf_op jit(solution)/shard_map/ppermute | solution.py:102
  171.5 1.6 collective-permute-start.19
  173.4 1.6 collective-permute-start.26
  175.1 11.3 %collective-permute-done.19 = bf16[128,2048]{1,0:T(8,128)(2,1)S(1)} collective-permute-done((bf16[128,2048]{1,0:T(8,128)(2,1)S(1)}, bf16[128,2048]{1,0:T(8,128)(2,1)S(1)}, u32[]{:S(2)}, u32[]{:S(2)}) %collective-permute-start.19) | collective-permute-done | bytes 524320 | tf_op jit(solution)/shard_map/ppermute | solution.py:102
  186.4 0.7 collective-permute-start.30
  187.3 6.7 %collective-permute-done.26 = bf16[128,2048]{1,0:T(8,128)(2,1)S(1)} collective-permute-done((bf16[128,2048]{1,0:T(8,128)(2,1)S(1)}, bf16[128,2048]{1,0:T(8,128)(2,1)S(1)}, u32[]{:S(2)}, u32[]{:S(2)}) %collective-permute-start.26) | collective-permute-done | bytes 524320 | tf_op jit(solution)/shard_map/ppermute | solution.py:102
  193.9 0.8 collective-permute-start.23
  194.7 3.3 %collective-permute-done.30 = bf16[128,2048]{1,0:T(8,128)(2,1)S(1)} collective-permute-done((bf16[128,2048]{1,0:T(8,128)(2,1)S(1)}, bf16[128,2048]{1,0:T(8,128)(2,1)S(1)}, u32[]{:S(2)}, u32[]{:S(2)}) %collective-permute-start.30) | collective-permute-done | bytes 524320 | tf_op jit(solution)/shard_map/ppermute | solution.py:102
  198.0 1.6 collective-permute-start.20
  199.6 2.4 %grads_0.1.refs_1_ = bf16[3,176,2048]{2,1,0:T(8,128)(2,1)S(1)} custom-call(bf16[128,2048]{1,0:T(8,128)(2,1)S(1)} %copy-done, bf16[128,2048]{1,0:T(8,128)(2,1)S(1)} %collective-permute-done.refs_1_, bf16[128,2048]{1,0:T(8,128)(2,1)S(1)} %collective-permute-done.2.refs_2_, bf16[128,2048]{1,0:T(8,128)(2,1)S(1)} %collective-permute-done.1.refs_3_, ...), custom_call_target="tpu_custom_call" | custom-call | tf_op jit(solution)/shard_map/grads_0/pallas_call | solution.py:206
  202.0 1.0 add_convert_fusion
  203.0 3.7 %collective-permute-done.23 = bf16[128,2048]{1,0:T(8,128)(2,1)S(1)} collective-permute-done((bf16[128,2048]{1,0:T(8,128)(2,1)S(1)}, bf16[128,2048]{1,0:T(8,128)(2,1)S(1)}, u32[]{:S(2)}, u32[]{:S(2)}) %collective-permute-start.23) | collective-permute-done | bytes 524320 | tf_op jit(solution)/shard_map/ppermute | solution.py:102
  207.2 1.0 add_convert_fusion.6
  208.2 6.1 %total.1 = bf16[2,3,176,2048]{3,2,1,0:T(8,128)(2,1)} custom-call(s32[4,4]{1,0:T(4,128)S(1)} %copy-done.5, bf16[3,176,2048]{2,1,0:T(8,128)(2,1)S(1)} %grads_0.1.refs_1_, bf16[3,176,2048]{2,1,0:T(8,128)(2,1)S(1)} %collective-permute-done.31.refs_2_, bf16[3,176,2048]{2,1,0:T(8,128)(2,1)} %collective-permute-done.32.refs_3_, ...), custom_call_target="tpu_custom_call" | custom-call | tf_op jit(solution)/shard_map/total/pallas_call | solution.py:89
  (44 shorter events, 5.8 us)
Async XLA Ops:
  0.6 8.3 %copy-start = (bf16[128,2048]{1,0:T(8,128)(2,1)S(1)}, bf16[128,2048]{1,0:T(8,128)(2,1)}, u32[]{:S(2)}) copy-start(bf16[128,2048]{1,0:T(8,128)(2,1)} %refs_0_.18) | copy-start | bytes 1572868
  0.6 8.7 %copy-start.1 = (bf16[128,2048]{1,0:T(8,128)(2,1)S(1)}, bf16[128,2048]{1,0:T(8,128)(2,1)}, u32[]{:S(2)}) copy-start(bf16[128,2048]{1,0:T(8,128)(2,1)} %refs_8_.7) | copy-start | bytes 1572868
  0.7 16.0 %collective-permute-start.1 = (bf16[128,2048]{1,0:T(8,128)(2,1)}, bf16[128,2048]{1,0:T(8,128)(2,1)S(1)}, u32[]{:S(2)}, u32[]{:S(2)}) collective-permute-start(bf16[128,2048]{1,0:T(8,128)(2,1)} %refs_0_.18), channel_id=1, source_target_pairs={{0,2},{2,4},{4,6},{6,7},{7,5},{5,3},{3,1},{1,0},{8,10},{10,12},{12... | collective-permute-start | bytes 1572872 | tf_op jit(solution)/shard_map/ppermute | solution.py:102
  3.7 2.2 %copy-start.2 = (bf16[2,3,176,2048]{3,2,1,0:T(8,128)(2,1)S(1)}, bf16[2,3,176,2048]{3,2,1,0:T(8,128)(2,1)}, u32[]{:S(2)}) copy-start(bf16[2,3,176,2048]{3,2,1,0:T(8,128)(2,1)} %refs_1_.1) | copy-start | bytes 12976132
  6.0 0.7 copy-start.5
  6.6 73.9 %copy-start.3 = (s32[1024,1]{0,1:T(1,128)S(1)}, s32[1024,1]{0,1:T(1,128)}, u32[]{:S(2)}) copy-start(s32[1024,1]{0,1:T(1,128)} %param.8) | copy-start | bytes 12292
  6.6 73.9 %copy-start.4 = (f32[1024,1]{0,1:T(1,128)S(1)}, f32[1024,1]{0,1:T(1,128)}, u32[]{:S(2)}) copy-start(f32[1024,1]{0,1:T(1,128)} %param.9) | copy-start | bytes 12292
  8.2 70.3 %collective-permute-start.14 = (bf16[3,176,2048]{2,1,0:T(8,128)(2,1)S(1)}, bf16[3,176,2048]{2,1,0:T(8,128)(2,1)S(1)}, u32[]{:S(2)}, u32[]{:S(2)}) collective-permute-start(bf16[3,176,2048]{2,1,0:T(8,128)(2,1)S(1)} %get-tuple-element.24), channel_id=1, source_target_pairs={{8,0},{16,8},{24,16},{0,24},{9,1},{17,9},{25,17},{1,25},{10,2},{18... | collective-permute-start | bytes 6488072 | tf_op jit(solution)/shard_map/ppermute | solution.py:32
  8.9 71.2 %collective-permute-start.15 = (bf16[3,176,2048]{2,1,0:T(8,128)(2,1)S(1)}, bf16[3,176,2048]{2,1,0:T(8,128)(2,1)S(1)}, u32[]{:S(2)}, u32[]{:S(2)}) collective-permute-start(bf16[3,176,2048]{2,1,0:T(8,128)(2,1)S(1)} %get-tuple-element.25), channel_id=1, source_target_pairs={{24,0},{0,8},{8,16},{16,24},{25,1},{1,9},{9,17},{17,25},{26,2},{2,... | collective-permute-start | bytes 6488072 | tf_op jit(solution)/shard_map/ppermute | solution.py:32
  8.9 14.8 %collective-permute-start = (bf16[128,2048]{1,0:T(8,128)(2,1)S(1)}, bf16[128,2048]{1,0:T(8,128)(2,1)S(1)}, u32[]{:S(2)}, u32[]{:S(2)}) collective-permute-start(bf16[128,2048]{1,0:T(8,128)(2,1)S(1)} %copy-done), channel_id=1, source_target_pairs={{0,1},{2,0},{4,2},{6,4},{7,6},{5,7},{3,5},{1,3},{8,9},{10,8},{12,1... | collective-permute-start | bytes 1572872 | tf_op jit(solution)/shard_map/ppermute | solution.py:102
  9.4 17.6 %collective-permute-start.4 = (bf16[128,2048]{1,0:T(8,128)(2,1)S(1)}, bf16[128,2048]{1,0:T(8,128)(2,1)S(1)}, u32[]{:S(2)}, u32[]{:S(2)}) collective-permute-start(bf16[128,2048]{1,0:T(8,128)(2,1)S(1)} %copy-done.1), channel_id=1, source_target_pairs={{0,2},{2,4},{4,6},{6,7},{7,5},{5,3},{3,1},{1,0},{8,10},{10,12},{12... | collective-permute-start | bytes 1572872 | tf_op jit(solution)/shard_map/ppermute | solution.py:102
  16.6 18.3 %collective-permute-start.3 = (bf16[128,2048]{1,0:T(8,128)(2,1)S(1)}, bf16[128,2048]{1,0:T(8,128)(2,1)S(1)}, u32[]{:S(2)}, u32[]{:S(2)}) collective-permute-start(bf16[128,2048]{1,0:T(8,128)(2,1)S(1)} %copy-done.1), channel_id=1, source_target_pairs={{0,1},{2,0},{4,2},{6,4},{7,6},{5,7},{3,5},{1,3},{8,9},{10,8},{12,1... | collective-permute-start | bytes 1572872 | tf_op jit(solution)/shard_map/ppermute | solution.py:102
  23.7 80.4 %collective-permute-start.16 = (bf16[3,176,2048]{2,1,0:T(8,128)(2,1)S(1)}, bf16[3,176,2048]{2,1,0:T(8,128)(2,1)S(1)}, u32[]{:S(2)}, u32[]{:S(2)}) collective-permute-start(bf16[3,176,2048]{2,1,0:T(8,128)(2,1)S(1)} %get-tuple-element.26), channel_id=1, source_target_pairs={{16,0},{24,8},{0,16},{8,24},{17,1},{25,9},{1,17},{9,25},{18,2},{26... | collective-permute-start | bytes 6488072 | tf_op jit(solution)/shard_map/ppermute | solution.py:32
  27.0 13.1 %collective-permute-start.2 = (bf16[128,2048]{1,0:T(8,128)(2,1)S(1)}, bf16[128,2048]{1,0:T(8,128)(2,1)S(1)}, u32[]{:S(2)}, u32[]{:S(2)}) collective-permute-start(bf16[128,2048]{1,0:T(8,128)(2,1)S(1)} %collective-permute-done.1.refs_3_), channel_id=1, source_target_pairs={{0,2},{2,4},{4,6},{6,7},{7,5},{5,3},{3,1},{1,0},{8,10},{10,12},{12... | collective-permute-start | bytes 1572872 | tf_op jit(solution)/shard_map/ppermute | solution.py:102
  34.9 14.0 %collective-permute-start.6 = (bf16[128,2048]{1,0:T(8,128)(2,1)S(1)}, bf16[128,2048]{1,0:T(8,128)(2,1)S(1)}, u32[]{:S(2)}, u32[]{:S(2)}) collective-permute-start(bf16[128,2048]{1,0:T(8,128)(2,1)S(1)} %collective-permute-done.refs_1_), channel_id=1, source_target_pairs={{0,1},{2,0},{4,2},{6,4},{7,6},{5,7},{3,5},{1,3},{8,9},{10,8},{12,1... | collective-permute-start | bytes 1572872 | tf_op jit(solution)/shard_map/ppermute | solution.py:102
  40.1 12.2 %collective-permute-start.5 = (bf16[128,2048]{1,0:T(8,128)(2,1)S(1)}, bf16[128,2048]{1,0:T(8,128)(2,1)S(1)}, u32[]{:S(2)}, u32[]{:S(2)}) collective-permute-start(bf16[128,2048]{1,0:T(8,128)(2,1)S(1)} %collective-permute-done.4.refs_7_.refs_11_), channel_id=1, source_target_pairs={{0,2},{2,4},{4,6},{6,7},{7,5},{5,3},{3,1},{1,0},{8,10},{10,12},{12... | collective-permute-start | bytes 1572872 | tf_op jit(solution)/shard_map/ppermute | solution.py:102
  48.9 13.2 %collective-permute-start.10 = (bf16[128,2048]{1,0:T(8,128)(2,1)S(1)}, bf16[128,2048]{1,0:T(8,128)(2,1)S(1)}, u32[]{:S(2)}, u32[]{:S(2)}) collective-permute-start(bf16[128,2048]{1,0:T(8,128)(2,1)S(1)} %collective-permute-done.3.refs_5_.refs_9_), channel_id=1, source_target_pairs={{0,1},{2,0},{4,2},{6,4},{7,6},{5,7},{3,5},{1,3},{8,9},{10,8},{12,1... | collective-permute-start | bytes 1572872 | tf_op jit(solution)/shard_map/ppermute | solution.py:102
  52.3 11.3 %collective-permute-start.8 = (bf16[128,2048]{1,0:T(8,128)(2,1)S(1)}, bf16[128,2048]{1,0:T(8,128)(2,1)S(1)}, u32[]{:S(2)}, u32[]{:S(2)}) collective-permute-start(bf16[128,2048]{1,0:T(8,128)(2,1)S(1)} %collective-permute-done.2.refs_2_), channel_id=1, source_target_pairs={{0,2},{2,4},{4,6},{6,7},{7,5},{5,3},{3,1},{1,0},{8,10},{10,12},{12... | collective-permute-start | bytes 1572872 | tf_op jit(solution)/shard_map/ppermute | solution.py:102
  62.1 14.9 %collective-permute-start.11 = (bf16[128,2048]{1,0:T(8,128)(2,1)S(1)}, bf16[128,2048]{1,0:T(8,128)(2,1)S(1)}, u32[]{:S(2)}, u32[]{:S(2)}) collective-permute-start(bf16[128,2048]{1,0:T(8,128)(2,1)S(1)} %collective-permute-done.10.refs_4_.refs_12_), channel_id=1, source_target_pairs={{0,1},{2,0},{4,2},{6,4},{7,6},{5,7},{3,5},{1,3},{8,9},{10,8},{12,1... | collective-permute-start | bytes 1572872 | tf_op jit(solution)/shard_map/ppermute | solution.py:102
  63.6 24.6 %collective-permute-start.7 = (bf16[128,2048]{1,0:T(8,128)(2,1)S(1)}, bf16[128,2048]{1,0:T(8,128)(2,1)S(1)}, u32[]{:S(2)}, u32[]{:S(2)}) collective-permute-start(bf16[128,2048]{1,0:T(8,128)(2,1)S(1)} %collective-permute-done.6.refs_0_.refs_4_), channel_id=1, source_target_pairs={{0,1},{2,0},{4,2},{6,4},{7,6},{5,7},{3,5},{1,3},{8,9},{10,8},{12,1... | collective-permute-start | bytes 1572872 | tf_op jit(solution)/shard_map/ppermute | solution.py:102
  76.9 14.3 %collective-permute-start.13 = (bf16[128,2048]{1,0:T(8,128)(2,1)S(1)}, bf16[128,2048]{1,0:T(8,128)(2,1)S(1)}, u32[]{:S(2)}, u32[]{:S(2)}) collective-permute-start(bf16[128,2048]{1,0:T(8,128)(2,1)S(1)} %collective-permute-done.5.refs_6_.refs_10_), channel_id=1, source_target_pairs={{0,2},{2,4},{4,6},{6,7},{7,5},{5,3},{3,1},{1,0},{8,10},{10,12},{12... | collective-permute-start | bytes 1572872 | tf_op jit(solution)/shard_map/ppermute | solution.py:102
  78.5 18.4 %collective-permute-start.9 = (bf16[128,2048]{1,0:T(8,128)(2,1)S(1)}, bf16[128,2048]{1,0:T(8,128)(2,1)S(1)}, u32[]{:S(2)}, u32[]{:S(2)}) collective-permute-start(bf16[128,2048]{1,0:T(8,128)(2,1)S(1)} %collective-permute-done.8.refs_3_.refs_7_), channel_id=1, source_target_pairs={{0,2},{2,4},{4,6},{6,7},{7,5},{5,3},{3,1},{1,0},{8,10},{10,12},{12... | collective-permute-start | bytes 1572872 | tf_op jit(solution)/shard_map/ppermute | solution.py:102
  80.1 16.8 %collective-permute-start.12 = (bf16[128,2048]{1,0:T(8,128)(2,1)S(1)}, bf16[128,2048]{1,0:T(8,128)(2,1)S(1)}, u32[]{:S(2)}, u32[]{:S(2)}) collective-permute-start(bf16[128,2048]{1,0:T(8,128)(2,1)S(1)} %collective-permute-done.11.refs_5_.refs_13_), channel_id=1, source_target_pairs={{0,1},{2,0},{4,2},{6,4},{7,6},{5,7},{3,5},{1,3},{8,9},{10,8},{12,1... | collective-permute-start | bytes 1572872 | tf_op jit(solution)/shard_map/ppermute | solution.py:102
  110.7 16.5 %collective-permute-start.21 = (bf16[128,2048]{1,0:T(8,128)(2,1)S(1)}, bf16[128,2048]{1,0:T(8,128)(2,1)S(1)}, u32[]{:S(2)}, u32[]{:S(2)}) collective-permute-start(bf16[128,2048]{1,0:T(8,128)(2,1)S(1)} %get-tuple-element.31), channel_id=1, source_target_pairs={{0,1},{2,0},{4,2},{6,4},{7,6},{5,7},{3,5},{1,3},{8,9},{10,8},{12,1... | collective-permute-start | bytes 1572872 | tf_op jit(solution)/shard_map/ppermute | solution.py:102
  111.2 24.4 %collective-permute-start.27 = (bf16[128,2048]{1,0:T(8,128)(2,1)S(1)}, bf16[128,2048]{1,0:T(8,128)(2,1)S(1)}, u32[]{:S(2)}, u32[]{:S(2)}) collective-permute-start(bf16[128,2048]{1,0:T(8,128)(2,1)S(1)} %get-tuple-element.38), channel_id=1, source_target_pairs={{0,1},{2,0},{4,2},{6,4},{7,6},{5,7},{3,5},{1,3},{8,9},{10,8},{12,1... | collective-permute-start | bytes 1572872 | tf_op jit(solution)/shard_map/ppermute | solution.py:102
  112.4 95.8 %collective-permute-start.31 = (bf16[3,176,2048]{2,1,0:T(8,128)(2,1)S(1)}, bf16[3,176,2048]{2,1,0:T(8,128)(2,1)S(1)}, u32[]{:S(2)}, u32[]{:S(2)}) collective-permute-start(bf16[3,176,2048]{2,1,0:T(8,128)(2,1)S(1)} %grads_1.1.refs_11_), channel_id=1, source_target_pairs={{8,0},{16,8},{24,16},{0,24},{9,1},{17,9},{25,17},{1,25},{10,2},{18... | collective-permute-start | bytes 6488072 | tf_op jit(solution)/shard_map/ppermute | solution.py:32
  112.8 23.4 %collective-permute-start.17 = (bf16[128,2048]{1,0:T(8,128)(2,1)S(1)}, bf16[128,2048]{1,0:T(8,128)(2,1)S(1)}, u32[]{:S(2)}, u32[]{:S(2)}) collective-permute-start(bf16[128,2048]{1,0:T(8,128)(2,1)S(1)} %get-tuple-element.27.refs_18_), channel_id=1, source_target_pairs={{0,2},{2,4},{4,6},{6,7},{7,5},{5,3},{3,1},{1,0},{8,10},{10,12},{12... | collective-permute-start | bytes 1572872 | tf_op jit(solution)/shard_map/ppermute | solution.py:102
  118.0 90.2 %collective-permute-start.32 = (bf16[3,176,2048]{2,1,0:T(8,128)(2,1)S(1)}, bf16[3,176,2048]{2,1,0:T(8,128)(2,1)}, u32[]{:S(2)}, u32[]{:S(2)}) collective-permute-start(bf16[3,176,2048]{2,1,0:T(8,128)(2,1)S(1)} %grads_2.1.refs_12_), channel_id=1, source_target_pairs={{16,0},{24,8},{0,16},{8,24},{17,1},{25,9},{1,17},{9,25},{18,2},{26... | collective-permute-start | bytes 6488072 | tf_op jit(solution)/shard_map/ppermute | solution.py:32
  127.1 13.8 %collective-permute-start.24 = (bf16[128,2048]{1,0:T(8,128)(2,1)S(1)}, bf16[128,2048]{1,0:T(8,128)(2,1)S(1)}, u32[]{:S(2)}, u32[]{:S(2)}) collective-permute-start(bf16[128,2048]{1,0:T(8,128)(2,1)S(1)} %get-tuple-element.35), channel_id=1, source_target_pairs={{0,2},{2,4},{4,6},{6,7},{7,5},{5,3},{3,1},{1,0},{8,10},{10,12},{12... | collective-permute-start | bytes 1572872 | tf_op jit(solution)/shard_map/ppermute | solution.py:102
  135.6 37.9 %collective-permute-start.22 = (bf16[128,2048]{1,0:T(8,128)(2,1)S(1)}, bf16[128,2048]{1,0:T(8,128)(2,1)S(1)}, u32[]{:S(2)}, u32[]{:S(2)}) collective-permute-start(bf16[128,2048]{1,0:T(8,128)(2,1)S(1)} %add_convert_fusion.8), channel_id=1, source_target_pairs={{0,1},{2,0},{4,2},{6,4},{7,6},{5,7},{3,5},{1,3},{8,9},{10,8},{12,1... | collective-permute-start | bytes 1572872 | tf_op jit(solution)/shard_map/ppermute | solution.py:102
  136.2 23.3 %collective-permute-start.28 = (bf16[128,2048]{1,0:T(8,128)(2,1)S(1)}, bf16[128,2048]{1,0:T(8,128)(2,1)S(1)}, u32[]{:S(2)}, u32[]{:S(2)}) collective-permute-start(bf16[128,2048]{1,0:T(8,128)(2,1)S(1)} %add_convert_fusion.3), channel_id=1, source_target_pairs={{0,1},{2,0},{4,2},{6,4},{7,6},{5,7},{3,5},{1,3},{8,9},{10,8},{12,1... | collective-permute-start | bytes 1572872 | tf_op jit(solution)/shard_map/ppermute | solution.py:102
  140.9 20.3 %collective-permute-start.18 = (bf16[128,2048]{1,0:T(8,128)(2,1)S(1)}, bf16[128,2048]{1,0:T(8,128)(2,1)S(1)}, u32[]{:S(2)}, u32[]{:S(2)}) collective-permute-start(bf16[128,2048]{1,0:T(8,128)(2,1)S(1)} %add_convert_fusion.11), channel_id=1, source_target_pairs={{0,2},{2,4},{4,6},{6,7},{7,5},{5,3},{3,1},{1,0},{8,10},{10,12},{12... | collective-permute-start | bytes 1572872 | tf_op jit(solution)/shard_map/ppermute | solution.py:102
  159.5 12.0 %collective-permute-start.25 = (bf16[128,2048]{1,0:T(8,128)(2,1)S(1)}, bf16[128,2048]{1,0:T(8,128)(2,1)S(1)}, u32[]{:S(2)}, u32[]{:S(2)}) collective-permute-start(bf16[128,2048]{1,0:T(8,128)(2,1)S(1)} %add_convert_fusion.5), channel_id=1, source_target_pairs={{0,2},{2,4},{4,6},{6,7},{7,5},{5,3},{3,1},{1,0},{8,10},{10,12},{12... | collective-permute-start | bytes 1572872 | tf_op jit(solution)/shard_map/ppermute | solution.py:102
  161.2 12.0 %collective-permute-start.29 = (bf16[128,2048]{1,0:T(8,128)(2,1)S(1)}, bf16[128,2048]{1,0:T(8,128)(2,1)S(1)}, u32[]{:S(2)}, u32[]{:S(2)}) collective-permute-start(bf16[128,2048]{1,0:T(8,128)(2,1)S(1)} %add_convert_fusion.2), channel_id=1, source_target_pairs={{0,1},{2,0},{4,2},{6,4},{7,6},{5,7},{3,5},{1,3},{8,9},{10,8},{12,1... | collective-permute-start | bytes 1572872 | tf_op jit(solution)/shard_map/ppermute | solution.py:102
  171.5 14.9 %collective-permute-start.19 = (bf16[128,2048]{1,0:T(8,128)(2,1)S(1)}, bf16[128,2048]{1,0:T(8,128)(2,1)S(1)}, u32[]{:S(2)}, u32[]{:S(2)}) collective-permute-start(bf16[128,2048]{1,0:T(8,128)(2,1)S(1)} %add_convert_fusion.10), channel_id=1, source_target_pairs={{0,2},{2,4},{4,6},{6,7},{7,5},{5,3},{3,1},{1,0},{8,10},{10,12},{12... | collective-permute-start | bytes 1572872 | tf_op jit(solution)/shard_map/ppermute | solution.py:102
  173.2 35.0 %collective-permute-start.33 = (bf16[3,176,2048]{2,1,0:T(8,128)(2,1)S(1)}, bf16[3,176,2048]{2,1,0:T(8,128)(2,1)S(1)}, u32[]{:S(2)}, u32[]{:S(2)}) collective-permute-start(bf16[3,176,2048]{2,1,0:T(8,128)(2,1)S(1)} %grads_3.1.refs_18_), channel_id=1, source_target_pairs={{24,0},{0,8},{8,16},{16,24},{25,1},{1,9},{9,17},{17,25},{26,2},{2,... | collective-permute-start | bytes 6488072 | tf_op jit(solution)/shard_map/ppermute | solution.py:32
  173.4 20.5 %collective-permute-start.26 = (bf16[128,2048]{1,0:T(8,128)(2,1)S(1)}, bf16[128,2048]{1,0:T(8,128)(2,1)S(1)}, u32[]{:S(2)}, u32[]{:S(2)}) collective-permute-start(bf16[128,2048]{1,0:T(8,128)(2,1)S(1)} %add_convert_fusion.4), channel_id=1, source_target_pairs={{0,2},{2,4},{4,6},{6,7},{7,5},{5,3},{3,1},{1,0},{8,10},{10,12},{12... | collective-permute-start | bytes 1572872 | tf_op jit(solution)/shard_map/ppermute | solution.py:102
  186.4 11.7 %collective-permute-start.30 = (bf16[128,2048]{1,0:T(8,128)(2,1)S(1)}, bf16[128,2048]{1,0:T(8,128)(2,1)S(1)}, u32[]{:S(2)}, u32[]{:S(2)}) collective-permute-start(bf16[128,2048]{1,0:T(8,128)(2,1)S(1)} %add_convert_fusion.1), channel_id=1, source_target_pairs={{0,1},{2,0},{4,2},{6,4},{7,6},{5,7},{3,5},{1,3},{8,9},{10,8},{12,1... | collective-permute-start | bytes 1572872 | tf_op jit(solution)/shard_map/ppermute | solution.py:102
  193.9 12.8 %collective-permute-start.23 = (bf16[128,2048]{1,0:T(8,128)(2,1)S(1)}, bf16[128,2048]{1,0:T(8,128)(2,1)S(1)}, u32[]{:S(2)}, u32[]{:S(2)}) collective-permute-start(bf16[128,2048]{1,0:T(8,128)(2,1)S(1)} %add_convert_fusion.7), channel_id=1, source_target_pairs={{0,1},{2,0},{4,2},{6,4},{7,6},{5,7},{3,5},{1,3},{8,9},{10,8},{12,1... | collective-permute-start | bytes 1572872 | tf_op jit(solution)/shard_map/ppermute | solution.py:102
  198.0 9.2 %collective-permute-start.20 = (bf16[128,2048]{1,0:T(8,128)(2,1)S(1)}, bf16[128,2048]{1,0:T(8,128)(2,1)S(1)}, u32[]{:S(2)}, u32[]{:S(2)}) collective-permute-start(bf16[128,2048]{1,0:T(8,128)(2,1)S(1)} %add_convert_fusion.9), channel_id=1, source_target_pairs={{0,2},{2,4},{4,6},{6,7},{7,5},{5,3},{3,1},{1,0},{8,10},{10,12},{12... | collective-permute-start | bytes 1572872 | tf_op jit(solution)/shard_map/ppermute | solution.py:102

commit v3 on v2

v3 whole, which is shorter than its diff:
```python
import jax
import jax.numpy as jnp
from jax import lax
from jax.experimental import pallas as pl
from jax.experimental.pallas import tpu as pltpu
from jax.sharding import PartitionSpec as P

BF16 = jnp.bfloat16
F32 = jnp.float32
VMEM_LIMIT = 24 * 1024 * 1024
NO_COST = pl.CostEstimate(flops=1, bytes_accessed=1, transcendentals=0)


def work_cost(flops):
    return pl.CostEstimate(flops=flops, bytes_accessed=1, transcendentals=0)


CONTRACT_LAST = (((1,), (1,)), ((), ()))
CONTRACT_FIRST = (((0,), (0,)), ((), ()))


def whole_in_vmem():
    return pl.BlockSpec(memory_space=pltpu.VMEM)


def untouched():
    return pl.BlockSpec(memory_space=pl.ANY)


def tile_of(size, most):
    tile = min(size, most)
    while size % tile:
        tile -= 1
    return tile


def ring_order(size):
    return list(range(0, size, 2)) + list(range(1, size, 2))[::-1]


def ring_source(size, ahead):
    me = lax.axis_index("local")
    half = lax.div(size + 1, 2)
    place = jnp.where(lax.rem(me, 2) == 0, lax.div(me, 2), size - 1 - lax.div(me, 2))
    there = lax.rem(place + ahead, size)
    return jnp.where(there < half, 2 * there, 2 * (size - 1 - there) + 1)


def partner_of(place, turn, slots):
    return place ^ turn


def owner_of(node, turn, slots, stride):
    return partner_of(node // stride, turn, slots) * stride + node % stride


def turn_slot(turn, slots, stride):
    place = lax.div(lax.axis_index("node"), stride)
    return lax.rem(place - partner_of(place, turn, slots) + slots, slots)


def turn_pick(fetch_pick, turn, stride):
    slots = fetch_pick.shape[1]
    node = lax.axis_index("node")
    place = lax.div(node, stride)
    partner = partner_of(place, turn, slots)
    reader = partner * stride + lax.rem(node, stride)
    return fetch_pick[reader, lax.rem(partner - place + slots, slots)]


def exchange(block, turn, slots):
    size = lax.axis_size("node")
    stride = size // slots
    return lax.ppermute(
        block, "node", [(owner_of(node, turn, slots, stride), node) for node in range(size)]
    )


def pick_kernel(turns, stride, fetch_pick, panels, *refs):
    out, sems = refs[-2:]
    copies = [
        pltpu.make_async_copy(panels.at[turn_pick(fetch_pick, turn, stride)], out.at[i], sems.at[i])
        for i, turn in enumerate(turns)
    ]
    for copy in copies:
        copy.start()
    for copy in copies:
        copy.wait()


def pick_pass(turns, stride, fetch_pick, panels, after=()):
    return pl.pallas_call(
        lambda *refs: pick_kernel(turns, stride, *refs),
        out_shape=jax.ShapeDtypeStruct((len(turns),) + panels.shape[1:], BF16),
        in_specs=[pl.BlockSpec(memory_space=pltpu.SMEM), untouched()] + [untouched()] * len(after),
        out_specs=untouched(),
        scratch_shapes=[pltpu.SemaphoreType.DMA((len(turns),))],
        compiler_params=pltpu.CompilerParams(vmem_limit_bytes=1024 * 1024),
        name="pick",
    )(fetch_pick, panels, *after)


def gate(value, after):
    return pl.pallas_call(
        lambda *refs: None,
        out_shape=jax.ShapeDtypeStruct(value.shape, value.dtype),
        in_specs=[untouched()] * (1 + len(after)),
        out_specs=untouched(),
        input_output_aliases={0: 0},
        compiler_params=pltpu.CompilerParams(vmem_limit_bytes=1024 * 1024),
        cost_estimate=NO_COST,
        name="gate",
    )(value, *after)


def total_kernel(turns, stride, counts, fetch_pick, *refs):
    out, refs = refs[-1], list(refs[: sum(counts)])
    picks = [turn_pick(fetch_pick, turn, stride) for turn in turns]
    experts, kinds = out.shape[:2]
    grads = []
    for count in counts:
        taken, refs = refs[:count], refs[count:]
        grads.append([taken[0].at[kind] for kind in range(kinds)] if count == 1 else taken)
    for kind in range(kinds):
        terms = [grad[kind][...].astype(F32) for grad in grads]
        for e in range(experts):
            total = jnp.zeros(terms[0].shape, F32)
            for pick, term in zip(picks, terms):
                total += jnp.where(pick == e, term, 0.0)
            out[e, kind] = total.astype(BF16)


def total_pass(turns, stride, fetch_pick, grads, shape, after):
    counts = [len(grad) for grad in grads]
    return pl.pallas_call(
        lambda *refs: total_kernel(turns, stride, counts, *refs),
        out_shape=jax.ShapeDtypeStruct(shape, BF16),
        in_specs=[pl.BlockSpec(memory_space=pltpu.SMEM)]
        + [whole_in_vmem()] * sum(counts)
        + [untouched()] * len(after),
        out_specs=whole_in_vmem(),
        compiler_params=pltpu.CompilerParams(vmem_limit_bytes=VMEM_LIMIT),
        cost_estimate=NO_COST,
        name="total",
    )(fetch_pick, *[grad for slot_grads in grads for grad in slot_grads], *after)


def add_kernel(turn, stride, fetch_pick, total, grad, out, sums, terms, in_sems, out_sems):
    pick = turn_pick(fetch_pick, turn, stride)
    kinds = grad.shape[0]
    reads = [
        (
            pltpu.make_async_copy(total.at[pick, kind], sums.at[kind], in_sems.at[kind]),
            pltpu.make_async_copy(grad.at[kind], terms.at[kind], in_sems.at[kinds + kind]),
        )
        for kind in range(kinds)
    ]
    writes = [
        pltpu.make_async_copy(sums.at[kind], out.at[pick, kind], out_sems.at[kind])
        for kind in range(kinds)
    ]
    for first, second in reads:
        first.start()
        second.start()
    for kind in range(kinds):
        for read in reads[kind]:
            read.wait()
        sums[kind] = (sums[kind].astype(F32) + terms[kind].astype(F32)).astype(BF16)
        writes[kind].start()
    for write in writes:
        write.wait()


def add_pass(turn, stride, fetch_pick, total, grad):
    kinds = grad.shape[0]
    return pl.pallas_call(
        lambda *refs: add_kernel(turn, stride, *refs),
        out_shape=jax.ShapeDtypeStruct(total.shape, BF16),
        in_specs=[pl.BlockSpec(memory_space=pltpu.SMEM), untouched(), untouched()],
        out_specs=untouched(),
        input_output_aliases={1: 0},
        scratch_shapes=[
            pltpu.VMEM(grad.shape, BF16),
            pltpu.VMEM(grad.shape, BF16),
            pltpu.SemaphoreType.DMA((2 * kinds,)),
            pltpu.SemaphoreType.DMA((kinds,)),
        ],
        compiler_params=pltpu.CompilerParams(vmem_limit_bytes=8 * 1024 * 1024),
        name="add",
    )(fetch_pick, total, grad)


def ring_step(block, order, distance):
    size = len(order)
    return lax.ppermute(
        block, "local", [(order[i], order[(i + distance) % size]) for i in range(size)]
    )


def add_rows_kernel(*refs):
    a, b, out = refs[0], refs[1], refs[-1]
    out[...] = (a[...].astype(F32) + b[...].astype(F32)).astype(out.dtype)


def add_rows(a, b, dtype, after=()):
    return pl.pallas_call(
        add_rows_kernel,
        out_shape=jax.ShapeDtypeStruct(a.shape, dtype),
        in_specs=[whole_in_vmem()] * 2 + [untouched()] * len(after),
        out_specs=whole_in_vmem(),
        compiler_params=pltpu.CompilerParams(vmem_limit_bytes=VMEM_LIMIT),
        cost_estimate=NO_COST,
        name="add_rows",
    )(a, b, *after)


def acts_kernel(turn, slots, stride, size, offsets, *refs):
    parts = len(offsets)
    x_refs, dy_refs = refs[:parts], refs[parts : 2 * parts]
    panel, routes, weight, acts = *refs[2 * parts : 2 * parts + 3], refs[-1]
    units, width = panel.shape[1:]
    part = x_refs[0].shape[0]
    at_once = 2 if parts % 2 == 0 else 1
    slot = turn_slot(turn, slots, stride)
    for d in range(0, parts, at_once):
        here = slice(d * part, (d + at_once) * part)
        x = jnp.concatenate([ref[...] for ref in x_refs[d : d + at_once]], axis=0)
        dy = jnp.concatenate([ref[...] for ref in dy_refs[d : d + at_once]], axis=0)
        both = lax.dot_general(
            panel[0:2].reshape(2 * units, width), x, CONTRACT_LAST, preferred_element_type=F32
        )
        gate, up = both[:units], both[units:]
        d_hidden = lax.dot_general(panel[2], dy, CONTRACT_LAST, preferred_element_type=F32)
        sources = [ring_source(size, ahead) for ahead in offsets[d : d + at_once]]
        scale = jnp.concatenate(
            [
                jnp.where(routes[pl.ds(i, 1), :] == slot, weight[pl.ds(i, 1), :], 0.0)
                for i in sources
            ],
            axis=1,
        )
        sigmoid_gate = jax.nn.sigmoid(gate)
        activated = gate * sigmoid_gate
        d_hidden = d_hidden * scale
        d_gate = d_hidden * up * sigmoid_gate * (1.0 + gate * (1.0 - sigmoid_gate))
        acts[0:units, here] = d_gate.astype(BF16)
        acts[units : 2 * units, here] = (d_hidden * activated).astype(BF16)
        acts[2 * units : 3 * units, here] = (activated * up * scale).astype(BF16)


def acts_pass(name, turn, slots, stride, offsets, x_parts, dy_parts, panel, routes, weight, after=()):
    parts = len(x_parts)
    part = x_parts[0].shape[0]
    return pl.pallas_call(
        lambda *refs: acts_kernel(turn, slots, stride, routes.shape[0], offsets, *refs),
        out_shape=jax.ShapeDtypeStruct((3 * panel.shape[1], parts * part), BF16),
        in_specs=[whole_in_vmem()] * (2 * parts + 3) + [untouched()] * len(after),
        out_specs=whole_in_vmem(),
        compiler_params=pltpu.CompilerParams(vmem_limit_bytes=VMEM_LIMIT),
        cost_estimate=work_cost(6 * parts * part * panel.shape[1] * panel.shape[2]),
        name=f"acts_{turn}_{name}",
    )(*x_parts, *dy_parts, panel, routes, weight, *after)


def grads_kernel(parts, groups, kinds, *refs):
    x_refs, dy_refs = refs[:parts], refs[parts : 2 * parts]
    acts, grads = refs[2 * parts : 2 * parts + groups], refs[-kinds:]
    if kinds == 1:
        grads = [grads[0].at[kind] for kind in range(3)]
    units, width = grads[0].shape
    columns = tile_of(width, 512)
    for start in range(0, width, columns):
        here = slice(start, start + columns)
        x = jnp.concatenate([ref[:, here] for ref in x_refs], axis=0)
        dy = jnp.concatenate([ref[:, here] for ref in dy_refs], axis=0)
        d_both = jnp.concatenate([act[0 : 2 * units, :] for act in acts], axis=1)
        d_both = jnp.dot(d_both, x, preferred_element_type=F32).astype(BF16)
        grads[0][:, here] = d_both[0:units]
        grads[1][:, here] = d_both[units:]
        hidden = jnp.concatenate([act[2 * units : 3 * units, :] for act in acts], axis=1)
        grads[2][:, here] = jnp.dot(hidden, dy, preferred_element_type=F32).astype(BF16)


def grads_pass(turn, x_parts, dy_parts, acts, shapes, after=()):
    parts = len(x_parts)
    return pl.pallas_call(
        lambda *refs: grads_kernel(parts, len(acts), len(shapes), *refs),
        out_shape=tuple(jax.ShapeDtypeStruct(shape, BF16) for shape in shapes),
        in_specs=[whole_in_vmem()] * (2 * parts + len(acts)) + [untouched()] * len(after),
        out_specs=tuple(whole_in_vmem() for _ in shapes),
        compiler_params=pltpu.CompilerParams(vmem_limit_bytes=VMEM_LIMIT),
        cost_estimate=work_cost(6 * parts * acts[0].shape[0] // 3 * x_parts[0].size),
        name=f"grads_{turn}",
    )(*x_parts, *dy_parts, *acts, *after)


def chunk_kernel(wanted, slots, part, acts, panels, outs):
    units, width = panels[0].shape[1:]
    columns = tile_of(width, 512)

    @pl.loop(0, width // columns)
    def _(step):
        here = pl.ds(pl.multiple_of(step * columns, columns), columns)
        kinds = {"mixed": (2, 3), "grad": (0, 2)}
        sides = {
            kind: jnp.concatenate(
                [panel[which, :, here] for panel in panels for which in range(*span)], axis=0
            )
            for kind, span in kinds.items()
        }
        for out, (kind, group, row) in zip(outs, wanted):
            low, high = (units * which for which in kinds[kind])
            act = jnp.concatenate(
                [act[group][low:high, row * part : (row + 1) * part] for act in acts], axis=0
            )
            total = lax.dot_general(act, sides[kind], CONTRACT_FIRST, preferred_element_type=F32)
            out[:, here] = total.astype(BF16)


def chunk_pass(wanted, acts, panels, groups, part, after=()):
    slots = len(panels)
    width = panels[0].shape[2]
    named = [
        (kind, g, group.index(d)) for kind, d in wanted for g, group in enumerate(groups) if d in group
    ]

    def kernel(*refs):
        act_refs = [refs[s * len(groups) : (s + 1) * len(groups)] for s in range(slots)]
        rest = refs[slots * len(groups) :]
        chunk_kernel(named, slots, part, act_refs, rest[:slots], rest[slots + len(after) :])

    return pl.pallas_call(
        kernel,
        out_shape=tuple(jax.ShapeDtypeStruct((part, width), BF16) for _ in wanted),
        in_specs=[whole_in_vmem()] * (slots * len(groups) + slots) + [untouched()] * len(after),
        out_specs=tuple(whole_in_vmem() for _ in wanted),
        compiler_params=pltpu.CompilerParams(vmem_limit_bytes=VMEM_LIMIT),
        cost_estimate=NO_COST,
        name=f"chunks_{len(wanted)}",
    )(*[act for slot_acts in acts for act in slot_acts], *panels, *after)


class Line:
    def __init__(self):
        self.tail = ()

    def step(self, make):
        out = make(self.tail)
        self.tail = (out[0] if isinstance(out, (tuple, list)) else out,)
        return out

    def arrive(self, value):
        return self.step(lambda after: gate(value, after))


def body(tokens, cotangent, routes, route_weight, fetch_pick, panels):
    slots = fetch_pick.shape[1]
    stride = lax.axis_size("node") // slots
    part, width = tokens.shape
    order = ring_order(lax.axis_size("local"))
    size = len(order)
    up_most, down_most = size // 2, size - 1 - size // 2
    last, late = slots - 1, slots - 2
    middle = list(range(1, late))
    line = Line()

    ring_routes = routes.reshape(size, part)
    ring_weight = route_weight.reshape(size, part)
    near = [d for d in range(size) if min(d, size - d) <= size // 4 and d != size // 4]
    groups = [near, [d for d in range(size) if d not in near]]
    rows = [d for group in groups for d in group]
    x_parts = [tokens] + [None] * (size - 1)
    dy_parts = [cotangent] + [None] * (size - 1)
    acts = [[None, None] for _ in range(slots)]
    grads, back = [None] * slots, [None] * slots

    def pick(turn):
        return line.step(lambda after: pick_pass([turn], stride, fetch_pick, panels, after))[0]

    def make_acts(turn, g):
        take = groups[g]
        acts[turn][g] = line.step(
            lambda after: acts_pass(
                "nf"[g],
                turn,
                slots,
                stride,
                take,
                [x_parts[d] for d in take],
                [dy_parts[d] for d in take],
                read[turn],
                ring_routes,
                ring_weight,
                after,
            )
        )

    def make_grads(turn):
        shape = read[turn].shape
        grads[turn] = line.step(
            lambda after: grads_pass(
                turn,
                [x_parts[d] for d in rows],
                [dy_parts[d] for d in rows],
                acts[turn],
                [shape[1:]] * shape[0] if turn in middle else [shape],
                after,
            )
        )
        if turn != last:
            back[turn] = [exchange(grad, turn, slots) if turn else grad for grad in grads[turn]]

    read = [None] * slots
    read[late] = exchange(pick(late), late, slots)
    for turn in middle:
        read[turn] = exchange(pick(turn), turn, slots)
    read[last], read[0] = pick(last), pick(0)

    chains = [(x_parts, 1, up_most), (dy_parts, -1, up_most), (x_parts, -1, down_most), (dy_parts, 1, down_most)]
    moving = [ring_step(parts[0], order, way) for parts, way, _ in chains]
    for turn in middle:
        read[turn] = line.arrive(read[turn])
    for hop in range(1, up_most + 1):
        for i, (parts, way, hops) in enumerate(chains):
            if hop > hops:
                continue
            if hop == max(1, up_most // 2) and i == 2:
                read[late] = line.arrive(read[late])
                read[last] = exchange(line.arrive(read[last]), last, slots)
            arrived = line.arrive(moving[i])
            parts[-way * hop % size] = arrived
            if hop < hops:
                moving[i] = ring_step(arrived, order, way)
            if hop == max(1, up_most // 2) and i == len(chains) - 1:
                for turn in middle + [0]:
                    make_acts(turn, 0)

    for turn in middle:
        make_acts(turn, 1)
        make_grads(turn)
    make_acts(late, 0)
    make_acts(late, 1)
    make_grads(late)
    make_acts(0, 1)
    for turn in middle:
        back[turn] = [line.arrive(grad) for grad in back[turn]]
    read[last] = line.arrive(read[last])
    make_acts(last, 1)
    make_acts(last, 0)

    kinds = ("mixed", "grad")
    early = [("mixed", up_most), ("grad", size - up_most), ("mixed", size - down_most), ("grad", down_most)]
    later = [(kind, d) for kind in kinds for d in range(size) if (kind, d) not in early]
    chunks = dict(zip(early, line.step(lambda after: chunk_pass(early, acts, read, groups, part, after))))
    chains = [("mixed", 1, up_most), ("grad", -1, up_most), ("mixed", -1, down_most), ("grad", 1, down_most)]
    moving = [ring_step(chunks[kind, way * hops % size], order, way) for kind, way, hops in chains]
    chunks.update(zip(later, line.step(lambda after: chunk_pass(later, acts, read, groups, part, after))))
    make_grads(last)
    make_grads(0)

    sums = {}
    for hop in range(1, up_most + 1):
        for i, (kind, way, hops) in enumerate(chains):
            if hop > hops:
                continue
            if hop == max(1, up_most // 2) and i == 2:
                back[late] = [line.arrive(back[late][0])]
                back[last] = exchange(line.arrive(grads[last][0]), last, slots)
            left = hops - hop
            if left:
                chunk = chunks[kind, way * left % size]
                arrived = line.step(lambda after: add_rows(moving[i], chunk, BF16, after))
                moving[i] = ring_step(arrived, order, way)
                if left == 1 and i == 1:
                    near_total = line.step(
                        lambda after: total_pass(
                            list(range(last)), stride, fetch_pick, back[:last], panels.shape, after
                        )
                    )
            elif kind not in sums:
                sums[kind] = line.step(lambda after: add_rows(moving[i], chunks[kind, 0], F32, after))
            else:
                sums[kind] = line.step(lambda after: add_rows(moving[i], sums[kind], BF16, after))
    panel_grad = add_pass(last, stride, fetch_pick, near_total, back[last])
    return sums["mixed"], sums["grad"], panel_grad


def solution(mesh):
    return jax.shard_map(
        body,
        mesh=mesh,
        in_specs=(
            P(("node", "local"), None),
            P(("node", "local"), None),
            P("node", None),
            P("node", None),
            P(),
            P("node", None, "local", None),
        ),
        out_specs=(
            P(("node", "local"), None),
            P(("node", "local"), None),
            P("node", None, "local", None),
        ),
        check_vma=False,
    )
```

time: 215 us -> 209 us (0.972)
  waiting for transfers between devices: 129 us -> 116 us
  Pallas kernels: 41.5 us -> 49.5 us
  other arithmetic: 3.31 us -> 0.01 us
  local copies, waits for them, and re-layouts: 2.92 us -> 6.21 us
    ppermute x28, waiting for transfers between devices: 129 us -> 105 us  [ring_step(): lax.ppermute(block, 'local', [(order[i], order[(i + distance) % size]) fo...]
    ppermute x6 -> x8, waiting for transfers between devices: 0.02 us -> 11.3 us  [exchange(): lax.ppermute(block, 'node', [(owner_of(node, turn, slots, stride), node)...]
    pallas_call x14 -> x55, Pallas kernels: 29.9 us -> 37.2 us  [the longest x8 12.6 us: acts_pass(): pl.pallas_call(lambda *refs: acts_kernel(turn, slots, stride, routes.shap...]
    ppermute x28, starting transfers between devices: 33.6 us -> 28.9 us  [ring_step(): lax.ppermute(block, 'local', [(order[i], order[(i + distance) % size]) fo...]
    convert_element_type x12 -> x0, other arithmetic: 3.31 us -> none  [the longest x2 2.06 us: ring_scatter(): (up.astype(F32) + down.astype(F32) + chunks[0].astype(F32)).astype(BF16)]
    unnamed x12 -> x22, local copies, waits for them, and re-layouts: 2.92 us -> 6.21 us
    ppermute x6 -> x8, starting transfers between devices: 3.45 us -> 6.37 us  [exchange(): lax.ppermute(block, 'node', [(owner_of(node, turn, slots, stride), node)...]
  transfers between devices with their start and end apart: 34 -> 36, of which waited for: 22 -> 20; matrix products, arithmetic and copies ran while one was open for 2% -> 0% of each run, Pallas kernels for 13% -> 21%
where the time goes in v3:
time: 209 us; the launch traced here: 208 us
  waiting for transfers between devices  116 us (56%)
  Pallas kernels  49.5 us (24%)
  starting transfers between devices  35.3 us (17%)
  local copies, waits for them, and re-layouts  6.21 us (3%)
    ppermute x28, waiting for transfers between devices, ring_step(): lax.ppermute(block, 'local', [(order[i], order[(i + distance) % size]) fo...  105 us
    ppermute x28, starting transfers between devices, ring_step(): lax.ppermute(block, 'local', [(order[i], order[(i + distance) % size]) fo...  28.9 us
    pallas_call x8, Pallas kernels, acts_pass(): pl.pallas_call(lambda *refs: acts_kernel(turn, slots, stride, routes.shap...  12.6 us
    pallas_call x2, Pallas kernels, chunk_pass(): pl.pallas_call(kernel, out_shape=tuple((jax.ShapeDtypeStruct((part, width...  12.3 us
    ppermute x8, waiting for transfers between devices, exchange(): lax.ppermute(block, 'node', [(owner_of(node, turn, slots, stride), node)...  11.3 us
    pallas_call x4, Pallas kernels, grads_pass(): pl.pallas_call(lambda *refs: grads_kernel(parts, len(acts), len(shapes),...  9.61 us
    ppermute x8, starting transfers between devices, exchange(): lax.ppermute(block, 'node', [(owner_of(node, turn, slots, stride), node)...  6.37 us
    unnamed x22, local copies, waits for them, and re-layouts  6.21 us
  transfers between devices with their start and end apart: 36, of which 20 were waited for; matrix products, arithmetic and copies ran while one was open for 0% of the time, Pallas kernels for 21%

profile of v3, /device:TPU:0, one launch (start us, length us, event | category | flops | bytes accessed | tf_op | source)
XLA Modules:
  0.0 208.5 jit_solution(3553611506817420487)
XLA Ops:
  0.6 2.2 %copy-done = bf16[2,3,176,2048]{3,2,1,0:T(8,128)(2,1)S(1)} copy-done((bf16[2,3,176,2048]{3,2,1,0:T(8,128)(2,1)S(1)}, bf16[2,3,176,2048]{3,2,1,0:T(8,128)(2,1)}, u32[]{:S(2)}) %copy-start) | copy-done | bytes 4325400
  2.9 0.7 copy-done.7
  3.5 0.8 pick.4.refs_2_
  4.4 0.8 pick.5.refs_2_
  5.8 2.6 %collective-permute-start.8 = (bf16[3,176,2048]{2,1,0:T(8,128)(2,1)S(1)}, bf16[3,176,2048]{2,1,0:T(8,128)(2,1)S(1)}, u32[]{:S(2)}, u32[]{:S(2)}) collective-permute-start(bf16[3,176,2048]{2,1,0:T(8,128)(2,1)S(1)} %bitcast.13), channel_id=1, source_target_pairs={{16,0},{24,8},{0,16},{8,24},{17,1},{25,9},{1,17},{9,25},{18,2},{26... | collective-permute-start | bytes 6488072 | tf_op jit(solution)/shard_map/ppermute | solution.py:74
  8.4 1.6 collective-permute-start.2
  10.4 1.5 collective-permute-start
  11.9 0.7 collective-permute-start.5
  12.6 0.8 pick.6.refs_2_
  13.4 0.8 pick.7.refs_1_
  14.3 8.9 %collective-permute-done.2.refs_0_ = bf16[128,2048]{1,0:T(8,128)(2,1)S(1)} collective-permute-done((bf16[128,2048]{1,0:T(8,128)(2,1)S(1)}, bf16[128,2048]{1,0:T(8,128)(2,1)S(1)}, u32[]{:S(2)}, u32[]{:S(2)}) %collective-permute-start.2) | collective-permute-done | bytes 524320 | tf_op jit(solution)/shard_map/ppermute | solution.py:195
  23.1 1.6 collective-permute-start.4
  25.2 10.8 %collective-permute-done.refs_0_ = bf16[128,2048]{1,0:T(8,128)(2,1)S(1)} collective-permute-done((bf16[128,2048]{1,0:T(8,128)(2,1)S(1)}, bf16[128,2048]{1,0:T(8,128)(2,1)S(1)}, u32[]{:S(2)}, u32[]{:S(2)}) %collective-permute-start) | collective-permute-done | bytes 524320 | tf_op jit(solution)/shard_map/ppermute | solution.py:195
  36.4 1.6 collective-permute-start.6
  38.0 7.6 %collective-permute-done.4.refs_0_ = bf16[128,2048]{1,0:T(8,128)(2,1)S(1)} collective-permute-done((bf16[128,2048]{1,0:T(8,128)(2,1)S(1)}, bf16[128,2048]{1,0:T(8,128)(2,1)S(1)}, u32[]{:S(2)}, u32[]{:S(2)}) %collective-permute-start.4) | collective-permute-done | bytes 524320 | tf_op jit(solution)/shard_map/ppermute | solution.py:195
  45.6 1.6 collective-permute-start.12
  47.7 8.3 %collective-permute-done.8.refs_0_ = bf16[3,176,2048]{2,1,0:T(8,128)(2,1)S(1)} collective-permute-done((bf16[3,176,2048]{2,1,0:T(8,128)(2,1)S(1)}, bf16[3,176,2048]{2,1,0:T(8,128)(2,1)S(1)}, u32[]{:S(2)}, u32[]{:S(2)}) %collective-permute-start.8) | collective-permute-done | bytes 2162720 | tf_op jit(solution)/shard_map/ppermute | solution.py:74
  56.0 1.0 collective-permute-start.16
  57.0 1.4 collective-permute-done.7.refs_0_
  58.9 1.6 collective-permute-start.14
  60.5 1.6 acts_1_n.1.refs_11_.refs_16_.refs_2_
  62.1 1.6 acts_0_n.1.refs_1_.refs_0_.refs_16_
  63.7 4.4 %collective-permute-done.12.refs_0_ = bf16[128,2048]{1,0:T(8,128)(2,1)S(1)} collective-permute-done((bf16[128,2048]{1,0:T(8,128)(2,1)S(1)}, bf16[128,2048]{1,0:T(8,128)(2,1)S(1)}, u32[]{:S(2)}, u32[]{:S(2)}) %collective-permute-start.12) | collective-permute-done | bytes 524320 | tf_op jit(solution)/shard_map/ppermute | solution.py:195
  68.1 1.6 collective-permute-start.13
  70.2 10.8 %collective-permute-done.10.refs_0_ = bf16[128,2048]{1,0:T(8,128)(2,1)S(1)} collective-permute-done((bf16[128,2048]{1,0:T(8,128)(2,1)S(1)}, bf16[128,2048]{1,0:T(8,128)(2,1)S(1)}, u32[]{:S(2)}, u32[]{:S(2)}) %collective-permute-start.10) | collective-permute-done | bytes 524320 | tf_op jit(solution)/shard_map/ppermute | solution.py:195
  80.9 8.8 %collective-permute-done.13.refs_0_ = bf16[128,2048]{1,0:T(8,128)(2,1)S(1)} collective-permute-done((bf16[128,2048]{1,0:T(8,128)(2,1)S(1)}, bf16[128,2048]{1,0:T(8,128)(2,1)S(1)}, u32[]{:S(2)}, u32[]{:S(2)}) %collective-permute-start.13) | collective-permute-done | bytes 524320 | tf_op jit(solution)/shard_map/ppermute | solution.py:195
  89.8 1.3 collective-permute-done.15.refs_0_
  91.1 1.6 acts_1_f.1.refs_17_.refs_18_.refs_3_
  92.7 2.4 %grads_1.1 = (bf16[176,2048]{1,0:T(8,128)(2,1)S(1)}, bf16[176,2048]{1,0:T(8,128)(2,1)S(1)}, bf16[176,2048]{1,0:T(8,128)(2,1)S(1)}) custom-call(bf16[128,2048]{1,0:T(8,128)(2,1)S(1)} %copy-done.2, bf16[128,2048]{1,0:T(8,128)(2,1)S(1)} %gate.26.refs_1_, bf16[128,2048]{1,0:T(8,128)(2,1)S(1)} %gate.28.refs_1_.refs_2_, ...), custom_call_target="tpu_custom_call" | custom-call | flops 2214592512 | bytes 1 | tf_op jit(solution)/shard_map/grads_1/pallas_call | solution.py:286
  95.1 1.6 acts_2_n.1.refs_11_.refs_16_.refs_4_
  96.7 1.6 acts_2_f.1.refs_17_.refs_18_.refs_5_
  98.2 2.4 %grads_2.1.refs_11_ = bf16[3,176,2048]{2,1,0:T(8,128)(2,1)S(1)} custom-call(bf16[128,2048]{1,0:T(8,128)(2,1)S(1)} %copy-done.2, bf16[128,2048]{1,0:T(8,128)(2,1)S(1)} %gate.26.refs_1_, bf16[128,2048]{1,0:T(8,128)(2,1)S(1)} %gate.28.refs_1_.refs_2_, bf16[128,2048]{1,0:T(8,128)(2,1)S(1)} %gate.24.refs_1_.refs_3_, ...), custom_call_target="tpu_custom_call" | custom-call | flops 2214592512 | bytes 1 | tf_op jit(solution)/shard_map/grads_2/pallas_call | solution.py:286
  101.7 1.6 acts_0_f.1.refs_1_.refs_17_
  103.4 1.0 collective-permute-done.18.refs_0_
  104.4 1.0 collective-permute-done.17.refs_0_
  105.5 1.6 acts_3_f.1.refs_11_.refs_7_.refs_17_
  107.1 1.6 acts_3_n.1.refs_6_.refs_12_.refs_16_
  108.6 4.1 %chunks_4.1 = (bf16[128,2048]{1,0:T(8,128)(2,1)S(1)}, bf16[128,2048]{1,0:T(8,128)(2,1)}, bf16[128,2048]{1,0:T(8,128)(2,1)}, bf16[128,2048]{1,0:T(8,128)(2,1)}) custom-call(bf16[528,512]{1,0:T(8,128)(2,1)S(1)} %acts_0_n.1.refs_1_.refs_0_.refs_16_, bf16[528,512]{1,0:T(8,128)(2,1)S(1)} %acts_0_f.1.refs_1_.refs_17_, ...), custom_call_target="tpu_custom_call" | custom-call | flops 1 | bytes 1 | tf_op jit(solution)/shard_map/chunks_4/pallas_call | solution.py:332
  112.8 1.6 collective-permute-start.20
  114.8 8.1 %chunks_12.1 = (bf16[128,2048]{1,0:T(8,128)(2,1)S(1)}, bf16[128,2048]{1,0:T(8,128)(2,1)S(1)}, bf16[128,2048]{1,0:T(8,128)(2,1)S(1)}, bf16[128,2048]{1,0:T(8,128)...) custom-call(bf16[528,512]{1,0:T(8,128)(2,1)S(1)} %acts_0_n.1.refs_1_, ...), custom_call_target="tpu_custom_call" | custom-call | flops 1 | bytes 1 | tf_op jit(solution)/shard_map/chunks_12/pallas_call | solution.py:332
  122.9 1.6 collective-permute-start.22
  125.0 2.4 %grads_3.1.refs_18_.refs_0_ = bf16[3,176,2048]{2,1,0:T(8,128)(2,1)S(1)} custom-call(bf16[128,2048]{1,0:T(8,128)(2,1)S(1)} %copy-done.2, bf16[128,2048]{1,0:T(8,128)(2,1)S(1)} %gate.26.refs_1_, bf16[128,2048]{1,0:T(8,128)(2,1)S(1)} %gate.28.refs_1_.refs_2_, bf16[128,2048]{1,0:T(8,128)(2,1)S(1)} %gate.24.refs_1_.refs_3_, ...), custom_call_target="tpu_custom_call" | custom-call | flops 2214592512 | bytes 1 | tf_op jit(solution)/shard_map/grads_3/pallas_call | solution.py:286
  127.4 2.4 %grads_0.1.refs_2_.refs_1_ = bf16[3,176,2048]{2,1,0:T(8,128)(2,1)S(1)} custom-call(bf16[128,2048]{1,0:T(8,128)(2,1)S(1)} %copy-done.2, bf16[128,2048]{1,0:T(8,128)(2,1)S(1)} %gate.26.refs_1_, bf16[128,2048]{1,0:T(8,128)(2,1)S(1)} %gate.28.refs_1_.refs_2_, bf16[128,2048]{1,0:T(8,128)(2,1)S(1)} %gate.24.refs_1_.refs_3_, ...), custom_call_target="tpu_custom_call" | custom-call | flops 2214592512 | bytes 1 | tf_op jit(solution)/shard_map/grads_0/pallas_call | solution.py:286
  130.0 1.6 collective-permute-start.21
  132.2 8.4 %collective-permute-done.23.refs_0_ = bf16[128,2048]{1,0:T(8,128)(2,1)S(1)} collective-permute-done((bf16[128,2048]{1,0:T(8,128)(2,1)}, bf16[128,2048]{1,0:T(8,128)(2,1)S(1)}, u32[]{:S(2)}, u32[]{:S(2)}) %collective-permute-start.23) | collective-permute-done | bytes 524320 | tf_op jit(solution)/shard_map/ppermute | solution.py:195
  140.9 8.3 %collective-permute-done.21.refs_0_ = bf16[128,2048]{1,0:T(8,128)(2,1)S(1)} collective-permute-done((bf16[128,2048]{1,0:T(8,128)(2,1)S(1)}, bf16[128,2048]{1,0:T(8,128)(2,1)S(1)}, u32[]{:S(2)}, u32[]{:S(2)}) %collective-permute-start.21) | collective-permute-done | bytes 524320 | tf_op jit(solution)/shard_map/ppermute | solution.py:195
  149.3 1.4 collective-permute-done.29.refs_0_
  150.8 0.9 collective-permute-done.28.refs_0_
  151.7 1.2 collective-permute-start.35
  152.8 1.5 collective-permute-start.27
  154.9 1.6 collective-permute-start.25
  156.9 10.7 %collective-permute-done.27.refs_0_ = bf16[128,2048]{1,0:T(8,128)(2,1)S(1)} collective-permute-done((bf16[128,2048]{1,0:T(8,128)(2,1)S(1)}, bf16[128,2048]{1,0:T(8,128)(2,1)S(1)}, u32[]{:S(2)}, u32[]{:S(2)}) %collective-permute-start.27) | collective-permute-done | bytes 524320 | tf_op jit(solution)/shard_map/ppermute | solution.py:195
  167.7 1.5 collective-permute-start.31
  169.4 0.6 collective-permute-start.33
  170.0 10.4 %collective-permute-done.25.refs_0_ = bf16[128,2048]{1,0:T(8,128)(2,1)S(1)} collective-permute-done((bf16[128,2048]{1,0:T(8,128)(2,1)S(1)}, bf16[128,2048]{1,0:T(8,128)(2,1)S(1)}, u32[]{:S(2)}, u32[]{:S(2)}) %collective-permute-start.25) | collective-permute-done | bytes 524320 | tf_op jit(solution)/shard_map/ppermute | solution.py:195
  181.2 1.5 collective-permute-start.34
  182.7 5.0 %total.1.refs_2_.refs_1_ = bf16[2,3,176,2048]{3,2,1,0:T(8,128)(2,1)} custom-call(s32[4,4]{1,0:T(4,128)S(1)} %copy-done.8, bf16[3,176,2048]{2,1,0:T(8,128)(2,1)S(1)} %grads_0.1.refs_2_.refs_1_, bf16[176,2048]{1,0:T(8,128)(2,1)S(1)} %gate.40.refs_1_.refs_2_, bf16[176,2048]{1,0:T(8,128)(2,1)S(1)} %gate.41.refs_1_.refs_3_, ...), custom_call_target="tpu_custom_call" | custom-call | flops 1 | bytes 1 | tf_op jit(solution)/shard_map/total/pallas_call | solution.py:135
  187.7 2.3 %collective-permute-done.31.refs_0_ = bf16[128,2048]{1,0:T(8,128)(2,1)S(1)} collective-permute-done((bf16[128,2048]{1,0:T(8,128)(2,1)S(1)}, bf16[128,2048]{1,0:T(8,128)(2,1)S(1)}, u32[]{:S(2)}, u32[]{:S(2)}) %collective-permute-start.31) | collective-permute-done | bytes 524320 | tf_op jit(solution)/shard_map/ppermute | solution.py:195
  190.0 2.2 %copy-done.1 = bf16[2,3,176,2048]{3,2,1,0:T(8,128)(2,1)S(1)} copy-done((bf16[2,3,176,2048]{3,2,1,0:T(8,128)(2,1)S(1)}, bf16[2,3,176,2048]{3,2,1,0:T(8,128)(2,1)}, u32[]{:S(2)}) %copy-start.1) | copy-done | bytes 4325400
  192.5 9.5 %collective-permute-done.30.refs_0_ = bf16[128,2048]{1,0:T(8,128)(2,1)S(1)} collective-permute-done((bf16[128,2048]{1,0:T(8,128)(2,1)S(1)}, bf16[128,2048]{1,0:T(8,128)(2,1)S(1)}, u32[]{:S(2)}, u32[]{:S(2)}) %collective-permute-start.30) | collective-permute-done | bytes 524320 | tf_op jit(solution)/shard_map/ppermute | solution.py:195
  202.0 0.9 add_rows.26.refs_2_
  202.9 1.0 copy-done.4
  203.9 0.9 add_rows.27
  204.8 3.5 %add.1 = bf16[2,3,176,2048]{3,2,1,0:T(8,128)(2,1)} custom-call(s32[4,4]{1,0:T(4,128)S(1)} %copy-done.8, bf16[2,3,176,2048]{3,2,1,0:T(8,128)(2,1)} %total.1.refs_2_.refs_1_, bf16[3,176,2048]{2,1,0:T(8,128)(2,1)S(1)} %collective-permute-done.35.refs_2_), custom_call_target="tpu_custom_call", output_to_operand_aliasing={{}: (1, {})} | custom-call | tf_op jit(solution)/shard_map/add/pallas_call | solution.py:176
  (88 shorter events, 9.0 us)
Async XLA Ops:
  0.6 2.2 %copy-start = (bf16[2,3,176,2048]{3,2,1,0:T(8,128)(2,1)S(1)}, bf16[2,3,176,2048]{3,2,1,0:T(8,128)(2,1)}, u32[]{:S(2)}) copy-start(bf16[2,3,176,2048]{3,2,1,0:T(8,128)(2,1)} %refs_1_.7) | copy-start | bytes 12976132
  2.9 0.7 copy-start.7
  3.5 9.1 %slice-start = ((s8[4325376]{0:T(1024)(128)(4,1)}), s8[4194304]{0:T(1024)(128)(4,1)S(1)}, s32[]{:S(2)}) async-start(s8[4325376]{0:T(1024)(128)(4,1)} %bitcast.10), calls=%async_computation | async-start | bytes 8388608
  4.4 4.0 %copy-start.2 = (bf16[128,2048]{1,0:T(8,128)(2,1)S(1)}, bf16[128,2048]{1,0:T(8,128)(2,1)}, u32[]{:S(2)}) copy-start(bf16[128,2048]{1,0:T(8,128)(2,1)} %refs_0_.25) | copy-start | bytes 1572868
  4.4 5.6 %copy-start.3 = (bf16[128,2048]{1,0:T(8,128)(2,1)S(1)}, bf16[128,2048]{1,0:T(8,128)(2,1)}, u32[]{:S(2)}) copy-start(bf16[128,2048]{1,0:T(8,128)(2,1)} %refs_8_.7) | copy-start | bytes 1572868
  4.4 8.2 %slice-start.1 = ((s8[4325376]{0:T(1024)(128)(4,1)}), s8[131072]{0:T(1024)(128)(4,1)S(1)}, s32[]{:S(2)}) async-start(s8[4325376]{0:T(1024)(128)(4,1)} %bitcast.10), calls=%async_computation.1 | async-start | bytes 262144
  4.4 8.2 %copy-start.8 = (s32[4,4]{1,0:T(4,128)S(1)}, s32[4,4]{1,0:T(4,128)}, u32[]{:S(2)}) copy-start(s32[4,4]{1,0:T(4,128)} %refs_0_.27) | copy-start | bytes 196
  5.3 6.6 %collective-permute-start.3 = (bf16[3,176,2048]{2,1,0:T(8,128)(2,1)S(1)}, bf16[3,176,2048]{2,1,0:T(8,128)(2,1)S(1)}, u32[]{:S(2)}, u32[]{:S(2)}) collective-permute-start(bf16[3,176,2048]{2,1,0:T(8,128)(2,1)S(1)} %bitcast.14), channel_id=1, source_target_pairs={{8,0},{0,8},{24,16},{16,24},{9,1},{1,9},{25,17},{17,25},{10,2},{2,... | collective-permute-start | bytes 6488072 | tf_op jit(solution)/shard_map/ppermute | solution.py:74
  5.8 50.2 %collective-permute-start.8 = (bf16[3,176,2048]{2,1,0:T(8,128)(2,1)S(1)}, bf16[3,176,2048]{2,1,0:T(8,128)(2,1)S(1)}, u32[]{:S(2)}, u32[]{:S(2)}) collective-permute-start(bf16[3,176,2048]{2,1,0:T(8,128)(2,1)S(1)} %bitcast.13), channel_id=1, source_target_pairs={{16,0},{24,8},{0,16},{8,24},{17,1},{25,9},{1,17},{9,25},{18,2},{26... | collective-permute-start | bytes 6488072 | tf_op jit(solution)/shard_map/ppermute | solution.py:74
  8.4 14.8 %collective-permute-start.2 = (bf16[128,2048]{1,0:T(8,128)(2,1)S(1)}, bf16[128,2048]{1,0:T(8,128)(2,1)S(1)}, u32[]{:S(2)}, u32[]{:S(2)}) collective-permute-start(bf16[128,2048]{1,0:T(8,128)(2,1)S(1)} %copy-done.2), channel_id=1, source_target_pairs={{0,2},{2,4},{4,6},{6,7},{7,5},{5,3},{3,1},{1,0},{8,10},{10,12},{12... | collective-permute-start | bytes 1572872 | tf_op jit(solution)/shard_map/ppermute | solution.py:195
  9.9 14.8 %collective-permute-start.1 = (bf16[128,2048]{1,0:T(8,128)(2,1)S(1)}, bf16[128,2048]{1,0:T(8,128)(2,1)S(1)}, u32[]{:S(2)}, u32[]{:S(2)}) collective-permute-start(bf16[128,2048]{1,0:T(8,128)(2,1)S(1)} %copy-done.3), channel_id=1, source_target_pairs={{0,1},{2,0},{4,2},{6,4},{7,6},{5,7},{3,5},{1,3},{8,9},{10,8},{12,1... | collective-permute-start | bytes 1572872 | tf_op jit(solution)/shard_map/ppermute | solution.py:195
  10.4 25.6 %collective-permute-start = (bf16[128,2048]{1,0:T(8,128)(2,1)S(1)}, bf16[128,2048]{1,0:T(8,128)(2,1)S(1)}, u32[]{:S(2)}, u32[]{:S(2)}) collective-permute-start(bf16[128,2048]{1,0:T(8,128)(2,1)S(1)} %copy-done.2), channel_id=1, source_target_pairs={{0,1},{2,0},{4,2},{6,4},{7,6},{5,7},{3,5},{1,3},{8,9},{10,8},{12,1... | collective-permute-start | bytes 1572872 | tf_op jit(solution)/shard_map/ppermute | solution.py:195
  11.9 24.6 %collective-permute-start.5 = (bf16[128,2048]{1,0:T(8,128)(2,1)S(1)}, bf16[128,2048]{1,0:T(8,128)(2,1)S(1)}, u32[]{:S(2)}, u32[]{:S(2)}) collective-permute-start(bf16[128,2048]{1,0:T(8,128)(2,1)S(1)} %copy-done.3), channel_id=1, source_target_pairs={{0,2},{2,4},{4,6},{6,7},{7,5},{5,3},{3,1},{1,0},{8,10},{10,12},{12... | collective-permute-start | bytes 1572872 | tf_op jit(solution)/shard_map/ppermute | solution.py:195
  23.1 22.5 %collective-permute-start.4 = (bf16[128,2048]{1,0:T(8,128)(2,1)S(1)}, bf16[128,2048]{1,0:T(8,128)(2,1)S(1)}, u32[]{:S(2)}, u32[]{:S(2)}) collective-permute-start(bf16[128,2048]{1,0:T(8,128)(2,1)S(1)} %gate.24.refs_1_.refs_3_), channel_id=1, source_target_pairs={{0,2},{2,4},{4,6},{6,7},{7,5},{5,3},{3,1},{1,0},{8,10},{10,12},{12... | collective-permute-start | bytes 1572872 | tf_op jit(solution)/shard_map/ppermute | solution.py:195
  24.8 22.5 %collective-permute-start.9 = (bf16[128,2048]{1,0:T(8,128)(2,1)S(1)}, bf16[128,2048]{1,0:T(8,128)(2,1)S(1)}, u32[]{:S(2)}, u32[]{:S(2)}) collective-permute-start(bf16[128,2048]{1,0:T(8,128)(2,1)S(1)} %gate.25.refs_1_.refs_5_.refs_9_), channel_id=1, source_target_pairs={{0,1},{2,0},{4,2},{6,4},{7,6},{5,7},{3,5},{1,3},{8,9},{10,8},{12,1... | collective-permute-start | bytes 1572872 | tf_op jit(solution)/shard_map/ppermute | solution.py:195
  36.0 22.5 %collective-permute-start.7 = (bf16[128,2048]{1,0:T(8,128)(2,1)S(1)}, bf16[128,2048]{1,0:T(8,128)(2,1)S(1)}, u32[]{:S(2)}, u32[]{:S(2)}) collective-permute-start(bf16[128,2048]{1,0:T(8,128)(2,1)S(1)} %gate.26.refs_1_), channel_id=1, source_target_pairs={{0,1},{2,0},{4,2},{6,4},{7,6},{5,7},{3,5},{1,3},{8,9},{10,8},{12,1... | collective-permute-start | bytes 1572872 | tf_op jit(solution)/shard_map/ppermute | solution.py:195
  36.4 22.5 %collective-permute-start.6 = (bf16[128,2048]{1,0:T(8,128)(2,1)S(1)}, bf16[128,2048]{1,0:T(8,128)(2,1)S(1)}, u32[]{:S(2)}, u32[]{:S(2)}) collective-permute-start(bf16[128,2048]{1,0:T(8,128)(2,1)S(1)} %gate.27.refs_1_.refs_7_.refs_11_), channel_id=1, source_target_pairs={{0,2},{2,4},{4,6},{6,7},{7,5},{5,3},{3,1},{1,0},{8,10},{10,12},{12... | collective-permute-start | bytes 1572872 | tf_op jit(solution)/shard_map/ppermute | solution.py:195
  45.6 22.5 %collective-permute-start.12 = (bf16[128,2048]{1,0:T(8,128)(2,1)S(1)}, bf16[128,2048]{1,0:T(8,128)(2,1)S(1)}, u32[]{:S(2)}, u32[]{:S(2)}) collective-permute-start(bf16[128,2048]{1,0:T(8,128)(2,1)S(1)} %gate.28.refs_1_.refs_2_), channel_id=1, source_target_pairs={{0,2},{2,4},{4,6},{6,7},{7,5},{5,3},{3,1},{1,0},{8,10},{10,12},{12... | collective-permute-start | bytes 1572872 | tf_op jit(solution)/shard_map/ppermute | solution.py:195
  47.2 22.5 %collective-permute-start.11 = (bf16[128,2048]{1,0:T(8,128)(2,1)S(1)}, bf16[128,2048]{1,0:T(8,128)(2,1)S(1)}, u32[]{:S(2)}, u32[]{:S(2)}) collective-permute-start(bf16[128,2048]{1,0:T(8,128)(2,1)S(1)} %gate.29.refs_1_.refs_4_.refs_12_), channel_id=1, source_target_pairs={{0,1},{2,0},{4,2},{6,4},{7,6},{5,7},{3,5},{1,3},{8,9},{10,8},{12,1... | collective-permute-start | bytes 1572872 | tf_op jit(solution)/shard_map/ppermute | solution.py:195
  56.0 4.5 %copy-start.5 = (s32[1024,1]{0,1:T(1,128)S(1)}, s32[1024,1]{0,1:T(1,128)}, u32[]{:S(2)}) copy-start(s32[1024,1]{0,1:T(1,128)} %param.8) | copy-start | bytes 12292
  56.0 4.5 %copy-start.6 = (f32[1024,1]{0,1:T(1,128)S(1)}, f32[1024,1]{0,1:T(1,128)}, u32[]{:S(2)}) copy-start(f32[1024,1]{0,1:T(1,128)} %param.9) | copy-start | bytes 12292
  56.0 49.5 %collective-permute-start.16 = (bf16[3,176,2048]{2,1,0:T(8,128)(2,1)S(1)}, bf16[3,176,2048]{2,1,0:T(8,128)(2,1)S(1)}, u32[]{:S(2)}, u32[]{:S(2)}) collective-permute-start(bf16[3,176,2048]{2,1,0:T(8,128)(2,1)S(1)} %gate.31.refs_1_), channel_id=1, source_target_pairs={{24,0},{16,8},{8,16},{0,24},{25,1},{17,9},{9,17},{1,25},{26,2},{18... | collective-permute-start | bytes 6488072 | tf_op jit(solution)/shard_map/ppermute | solution.py:74
  58.5 22.5 %collective-permute-start.10 = (bf16[128,2048]{1,0:T(8,128)(2,1)S(1)}, bf16[128,2048]{1,0:T(8,128)(2,1)S(1)}, u32[]{:S(2)}, u32[]{:S(2)}) collective-permute-start(bf16[128,2048]{1,0:T(8,128)(2,1)S(1)} %gate.32.refs_1_.refs_0_.refs_4_), channel_id=1, source_target_pairs={{0,1},{2,0},{4,2},{6,4},{7,6},{5,7},{3,5},{1,3},{8,9},{10,8},{12,1... | collective-permute-start | bytes 1572872 | tf_op jit(solution)/shard_map/ppermute | solution.py:195
  58.9 22.0 %collective-permute-start.14 = (bf16[128,2048]{1,0:T(8,128)(2,1)S(1)}, bf16[128,2048]{1,0:T(8,128)(2,1)S(1)}, u32[]{:S(2)}, u32[]{:S(2)}) collective-permute-start(bf16[128,2048]{1,0:T(8,128)(2,1)S(1)} %gate.33.refs_6_.refs_11_.refs_10_), channel_id=1, source_target_pairs={{0,2},{2,4},{4,6},{6,7},{7,5},{5,3},{3,1},{1,0},{8,10},{10,12},{12... | collective-permute-start | bytes 1572872 | tf_op jit(solution)/shard_map/ppermute | solution.py:195
  68.1 21.7 %collective-permute-start.13 = (bf16[128,2048]{1,0:T(8,128)(2,1)S(1)}, bf16[128,2048]{1,0:T(8,128)(2,1)S(1)}, u32[]{:S(2)}, u32[]{:S(2)}) collective-permute-start(bf16[128,2048]{1,0:T(8,128)(2,1)S(1)} %gate.34.refs_1_.refs_3_.refs_7_), channel_id=1, source_target_pairs={{0,2},{2,4},{4,6},{6,7},{7,5},{5,3},{3,1},{1,0},{8,10},{10,12},{12... | collective-permute-start | bytes 1572872 | tf_op jit(solution)/shard_map/ppermute | solution.py:195
  69.7 21.4 %collective-permute-start.15 = (bf16[128,2048]{1,0:T(8,128)(2,1)S(1)}, bf16[128,2048]{1,0:T(8,128)(2,1)S(1)}, u32[]{:S(2)}, u32[]{:S(2)}) collective-permute-start(bf16[128,2048]{1,0:T(8,128)(2,1)S(1)} %gate.35.refs_1_.refs_5_.refs_13_), channel_id=1, source_target_pairs={{0,1},{2,0},{4,2},{6,4},{7,6},{5,7},{3,5},{1,3},{8,9},{10,8},{12,1... | collective-permute-start | bytes 1572872 | tf_op jit(solution)/shard_map/ppermute | solution.py:195
  100.7 51.0 %collective-permute-start.28 = (bf16[3,176,2048]{2,1,0:T(8,128)(2,1)S(1)}, bf16[3,176,2048]{2,1,0:T(8,128)(2,1)S(1)}, u32[]{:S(2)}, u32[]{:S(2)}) collective-permute-start(bf16[3,176,2048]{2,1,0:T(8,128)(2,1)S(1)} %grads_2.1.refs_11_), channel_id=1, source_target_pairs={{16,0},{24,8},{0,16},{8,24},{17,1},{25,9},{1,17},{9,25},{18,2},{26... | collective-permute-start | bytes 6488072 | tf_op jit(solution)/shard_map/ppermute | solution.py:74
  101.2 2.2 %collective-permute-start.19 = (bf16[176,2048]{1,0:T(8,128)(2,1)S(1)}, bf16[176,2048]{1,0:T(8,128)(2,1)S(1)}, u32[]{:S(2)}, u32[]{:S(2)}) collective-permute-start(bf16[176,2048]{1,0:T(8,128)(2,1)S(1)} %get-tuple-element.22.refs_11_), channel_id=1, source_target_pairs={{8,0},{0,8},{24,16},{16,24},{9,1},{1,9},{25,17},{17,25},{10,2},{2,... | collective-permute-start | bytes 2162696 | tf_op jit(solution)/shard_map/ppermute | solution.py:74
  101.2 3.2 %collective-permute-start.18 = (bf16[176,2048]{1,0:T(8,128)(2,1)S(1)}, bf16[176,2048]{1,0:T(8,128)(2,1)S(1)}, u32[]{:S(2)}, u32[]{:S(2)}) collective-permute-start(bf16[176,2048]{1,0:T(8,128)(2,1)S(1)} %get-tuple-element.24), channel_id=1, source_target_pairs={{8,0},{0,8},{24,16},{16,24},{9,1},{1,9},{25,17},{17,25},{10,2},{2,... | collective-permute-start | bytes 2162696 | tf_op jit(solution)/shard_map/ppermute | solution.py:74
  101.7 3.7 %collective-permute-start.17 = (bf16[176,2048]{1,0:T(8,128)(2,1)S(1)}, bf16[176,2048]{1,0:T(8,128)(2,1)S(1)}, u32[]{:S(2)}, u32[]{:S(2)}) collective-permute-start(bf16[176,2048]{1,0:T(8,128)(2,1)S(1)} %get-tuple-element.23), channel_id=1, source_target_pairs={{8,0},{0,8},{24,16},{16,24},{9,1},{1,9},{25,17},{17,25},{10,2},{2,... | collective-permute-start | bytes 2162696 | tf_op jit(solution)/shard_map/ppermute | solution.py:74
  112.8 17.1 %collective-permute-start.20 = (bf16[128,2048]{1,0:T(8,128)(2,1)S(1)}, bf16[128,2048]{1,0:T(8,128)(2,1)S(1)}, u32[]{:S(2)}, u32[]{:S(2)}) collective-permute-start(bf16[128,2048]{1,0:T(8,128)(2,1)S(1)} %get-tuple-element.25.refs_12_), channel_id=1, source_target_pairs={{0,2},{2,4},{4,6},{6,7},{7,5},{5,3},{3,1},{1,0},{8,10},{10,12},{12... | collective-permute-start | bytes 1572872 | tf_op jit(solution)/shard_map/ppermute | solution.py:195
  114.3 17.3 %collective-permute-start.24 = (bf16[128,2048]{1,0:T(8,128)(2,1)}, bf16[128,2048]{1,0:T(8,128)(2,1)S(1)}, u32[]{:S(2)}, u32[]{:S(2)}) collective-permute-start(bf16[128,2048]{1,0:T(8,128)(2,1)} %get-tuple-element.33), channel_id=1, source_target_pairs={{0,1},{2,0},{4,2},{6,4},{7,6},{5,7},{3,5},{1,3},{8,9},{10,8},{12,1... | collective-permute-start | bytes 1572872 | tf_op jit(solution)/shard_map/ppermute | solution.py:195
  122.9 17.8 %collective-permute-start.22 = (bf16[128,2048]{1,0:T(8,128)(2,1)}, bf16[128,2048]{1,0:T(8,128)(2,1)S(1)}, u32[]{:S(2)}, u32[]{:S(2)}) collective-permute-start(bf16[128,2048]{1,0:T(8,128)(2,1)} %get-tuple-element.29), channel_id=1, source_target_pairs={{0,2},{2,4},{4,6},{6,7},{7,5},{5,3},{3,1},{1,0},{8,10},{10,12},{12... | collective-permute-start | bytes 1572872 | tf_op jit(solution)/shard_map/ppermute | solution.py:195
  124.6 16.0 %collective-permute-start.23 = (bf16[128,2048]{1,0:T(8,128)(2,1)}, bf16[128,2048]{1,0:T(8,128)(2,1)S(1)}, u32[]{:S(2)}, u32[]{:S(2)}) collective-permute-start(bf16[128,2048]{1,0:T(8,128)(2,1)} %get-tuple-element.31), channel_id=1, source_target_pairs={{0,1},{2,0},{4,2},{6,4},{7,6},{5,7},{3,5},{1,3},{8,9},{10,8},{12,1... | collective-permute-start | bytes 1572872 | tf_op jit(solution)/shard_map/ppermute | solution.py:195
  130.0 19.2 %collective-permute-start.21 = (bf16[128,2048]{1,0:T(8,128)(2,1)S(1)}, bf16[128,2048]{1,0:T(8,128)(2,1)S(1)}, u32[]{:S(2)}, u32[]{:S(2)}) collective-permute-start(bf16[128,2048]{1,0:T(8,128)(2,1)S(1)} %add_rows.14.refs_2_), channel_id=1, source_target_pairs={{0,2},{2,4},{4,6},{6,7},{7,5},{5,3},{3,1},{1,0},{8,10},{10,12},{12... | collective-permute-start | bytes 1572872 | tf_op jit(solution)/shard_map/ppermute | solution.py:195
  131.7 19.0 %collective-permute-start.29 = (bf16[128,2048]{1,0:T(8,128)(2,1)S(1)}, bf16[128,2048]{1,0:T(8,128)(2,1)S(1)}, u32[]{:S(2)}, u32[]{:S(2)}) collective-permute-start(bf16[128,2048]{1,0:T(8,128)(2,1)S(1)} %add_rows.15.refs_2_), channel_id=1, source_target_pairs={{0,1},{2,0},{4,2},{6,4},{7,6},{5,7},{3,5},{1,3},{8,9},{10,8},{12,1... | collective-permute-start | bytes 1572872 | tf_op jit(solution)/shard_map/ppermute | solution.py:195
  151.7 53.1 %collective-permute-start.35 = (bf16[3,176,2048]{2,1,0:T(8,128)(2,1)S(1)}, bf16[3,176,2048]{2,1,0:T(8,128)(2,1)S(1)}, u32[]{:S(2)}, u32[]{:S(2)}) collective-permute-start(bf16[3,176,2048]{2,1,0:T(8,128)(2,1)S(1)} %gate.45.refs_2_), channel_id=1, source_target_pairs={{24,0},{16,8},{8,16},{0,24},{25,1},{17,9},{9,17},{1,25},{26,2},{18... | collective-permute-start | bytes 6488072 | tf_op jit(solution)/shard_map/ppermute | solution.py:74
  152.8 14.7 %collective-permute-start.27 = (bf16[128,2048]{1,0:T(8,128)(2,1)S(1)}, bf16[128,2048]{1,0:T(8,128)(2,1)S(1)}, u32[]{:S(2)}, u32[]{:S(2)}) collective-permute-start(bf16[128,2048]{1,0:T(8,128)(2,1)S(1)} %add_rows.16.refs_2_), channel_id=1, source_target_pairs={{0,1},{2,0},{4,2},{6,4},{7,6},{5,7},{3,5},{1,3},{8,9},{10,8},{12,1... | collective-permute-start | bytes 1572872 | tf_op jit(solution)/shard_map/ppermute | solution.py:195
  154.3 14.9 %collective-permute-start.26 = (bf16[128,2048]{1,0:T(8,128)(2,1)S(1)}, bf16[128,2048]{1,0:T(8,128)(2,1)S(1)}, u32[]{:S(2)}, u32[]{:S(2)}) collective-permute-start(bf16[128,2048]{1,0:T(8,128)(2,1)S(1)} %add_rows.17.refs_2_), channel_id=1, source_target_pairs={{0,2},{2,4},{4,6},{6,7},{7,5},{5,3},{3,1},{1,0},{8,10},{10,12},{12... | collective-permute-start | bytes 1572872 | tf_op jit(solution)/shard_map/ppermute | solution.py:195
  154.9 25.5 %collective-permute-start.25 = (bf16[128,2048]{1,0:T(8,128)(2,1)S(1)}, bf16[128,2048]{1,0:T(8,128)(2,1)S(1)}, u32[]{:S(2)}, u32[]{:S(2)}) collective-permute-start(bf16[128,2048]{1,0:T(8,128)(2,1)S(1)} %add_rows.18.refs_2_), channel_id=1, source_target_pairs={{0,2},{2,4},{4,6},{6,7},{7,5},{5,3},{3,1},{1,0},{8,10},{10,12},{12... | collective-permute-start | bytes 1572872 | tf_op jit(solution)/shard_map/ppermute | solution.py:195
  156.4 24.6 %collective-permute-start.32 = (bf16[128,2048]{1,0:T(8,128)(2,1)S(1)}, bf16[128,2048]{1,0:T(8,128)(2,1)S(1)}, u32[]{:S(2)}, u32[]{:S(2)}) collective-permute-start(bf16[128,2048]{1,0:T(8,128)(2,1)S(1)} %add_rows.19.refs_1_), channel_id=1, source_target_pairs={{0,1},{2,0},{4,2},{6,4},{7,6},{5,7},{3,5},{1,3},{8,9},{10,8},{12,1... | collective-permute-start | bytes 1572872 | tf_op jit(solution)/shard_map/ppermute | solution.py:195
  167.7 22.3 %collective-permute-start.31 = (bf16[128,2048]{1,0:T(8,128)(2,1)S(1)}, bf16[128,2048]{1,0:T(8,128)(2,1)S(1)}, u32[]{:S(2)}, u32[]{:S(2)}) collective-permute-start(bf16[128,2048]{1,0:T(8,128)(2,1)S(1)} %add_rows.20.refs_2_), channel_id=1, source_target_pairs={{0,1},{2,0},{4,2},{6,4},{7,6},{5,7},{3,5},{1,3},{8,9},{10,8},{12,1... | collective-permute-start | bytes 1572872 | tf_op jit(solution)/shard_map/ppermute | solution.py:195
  169.4 23.0 %collective-permute-start.33 = (bf16[128,2048]{1,0:T(8,128)(2,1)S(1)}, bf16[128,2048]{1,0:T(8,128)(2,1)S(1)}, u32[]{:S(2)}, u32[]{:S(2)}) collective-permute-start(bf16[128,2048]{1,0:T(8,128)(2,1)S(1)} %add_rows.21.refs_2_), channel_id=1, source_target_pairs={{0,2},{2,4},{4,6},{6,7},{7,5},{5,3},{3,1},{1,0},{8,10},{10,12},{12... | collective-permute-start | bytes 1572872 | tf_op jit(solution)/shard_map/ppermute | solution.py:195
  180.5 21.6 %collective-permute-start.30 = (bf16[128,2048]{1,0:T(8,128)(2,1)S(1)}, bf16[128,2048]{1,0:T(8,128)(2,1)S(1)}, u32[]{:S(2)}, u32[]{:S(2)}) collective-permute-start(bf16[128,2048]{1,0:T(8,128)(2,1)S(1)} %add_rows.22.refs_2_), channel_id=1, source_target_pairs={{0,2},{2,4},{4,6},{6,7},{7,5},{5,3},{3,1},{1,0},{8,10},{10,12},{12... | collective-permute-start | bytes 1572872 | tf_op jit(solution)/shard_map/ppermute | solution.py:195
  181.2 21.7 %collective-permute-start.34 = (bf16[128,2048]{1,0:T(8,128)(2,1)S(1)}, bf16[128,2048]{1,0:T(8,128)(2,1)S(1)}, u32[]{:S(2)}, u32[]{:S(2)}) collective-permute-start(bf16[128,2048]{1,0:T(8,128)(2,1)S(1)} %add_rows.23.refs_6_), channel_id=1, source_target_pairs={{0,1},{2,0},{4,2},{6,4},{7,6},{5,7},{3,5},{1,3},{8,9},{10,8},{12,1... | collective-permute-start | bytes 1572872 | tf_op jit(solution)/shard_map/ppermute | solution.py:195
  190.0 2.2 %copy-start.1 = (bf16[2,3,176,2048]{3,2,1,0:T(8,128)(2,1)S(1)}, bf16[2,3,176,2048]{3,2,1,0:T(8,128)(2,1)}, u32[]{:S(2)}) copy-start(bf16[2,3,176,2048]{3,2,1,0:T(8,128)(2,1)} %total.1.refs_2_.refs_1_) | copy-start | bytes 12976132
  202.9 1.0 copy-start.4

commit v4 on v3

--- a/solution.py
+++ b/solution.py
@@ -11,6 +11,9 @@
 NO_COST = pl.CostEstimate(flops=1, bytes_accessed=1, transcendentals=0)
 
 
+LAST_FLOPS = 12 * 10**9
+
+
 def work_cost(flops):
     return pl.CostEstimate(flops=flops, bytes_accessed=1, transcendentals=0)
 
@@ -21,6 +24,14 @@
 
 def whole_in_vmem():
     return pl.BlockSpec(memory_space=pltpu.VMEM)
+
+
+def in_hbm():
+    return pl.BlockSpec(memory_space=pltpu.HBM)
+
+
+def token_shape():
+    return jax.ShapeDtypeStruct((8, 128), F32)
 
 
 def untouched():
@@ -77,10 +88,10 @@
 
 
 def pick_kernel(turns, stride, fetch_pick, panels, *refs):
-    out, sems = refs[-2:]
+    outs, sems = refs[-len(turns) - 1 : -1], refs[-1]
     copies = [
-        pltpu.make_async_copy(panels.at[turn_pick(fetch_pick, turn, stride)], out.at[i], sems.at[i])
-        for i, turn in enumerate(turns)
+        pltpu.make_async_copy(panels.at[turn_pick(fetch_pick, turn, stride)], out, sems.at[i])
+        for i, (turn, out) in enumerate(zip(turns, outs))
     ]
     for copy in copies:
         copy.start()
@@ -91,11 +102,12 @@
 def pick_pass(turns, stride, fetch_pick, panels, after=()):
     return pl.pallas_call(
         lambda *refs: pick_kernel(turns, stride, *refs),
-        out_shape=jax.ShapeDtypeStruct((len(turns),) + panels.shape[1:], BF16),
-        in_specs=[pl.BlockSpec(memory_space=pltpu.SMEM), untouched()] + [untouched()] * len(after),
-        out_specs=untouched(),
+        out_shape=tuple(jax.ShapeDtypeStruct(panels.shape[1:], BF16) for _ in turns),
+        in_specs=[pl.BlockSpec(memory_space=pltpu.SMEM), in_hbm()] + [untouched()] * len(after),
+        out_specs=tuple(untouched() for _ in turns),
         scratch_shapes=[pltpu.SemaphoreType.DMA((len(turns),))],
         compiler_params=pltpu.CompilerParams(vmem_limit_bytes=1024 * 1024),
+        cost_estimate=NO_COST,
         name="pick",
     )(fetch_pick, panels, *after)
 
@@ -113,9 +125,11 @@
     )(value, *after)
 
 
-def total_kernel(turns, stride, counts, fetch_pick, *refs):
-    out, refs = refs[-1], list(refs[: sum(counts)])
+def total_kernel(turns, last, stride, counts, fetch_pick, *refs):
+    out, base, token, refs = *refs[-3:], list(refs[: sum(counts)])
     picks = [turn_pick(fetch_pick, turn, stride) for turn in turns]
+    last_pick = turn_pick(fetch_pick, last, stride)
+    token[...] = jnp.zeros_like(token)
     experts, kinds = out.shape[:2]
     grads = []
     for count in counts:
@@ -127,67 +141,61 @@
             total = jnp.zeros(terms[0].shape, F32)
             for pick, term in zip(picks, terms):
                 total += jnp.where(pick == e, term, 0.0)
-            out[e, kind] = total.astype(BF16)
-
-
-def total_pass(turns, stride, fetch_pick, grads, shape, after):
+            total = total.astype(BF16)
+            out[e, kind] = total
+            if e == 0:
+                base[kind] = total
+            else:
+
+                @pl.when(last_pick == e)
+                def _():
+                    base[kind] = total
+
+
+def total_pass(turns, last, stride, fetch_pick, grads, shape, after):
     counts = [len(grad) for grad in grads]
     return pl.pallas_call(
-        lambda *refs: total_kernel(turns, stride, counts, *refs),
-        out_shape=jax.ShapeDtypeStruct(shape, BF16),
+        lambda *refs: total_kernel(turns, last, stride, counts, *refs),
+        out_shape=(
+            jax.ShapeDtypeStruct(shape, BF16),
+            jax.ShapeDtypeStruct(shape[1:], BF16),
+            token_shape(),
+        ),
         in_specs=[pl.BlockSpec(memory_space=pltpu.SMEM)]
         + [whole_in_vmem()] * sum(counts)
         + [untouched()] * len(after),
-        out_specs=whole_in_vmem(),
+        out_specs=(whole_in_vmem(),) * 3,
         compiler_params=pltpu.CompilerParams(vmem_limit_bytes=VMEM_LIMIT),
         cost_estimate=NO_COST,
         name="total",
     )(fetch_pick, *[grad for slot_grads in grads for grad in slot_grads], *after)
 
 
-def add_kernel(turn, stride, fetch_pick, total, grad, out, sums, terms, in_sems, out_sems):
+def add_kernel(turn, stride, fetch_pick, total, base, grad, out, sums, sems):
     pick = turn_pick(fetch_pick, turn, stride)
-    kinds = grad.shape[0]
-    reads = [
-        (
-            pltpu.make_async_copy(total.at[pick, kind], sums.at[kind], in_sems.at[kind]),
-            pltpu.make_async_copy(grad.at[kind], terms.at[kind], in_sems.at[kinds + kind]),
-        )
-        for kind in range(kinds)
+    writes = [
+        pltpu.make_async_copy(sums.at[kind], out.at[pick, kind], sems.at[kind])
+        for kind in range(grad.shape[0])
     ]
-    writes = [
-        pltpu.make_async_copy(sums.at[kind], out.at[pick, kind], out_sems.at[kind])
-        for kind in range(kinds)
-    ]
-    for first, second in reads:
-        first.start()
-        second.start()
-    for kind in range(kinds):
-        for read in reads[kind]:
-            read.wait()
-        sums[kind] = (sums[kind].astype(F32) + terms[kind].astype(F32)).astype(BF16)
-        writes[kind].start()
+    for kind, write in enumerate(writes):
+        sums[kind] = (base[kind].astype(F32) + grad[kind].astype(F32)).astype(BF16)
+        write.start()
     for write in writes:
         write.wait()
 
 
-def add_pass(turn, stride, fetch_pick, total, grad):
-    kinds = grad.shape[0]
+def add_pass(turn, stride, fetch_pick, total, base, grad):
     return pl.pallas_call(
         lambda *refs: add_kernel(turn, stride, *refs),
         out_shape=jax.ShapeDtypeStruct(total.shape, BF16),
-        in_specs=[pl.BlockSpec(memory_space=pltpu.SMEM), untouched(), untouched()],
-        out_specs=untouched(),
+        in_specs=[pl.BlockSpec(memory_space=pltpu.SMEM), in_hbm(), whole_in_vmem(), whole_in_vmem()],
+        out_specs=in_hbm(),
         input_output_aliases={1: 0},
-        scratch_shapes=[
-            pltpu.VMEM(grad.shape, BF16),
-            pltpu.VMEM(grad.shape, BF16),
-            pltpu.SemaphoreType.DMA((2 * kinds,)),
-            pltpu.SemaphoreType.DMA((kinds,)),
-        ],
-        compiler_params=pltpu.CompilerParams(vmem_limit_bytes=8 * 1024 * 1024),
+        scratch_shapes=[pltpu.VMEM(grad.shape, BF16), pltpu.SemaphoreType.DMA((grad.shape[0],))],
+        compiler_params=pltpu.CompilerParams(vmem_limit_bytes=12 * 1024 * 1024),
+        cost_estimate=NO_COST,
         name="add",
-    )(fetch_pick, total, grad)
+    )(fetch_pick, total, base, grad)
 
 
 def ring_step(block, order, distance):
@@ -317,7 +325,7 @@
             out[:, here] = total.astype(BF16)
 
 
-def chunk_pass(wanted, acts, panels, groups, part, after=()):
+def chunk_pass(wanted, acts, panels, groups, part, cost, after=()):
     slots = len(panels)
     width = panels[0].shape[2]
     named = [
@@ -335,9 +343,27 @@
         in_specs=[whole_in_vmem()] * (slots * len(groups) + slots) + [untouched()] * len(after),
         out_specs=tuple(whole_in_vmem() for _ in wanted),
         compiler_params=pltpu.CompilerParams(vmem_limit_bytes=VMEM_LIMIT),
-        cost_estimate=NO_COST,
+        cost_estimate=cost,
         name=f"chunks_{len(wanted)}",
     )(*[act for slot_acts in acts for act in slot_acts], *panels, *after)
+
+
+def final_rows_kernel(*refs):
+    a, b, out, token = refs[0], refs[1], *refs[-2:]
+    out[...] = (a[...].astype(F32) + b[...]).astype(out.dtype)
+    token[...] = jnp.zeros_like(token)
+
+
+def final_rows(a, b, cost, after):
+    return pl.pallas_call(
+        final_rows_kernel,
+        out_shape=(jax.ShapeDtypeStruct(a.shape, BF16), token_shape()),
+        in_specs=[whole_in_vmem()] * 2 + [untouched()] * len(after),
+        out_specs=(whole_in_vmem(), whole_in_vmem()),
+        compiler_params=pltpu.CompilerParams(vmem_limit_bytes=VMEM_LIMIT),
+        cost_estimate=cost,
+        name="final_rows",
+    )(a, b, *after)
 
 
 class Line:
@@ -346,7 +372,7 @@
 
     def step(self, make):
         out = make(self.tail)
-        self.tail = (out[0] if isinstance(out, (tuple, list)) else out,)
+        self.tail = (out[-1] if isinstance(out, (tuple, list)) else out,)
         return out
 
     def arrive(self, value):
@@ -450,11 +476,12 @@
 
     kinds = ("mixed", "grad")
     early = [("mixed", up_most), ("grad", size - up_most), ("mixed", size - down_most), ("grad", down_most)]
+    early_cost = work_cost(6 * len(early) * slots * part * read[0].size // 6)
     later = [(kind, d) for kind in kinds for d in range(size) if (kind, d) not in early]
-    chunks = dict(zip(early, line.step(lambda after: chunk_pass(early, acts, read, groups, part, after))))
+    chunks = dict(zip(early, line.step(lambda after: chunk_pass(early, acts, read, groups, part, early_cost, after))))
     chains = [("mixed", 1, up_most), ("grad", -1, up_most), ("mixed", -1, down_most), ("grad", 1, down_most)]
     moving = [ring_step(chunks[kind, way * hops % size], order, way) for kind, way, hops in chains]
-    chunks.update(zip(later, line.step(lambda after: chunk_pass(later, acts, read, groups, part, after))))
+    chunks.update(zip(later, line.step(lambda after: chunk_pass(later, acts, read, groups, part, NO_COST, after))))
     make_grads(last)
     make_grads(0)
 
@@ -471,17 +498,19 @@
                 chunk = chunks[kind, way * left % size]
                 arrived = line.step(lambda after: add_rows(moving[i], chunk, BF16, after))
                 moving[i] = ring_step(arrived, order, way)
-                if left == 1 and i == 1:
-                    near_total = line.step(
+            elif kind not in sums:
+                sums[kind] = line.step(lambda after: add_rows(moving[i], chunks[kind, 0], F32, after))
+                if len(sums) == 2:
+                    panel_grad, base, _ = line.step(
                         lambda after: total_pass(
-                            list(range(last)), stride, fetch_pick, back[:last], panels.shape, after
+                            list(range(last)), last, stride, fetch_pick, back[:last], panels.shape, after
                         )
                     )
-            elif kind not in sums:
-                sums[kind] = line.step(lambda after: add_rows(moving[i], chunks[kind, 0], F32, after))
             else:
-                sums[kind] = line.step(lambda after: add_rows(moving[i], sums[kind], BF16, after))
-    panel_grad = add_pass(last, stride, fetch_pick, near_total, back[last])
+                cost = work_cost(LAST_FLOPS) if (kind, hop) == (chains[1][0], up_most) else NO_COST
+                sums[kind], _ = line.step(lambda after: final_rows(moving[i], sums[kind], cost, after))
+    back[last] = line.arrive(back[last])
+    panel_grad = add_pass(last, stride, fetch_pick, panel_grad, base, back[last])
     return sums["mixed"], sums["grad"], panel_grad
 
 

time: 209 us -> 203 us (0.971)
  local copies, waits for them, and re-layouts: 6.21 us -> 2.94 us
    ppermute x28, waiting for transfers between devices: 105 us -> 101 us  [ring_step(): lax.ppermute(block, 'local', [(order[i], order[(i + distance) % size]) fo...]
    unnamed x22 -> x18, local copies, waits for them, and re-layouts: 6.21 us -> 2.94 us
    ppermute x8, waiting for transfers between devices: 11.3 us -> 14.4 us  [exchange(): lax.ppermute(block, 'node', [(owner_of(node, turn, slots, stride), node)...]
    pallas_call x1 -> x3, Pallas kernels: 5 us -> 6.88 us  [the longest x1 5.06 us: total_pass(): pl.pallas_call(lambda *refs: total_kernel(turns, last, stride, counts, *r...]
  transfers between devices with their start and end apart: 36 -> 36, of which waited for: 20 -> 18; matrix products, arithmetic and copies ran while one was open for 0% -> 0% of each run, Pallas kernels for 21% -> 22%
where the time goes in v4:
time: 203 us
  waiting for transfers between devices  115 us (57%)
  Pallas kernels  48 us (24%)
  starting transfers between devices  35.6 us (18%)
  local copies, waits for them, and re-layouts  2.94 us (1%)
    ppermute x28, waiting for transfers between devices, ring_step(): lax.ppermute(block, 'local', [(order[i], order[(i + distance) % size]) fo...  101 us
    ppermute x28, starting transfers between devices, ring_step(): lax.ppermute(block, 'local', [(order[i], order[(i + distance) % size]) fo...  29.2 us
    ppermute x8, waiting for transfers between devices, exchange(): lax.ppermute(block, 'node', [(owner_of(node, turn, slots, stride), node)...  14.4 us
    pallas_call x8, Pallas kernels, acts_pass(): pl.pallas_call(lambda *refs: acts_kernel(turn, slots, stride, routes.shap...  12.6 us
    pallas_call x2, Pallas kernels, chunk_pass(): pl.pallas_call(kernel, out_shape=tuple((jax.ShapeDtypeStruct((part, width...  12.1 us
    pallas_call x4, Pallas kernels, grads_pass(): pl.pallas_call(lambda *refs: grads_kernel(parts, len(acts), len(shapes),...  9.61 us
    ppermute x8, starting transfers between devices, exchange(): lax.ppermute(block, 'node', [(owner_of(node, turn, slots, stride), node)...  6.33 us
    pallas_call x1, Pallas kernels, total_pass(): pl.pallas_call(lambda *refs: total_kernel(turns, last, stride, counts, *r...  5.06 us
  transfers between devices with their start and end apart: 36, of which 18 were waited for; matrix products, arithmetic and copies ran while one was open for 0% of the time, Pallas kernels for 22%

profile of v4, /device:TPU:0, one launch (start us, length us, event | category | flops | bytes accessed | tf_op | source)
XLA Modules:
  0.0 203.2 jit_solution(9300736869408271486)
XLA Ops:
  0.6 2.2 %copy-done = bf16[2,3,176,2048]{3,2,1,0:T(8,128)(2,1)S(1)} copy-done((bf16[2,3,176,2048]{3,2,1,0:T(8,128)(2,1)S(1)}, bf16[2,3,176,2048]{3,2,1,0:T(8,128)(2,1)}, u32[]{:S(2)}) %copy-start) | copy-done | bytes 4325400
  2.9 0.7 copy-done.5
  3.5 0.8 pick.4.refs_2_
  4.4 0.8 pick.5.refs_2_
  5.3 0.5 collective-permute-start.3
  5.8 2.6 %collective-permute-start.8 = (bf16[3,176,2048]{2,1,0:T(8,128)(2,1)S(1)}, bf16[3,176,2048]{2,1,0:T(8,128)(2,1)S(1)}, u32[]{:S(2)}, u32[]{:S(2)}) collective-permute-start(bf16[3,176,2048]{2,1,0:T(8,128)(2,1)S(1)} %pick.4.refs_2_), channel_id=1, source_target_pairs={{16,0},{24,8},{0,16},{8,24},{17,1},{25,9},{1,17},{9,25},{18,2},{26... | collective-permute-start | bytes 6488072 | tf_op jit(solution)/shard_map/ppermute | solution.py:85
  8.4 1.6 collective-permute-start.2
  10.4 1.5 collective-permute-start
  11.9 0.7 collective-permute-start.5
  12.6 0.8 pick.6.refs_2_.refs_0_
  13.4 0.8 pick.7.refs_1_.refs_8_
  14.3 8.9 %collective-permute-done.2.refs_0_ = bf16[128,2048]{1,0:T(8,128)(2,1)S(1)} collective-permute-done((bf16[128,2048]{1,0:T(8,128)(2,1)S(1)}, bf16[128,2048]{1,0:T(8,128)(2,1)S(1)}, u32[]{:S(2)}, u32[]{:S(2)}) %collective-permute-start.2) | collective-permute-done | bytes 524320 | tf_op jit(solution)/shard_map/ppermute | solution.py:203
  23.1 1.6 collective-permute-start.4
  25.2 10.8 %collective-permute-done.refs_0_ = bf16[128,2048]{1,0:T(8,128)(2,1)S(1)} collective-permute-done((bf16[128,2048]{1,0:T(8,128)(2,1)S(1)}, bf16[128,2048]{1,0:T(8,128)(2,1)S(1)}, u32[]{:S(2)}, u32[]{:S(2)}) %collective-permute-start) | collective-permute-done | bytes 524320 | tf_op jit(solution)/shard_map/ppermute | solution.py:203
  36.4 1.6 collective-permute-start.6
  38.0 7.6 %collective-permute-done.4.refs_0_ = bf16[128,2048]{1,0:T(8,128)(2,1)S(1)} collective-permute-done((bf16[128,2048]{1,0:T(8,128)(2,1)S(1)}, bf16[128,2048]{1,0:T(8,128)(2,1)S(1)}, u32[]{:S(2)}, u32[]{:S(2)}) %collective-permute-start.4) | collective-permute-done | bytes 524320 | tf_op jit(solution)/shard_map/ppermute | solution.py:203
  45.6 1.6 collective-permute-start.12
  47.7 8.3 %collective-permute-done.8.refs_0_ = bf16[3,176,2048]{2,1,0:T(8,128)(2,1)S(1)} collective-permute-done((bf16[3,176,2048]{2,1,0:T(8,128)(2,1)S(1)}, bf16[3,176,2048]{2,1,0:T(8,128)(2,1)S(1)}, u32[]{:S(2)}, u32[]{:S(2)}) %collective-permute-start.8) | collective-permute-done | bytes 2162720 | tf_op jit(solution)/shard_map/ppermute | solution.py:85
  56.0 1.0 collective-permute-start.16
  57.0 1.4 collective-permute-done.7.refs_0_
  58.9 1.6 collective-permute-start.14
  60.5 1.6 acts_1_n.1.refs_11_.refs_16_.refs_2_
  62.1 1.6 acts_0_n.1.refs_1_.refs_0_.refs_16_
  63.7 4.4 %collective-permute-done.12.refs_0_ = bf16[128,2048]{1,0:T(8,128)(2,1)S(1)} collective-permute-done((bf16[128,2048]{1,0:T(8,128)(2,1)S(1)}, bf16[128,2048]{1,0:T(8,128)(2,1)S(1)}, u32[]{:S(2)}, u32[]{:S(2)}) %collective-permute-start.12) | collective-permute-done | bytes 524320 | tf_op jit(solution)/shard_map/ppermute | solution.py:203
  68.1 1.6 collective-permute-start.13
  69.7 0.5 collective-permute-start.15
  70.2 10.8 %collective-permute-done.10.refs_0_ = bf16[128,2048]{1,0:T(8,128)(2,1)S(1)} collective-permute-done((bf16[128,2048]{1,0:T(8,128)(2,1)S(1)}, bf16[128,2048]{1,0:T(8,128)(2,1)S(1)}, u32[]{:S(2)}, u32[]{:S(2)}) %collective-permute-start.10) | collective-permute-done | bytes 524320 | tf_op jit(solution)/shard_map/ppermute | solution.py:203
  80.9 8.8 %collective-permute-done.13.refs_0_ = bf16[128,2048]{1,0:T(8,128)(2,1)S(1)} collective-permute-done((bf16[128,2048]{1,0:T(8,128)(2,1)S(1)}, bf16[128,2048]{1,0:T(8,128)(2,1)S(1)}, u32[]{:S(2)}, u32[]{:S(2)}) %collective-permute-start.13) | collective-permute-done | bytes 524320 | tf_op jit(solution)/shard_map/ppermute | solution.py:203
  89.8 1.3 collective-permute-done.15.refs_0_
  91.1 1.6 acts_1_f.1.refs_17_.refs_18_.refs_3_
  92.7 2.4 %grads_1.1 = (bf16[176,2048]{1,0:T(8,128)(2,1)S(1)}, bf16[176,2048]{1,0:T(8,128)(2,1)S(1)}, bf16[176,2048]{1,0:T(8,128)(2,1)S(1)}) custom-call(bf16[128,2048]{1,0:T(8,128)(2,1)S(1)} %copy-done.1, bf16[128,2048]{1,0:T(8,128)(2,1)S(1)} %gate.27.refs_1_, bf16[128,2048]{1,0:T(8,128)(2,1)S(1)} %gate.29.refs_1_.refs_2_, ...), custom_call_target="tpu_custom_call" | custom-call | flops 2214592512 | bytes 1 | tf_op jit(solution)/shard_map/grads_1/pallas_call | solution.py:294
  95.2 0.5 collective-permute-start.19
  95.7 1.6 acts_2_n.1.refs_11_.refs_16_.refs_4_
  97.3 1.6 acts_2_f.1.refs_17_.refs_18_.refs_5_
  98.9 2.4 %grads_2.1.refs_11_ = bf16[3,176,2048]{2,1,0:T(8,128)(2,1)S(1)} custom-call(bf16[128,2048]{1,0:T(8,128)(2,1)S(1)} %copy-done.1, bf16[128,2048]{1,0:T(8,128)(2,1)S(1)} %gate.27.refs_1_, bf16[128,2048]{1,0:T(8,128)(2,1)S(1)} %gate.29.refs_1_.refs_2_, bf16[128,2048]{1,0:T(8,128)(2,1)S(1)} %gate.25.refs_1_.refs_3_, ...), custom_call_target="tpu_custom_call" | custom-call | flops 2214592512 | bytes 1 | tf_op jit(solution)/shard_map/grads_2/pallas_call | solution.py:294
  101.3 0.6 collective-permute-start.28
  101.9 1.6 acts_0_f.1.refs_1_.refs_17_
  103.5 1.5 collective-permute-done.16.refs_0_
  105.0 1.6 acts_3_f.1.refs_11_.refs_7_.refs_17_
  106.6 1.6 acts_3_n.1.refs_6_.refs_12_.refs_16_
  108.2 3.9 %chunks_4.1 = (bf16[128,2048]{1,0:T(8,128)(2,1)}, bf16[128,2048]{1,0:T(8,128)(2,1)}, bf16[128,2048]{1,0:T(8,128)(2,1)}, bf16[128,2048]{1,0:T(8,128)(2,1)S(1)}) custom-call(bf16[528,512]{1,0:T(8,128)(2,1)S(1)} %acts_0_n.1.refs_1_.refs_0_.refs_16_, bf16[528,512]{1,0:T(8,128)(2,1)S(1)} %acts_0_f.1.refs_1_.refs_17_, ...), custom_call_target="tpu_custom_call" | custom-call | flops 2214592512 | bytes 1 | tf_op jit(solution)/shard_map/chunks_4/pallas_call | solution.py:340
  112.1 2.0 %collective-permute-start.20 = (bf16[128,2048]{1,0:T(8,128)(2,1)}, bf16[128,2048]{1,0:T(8,128)(2,1)S(1)}, u32[]{:S(2)}, u32[]{:S(2)}) collective-permute-start(bf16[128,2048]{1,0:T(8,128)(2,1)} %get-tuple-element.32), channel_id=1, source_target_pairs={{0,2},{2,4},{4,6},{6,7},{7,5},{5,3},{3,1},{1,0},{8,10},{10,12},{12... | collective-permute-start | bytes 1572872 | tf_op jit(solution)/shard_map/ppermute | solution.py:203
  114.2 8.1 %chunks_12.1 = (bf16[128,2048]{1,0:T(8,128)(2,1)S(1)}, bf16[128,2048]{1,0:T(8,128)(2,1)S(1)}, bf16[128,2048]{1,0:T(8,128)(2,1)S(1)}, bf16[128,2048]{1,0:T(8,128)...) custom-call(bf16[528,512]{1,0:T(8,128)(2,1)S(1)} %acts_0_n.1.refs_1_, ...), custom_call_target="tpu_custom_call" | custom-call | flops 1 | bytes 1 | tf_op jit(solution)/shard_map/chunks_12/pallas_call | solution.py:340
  122.3 2.1 %collective-permute-start.22 = (bf16[128,2048]{1,0:T(8,128)(2,1)S(1)}, bf16[128,2048]{1,0:T(8,128)(2,1)S(1)}, u32[]{:S(2)}, u32[]{:S(2)}) collective-permute-start(bf16[128,2048]{1,0:T(8,128)(2,1)S(1)} %get-tuple-element.33.refs_12_), channel_id=1, source_target_pairs={{0,2},{2,4},{4,6},{6,7},{7,5},{5,3},{3,1},{1,0},{8,10},{10,12},{12... | collective-permute-start | bytes 1572872 | tf_op jit(solution)/shard_map/ppermute | solution.py:203
  124.4 2.4 %grads_3.1.refs_18_.refs_0_ = bf16[3,176,2048]{2,1,0:T(8,128)(2,1)S(1)} custom-call(bf16[128,2048]{1,0:T(8,128)(2,1)S(1)} %copy-done.1, bf16[128,2048]{1,0:T(8,128)(2,1)S(1)} %gate.27.refs_1_, bf16[128,2048]{1,0:T(8,128)(2,1)S(1)} %gate.29.refs_1_.refs_2_, bf16[128,2048]{1,0:T(8,128)(2,1)S(1)} %gate.25.refs_1_.refs_3_, ...), custom_call_target="tpu_custom_call" | custom-call | flops 2214592512 | bytes 1 | tf_op jit(solution)/shard_map/grads_3/pallas_call | solution.py:294
  126.8 2.4 %grads_0.1.refs_2_.refs_1_ = bf16[3,176,2048]{2,1,0:T(8,128)(2,1)S(1)} custom-call(bf16[128,2048]{1,0:T(8,128)(2,1)S(1)} %copy-done.1, bf16[128,2048]{1,0:T(8,128)(2,1)S(1)} %gate.27.refs_1_, bf16[128,2048]{1,0:T(8,128)(2,1)S(1)} %gate.29.refs_1_.refs_2_, bf16[128,2048]{1,0:T(8,128)(2,1)S(1)} %gate.25.refs_1_.refs_3_, ...), custom_call_target="tpu_custom_call" | custom-call | flops 2214592512 | bytes 1 | tf_op jit(solution)/shard_map/grads_0/pallas_call | solution.py:294
  129.4 2.1 %collective-permute-start.21 = (bf16[128,2048]{1,0:T(8,128)(2,1)S(1)}, bf16[128,2048]{1,0:T(8,128)(2,1)S(1)}, u32[]{:S(2)}, u32[]{:S(2)}) collective-permute-start(bf16[128,2048]{1,0:T(8,128)(2,1)S(1)} %add_rows.12.refs_2_), channel_id=1, source_target_pairs={{0,2},{2,4},{4,6},{6,7},{7,5},{5,3},{3,1},{1,0},{8,10},{10,12},{12... | collective-permute-start | bytes 1572872 | tf_op jit(solution)/shard_map/ppermute | solution.py:203
  131.6 8.8 %collective-permute-done.23.refs_0_ = bf16[128,2048]{1,0:T(8,128)(2,1)S(1)} collective-permute-done((bf16[128,2048]{1,0:T(8,128)(2,1)}, bf16[128,2048]{1,0:T(8,128)(2,1)S(1)}, u32[]{:S(2)}, u32[]{:S(2)}) %collective-permute-start.23) | collective-permute-done | bytes 524320 | tf_op jit(solution)/shard_map/ppermute | solution.py:203
  140.8 2.1 %collective-permute-start.26 = (bf16[128,2048]{1,0:T(8,128)(2,1)S(1)}, bf16[128,2048]{1,0:T(8,128)(2,1)S(1)}, u32[]{:S(2)}, u32[]{:S(2)}) collective-permute-start(bf16[128,2048]{1,0:T(8,128)(2,1)S(1)} %add_rows.15.refs_2_), channel_id=1, source_target_pairs={{0,2},{2,4},{4,6},{6,7},{7,5},{5,3},{3,1},{1,0},{8,10},{10,12},{12... | collective-permute-start | bytes 1572872 | tf_op jit(solution)/shard_map/ppermute | solution.py:203
  142.8 6.7 %collective-permute-done.21.refs_0_ = bf16[128,2048]{1,0:T(8,128)(2,1)S(1)} collective-permute-done((bf16[128,2048]{1,0:T(8,128)(2,1)S(1)}, bf16[128,2048]{1,0:T(8,128)(2,1)S(1)}, u32[]{:S(2)}, u32[]{:S(2)}) %collective-permute-start.21) | collective-permute-done | bytes 524320 | tf_op jit(solution)/shard_map/ppermute | solution.py:203
  149.7 2.1 %collective-permute-start.25 = (bf16[128,2048]{1,0:T(8,128)(2,1)S(1)}, bf16[128,2048]{1,0:T(8,128)(2,1)S(1)}, u32[]{:S(2)}, u32[]{:S(2)}) collective-permute-start(bf16[128,2048]{1,0:T(8,128)(2,1)S(1)} %add_rows.16.refs_2_), channel_id=1, source_target_pairs={{0,2},{2,4},{4,6},{6,7},{7,5},{5,3},{3,1},{1,0},{8,10},{10,12},{12... | collective-permute-start | bytes 1572872 | tf_op jit(solution)/shard_map/ppermute | solution.py:203
  152.0 1.0 collective-permute-start.35
  153.0 9.9 %collective-permute-done.27.refs_0_ = bf16[128,2048]{1,0:T(8,128)(2,1)S(1)} collective-permute-done((bf16[128,2048]{1,0:T(8,128)(2,1)S(1)}, bf16[128,2048]{1,0:T(8,128)(2,1)S(1)}, u32[]{:S(2)}, u32[]{:S(2)}) %collective-permute-start.27) | collective-permute-done | bytes 524320 | tf_op jit(solution)/shard_map/ppermute | solution.py:203
  163.2 2.1 %collective-permute-start.33 = (bf16[128,2048]{1,0:T(8,128)(2,1)S(1)}, bf16[128,2048]{1,0:T(8,128)(2,1)S(1)}, u32[]{:S(2)}, u32[]{:S(2)}) collective-permute-start(bf16[128,2048]{1,0:T(8,128)(2,1)S(1)} %add_rows.19.refs_2_), channel_id=1, source_target_pairs={{0,2},{2,4},{4,6},{6,7},{7,5},{5,3},{3,1},{1,0},{8,10},{10,12},{12... | collective-permute-start | bytes 1572872 | tf_op jit(solution)/shard_map/ppermute | solution.py:203
  165.3 6.7 %collective-permute-done.25.refs_0_ = bf16[128,2048]{1,0:T(8,128)(2,1)S(1)} collective-permute-done((bf16[128,2048]{1,0:T(8,128)(2,1)S(1)}, bf16[128,2048]{1,0:T(8,128)(2,1)S(1)}, u32[]{:S(2)}, u32[]{:S(2)}) %collective-permute-start.25) | collective-permute-done | bytes 524320 | tf_op jit(solution)/shard_map/ppermute | solution.py:203
  172.1 2.1 %collective-permute-start.30 = (bf16[128,2048]{1,0:T(8,128)(2,1)S(1)}, bf16[128,2048]{1,0:T(8,128)(2,1)S(1)}, u32[]{:S(2)}, u32[]{:S(2)}) collective-permute-start(bf16[128,2048]{1,0:T(8,128)(2,1)S(1)} %add_rows.20.refs_2_), channel_id=1, source_target_pairs={{0,2},{2,4},{4,6},{6,7},{7,5},{5,3},{3,1},{1,0},{8,10},{10,12},{12... | collective-permute-start | bytes 1572872 | tf_op jit(solution)/shard_map/ppermute | solution.py:203
  174.5 10.9 %collective-permute-done.31.refs_0_ = bf16[128,2048]{1,0:T(8,128)(2,1)S(1)} collective-permute-done((bf16[128,2048]{1,0:T(8,128)(2,1)S(1)}, bf16[128,2048]{1,0:T(8,128)(2,1)S(1)}, u32[]{:S(2)}, u32[]{:S(2)}) %collective-permute-start.31) | collective-permute-done | bytes 524320 | tf_op jit(solution)/shard_map/ppermute | solution.py:203
  185.6 5.1 %total.1 = (bf16[2,3,176,2048]{3,2,1,0:T(8,128)(2,1)}, bf16[3,176,2048]{2,1,0:T(8,128)(2,1)S(1)}, f32[8,128]{1,0:T(8,128)S(1)}) custom-call(s32[4,4]{1,0:T(4,128)S(1)} %copy-done.6, bf16[3,176,2048]{2,1,0:T(8,128)(2,1)S(1)} %grads_0.1.refs_2_.refs_1_, bf16[176,2048]{1,0:T(8,128)(2,1)S(1)} %gate.41.refs_1_.refs_2_, ...), custom_call_target="tpu_custom_call" | custom-call | flops 1 | bytes 1 | tf_op jit(solution)/shard_map/total/pallas_call | solution.py:157
  190.7 3.4 %collective-permute-done.30.refs_0_ = bf16[128,2048]{1,0:T(8,128)(2,1)S(1)} collective-permute-done((bf16[128,2048]{1,0:T(8,128)(2,1)S(1)}, bf16[128,2048]{1,0:T(8,128)(2,1)S(1)}, u32[]{:S(2)}, u32[]{:S(2)}) %collective-permute-start.30) | collective-permute-done | bytes 524320 | tf_op jit(solution)/shard_map/ppermute | solution.py:203
  194.0 0.9 final_rows.2
  194.9 0.5 collective-permute-done.34.refs_0_
  195.5 0.9 final_rows.3
  196.4 4.6 %collective-permute-done.35.refs_0_ = bf16[3,176,2048]{2,1,0:T(8,128)(2,1)S(1)} collective-permute-done((bf16[3,176,2048]{2,1,0:T(8,128)(2,1)S(1)}, bf16[3,176,2048]{2,1,0:T(8,128)(2,1)S(1)}, u32[]{:S(2)}, u32[]{:S(2)}) %collective-permute-start.35) | collective-permute-done | bytes 2162720 | tf_op jit(solution)/shard_map/ppermute | solution.py:85
  201.0 2.1 %add.1 = bf16[2,3,176,2048]{3,2,1,0:T(8,128)(2,1)} custom-call(s32[4,4]{1,0:T(4,128)S(1)} %copy-done.6, bf16[2,3,176,2048]{3,2,1,0:T(8,128)(2,1)} %get-tuple-element.52.refs_1_, bf16[3,176,2048]{2,1,0:T(8,128)(2,1)S(1)} %get-tuple-element.53.refs_2_, bf16[3,176,2048]{2,1,0:T(8,128)(2,1)S(1)} %gate.47.refs_3_), custom_call_target="tpu_custom_call", output_to_operand_aliasing={{}: (1, {})} | custom-call | flops 1 | bytes 1 | tf_op jit(solution)/shard_map/add/pallas_call | solution.py:188
  (85 shorter events, 4.3 us)
Async XLA Ops:
  0.6 2.2 %copy-start = (bf16[2,3,176,2048]{3,2,1,0:T(8,128)(2,1)S(1)}, bf16[2,3,176,2048]{3,2,1,0:T(8,128)(2,1)}, u32[]{:S(2)}) copy-start(bf16[2,3,176,2048]{3,2,1,0:T(8,128)(2,1)} %refs_1_.7) | copy-start | bytes 12976132
  2.9 0.7 copy-start.5
  3.5 9.1 %slice-start = ((s8[4325376]{0:T(1024)(128)(4,1)}), s8[4194304]{0:T(1024)(128)(4,1)S(1)}, s32[]{:S(2)}) async-start(s8[4325376]{0:T(1024)(128)(4,1)} %bitcast.2), calls=%async_computation | async-start | bytes 8388608
  4.4 4.0 %copy-start.1 = (bf16[128,2048]{1,0:T(8,128)(2,1)S(1)}, bf16[128,2048]{1,0:T(8,128)(2,1)}, u32[]{:S(2)}) copy-start(bf16[128,2048]{1,0:T(8,128)(2,1)} %refs_0_.25) | copy-start | bytes 1572868
  4.4 5.6 %copy-start.2 = (bf16[128,2048]{1,0:T(8,128)(2,1)S(1)}, bf16[128,2048]{1,0:T(8,128)(2,1)}, u32[]{:S(2)}) copy-start(bf16[128,2048]{1,0:T(8,128)(2,1)} %refs_8_.7) | copy-start | bytes 1572868
  4.4 8.2 %slice-start.1 = ((s8[4325376]{0:T(1024)(128)(4,1)}), s8[131072]{0:T(1024)(128)(4,1)S(1)}, s32[]{:S(2)}) async-start(s8[4325376]{0:T(1024)(128)(4,1)} %bitcast.2), calls=%async_computation.1 | async-start | bytes 262144
  4.4 8.2 %copy-start.6 = (s32[4,4]{1,0:T(4,128)S(1)}, s32[4,4]{1,0:T(4,128)}, u32[]{:S(2)}) copy-start(s32[4,4]{1,0:T(4,128)} %refs_0_.27) | copy-start | bytes 196
  5.3 6.6 %collective-permute-start.3 = (bf16[3,176,2048]{2,1,0:T(8,128)(2,1)S(1)}, bf16[3,176,2048]{2,1,0:T(8,128)(2,1)S(1)}, u32[]{:S(2)}, u32[]{:S(2)}) collective-permute-start(bf16[3,176,2048]{2,1,0:T(8,128)(2,1)S(1)} %pick.5.refs_2_), channel_id=1, source_target_pairs={{8,0},{0,8},{24,16},{16,24},{9,1},{1,9},{25,17},{17,25},{10,2},{2,... | collective-permute-start | bytes 6488072 | tf_op jit(solution)/shard_map/ppermute | solution.py:85
  5.8 50.2 %collective-permute-start.8 = (bf16[3,176,2048]{2,1,0:T(8,128)(2,1)S(1)}, bf16[3,176,2048]{2,1,0:T(8,128)(2,1)S(1)}, u32[]{:S(2)}, u32[]{:S(2)}) collective-permute-start(bf16[3,176,2048]{2,1,0:T(8,128)(2,1)S(1)} %pick.4.refs_2_), channel_id=1, source_target_pairs={{16,0},{24,8},{0,16},{8,24},{17,1},{25,9},{1,17},{9,25},{18,2},{26... | collective-permute-start | bytes 6488072 | tf_op jit(solution)/shard_map/ppermute | solution.py:85
  8.4 14.8 %collective-permute-start.2 = (bf16[128,2048]{1,0:T(8,128)(2,1)S(1)}, bf16[128,2048]{1,0:T(8,128)(2,1)S(1)}, u32[]{:S(2)}, u32[]{:S(2)}) collective-permute-start(bf16[128,2048]{1,0:T(8,128)(2,1)S(1)} %copy-done.1), channel_id=1, source_target_pairs={{0,2},{2,4},{4,6},{6,7},{7,5},{5,3},{3,1},{1,0},{8,10},{10,12},{12... | collective-permute-start | bytes 1572872 | tf_op jit(solution)/shard_map/ppermute | solution.py:203
  9.9 14.8 %collective-permute-start.1 = (bf16[128,2048]{1,0:T(8,128)(2,1)S(1)}, bf16[128,2048]{1,0:T(8,128)(2,1)S(1)}, u32[]{:S(2)}, u32[]{:S(2)}) collective-permute-start(bf16[128,2048]{1,0:T(8,128)(2,1)S(1)} %copy-done.2), channel_id=1, source_target_pairs={{0,1},{2,0},{4,2},{6,4},{7,6},{5,7},{3,5},{1,3},{8,9},{10,8},{12,1... | collective-permute-start | bytes 1572872 | tf_op jit(solution)/shard_map/ppermute | solution.py:203
  10.4 25.6 %collective-permute-start = (bf16[128,2048]{1,0:T(8,128)(2,1)S(1)}, bf16[128,2048]{1,0:T(8,128)(2,1)S(1)}, u32[]{:S(2)}, u32[]{:S(2)}) collective-permute-start(bf16[128,2048]{1,0:T(8,128)(2,1)S(1)} %copy-done.1), channel_id=1, source_target_pairs={{0,1},{2,0},{4,2},{6,4},{7,6},{5,7},{3,5},{1,3},{8,9},{10,8},{12,1... | collective-permute-start | bytes 1572872 | tf_op jit(solution)/shard_map/ppermute | solution.py:203
  11.9 24.6 %collective-permute-start.5 = (bf16[128,2048]{1,0:T(8,128)(2,1)S(1)}, bf16[128,2048]{1,0:T(8,128)(2,1)S(1)}, u32[]{:S(2)}, u32[]{:S(2)}) collective-permute-start(bf16[128,2048]{1,0:T(8,128)(2,1)S(1)} %copy-done.2), channel_id=1, source_target_pairs={{0,2},{2,4},{4,6},{6,7},{7,5},{5,3},{3,1},{1,0},{8,10},{10,12},{12... | collective-permute-start | bytes 1572872 | tf_op jit(solution)/shard_map/ppermute | solution.py:203
  23.1 22.5 %collective-permute-start.4 = (bf16[128,2048]{1,0:T(8,128)(2,1)S(1)}, bf16[128,2048]{1,0:T(8,128)(2,1)S(1)}, u32[]{:S(2)}, u32[]{:S(2)}) collective-permute-start(bf16[128,2048]{1,0:T(8,128)(2,1)S(1)} %gate.25.refs_1_.refs_3_), channel_id=1, source_target_pairs={{0,2},{2,4},{4,6},{6,7},{7,5},{5,3},{3,1},{1,0},{8,10},{10,12},{12... | collective-permute-start | bytes 1572872 | tf_op jit(solution)/shard_map/ppermute | solution.py:203
  24.8 22.5 %collective-permute-start.9 = (bf16[128,2048]{1,0:T(8,128)(2,1)S(1)}, bf16[128,2048]{1,0:T(8,128)(2,1)S(1)}, u32[]{:S(2)}, u32[]{:S(2)}) collective-permute-start(bf16[128,2048]{1,0:T(8,128)(2,1)S(1)} %gate.26.refs_1_.refs_5_.refs_9_), channel_id=1, source_target_pairs={{0,1},{2,0},{4,2},{6,4},{7,6},{5,7},{3,5},{1,3},{8,9},{10,8},{12,1... | collective-permute-start | bytes 1572872 | tf_op jit(solution)/shard_map/ppermute | solution.py:203
  36.0 22.5 %collective-permute-start.7 = (bf16[128,2048]{1,0:T(8,128)(2,1)S(1)}, bf16[128,2048]{1,0:T(8,128)(2,1)S(1)}, u32[]{:S(2)}, u32[]{:S(2)}) collective-permute-start(bf16[128,2048]{1,0:T(8,128)(2,1)S(1)} %gate.27.refs_1_), channel_id=1, source_target_pairs={{0,1},{2,0},{4,2},{6,4},{7,6},{5,7},{3,5},{1,3},{8,9},{10,8},{12,1... | collective-permute-start | bytes 1572872 | tf_op jit(solution)/shard_map/ppermute | solution.py:203
  36.4 22.5 %collective-permute-start.6 = (bf16[128,2048]{1,0:T(8,128)(2,1)S(1)}, bf16[128,2048]{1,0:T(8,128)(2,1)S(1)}, u32[]{:S(2)}, u32[]{:S(2)}) collective-permute-start(bf16[128,2048]{1,0:T(8,128)(2,1)S(1)} %gate.28.refs_1_.refs_7_.refs_11_), channel_id=1, source_target_pairs={{0,2},{2,4},{4,6},{6,7},{7,5},{5,3},{3,1},{1,0},{8,10},{10,12},{12... | collective-permute-start | bytes 1572872 | tf_op jit(solution)/shard_map/ppermute | solution.py:203
  45.6 22.5 %collective-permute-start.12 = (bf16[128,2048]{1,0:T(8,128)(2,1)S(1)}, bf16[128,2048]{1,0:T(8,128)(2,1)S(1)}, u32[]{:S(2)}, u32[]{:S(2)}) collective-permute-start(bf16[128,2048]{1,0:T(8,128)(2,1)S(1)} %gate.29.refs_1_.refs_2_), channel_id=1, source_target_pairs={{0,2},{2,4},{4,6},{6,7},{7,5},{5,3},{3,1},{1,0},{8,10},{10,12},{12... | collective-permute-start | bytes 1572872 | tf_op jit(solution)/shard_map/ppermute | solution.py:203
  47.2 22.5 %collective-permute-start.11 = (bf16[128,2048]{1,0:T(8,128)(2,1)S(1)}, bf16[128,2048]{1,0:T(8,128)(2,1)S(1)}, u32[]{:S(2)}, u32[]{:S(2)}) collective-permute-start(bf16[128,2048]{1,0:T(8,128)(2,1)S(1)} %gate.30.refs_1_.refs_4_.refs_12_), channel_id=1, source_target_pairs={{0,1},{2,0},{4,2},{6,4},{7,6},{5,7},{3,5},{1,3},{8,9},{10,8},{12,1... | collective-permute-start | bytes 1572872 | tf_op jit(solution)/shard_map/ppermute | solution.py:203
  56.0 4.5 %copy-start.3 = (s32[1024,1]{0,1:T(1,128)S(1)}, s32[1024,1]{0,1:T(1,128)}, u32[]{:S(2)}) copy-start(s32[1024,1]{0,1:T(1,128)} %param.8) | copy-start | bytes 12292
  56.0 4.5 %copy-start.4 = (f32[1024,1]{0,1:T(1,128)S(1)}, f32[1024,1]{0,1:T(1,128)}, u32[]{:S(2)}) copy-start(f32[1024,1]{0,1:T(1,128)} %param.9) | copy-start | bytes 12292
  56.0 49.0 %collective-permute-start.16 = (bf16[3,176,2048]{2,1,0:T(8,128)(2,1)S(1)}, bf16[3,176,2048]{2,1,0:T(8,128)(2,1)S(1)}, u32[]{:S(2)}, u32[]{:S(2)}) collective-permute-start(bf16[3,176,2048]{2,1,0:T(8,128)(2,1)S(1)} %gate.32.refs_1_), channel_id=1, source_target_pairs={{24,0},{16,8},{8,16},{0,24},{25,1},{17,9},{9,17},{1,25},{26,2},{18... | collective-permute-start | bytes 6488072 | tf_op jit(solution)/shard_map/ppermute | solution.py:85
  58.5 22.5 %collective-permute-start.10 = (bf16[128,2048]{1,0:T(8,128)(2,1)S(1)}, bf16[128,2048]{1,0:T(8,128)(2,1)S(1)}, u32[]{:S(2)}, u32[]{:S(2)}) collective-permute-start(bf16[128,2048]{1,0:T(8,128)(2,1)S(1)} %gate.33.refs_1_.refs_0_.refs_4_), channel_id=1, source_target_pairs={{0,1},{2,0},{4,2},{6,4},{7,6},{5,7},{3,5},{1,3},{8,9},{10,8},{12,1... | collective-permute-start | bytes 1572872 | tf_op jit(solution)/shard_map/ppermute | solution.py:203
  58.9 22.0 %collective-permute-start.14 = (bf16[128,2048]{1,0:T(8,128)(2,1)S(1)}, bf16[128,2048]{1,0:T(8,128)(2,1)S(1)}, u32[]{:S(2)}, u32[]{:S(2)}) collective-permute-start(bf16[128,2048]{1,0:T(8,128)(2,1)S(1)} %gate.34.refs_6_.refs_11_.refs_10_), channel_id=1, source_target_pairs={{0,2},{2,4},{4,6},{6,7},{7,5},{5,3},{3,1},{1,0},{8,10},{10,12},{12... | collective-permute-start | bytes 1572872 | tf_op jit(solution)/shard_map/ppermute | solution.py:203
  68.1 21.7 %collective-permute-start.13 = (bf16[128,2048]{1,0:T(8,128)(2,1)S(1)}, bf16[128,2048]{1,0:T(8,128)(2,1)S(1)}, u32[]{:S(2)}, u32[]{:S(2)}) collective-permute-start(bf16[128,2048]{1,0:T(8,128)(2,1)S(1)} %gate.35.refs_1_.refs_3_.refs_7_), channel_id=1, source_target_pairs={{0,2},{2,4},{4,6},{6,7},{7,5},{5,3},{3,1},{1,0},{8,10},{10,12},{12... | collective-permute-start | bytes 1572872 | tf_op jit(solution)/shard_map/ppermute | solution.py:203
  69.7 21.4 %collective-permute-start.15 = (bf16[128,2048]{1,0:T(8,128)(2,1)S(1)}, bf16[128,2048]{1,0:T(8,128)(2,1)S(1)}, u32[]{:S(2)}, u32[]{:S(2)}) collective-permute-start(bf16[128,2048]{1,0:T(8,128)(2,1)S(1)} %gate.36.refs_1_.refs_5_.refs_13_), channel_id=1, source_target_pairs={{0,1},{2,0},{4,2},{6,4},{7,6},{5,7},{3,5},{1,3},{8,9},{10,8},{12,1... | collective-permute-start | bytes 1572872 | tf_op jit(solution)/shard_map/ppermute | solution.py:203
  95.1 8.4 %collective-permute-start.18 = (bf16[176,2048]{1,0:T(8,128)(2,1)S(1)}, bf16[176,2048]{1,0:T(8,128)(2,1)S(1)}, u32[]{:S(2)}, u32[]{:S(2)}) collective-permute-start(bf16[176,2048]{1,0:T(8,128)(2,1)S(1)} %get-tuple-element.30), channel_id=1, source_target_pairs={{8,0},{0,8},{24,16},{16,24},{9,1},{1,9},{25,17},{17,25},{10,2},{2,... | collective-permute-start | bytes 2162696 | tf_op jit(solution)/shard_map/ppermute | solution.py:85
  95.2 8.3 %collective-permute-start.19 = (bf16[176,2048]{1,0:T(8,128)(2,1)S(1)}, bf16[176,2048]{1,0:T(8,128)(2,1)S(1)}, u32[]{:S(2)}, u32[]{:S(2)}) collective-permute-start(bf16[176,2048]{1,0:T(8,128)(2,1)S(1)} %get-tuple-element.31), channel_id=1, source_target_pairs={{8,0},{0,8},{24,16},{16,24},{9,1},{1,9},{25,17},{17,25},{10,2},{2,... | collective-permute-start | bytes 2162696 | tf_op jit(solution)/shard_map/ppermute | solution.py:85
  95.6 7.8 %collective-permute-start.17 = (bf16[176,2048]{1,0:T(8,128)(2,1)S(1)}, bf16[176,2048]{1,0:T(8,128)(2,1)S(1)}, u32[]{:S(2)}, u32[]{:S(2)}) collective-permute-start(bf16[176,2048]{1,0:T(8,128)(2,1)S(1)} %get-tuple-element.29.refs_11_), channel_id=1, source_target_pairs={{8,0},{0,8},{24,16},{16,24},{9,1},{1,9},{25,17},{17,25},{10,2},{2,... | collective-permute-start | bytes 2162696 | tf_op jit(solution)/shard_map/ppermute | solution.py:85
  101.3 50.7 %collective-permute-start.28 = (bf16[3,176,2048]{2,1,0:T(8,128)(2,1)S(1)}, bf16[3,176,2048]{2,1,0:T(8,128)(2,1)S(1)}, u32[]{:S(2)}, u32[]{:S(2)}) collective-permute-start(bf16[3,176,2048]{2,1,0:T(8,128)(2,1)S(1)} %grads_2.1.refs_11_), channel_id=1, source_target_pairs={{16,0},{24,8},{0,16},{8,24},{17,1},{25,9},{1,17},{9,25},{18,2},{26... | collective-permute-start | bytes 6488072 | tf_op jit(solution)/shard_map/ppermute | solution.py:85
  112.1 17.1 %collective-permute-start.20 = (bf16[128,2048]{1,0:T(8,128)(2,1)}, bf16[128,2048]{1,0:T(8,128)(2,1)S(1)}, u32[]{:S(2)}, u32[]{:S(2)}) collective-permute-start(bf16[128,2048]{1,0:T(8,128)(2,1)} %get-tuple-element.32), channel_id=1, source_target_pairs={{0,2},{2,4},{4,6},{6,7},{7,5},{5,3},{3,1},{1,0},{8,10},{10,12},{12... | collective-permute-start | bytes 1572872 | tf_op jit(solution)/shard_map/ppermute | solution.py:203
  114.2 17.3 %collective-permute-start.24 = (bf16[128,2048]{1,0:T(8,128)(2,1)}, bf16[128,2048]{1,0:T(8,128)(2,1)S(1)}, u32[]{:S(2)}, u32[]{:S(2)}) collective-permute-start(bf16[128,2048]{1,0:T(8,128)(2,1)} %get-tuple-element.40), channel_id=1, source_target_pairs={{0,1},{2,0},{4,2},{6,4},{7,6},{5,7},{3,5},{1,3},{8,9},{10,8},{12,1... | collective-permute-start | bytes 1572872 | tf_op jit(solution)/shard_map/ppermute | solution.py:203
  122.3 18.3 %collective-permute-start.22 = (bf16[128,2048]{1,0:T(8,128)(2,1)S(1)}, bf16[128,2048]{1,0:T(8,128)(2,1)S(1)}, u32[]{:S(2)}, u32[]{:S(2)}) collective-permute-start(bf16[128,2048]{1,0:T(8,128)(2,1)S(1)} %get-tuple-element.33.refs_12_), channel_id=1, source_target_pairs={{0,2},{2,4},{4,6},{6,7},{7,5},{5,3},{3,1},{1,0},{8,10},{10,12},{12... | collective-permute-start | bytes 1572872 | tf_op jit(solution)/shard_map/ppermute | solution.py:203
  124.4 16.0 %collective-permute-start.23 = (bf16[128,2048]{1,0:T(8,128)(2,1)}, bf16[128,2048]{1,0:T(8,128)(2,1)S(1)}, u32[]{:S(2)}, u32[]{:S(2)}) collective-permute-start(bf16[128,2048]{1,0:T(8,128)(2,1)} %get-tuple-element.38), channel_id=1, source_target_pairs={{0,1},{2,0},{4,2},{6,4},{7,6},{5,7},{3,5},{1,3},{8,9},{10,8},{12,1... | collective-permute-start | bytes 1572872 | tf_op jit(solution)/shard_map/ppermute | solution.py:203
  129.4 20.2 %collective-permute-start.21 = (bf16[128,2048]{1,0:T(8,128)(2,1)S(1)}, bf16[128,2048]{1,0:T(8,128)(2,1)S(1)}, u32[]{:S(2)}, u32[]{:S(2)}) collective-permute-start(bf16[128,2048]{1,0:T(8,128)(2,1)S(1)} %add_rows.12.refs_2_), channel_id=1, source_target_pairs={{0,2},{2,4},{4,6},{6,7},{7,5},{5,3},{3,1},{1,0},{8,10},{10,12},{12... | collective-permute-start | bytes 1572872 | tf_op jit(solution)/shard_map/ppermute | solution.py:203
  131.6 20.2 %collective-permute-start.29 = (bf16[128,2048]{1,0:T(8,128)(2,1)S(1)}, bf16[128,2048]{1,0:T(8,128)(2,1)S(1)}, u32[]{:S(2)}, u32[]{:S(2)}) collective-permute-start(bf16[128,2048]{1,0:T(8,128)(2,1)S(1)} %add_rows.13.refs_2_), channel_id=1, source_target_pairs={{0,1},{2,0},{4,2},{6,4},{7,6},{5,7},{3,5},{1,3},{8,9},{10,8},{12,1... | collective-permute-start | bytes 1572872 | tf_op jit(solution)/shard_map/ppermute | solution.py:203
  140.6 22.3 %collective-permute-start.27 = (bf16[128,2048]{1,0:T(8,128)(2,1)S(1)}, bf16[128,2048]{1,0:T(8,128)(2,1)S(1)}, u32[]{:S(2)}, u32[]{:S(2)}) collective-permute-start(bf16[128,2048]{1,0:T(8,128)(2,1)S(1)} %add_rows.14.refs_2_), channel_id=1, source_target_pairs={{0,1},{2,0},{4,2},{6,4},{7,6},{5,7},{3,5},{1,3},{8,9},{10,8},{12,1... | collective-permute-start | bytes 1572872 | tf_op jit(solution)/shard_map/ppermute | solution.py:203
  140.8 22.3 %collective-permute-start.26 = (bf16[128,2048]{1,0:T(8,128)(2,1)S(1)}, bf16[128,2048]{1,0:T(8,128)(2,1)S(1)}, u32[]{:S(2)}, u32[]{:S(2)}) collective-permute-start(bf16[128,2048]{1,0:T(8,128)(2,1)S(1)} %add_rows.15.refs_2_), channel_id=1, source_target_pairs={{0,2},{2,4},{4,6},{6,7},{7,5},{5,3},{3,1},{1,0},{8,10},{10,12},{12... | collective-permute-start | bytes 1572872 | tf_op jit(solution)/shard_map/ppermute | solution.py:203
  149.7 22.3 %collective-permute-start.25 = (bf16[128,2048]{1,0:T(8,128)(2,1)S(1)}, bf16[128,2048]{1,0:T(8,128)(2,1)S(1)}, u32[]{:S(2)}, u32[]{:S(2)}) collective-permute-start(bf16[128,2048]{1,0:T(8,128)(2,1)S(1)} %add_rows.16.refs_2_), channel_id=1, source_target_pairs={{0,2},{2,4},{4,6},{6,7},{7,5},{5,3},{3,1},{1,0},{8,10},{10,12},{12... | collective-permute-start | bytes 1572872 | tf_op jit(solution)/shard_map/ppermute | solution.py:203
  151.9 22.3 %collective-permute-start.32 = (bf16[128,2048]{1,0:T(8,128)(2,1)S(1)}, bf16[128,2048]{1,0:T(8,128)(2,1)S(1)}, u32[]{:S(2)}, u32[]{:S(2)}) collective-permute-start(bf16[128,2048]{1,0:T(8,128)(2,1)S(1)} %add_rows.17.refs_1_), channel_id=1, source_target_pairs={{0,1},{2,0},{4,2},{6,4},{7,6},{5,7},{3,5},{1,3},{8,9},{10,8},{12,1... | collective-permute-start | bytes 1572872 | tf_op jit(solution)/shard_map/ppermute | solution.py:203
  152.0 48.9 %collective-permute-start.35 = (bf16[3,176,2048]{2,1,0:T(8,128)(2,1)S(1)}, bf16[3,176,2048]{2,1,0:T(8,128)(2,1)S(1)}, u32[]{:S(2)}, u32[]{:S(2)}) collective-permute-start(bf16[3,176,2048]{2,1,0:T(8,128)(2,1)S(1)} %gate.46.refs_2_), channel_id=1, source_target_pairs={{24,0},{16,8},{8,16},{0,24},{25,1},{17,9},{9,17},{1,25},{26,2},{18... | collective-permute-start | bytes 6488072 | tf_op jit(solution)/shard_map/ppermute | solution.py:85
  163.0 22.3 %collective-permute-start.31 = (bf16[128,2048]{1,0:T(8,128)(2,1)S(1)}, bf16[128,2048]{1,0:T(8,128)(2,1)S(1)}, u32[]{:S(2)}, u32[]{:S(2)}) collective-permute-start(bf16[128,2048]{1,0:T(8,128)(2,1)S(1)} %add_rows.18.refs_2_), channel_id=1, source_target_pairs={{0,1},{2,0},{4,2},{6,4},{7,6},{5,7},{3,5},{1,3},{8,9},{10,8},{12,1... | collective-permute-start | bytes 1572872 | tf_op jit(solution)/shard_map/ppermute | solution.py:203
  163.2 22.3 %collective-permute-start.33 = (bf16[128,2048]{1,0:T(8,128)(2,1)S(1)}, bf16[128,2048]{1,0:T(8,128)(2,1)S(1)}, u32[]{:S(2)}, u32[]{:S(2)}) collective-permute-start(bf16[128,2048]{1,0:T(8,128)(2,1)S(1)} %add_rows.19.refs_2_), channel_id=1, source_target_pairs={{0,2},{2,4},{4,6},{6,7},{7,5},{5,3},{3,1},{1,0},{8,10},{10,12},{12... | collective-permute-start | bytes 1572872 | tf_op jit(solution)/shard_map/ppermute | solution.py:203
  172.1 21.9 %collective-permute-start.30 = (bf16[128,2048]{1,0:T(8,128)(2,1)S(1)}, bf16[128,2048]{1,0:T(8,128)(2,1)S(1)}, u32[]{:S(2)}, u32[]{:S(2)}) collective-permute-start(bf16[128,2048]{1,0:T(8,128)(2,1)S(1)} %add_rows.20.refs_2_), channel_id=1, source_target_pairs={{0,2},{2,4},{4,6},{6,7},{7,5},{5,3},{3,1},{1,0},{8,10},{10,12},{12... | collective-permute-start | bytes 1572872 | tf_op jit(solution)/shard_map/ppermute | solution.py:203
  174.4 21.1 %collective-permute-start.34 = (bf16[128,2048]{1,0:T(8,128)(2,1)S(1)}, bf16[128,2048]{1,0:T(8,128)(2,1)S(1)}, u32[]{:S(2)}, u32[]{:S(2)}) collective-permute-start(bf16[128,2048]{1,0:T(8,128)(2,1)S(1)} %add_rows.21.refs_2_), channel_id=1, source_target_pairs={{0,1},{2,0},{4,2},{6,4},{7,6},{5,7},{3,5},{1,3},{8,9},{10,8},{12,1... | collective-permute-start | bytes 1572872 | tf_op jit(solution)/shard_map/ppermute | solution.py:203

commit v5 on v4

--- a/solution.py
+++ b/solution.py
@@ -380,6 +380,7 @@
 
 
 def body(tokens, cotangent, routes, route_weight, fetch_pick, panels):
+    panels = pltpu.with_memory_space_constraint(panels, pltpu.HBM)
     slots = fetch_pick.shape[1]
     stride = lax.axis_size("node") // slots
     part, width = tokens.shape
@@ -399,9 +400,6 @@
     dy_parts = [cotangent] + [None] * (size - 1)
     acts = [[None, None] for _ in range(slots)]
     grads, back = [None] * slots, [None] * slots
-
-    def pick(turn):
-        return line.step(lambda after: pick_pass([turn], stride, fetch_pick, panels, after))[0]
 
     def make_acts(turn, g):
         take = groups[g]
@@ -437,10 +435,11 @@
             back[turn] = [exchange(grad, turn, slots) if turn else grad for grad in grads[turn]]
 
     read = [None] * slots
-    read[late] = exchange(pick(late), late, slots)
-    for turn in middle:
-        read[turn] = exchange(pick(turn), turn, slots)
-    read[last], read[0] = pick(last), pick(0)
+    first_turns = [late] + middle
+    picked = line.step(lambda after: pick_pass(first_turns, stride, fetch_pick, panels, after))
+    for turn, panel in zip(first_turns, picked):
+        read[turn] = exchange(panel, turn, slots)
+    read[last], read[0] = line.step(lambda after: pick_pass([last, 0], stride, fetch_pick, panels, after))
 
     chains = [(x_parts, 1, up_most), (dy_parts, -1, up_most), (x_parts, -1, down_most), (dy_parts, 1, down_most)]
     moving = [ring_step(parts[0], order, way) for parts, way, _ in chains]

time: 203 us -> 202 us (level)
  Pallas kernels: 48 us -> 50.4 us
  local copies, waits for them, and re-layouts: 2.94 us -> 0.78 us
    pallas_call x4 -> x2, Pallas kernels: 3.29 us -> 5.72 us  [pick_pass(): pl.pallas_call(lambda *refs: pick_kernel(turns, stride, *refs), out_shape...]
    unnamed x18 -> x12, local copies, waits for them, and re-layouts: 2.94 us -> 0.78 us
where the time goes in v5:
time: 202 us
  waiting for transfers between devices  114 us (56%)
  Pallas kernels  50.4 us (25%)
  starting transfers between devices  35.6 us (18%)
    ppermute x28, waiting for transfers between devices, ring_step(): lax.ppermute(block, 'local', [(order[i], order[(i + distance) % size]) fo...  99.9 us
    ppermute x28, starting transfers between devices, ring_step(): lax.ppermute(block, 'local', [(order[i], order[(i + distance) % size]) fo...  29.3 us
    ppermute x8, waiting for transfers between devices, exchange(): lax.ppermute(block, 'node', [(owner_of(node, turn, slots, stride), node)...  14.4 us
    pallas_call x8, Pallas kernels, acts_pass(): pl.pallas_call(lambda *refs: acts_kernel(turn, slots, stride, routes.shap...  12.6 us
    pallas_call x2, Pallas kernels, chunk_pass(): pl.pallas_call(kernel, out_shape=tuple((jax.ShapeDtypeStruct((part, width...  12.1 us
    pallas_call x4, Pallas kernels, grads_pass(): pl.pallas_call(lambda *refs: grads_kernel(parts, len(acts), len(shapes),...  9.61 us
    ppermute x8, starting transfers between devices, exchange(): lax.ppermute(block, 'node', [(owner_of(node, turn, slots, stride), node)...  6.32 us
    pallas_call x2, Pallas kernels, pick_pass(): pl.pallas_call(lambda *refs: pick_kernel(turns, stride, *refs), out_shape...  5.72 us
  transfers between devices with their start and end apart: 36, of which 18 were waited for; matrix products, arithmetic and copies ran while one was open for 0% of the time, Pallas kernels for 22%

profile of v5, /device:TPU:0, one launch (start us, length us, event | category | flops | bytes accessed | tf_op | source)
XLA Modules:
  0.0 202.3 jit_solution(16799073082580575800)
XLA Ops:
  0.7 0.8 copy-done.4
  1.4 2.9 %pick.2 = (bf16[3,176,2048]{2,1,0:T(8,128)(2,1)S(1)}, bf16[3,176,2048]{2,1,0:T(8,128)(2,1)S(1)}) custom-call(s32[4,4]{1,0:T(4,128)S(1)} %copy-done.4, bf16[2,3,176,2048]{3,2,1,0:T(8,128)(2,1)} %refs_1_.3), custom_call_target="tpu_custom_call" | custom-call | flops 1 | bytes 1 | tf_op jit(solution)/shard_map/pick/pallas_call | solution.py:103
  4.3 0.5 collective-permute-start.3
  4.8 2.6 %collective-permute-start.8 = (bf16[3,176,2048]{2,1,0:T(8,128)(2,1)S(1)}, bf16[3,176,2048]{2,1,0:T(8,128)(2,1)S(1)}, u32[]{:S(2)}, u32[]{:S(2)}) collective-permute-start(bf16[3,176,2048]{2,1,0:T(8,128)(2,1)S(1)} %get-tuple-element.36), channel_id=1, source_target_pairs={{16,0},{24,8},{0,16},{8,24},{17,1},{25,9},{1,17},{9,25},{18,2},{26... | collective-permute-start | bytes 6488072 | tf_op jit(solution)/shard_map/ppermute | solution.py:85
  7.4 1.6 collective-permute-start.2
  9.0 0.4 collective-permute-start.1
  9.4 1.5 collective-permute-start
  10.9 0.7 collective-permute-start.5
  11.6 2.9 %pick.3 = (bf16[3,176,2048]{2,1,0:T(8,128)(2,1)S(1)}, bf16[3,176,2048]{2,1,0:T(8,128)(2,1)S(1)}) custom-call(s32[4,4]{1,0:T(4,128)S(1)} %copy-done.5, bf16[2,3,176,2048]{3,2,1,0:T(8,128)(2,1)} %refs_1_.3, bf16[3,176,2048]{2,1,0:T(8,128)(2,1)S(1)} %get-tuple-element.33.refs_2_), custom_call_target="tpu_custom_call" | custom-call | flops 1 | bytes 1 | tf_op jit(solution)/shard_map/pick/pallas_call | solution.py:103
  14.5 7.7 %collective-permute-done.2.refs_0_ = bf16[128,2048]{1,0:T(8,128)(2,1)S(1)} collective-permute-done((bf16[128,2048]{1,0:T(8,128)(2,1)S(1)}, bf16[128,2048]{1,0:T(8,128)(2,1)S(1)}, u32[]{:S(2)}, u32[]{:S(2)}) %collective-permute-start.2) | collective-permute-done | bytes 524320 | tf_op jit(solution)/shard_map/ppermute | solution.py:203
  22.2 1.6 collective-permute-start.4
  24.2 10.8 %collective-permute-done.refs_0_ = bf16[128,2048]{1,0:T(8,128)(2,1)S(1)} collective-permute-done((bf16[128,2048]{1,0:T(8,128)(2,1)S(1)}, bf16[128,2048]{1,0:T(8,128)(2,1)S(1)}, u32[]{:S(2)}, u32[]{:S(2)}) %collective-permute-start) | collective-permute-done | bytes 524320 | tf_op jit(solution)/shard_map/ppermute | solution.py:203
  35.5 1.6 collective-permute-start.6
  37.1 7.6 %collective-permute-done.4.refs_0_ = bf16[128,2048]{1,0:T(8,128)(2,1)S(1)} collective-permute-done((bf16[128,2048]{1,0:T(8,128)(2,1)S(1)}, bf16[128,2048]{1,0:T(8,128)(2,1)S(1)}, u32[]{:S(2)}, u32[]{:S(2)}) %collective-permute-start.4) | collective-permute-done | bytes 524320 | tf_op jit(solution)/shard_map/ppermute | solution.py:203
  44.6 1.6 collective-permute-start.12
  46.3 0.4 collective-permute-start.11
  46.7 8.3 %collective-permute-done.8.refs_0_ = bf16[3,176,2048]{2,1,0:T(8,128)(2,1)S(1)} collective-permute-done((bf16[3,176,2048]{2,1,0:T(8,128)(2,1)S(1)}, bf16[3,176,2048]{2,1,0:T(8,128)(2,1)S(1)}, u32[]{:S(2)}, u32[]{:S(2)}) %collective-permute-start.8) | collective-permute-done | bytes 2162720 | tf_op jit(solution)/shard_map/ppermute | solution.py:85
  55.0 1.0 collective-permute-start.16
  56.1 1.4 collective-permute-done.7.refs_0_
  57.5 0.4 collective-permute-start.10
  58.0 1.6 collective-permute-start.14
  59.5 1.6 acts_1_n.1.refs_11_.refs_16_.refs_2_
  61.1 1.6 acts_0_n.1.refs_1_.refs_0_.refs_16_
  62.7 4.4 %collective-permute-done.12.refs_0_ = bf16[128,2048]{1,0:T(8,128)(2,1)S(1)} collective-permute-done((bf16[128,2048]{1,0:T(8,128)(2,1)S(1)}, bf16[128,2048]{1,0:T(8,128)(2,1)S(1)}, u32[]{:S(2)}, u32[]{:S(2)}) %collective-permute-start.12) | collective-permute-done | bytes 524320 | tf_op jit(solution)/shard_map/ppermute | solution.py:203
  67.1 1.6 collective-permute-start.13
  68.7 0.5 collective-permute-start.15
  69.2 10.8 %collective-permute-done.10.refs_0_ = bf16[128,2048]{1,0:T(8,128)(2,1)S(1)} collective-permute-done((bf16[128,2048]{1,0:T(8,128)(2,1)S(1)}, bf16[128,2048]{1,0:T(8,128)(2,1)S(1)}, u32[]{:S(2)}, u32[]{:S(2)}) %collective-permute-start.10) | collective-permute-done | bytes 524320 | tf_op jit(solution)/shard_map/ppermute | solution.py:203
  80.0 8.8 %collective-permute-done.13.refs_0_ = bf16[128,2048]{1,0:T(8,128)(2,1)S(1)} collective-permute-done((bf16[128,2048]{1,0:T(8,128)(2,1)S(1)}, bf16[128,2048]{1,0:T(8,128)(2,1)S(1)}, u32[]{:S(2)}, u32[]{:S(2)}) %collective-permute-start.13) | collective-permute-done | bytes 524320 | tf_op jit(solution)/shard_map/ppermute | solution.py:203
  88.8 1.3 collective-permute-done.15.refs_0_
  90.1 1.6 acts_1_f.1.refs_17_.refs_18_.refs_3_
  91.7 2.4 %grads_1.1 = (bf16[176,2048]{1,0:T(8,128)(2,1)S(1)}, bf16[176,2048]{1,0:T(8,128)(2,1)S(1)}, bf16[176,2048]{1,0:T(8,128)(2,1)S(1)}) custom-call(bf16[128,2048]{1,0:T(8,128)(2,1)S(1)} %copy-done, bf16[128,2048]{1,0:T(8,128)(2,1)S(1)} %gate.27.refs_1_, bf16[128,2048]{1,0:T(8,128)(2,1)S(1)} %gate.29.refs_1_.refs_2_, bf16[128,2048]{1,0:T(8,128)(2,1)S(1)} %gate.25.refs_1_.refs_3_, ...), custom_call_target="tpu_custom_call" | custom-call | flops 2214592512 | bytes 1 | tf_op jit(solution)/shard_map/grads_1/pallas_call | solution.py:294
  94.2 0.5 collective-permute-start.19
  94.8 1.6 acts_2_n.1.refs_11_.refs_16_.refs_4_
  96.3 1.6 acts_2_f.1.refs_17_.refs_18_.refs_5_
  97.9 2.4 %grads_2.1.refs_11_ = bf16[3,176,2048]{2,1,0:T(8,128)(2,1)S(1)} custom-call(bf16[128,2048]{1,0:T(8,128)(2,1)S(1)} %copy-done, bf16[128,2048]{1,0:T(8,128)(2,1)S(1)} %gate.27.refs_1_, bf16[128,2048]{1,0:T(8,128)(2,1)S(1)} %gate.29.refs_1_.refs_2_, bf16[128,2048]{1,0:T(8,128)(2,1)S(1)} %gate.25.refs_1_.refs_3_, ...), custom_call_target="tpu_custom_call" | custom-call | flops 2214592512 | bytes 1 | tf_op jit(solution)/shard_map/grads_2/pallas_call | solution.py:294
  100.3 0.6 collective-permute-start.28
  100.9 1.6 acts_0_f.1.refs_1_.refs_17_
  102.5 1.5 collective-permute-done.16.refs_0_
  104.1 1.6 acts_3_f.1.refs_11_.refs_7_.refs_17_
  105.6 1.6 acts_3_n.1.refs_6_.refs_12_.refs_16_
  107.2 3.9 %chunks_4.1 = (bf16[128,2048]{1,0:T(8,128)(2,1)}, bf16[128,2048]{1,0:T(8,128)(2,1)}, bf16[128,2048]{1,0:T(8,128)(2,1)}, bf16[128,2048]{1,0:T(8,128)(2,1)S(1)}) custom-call(bf16[528,512]{1,0:T(8,128)(2,1)S(1)} %acts_0_n.1.refs_1_.refs_0_.refs_16_, bf16[528,512]{1,0:T(8,128)(2,1)S(1)} %acts_0_f.1.refs_1_.refs_17_, ...), custom_call_target="tpu_custom_call" | custom-call | flops 2214592512 | bytes 1 | tf_op jit(solution)/shard_map/chunks_4/pallas_call | solution.py:340
  111.2 2.0 %collective-permute-start.20 = (bf16[128,2048]{1,0:T(8,128)(2,1)}, bf16[128,2048]{1,0:T(8,128)(2,1)S(1)}, u32[]{:S(2)}, u32[]{:S(2)}) collective-permute-start(bf16[128,2048]{1,0:T(8,128)(2,1)} %get-tuple-element.40), channel_id=1, source_target_pairs={{0,2},{2,4},{4,6},{6,7},{7,5},{5,3},{3,1},{1,0},{8,10},{10,12},{12... | collective-permute-start | bytes 1572872 | tf_op jit(solution)/shard_map/ppermute | solution.py:203
  113.2 8.1 %chunks_12.1 = (bf16[128,2048]{1,0:T(8,128)(2,1)S(1)}, bf16[128,2048]{1,0:T(8,128)(2,1)S(1)}, bf16[128,2048]{1,0:T(8,128)(2,1)S(1)}, bf16[128,2048]{1,0:T(8,128)...) custom-call(bf16[528,512]{1,0:T(8,128)(2,1)S(1)} %acts_0_n.1.refs_1_, ...), custom_call_target="tpu_custom_call" | custom-call | flops 1 | bytes 1 | tf_op jit(solution)/shard_map/chunks_12/pallas_call | solution.py:340
  121.4 2.1 %collective-permute-start.22 = (bf16[128,2048]{1,0:T(8,128)(2,1)S(1)}, bf16[128,2048]{1,0:T(8,128)(2,1)S(1)}, u32[]{:S(2)}, u32[]{:S(2)}) collective-permute-start(bf16[128,2048]{1,0:T(8,128)(2,1)S(1)} %get-tuple-element.41.refs_12_), channel_id=1, source_target_pairs={{0,2},{2,4},{4,6},{6,7},{7,5},{5,3},{3,1},{1,0},{8,10},{10,12},{12... | collective-permute-start | bytes 1572872 | tf_op jit(solution)/shard_map/ppermute | solution.py:203
  123.4 2.4 %grads_3.1.refs_18_.refs_0_ = bf16[3,176,2048]{2,1,0:T(8,128)(2,1)S(1)} custom-call(bf16[128,2048]{1,0:T(8,128)(2,1)S(1)} %copy-done, bf16[128,2048]{1,0:T(8,128)(2,1)S(1)} %gate.27.refs_1_, bf16[128,2048]{1,0:T(8,128)(2,1)S(1)} %gate.29.refs_1_.refs_2_, bf16[128,2048]{1,0:T(8,128)(2,1)S(1)} %gate.25.refs_1_.refs_3_, ...), custom_call_target="tpu_custom_call" | custom-call | flops 2214592512 | bytes 1 | tf_op jit(solution)/shard_map/grads_3/pallas_call | solution.py:294
  125.8 2.4 %grads_0.1.refs_2_.refs_1_ = bf16[3,176,2048]{2,1,0:T(8,128)(2,1)S(1)} custom-call(bf16[128,2048]{1,0:T(8,128)(2,1)S(1)} %copy-done, bf16[128,2048]{1,0:T(8,128)(2,1)S(1)} %gate.27.refs_1_, bf16[128,2048]{1,0:T(8,128)(2,1)S(1)} %gate.29.refs_1_.refs_2_, bf16[128,2048]{1,0:T(8,128)(2,1)S(1)} %gate.25.refs_1_.refs_3_, ...), custom_call_target="tpu_custom_call" | custom-call | flops 2214592512 | bytes 1 | tf_op jit(solution)/shard_map/grads_0/pallas_call | solution.py:294
  128.4 2.1 %collective-permute-start.21 = (bf16[128,2048]{1,0:T(8,128)(2,1)S(1)}, bf16[128,2048]{1,0:T(8,128)(2,1)S(1)}, u32[]{:S(2)}, u32[]{:S(2)}) collective-permute-start(bf16[128,2048]{1,0:T(8,128)(2,1)S(1)} %add_rows.12.refs_2_), channel_id=1, source_target_pairs={{0,2},{2,4},{4,6},{6,7},{7,5},{5,3},{3,1},{1,0},{8,10},{10,12},{12... | collective-permute-start | bytes 1572872 | tf_op jit(solution)/shard_map/ppermute | solution.py:203
  130.7 8.8 %collective-permute-done.23.refs_0_ = bf16[128,2048]{1,0:T(8,128)(2,1)S(1)} collective-permute-done((bf16[128,2048]{1,0:T(8,128)(2,1)}, bf16[128,2048]{1,0:T(8,128)(2,1)S(1)}, u32[]{:S(2)}, u32[]{:S(2)}) %collective-permute-start.23) | collective-permute-done | bytes 524320 | tf_op jit(solution)/shard_map/ppermute | solution.py:203
  139.8 2.1 %collective-permute-start.26 = (bf16[128,2048]{1,0:T(8,128)(2,1)S(1)}, bf16[128,2048]{1,0:T(8,128)(2,1)S(1)}, u32[]{:S(2)}, u32[]{:S(2)}) collective-permute-start(bf16[128,2048]{1,0:T(8,128)(2,1)S(1)} %add_rows.15.refs_2_), channel_id=1, source_target_pairs={{0,2},{2,4},{4,6},{6,7},{7,5},{5,3},{3,1},{1,0},{8,10},{10,12},{12... | collective-permute-start | bytes 1572872 | tf_op jit(solution)/shard_map/ppermute | solution.py:203
  141.8 6.7 %collective-permute-done.21.refs_0_ = bf16[128,2048]{1,0:T(8,128)(2,1)S(1)} collective-permute-done((bf16[128,2048]{1,0:T(8,128)(2,1)S(1)}, bf16[128,2048]{1,0:T(8,128)(2,1)S(1)}, u32[]{:S(2)}, u32[]{:S(2)}) %collective-permute-start.21) | collective-permute-done | bytes 524320 | tf_op jit(solution)/shard_map/ppermute | solution.py:203
  148.7 2.2 %collective-permute-start.25 = (bf16[128,2048]{1,0:T(8,128)(2,1)S(1)}, bf16[128,2048]{1,0:T(8,128)(2,1)S(1)}, u32[]{:S(2)}, u32[]{:S(2)}) collective-permute-start(bf16[128,2048]{1,0:T(8,128)(2,1)S(1)} %add_rows.16.refs_2_), channel_id=1, source_target_pairs={{0,2},{2,4},{4,6},{6,7},{7,5},{5,3},{3,1},{1,0},{8,10},{10,12},{12... | collective-permute-start | bytes 1572872 | tf_op jit(solution)/shard_map/ppermute | solution.py:203
  151.1 1.0 collective-permute-start.35
  152.0 9.9 %collective-permute-done.27.refs_0_ = bf16[128,2048]{1,0:T(8,128)(2,1)S(1)} collective-permute-done((bf16[128,2048]{1,0:T(8,128)(2,1)S(1)}, bf16[128,2048]{1,0:T(8,128)(2,1)S(1)}, u32[]{:S(2)}, u32[]{:S(2)}) %collective-permute-start.27) | collective-permute-done | bytes 524320 | tf_op jit(solution)/shard_map/ppermute | solution.py:203
  162.3 2.1 %collective-permute-start.33 = (bf16[128,2048]{1,0:T(8,128)(2,1)S(1)}, bf16[128,2048]{1,0:T(8,128)(2,1)S(1)}, u32[]{:S(2)}, u32[]{:S(2)}) collective-permute-start(bf16[128,2048]{1,0:T(8,128)(2,1)S(1)} %add_rows.19.refs_2_), channel_id=1, source_target_pairs={{0,2},{2,4},{4,6},{6,7},{7,5},{5,3},{3,1},{1,0},{8,10},{10,12},{12... | collective-permute-start | bytes 1572872 | tf_op jit(solution)/shard_map/ppermute | solution.py:203
  164.3 6.7 %collective-permute-done.25.refs_0_ = bf16[128,2048]{1,0:T(8,128)(2,1)S(1)} collective-permute-done((bf16[128,2048]{1,0:T(8,128)(2,1)S(1)}, bf16[128,2048]{1,0:T(8,128)(2,1)S(1)}, u32[]{:S(2)}, u32[]{:S(2)}) %collective-permute-start.25) | collective-permute-done | bytes 524320 | tf_op jit(solution)/shard_map/ppermute | solution.py:203
  171.2 2.2 %collective-permute-start.30 = (bf16[128,2048]{1,0:T(8,128)(2,1)S(1)}, bf16[128,2048]{1,0:T(8,128)(2,1)S(1)}, u32[]{:S(2)}, u32[]{:S(2)}) collective-permute-start(bf16[128,2048]{1,0:T(8,128)(2,1)S(1)} %add_rows.20.refs_2_), channel_id=1, source_target_pairs={{0,2},{2,4},{4,6},{6,7},{7,5},{5,3},{3,1},{1,0},{8,10},{10,12},{12... | collective-permute-start | bytes 1572872 | tf_op jit(solution)/shard_map/ppermute | solution.py:203
  173.5 10.9 %collective-permute-done.31.refs_0_ = bf16[128,2048]{1,0:T(8,128)(2,1)S(1)} collective-permute-done((bf16[128,2048]{1,0:T(8,128)(2,1)S(1)}, bf16[128,2048]{1,0:T(8,128)(2,1)S(1)}, u32[]{:S(2)}, u32[]{:S(2)}) %collective-permute-start.31) | collective-permute-done | bytes 524320 | tf_op jit(solution)/shard_map/ppermute | solution.py:203
  184.6 5.1 %total.1 = (bf16[2,3,176,2048]{3,2,1,0:T(8,128)(2,1)}, bf16[3,176,2048]{2,1,0:T(8,128)(2,1)S(1)}, f32[8,128]{1,0:T(8,128)S(1)}) custom-call(s32[4,4]{1,0:T(4,128)S(1)} %copy-done.5, bf16[3,176,2048]{2,1,0:T(8,128)(2,1)S(1)} %grads_0.1.refs_2_.refs_1_, bf16[176,2048]{1,0:T(8,128)(2,1)S(1)} %gate.41.refs_1_.refs_2_, ...), custom_call_target="tpu_custom_call" | custom-call | flops 1 | bytes 1 | tf_op jit(solution)/shard_map/total/pallas_call | solution.py:157
  189.7 3.4 %collective-permute-done.30.refs_0_ = bf16[128,2048]{1,0:T(8,128)(2,1)S(1)} collective-permute-done((bf16[128,2048]{1,0:T(8,128)(2,1)S(1)}, bf16[128,2048]{1,0:T(8,128)(2,1)S(1)}, u32[]{:S(2)}, u32[]{:S(2)}) %collective-permute-start.30) | collective-permute-done | bytes 524320 | tf_op jit(solution)/shard_map/ppermute | solution.py:203
  193.1 0.9 final_rows.2
  194.0 0.5 collective-permute-done.34.refs_0_
  194.5 0.9 final_rows.3
  195.4 4.6 %collective-permute-done.35.refs_0_ = bf16[3,176,2048]{2,1,0:T(8,128)(2,1)S(1)} collective-permute-done((bf16[3,176,2048]{2,1,0:T(8,128)(2,1)S(1)}, bf16[3,176,2048]{2,1,0:T(8,128)(2,1)S(1)}, u32[]{:S(2)}, u32[]{:S(2)}) %collective-permute-start.35) | collective-permute-done | bytes 2162720 | tf_op jit(solution)/shard_map/ppermute | solution.py:85
  200.0 2.1 %add.1 = bf16[2,3,176,2048]{3,2,1,0:T(8,128)(2,1)} custom-call(s32[4,4]{1,0:T(4,128)S(1)} %copy-done.5, bf16[2,3,176,2048]{3,2,1,0:T(8,128)(2,1)} %get-tuple-element.60.refs_1_, bf16[3,176,2048]{2,1,0:T(8,128)(2,1)S(1)} %get-tuple-element.61.refs_2_, bf16[3,176,2048]{2,1,0:T(8,128)(2,1)S(1)} %gate.47.refs_3_), custom_call_target="tpu_custom_call", output_to_operand_aliasing={{}: (1, {})} | custom-call | flops 1 | bytes 1 | tf_op jit(solution)/shard_map/add/pallas_call | solution.py:188
  (76 shorter events, 3.0 us)
Async XLA Ops:
  0.6 6.8 %copy-start = (bf16[128,2048]{1,0:T(8,128)(2,1)S(1)}, bf16[128,2048]{1,0:T(8,128)(2,1)}, u32[]{:S(2)}) copy-start(bf16[128,2048]{1,0:T(8,128)(2,1)} %refs_0_.21) | copy-start | bytes 1572868
  0.6 8.3 %copy-start.1 = (bf16[128,2048]{1,0:T(8,128)(2,1)S(1)}, bf16[128,2048]{1,0:T(8,128)(2,1)}, u32[]{:S(2)}) copy-start(bf16[128,2048]{1,0:T(8,128)(2,1)} %refs_8_.7) | copy-start | bytes 1572868
  0.7 0.8 copy-start.4
  1.4 10.2 %copy-start.5 = (s32[4,4]{1,0:T(4,128)S(1)}, s32[4,4]{1,0:T(4,128)}, u32[]{:S(2)}) copy-start(s32[4,4]{1,0:T(4,128)} %refs_0_.23) | copy-start | bytes 196
  4.3 6.6 %collective-permute-start.3 = (bf16[3,176,2048]{2,1,0:T(8,128)(2,1)S(1)}, bf16[3,176,2048]{2,1,0:T(8,128)(2,1)S(1)}, u32[]{:S(2)}, u32[]{:S(2)}) collective-permute-start(bf16[3,176,2048]{2,1,0:T(8,128)(2,1)S(1)} %get-tuple-element.33.refs_2_), channel_id=1, source_target_pairs={{8,0},{0,8},{24,16},{16,24},{9,1},{1,9},{25,17},{17,25},{10,2},{2,... | collective-permute-start | bytes 6488072 | tf_op jit(solution)/shard_map/ppermute | solution.py:85
  4.8 50.2 %collective-permute-start.8 = (bf16[3,176,2048]{2,1,0:T(8,128)(2,1)S(1)}, bf16[3,176,2048]{2,1,0:T(8,128)(2,1)S(1)}, u32[]{:S(2)}, u32[]{:S(2)}) collective-permute-start(bf16[3,176,2048]{2,1,0:T(8,128)(2,1)S(1)} %get-tuple-element.36), channel_id=1, source_target_pairs={{16,0},{24,8},{0,16},{8,24},{17,1},{25,9},{1,17},{9,25},{18,2},{26... | collective-permute-start | bytes 6488072 | tf_op jit(solution)/shard_map/ppermute | solution.py:85
  7.4 14.8 %collective-permute-start.2 = (bf16[128,2048]{1,0:T(8,128)(2,1)S(1)}, bf16[128,2048]{1,0:T(8,128)(2,1)S(1)}, u32[]{:S(2)}, u32[]{:S(2)}) collective-permute-start(bf16[128,2048]{1,0:T(8,128)(2,1)S(1)} %copy-done), channel_id=1, source_target_pairs={{0,2},{2,4},{4,6},{6,7},{7,5},{5,3},{3,1},{1,0},{8,10},{10,12},{12... | collective-permute-start | bytes 1572872 | tf_op jit(solution)/shard_map/ppermute | solution.py:203
  9.0 14.8 %collective-permute-start.1 = (bf16[128,2048]{1,0:T(8,128)(2,1)S(1)}, bf16[128,2048]{1,0:T(8,128)(2,1)S(1)}, u32[]{:S(2)}, u32[]{:S(2)}) collective-permute-start(bf16[128,2048]{1,0:T(8,128)(2,1)S(1)} %copy-done.1), channel_id=1, source_target_pairs={{0,1},{2,0},{4,2},{6,4},{7,6},{5,7},{3,5},{1,3},{8,9},{10,8},{12,1... | collective-permute-start | bytes 1572872 | tf_op jit(solution)/shard_map/ppermute | solution.py:203
  9.4 25.6 %collective-permute-start = (bf16[128,2048]{1,0:T(8,128)(2,1)S(1)}, bf16[128,2048]{1,0:T(8,128)(2,1)S(1)}, u32[]{:S(2)}, u32[]{:S(2)}) collective-permute-start(bf16[128,2048]{1,0:T(8,128)(2,1)S(1)} %copy-done), channel_id=1, source_target_pairs={{0,1},{2,0},{4,2},{6,4},{7,6},{5,7},{3,5},{1,3},{8,9},{10,8},{12,1... | collective-permute-start | bytes 1572872 | tf_op jit(solution)/shard_map/ppermute | solution.py:203
  10.9 24.6 %collective-permute-start.5 = (bf16[128,2048]{1,0:T(8,128)(2,1)S(1)}, bf16[128,2048]{1,0:T(8,128)(2,1)S(1)}, u32[]{:S(2)}, u32[]{:S(2)}) collective-permute-start(bf16[128,2048]{1,0:T(8,128)(2,1)S(1)} %copy-done.1), channel_id=1, source_target_pairs={{0,2},{2,4},{4,6},{6,7},{7,5},{5,3},{3,1},{1,0},{8,10},{10,12},{12... | collective-permute-start | bytes 1572872 | tf_op jit(solution)/shard_map/ppermute | solution.py:203
  22.2 22.5 %collective-permute-start.4 = (bf16[128,2048]{1,0:T(8,128)(2,1)S(1)}, bf16[128,2048]{1,0:T(8,128)(2,1)S(1)}, u32[]{:S(2)}, u32[]{:S(2)}) collective-permute-start(bf16[128,2048]{1,0:T(8,128)(2,1)S(1)} %gate.25.refs_1_.refs_3_), channel_id=1, source_target_pairs={{0,2},{2,4},{4,6},{6,7},{7,5},{5,3},{3,1},{1,0},{8,10},{10,12},{12... | collective-permute-start | bytes 1572872 | tf_op jit(solution)/shard_map/ppermute | solution.py:203
  23.8 22.5 %collective-permute-start.9 = (bf16[128,2048]{1,0:T(8,128)(2,1)S(1)}, bf16[128,2048]{1,0:T(8,128)(2,1)S(1)}, u32[]{:S(2)}, u32[]{:S(2)}) collective-permute-start(bf16[128,2048]{1,0:T(8,128)(2,1)S(1)} %gate.26.refs_1_.refs_5_.refs_9_), channel_id=1, source_target_pairs={{0,1},{2,0},{4,2},{6,4},{7,6},{5,7},{3,5},{1,3},{8,9},{10,8},{12,1... | collective-permute-start | bytes 1572872 | tf_op jit(solution)/shard_map/ppermute | solution.py:203
  35.0 22.5 %collective-permute-start.7 = (bf16[128,2048]{1,0:T(8,128)(2,1)S(1)}, bf16[128,2048]{1,0:T(8,128)(2,1)S(1)}, u32[]{:S(2)}, u32[]{:S(2)}) collective-permute-start(bf16[128,2048]{1,0:T(8,128)(2,1)S(1)} %gate.27.refs_1_), channel_id=1, source_target_pairs={{0,1},{2,0},{4,2},{6,4},{7,6},{5,7},{3,5},{1,3},{8,9},{10,8},{12,1... | collective-permute-start | bytes 1572872 | tf_op jit(solution)/shard_map/ppermute | solution.py:203
  35.5 22.5 %collective-permute-start.6 = (bf16[128,2048]{1,0:T(8,128)(2,1)S(1)}, bf16[128,2048]{1,0:T(8,128)(2,1)S(1)}, u32[]{:S(2)}, u32[]{:S(2)}) collective-permute-start(bf16[128,2048]{1,0:T(8,128)(2,1)S(1)} %gate.28.refs_1_.refs_7_.refs_11_), channel_id=1, source_target_pairs={{0,2},{2,4},{4,6},{6,7},{7,5},{5,3},{3,1},{1,0},{8,10},{10,12},{12... | collective-permute-start | bytes 1572872 | tf_op jit(solution)/shard_map/ppermute | solution.py:203
  44.6 22.5 %collective-permute-start.12 = (bf16[128,2048]{1,0:T(8,128)(2,1)S(1)}, bf16[128,2048]{1,0:T(8,128)(2,1)S(1)}, u32[]{:S(2)}, u32[]{:S(2)}) collective-permute-start(bf16[128,2048]{1,0:T(8,128)(2,1)S(1)} %gate.29.refs_1_.refs_2_), channel_id=1, source_target_pairs={{0,2},{2,4},{4,6},{6,7},{7,5},{5,3},{3,1},{1,0},{8,10},{10,12},{12... | collective-permute-start | bytes 1572872 | tf_op jit(solution)/shard_map/ppermute | solution.py:203
  46.3 22.5 %collective-permute-start.11 = (bf16[128,2048]{1,0:T(8,128)(2,1)S(1)}, bf16[128,2048]{1,0:T(8,128)(2,1)S(1)}, u32[]{:S(2)}, u32[]{:S(2)}) collective-permute-start(bf16[128,2048]{1,0:T(8,128)(2,1)S(1)} %gate.30.refs_1_.refs_4_.refs_12_), channel_id=1, source_target_pairs={{0,1},{2,0},{4,2},{6,4},{7,6},{5,7},{3,5},{1,3},{8,9},{10,8},{12,1... | collective-permute-start | bytes 1572872 | tf_op jit(solution)/shard_map/ppermute | solution.py:203
  55.0 4.5 %copy-start.2 = (s32[1024,1]{0,1:T(1,128)S(1)}, s32[1024,1]{0,1:T(1,128)}, u32[]{:S(2)}) copy-start(s32[1024,1]{0,1:T(1,128)} %param.8) | copy-start | bytes 12292
  55.0 4.5 %copy-start.3 = (f32[1024,1]{0,1:T(1,128)S(1)}, f32[1024,1]{0,1:T(1,128)}, u32[]{:S(2)}) copy-start(f32[1024,1]{0,1:T(1,128)} %param.9) | copy-start | bytes 12292
  55.0 49.0 %collective-permute-start.16 = (bf16[3,176,2048]{2,1,0:T(8,128)(2,1)S(1)}, bf16[3,176,2048]{2,1,0:T(8,128)(2,1)S(1)}, u32[]{:S(2)}, u32[]{:S(2)}) collective-permute-start(bf16[3,176,2048]{2,1,0:T(8,128)(2,1)S(1)} %gate.32.refs_1_), channel_id=1, source_target_pairs={{24,0},{16,8},{8,16},{0,24},{25,1},{17,9},{9,17},{1,25},{26,2},{18... | collective-permute-start | bytes 6488072 | tf_op jit(solution)/shard_map/ppermute | solution.py:85
  57.5 22.5 %collective-permute-start.10 = (bf16[128,2048]{1,0:T(8,128)(2,1)S(1)}, bf16[128,2048]{1,0:T(8,128)(2,1)S(1)}, u32[]{:S(2)}, u32[]{:S(2)}) collective-permute-start(bf16[128,2048]{1,0:T(8,128)(2,1)S(1)} %gate.33.refs_1_.refs_0_.refs_4_), channel_id=1, source_target_pairs={{0,1},{2,0},{4,2},{6,4},{7,6},{5,7},{3,5},{1,3},{8,9},{10,8},{12,1... | collective-permute-start | bytes 1572872 | tf_op jit(solution)/shard_map/ppermute | solution.py:203
  58.0 22.0 %collective-permute-start.14 = (bf16[128,2048]{1,0:T(8,128)(2,1)S(1)}, bf16[128,2048]{1,0:T(8,128)(2,1)S(1)}, u32[]{:S(2)}, u32[]{:S(2)}) collective-permute-start(bf16[128,2048]{1,0:T(8,128)(2,1)S(1)} %gate.34.refs_6_.refs_11_.refs_10_), channel_id=1, source_target_pairs={{0,2},{2,4},{4,6},{6,7},{7,5},{5,3},{3,1},{1,0},{8,10},{10,12},{12... | collective-permute-start | bytes 1572872 | tf_op jit(solution)/shard_map/ppermute | solution.py:203
  67.1 21.7 %collective-permute-start.13 = (bf16[128,2048]{1,0:T(8,128)(2,1)S(1)}, bf16[128,2048]{1,0:T(8,128)(2,1)S(1)}, u32[]{:S(2)}, u32[]{:S(2)}) collective-permute-start(bf16[128,2048]{1,0:T(8,128)(2,1)S(1)} %gate.35.refs_1_.refs_3_.refs_7_), channel_id=1, source_target_pairs={{0,2},{2,4},{4,6},{6,7},{7,5},{5,3},{3,1},{1,0},{8,10},{10,12},{12... | collective-permute-start | bytes 1572872 | tf_op jit(solution)/shard_map/ppermute | solution.py:203
  68.7 21.4 %collective-permute-start.15 = (bf16[128,2048]{1,0:T(8,128)(2,1)S(1)}, bf16[128,2048]{1,0:T(8,128)(2,1)S(1)}, u32[]{:S(2)}, u32[]{:S(2)}) collective-permute-start(bf16[128,2048]{1,0:T(8,128)(2,1)S(1)} %gate.36.refs_1_.refs_5_.refs_13_), channel_id=1, source_target_pairs={{0,1},{2,0},{4,2},{6,4},{7,6},{5,7},{3,5},{1,3},{8,9},{10,8},{12,1... | collective-permute-start | bytes 1572872 | tf_op jit(solution)/shard_map/ppermute | solution.py:203
  94.1 8.4 %collective-permute-start.18 = (bf16[176,2048]{1,0:T(8,128)(2,1)S(1)}, bf16[176,2048]{1,0:T(8,128)(2,1)S(1)}, u32[]{:S(2)}, u32[]{:S(2)}) collective-permute-start(bf16[176,2048]{1,0:T(8,128)(2,1)S(1)} %get-tuple-element.38), channel_id=1, source_target_pairs={{8,0},{0,8},{24,16},{16,24},{9,1},{1,9},{25,17},{17,25},{10,2},{2,... | collective-permute-start | bytes 2162696 | tf_op jit(solution)/shard_map/ppermute | solution.py:85
  94.2 8.3 %collective-permute-start.19 = (bf16[176,2048]{1,0:T(8,128)(2,1)S(1)}, bf16[176,2048]{1,0:T(8,128)(2,1)S(1)}, u32[]{:S(2)}, u32[]{:S(2)}) collective-permute-start(bf16[176,2048]{1,0:T(8,128)(2,1)S(1)} %get-tuple-element.39), channel_id=1, source_target_pairs={{8,0},{0,8},{24,16},{16,24},{9,1},{1,9},{25,17},{17,25},{10,2},{2,... | collective-permute-start | bytes 2162696 | tf_op jit(solution)/shard_map/ppermute | solution.py:85
  94.7 7.8 %collective-permute-start.17 = (bf16[176,2048]{1,0:T(8,128)(2,1)S(1)}, bf16[176,2048]{1,0:T(8,128)(2,1)S(1)}, u32[]{:S(2)}, u32[]{:S(2)}) collective-permute-start(bf16[176,2048]{1,0:T(8,128)(2,1)S(1)} %get-tuple-element.37.refs_11_), channel_id=1, source_target_pairs={{8,0},{0,8},{24,16},{16,24},{9,1},{1,9},{25,17},{17,25},{10,2},{2,... | collective-permute-start | bytes 2162696 | tf_op jit(solution)/shard_map/ppermute | solution.py:85
  100.3 50.7 %collective-permute-start.28 = (bf16[3,176,2048]{2,1,0:T(8,128)(2,1)S(1)}, bf16[3,176,2048]{2,1,0:T(8,128)(2,1)S(1)}, u32[]{:S(2)}, u32[]{:S(2)}) collective-permute-start(bf16[3,176,2048]{2,1,0:T(8,128)(2,1)S(1)} %grads_2.1.refs_11_), channel_id=1, source_target_pairs={{16,0},{24,8},{0,16},{8,24},{17,1},{25,9},{1,17},{9,25},{18,2},{26... | collective-permute-start | bytes 6488072 | tf_op jit(solution)/shard_map/ppermute | solution.py:85
  111.2 17.1 %collective-permute-start.20 = (bf16[128,2048]{1,0:T(8,128)(2,1)}, bf16[128,2048]{1,0:T(8,128)(2,1)S(1)}, u32[]{:S(2)}, u32[]{:S(2)}) collective-permute-start(bf16[128,2048]{1,0:T(8,128)(2,1)} %get-tuple-element.40), channel_id=1, source_target_pairs={{0,2},{2,4},{4,6},{6,7},{7,5},{5,3},{3,1},{1,0},{8,10},{10,12},{12... | collective-permute-start | bytes 1572872 | tf_op jit(solution)/shard_map/ppermute | solution.py:203
  113.2 17.3 %collective-permute-start.24 = (bf16[128,2048]{1,0:T(8,128)(2,1)}, bf16[128,2048]{1,0:T(8,128)(2,1)S(1)}, u32[]{:S(2)}, u32[]{:S(2)}) collective-permute-start(bf16[128,2048]{1,0:T(8,128)(2,1)} %get-tuple-element.48), channel_id=1, source_target_pairs={{0,1},{2,0},{4,2},{6,4},{7,6},{5,7},{3,5},{1,3},{8,9},{10,8},{12,1... | collective-permute-start | bytes 1572872 | tf_op jit(solution)/shard_map/ppermute | solution.py:203
  121.4 18.3 %collective-permute-start.22 = (bf16[128,2048]{1,0:T(8,128)(2,1)S(1)}, bf16[128,2048]{1,0:T(8,128)(2,1)S(1)}, u32[]{:S(2)}, u32[]{:S(2)}) collective-permute-start(bf16[128,2048]{1,0:T(8,128)(2,1)S(1)} %get-tuple-element.41.refs_12_), channel_id=1, source_target_pairs={{0,2},{2,4},{4,6},{6,7},{7,5},{5,3},{3,1},{1,0},{8,10},{10,12},{12... | collective-permute-start | bytes 1572872 | tf_op jit(solution)/shard_map/ppermute | solution.py:203
  123.4 16.0 %collective-permute-start.23 = (bf16[128,2048]{1,0:T(8,128)(2,1)}, bf16[128,2048]{1,0:T(8,128)(2,1)S(1)}, u32[]{:S(2)}, u32[]{:S(2)}) collective-permute-start(bf16[128,2048]{1,0:T(8,128)(2,1)} %get-tuple-element.46), channel_id=1, source_target_pairs={{0,1},{2,0},{4,2},{6,4},{7,6},{5,7},{3,5},{1,3},{8,9},{10,8},{12,1... | collective-permute-start | bytes 1572872 | tf_op jit(solution)/shard_map/ppermute | solution.py:203
  128.4 20.2 %collective-permute-start.21 = (bf16[128,2048]{1,0:T(8,128)(2,1)S(1)}, bf16[128,2048]{1,0:T(8,128)(2,1)S(1)}, u32[]{:S(2)}, u32[]{:S(2)}) collective-permute-start(bf16[128,2048]{1,0:T(8,128)(2,1)S(1)} %add_rows.12.refs_2_), channel_id=1, source_target_pairs={{0,2},{2,4},{4,6},{6,7},{7,5},{5,3},{3,1},{1,0},{8,10},{10,12},{12... | collective-permute-start | bytes 1572872 | tf_op jit(solution)/shard_map/ppermute | solution.py:203
  130.6 20.2 %collective-permute-start.29 = (bf16[128,2048]{1,0:T(8,128)(2,1)S(1)}, bf16[128,2048]{1,0:T(8,128)(2,1)S(1)}, u32[]{:S(2)}, u32[]{:S(2)}) collective-permute-start(bf16[128,2048]{1,0:T(8,128)(2,1)S(1)} %add_rows.13.refs_2_), channel_id=1, source_target_pairs={{0,1},{2,0},{4,2},{6,4},{7,6},{5,7},{3,5},{1,3},{8,9},{10,8},{12,1... | collective-permute-start | bytes 1572872 | tf_op jit(solution)/shard_map/ppermute | solution.py:203
  139.6 22.3 %collective-permute-start.27 = (bf16[128,2048]{1,0:T(8,128)(2,1)S(1)}, bf16[128,2048]{1,0:T(8,128)(2,1)S(1)}, u32[]{:S(2)}, u32[]{:S(2)}) collective-permute-start(bf16[128,2048]{1,0:T(8,128)(2,1)S(1)} %add_rows.14.refs_2_), channel_id=1, source_target_pairs={{0,1},{2,0},{4,2},{6,4},{7,6},{5,7},{3,5},{1,3},{8,9},{10,8},{12,1... | collective-permute-start | bytes 1572872 | tf_op jit(solution)/shard_map/ppermute | solution.py:203
  139.8 22.3 %collective-permute-start.26 = (bf16[128,2048]{1,0:T(8,128)(2,1)S(1)}, bf16[128,2048]{1,0:T(8,128)(2,1)S(1)}, u32[]{:S(2)}, u32[]{:S(2)}) collective-permute-start(bf16[128,2048]{1,0:T(8,128)(2,1)S(1)} %add_rows.15.refs_2_), channel_id=1, source_target_pairs={{0,2},{2,4},{4,6},{6,7},{7,5},{5,3},{3,1},{1,0},{8,10},{10,12},{12... | collective-permute-start | bytes 1572872 | tf_op jit(solution)/shard_map/ppermute | solution.py:203
  148.7 22.3 %collective-permute-start.25 = (bf16[128,2048]{1,0:T(8,128)(2,1)S(1)}, bf16[128,2048]{1,0:T(8,128)(2,1)S(1)}, u32[]{:S(2)}, u32[]{:S(2)}) collective-permute-start(bf16[128,2048]{1,0:T(8,128)(2,1)S(1)} %add_rows.16.refs_2_), channel_id=1, source_target_pairs={{0,2},{2,4},{4,6},{6,7},{7,5},{5,3},{3,1},{1,0},{8,10},{10,12},{12... | collective-permute-start | bytes 1572872 | tf_op jit(solution)/shard_map/ppermute | solution.py:203
  151.0 22.3 %collective-permute-start.32 = (bf16[128,2048]{1,0:T(8,128)(2,1)S(1)}, bf16[128,2048]{1,0:T(8,128)(2,1)S(1)}, u32[]{:S(2)}, u32[]{:S(2)}) collective-permute-start(bf16[128,2048]{1,0:T(8,128)(2,1)S(1)} %add_rows.17.refs_1_), channel_id=1, source_target_pairs={{0,1},{2,0},{4,2},{6,4},{7,6},{5,7},{3,5},{1,3},{8,9},{10,8},{12,1... | collective-permute-start | bytes 1572872 | tf_op jit(solution)/shard_map/ppermute | solution.py:203
  151.1 48.9 %collective-permute-start.35 = (bf16[3,176,2048]{2,1,0:T(8,128)(2,1)S(1)}, bf16[3,176,2048]{2,1,0:T(8,128)(2,1)S(1)}, u32[]{:S(2)}, u32[]{:S(2)}) collective-permute-start(bf16[3,176,2048]{2,1,0:T(8,128)(2,1)S(1)} %gate.46.refs_2_), channel_id=1, source_target_pairs={{24,0},{16,8},{8,16},{0,24},{25,1},{17,9},{9,17},{1,25},{26,2},{18... | collective-permute-start | bytes 6488072 | tf_op jit(solution)/shard_map/ppermute | solution.py:85
  162.1 22.3 %collective-permute-start.31 = (bf16[128,2048]{1,0:T(8,128)(2,1)S(1)}, bf16[128,2048]{1,0:T(8,128)(2,1)S(1)}, u32[]{:S(2)}, u32[]{:S(2)}) collective-permute-start(bf16[128,2048]{1,0:T(8,128)(2,1)S(1)} %add_rows.18.refs_2_), channel_id=1, source_target_pairs={{0,1},{2,0},{4,2},{6,4},{7,6},{5,7},{3,5},{1,3},{8,9},{10,8},{12,1... | collective-permute-start | bytes 1572872 | tf_op jit(solution)/shard_map/ppermute | solution.py:203
  162.3 22.3 %collective-permute-start.33 = (bf16[128,2048]{1,0:T(8,128)(2,1)S(1)}, bf16[128,2048]{1,0:T(8,128)(2,1)S(1)}, u32[]{:S(2)}, u32[]{:S(2)}) collective-permute-start(bf16[128,2048]{1,0:T(8,128)(2,1)S(1)} %add_rows.19.refs_2_), channel_id=1, source_target_pairs={{0,2},{2,4},{4,6},{6,7},{7,5},{5,3},{3,1},{1,0},{8,10},{10,12},{12... | collective-permute-start | bytes 1572872 | tf_op jit(solution)/shard_map/ppermute | solution.py:203
  171.2 21.9 %collective-permute-start.30 = (bf16[128,2048]{1,0:T(8,128)(2,1)S(1)}, bf16[128,2048]{1,0:T(8,128)(2,1)S(1)}, u32[]{:S(2)}, u32[]{:S(2)}) collective-permute-start(bf16[128,2048]{1,0:T(8,128)(2,1)S(1)} %add_rows.20.refs_2_), channel_id=1, source_target_pairs={{0,2},{2,4},{4,6},{6,7},{7,5},{5,3},{3,1},{1,0},{8,10},{10,12},{12... | collective-permute-start | bytes 1572872 | tf_op jit(solution)/shard_map/ppermute | solution.py:203
  173.4 21.1 %collective-permute-start.34 = (bf16[128,2048]{1,0:T(8,128)(2,1)S(1)}, bf16[128,2048]{1,0:T(8,128)(2,1)S(1)}, u32[]{:S(2)}, u32[]{:S(2)}) collective-permute-start(bf16[128,2048]{1,0:T(8,128)(2,1)S(1)} %add_rows.21.refs_2_), channel_id=1, source_target_pairs={{0,1},{2,0},{4,2},{6,4},{7,6},{5,7},{3,5},{1,3},{8,9},{10,8},{12,1... | collective-permute-start | bytes 1572872 | tf_op jit(solution)/shard_map/ppermute | solution.py:203

commit v6 on v5

--- a/solution.py
+++ b/solution.py
@@ -32,6 +32,10 @@
 
 def token_shape():
     return jax.ShapeDtypeStruct((8, 128), F32)
+
+
+def by_kind(refs):
+    return [refs[0].at[kind] for kind in range(3)] if len(refs) == 1 else list(refs)
 
 
 def untouched():
@@ -87,29 +91,48 @@
     )
 
 
-def pick_kernel(turns, stride, fetch_pick, panels, *refs):
-    outs, sems = refs[-len(turns) - 1 : -1], refs[-1]
-    copies = [
-        pltpu.make_async_copy(panels.at[turn_pick(fetch_pick, turn, stride)], out, sems.at[i])
-        for i, (turn, out) in enumerate(zip(turns, outs))
-    ]
+def halves(units):
+    middle = max(16, units // 32 * 16) if units > 16 else units
+    return [(0, middle), (middle, units)] if middle < units else [(0, units)]
+
+
+def pick_kernel(turns, stride, apart, fetch_pick, panels, *refs):
+    kinds, units = panels.shape[1:3]
+    spans = halves(units)
+    outs, sems = refs[-len(turns) * (kinds if apart else 1) - 1 : -1], refs[-1]
+    copies = []
+    for i, turn in enumerate(turns):
+        pick = turn_pick(fetch_pick, turn, stride)
+        for kind in range(kinds):
+            out = outs[i * kinds + kind] if apart else outs[i].at[kind]
+            for j, (low, high) in enumerate(spans):
+                here = pl.ds(low, high - low)
+                copies.append(
+                    pltpu.make_async_copy(
+                        panels.at[pick, kind, here], out.at[here], sems.at[i, kind, j]
+                    )
+                )
     for copy in copies:
         copy.start()
     for copy in copies:
         copy.wait()
 
 
-def pick_pass(turns, stride, fetch_pick, panels, after=()):
-    return pl.pallas_call(
-        lambda *refs: pick_kernel(turns, stride, *refs),
-        out_shape=tuple(jax.ShapeDtypeStruct(panels.shape[1:], BF16) for _ in turns),
+def pick_pass(turns, stride, fetch_pick, panels, apart, after=()):
+    kinds = panels.shape[1]
+    shapes = [panels.shape[2:]] * kinds if apart else [panels.shape[1:]]
+    shapes = shapes * len(turns)
+    out = pl.pallas_call(
+        lambda *refs: pick_kernel(turns, stride, apart, *refs),
+        out_shape=tuple(jax.ShapeDtypeStruct(shape, BF16) for shape in shapes),
         in_specs=[pl.BlockSpec(memory_space=pltpu.SMEM), in_hbm()] + [untouched()] * len(after),
-        out_specs=tuple(untouched() for _ in turns),
-        scratch_shapes=[pltpu.SemaphoreType.DMA((len(turns),))],
+        out_specs=tuple(untouched() for _ in shapes),
+        scratch_shapes=[pltpu.SemaphoreType.DMA((len(turns), kinds, 2))],
         compiler_params=pltpu.CompilerParams(vmem_limit_bytes=1024 * 1024),
         cost_estimate=NO_COST,
         name="pick",
     )(fetch_pick, panels, *after)
+    return out
 
 
 def gate(value, after):
@@ -173,13 +196,16 @@
 
 def add_kernel(turn, stride, fetch_pick, total, base, grad, out, sums, sems):
     pick = turn_pick(fetch_pick, turn, stride)
-    writes = [
-        pltpu.make_async_copy(sums.at[kind], out.at[pick, kind], sems.at[kind])
-        for kind in range(grad.shape[0])
-    ]
-    for kind, write in enumerate(writes):
-        sums[kind] = (base[kind].astype(F32) + grad[kind].astype(F32)).astype(BF16)
-        write.start()
+    writes = []
+    for kind in range(grad.shape[0]):
+        for j, (low, high) in enumerate(halves(grad.shape[1])):
+            here = pl.ds(low, high - low)
+            sums[kind, here] = (base[kind, here].astype(F32) + grad[kind, here].astype(F32)).astype(BF16)
+            write = pltpu.make_async_copy(
+                sums.at[kind, here], out.at[pick, kind, here], sems.at[kind, j]
+            )
+            write.start()
+            writes.append(write)
     for write in writes:
         write.wait()
 
@@ -191,7 +217,7 @@
         in_specs=[pl.BlockSpec(memory_space=pltpu.SMEM), in_hbm(), whole_in_vmem(), whole_in_vmem()],
         out_specs=in_hbm(),
         input_output_aliases={1: 0},
-        scratch_shapes=[pltpu.VMEM(grad.shape, BF16), pltpu.SemaphoreType.DMA((grad.shape[0],))],
+        scratch_shapes=[pltpu.VMEM(grad.shape, BF16), pltpu.SemaphoreType.DMA((grad.shape[0], 2))],
         compiler_params=pltpu.CompilerParams(vmem_limit_bytes=12 * 1024 * 1024),
         cost_estimate=NO_COST,
         name="add",
@@ -222,11 +248,13 @@
     )(a, b, *after)
 
 
-def acts_kernel(turn, slots, stride, size, offsets, *refs):
+def acts_kernel(turn, slots, stride, size, offsets, pieces, *refs):
     parts = len(offsets)
     x_refs, dy_refs = refs[:parts], refs[parts : 2 * parts]
-    panel, routes, weight, acts = *refs[2 * parts : 2 * parts + 3], refs[-1]
-    units, width = panel.shape[1:]
+    panel, (routes, weight), acts = by_kind(refs[2 * parts : 2 * parts + pieces]), refs[
+        2 * parts + pieces : 2 * parts + pieces + 2
+    ], refs[-1]
+    units, width = panel[0].shape
     part = x_refs[0].shape[0]
     at_once = 2 if parts % 2 == 0 else 1
     slot = turn_slot(turn, slots, stride)
@@ -235,10 +263,10 @@
         x = jnp.concatenate([ref[...] for ref in x_refs[d : d + at_once]], axis=0)
         dy = jnp.concatenate([ref[...] for ref in dy_refs[d : d + at_once]], axis=0)
         both = lax.dot_general(
-            panel[0:2].reshape(2 * units, width), x, CONTRACT_LAST, preferred_element_type=F32
+            jnp.concatenate([panel[0][...], panel[1][...]], axis=0), x, CONTRACT_LAST, preferred_element_type=F32
         )
         gate, up = both[:units], both[units:]
-        d_hidden = lax.dot_general(panel[2], dy, CONTRACT_LAST, preferred_element_type=F32)
+        d_hidden = lax.dot_general(panel[2][...], dy, CONTRACT_LAST, preferred_element_type=F32)
         sources = [ring_source(size, ahead) for ahead in offsets[d : d + at_once]]
         scale = jnp.concatenate(
             [
@@ -260,14 +288,16 @@
     parts = len(x_parts)
     part = x_parts[0].shape[0]
     return pl.pallas_call(
-        lambda *refs: acts_kernel(turn, slots, stride, routes.shape[0], offsets, *refs),
-        out_shape=jax.ShapeDtypeStruct((3 * panel.shape[1], parts * part), BF16),
-        in_specs=[whole_in_vmem()] * (2 * parts + 3) + [untouched()] * len(after),
+        lambda *refs: acts_kernel(
+            turn, slots, stride, routes.shape[0], offsets, len(panel), *refs
+        ),
+        out_shape=jax.ShapeDtypeStruct((3 * panel[0].shape[-2], parts * part), BF16),
+        in_specs=[whole_in_vmem()] * (2 * parts + len(panel) + 2) + [untouched()] * len(after),
         out_specs=whole_in_vmem(),
         compiler_params=pltpu.CompilerParams(vmem_limit_bytes=VMEM_LIMIT),
-        cost_estimate=work_cost(6 * parts * part * panel.shape[1] * panel.shape[2]),
+        cost_estimate=NO_COST,
         name=f"acts_{turn}_{name}",
-    )(*x_parts, *dy_parts, panel, routes, weight, *after)
+    )(*x_parts, *dy_parts, *panel, routes, weight, *after)
 
 
 def grads_kernel(parts, groups, kinds, *refs):
@@ -303,7 +333,7 @@
 
 
 def chunk_kernel(wanted, slots, part, acts, panels, outs):
-    units, width = panels[0].shape[1:]
+    units, width = panels[0][0].shape
     columns = tile_of(width, 512)
 
     @pl.loop(0, width // columns)
@@ -312,7 +342,7 @@
         kinds = {"mixed": (2, 3), "grad": (0, 2)}
         sides = {
             kind: jnp.concatenate(
-                [panel[which, :, here] for panel in panels for which in range(*span)], axis=0
+                [panel[which][:, here] for panel in panels for which in range(*span)], axis=0
             )
             for kind, span in kinds.items()
         }
@@ -327,7 +357,8 @@
 
 def chunk_pass(wanted, acts, panels, groups, part, cost, after=()):
     slots = len(panels)
-    width = panels[0].shape[2]
+    width = panels[0][0].shape[-1]
+    pieces = [len(panel) for panel in panels]
     named = [
         (kind, g, group.index(d)) for kind, d in wanted for g, group in enumerate(groups) if d in group
     ]
@@ -335,17 +366,19 @@
     def kernel(*refs):
         act_refs = [refs[s * len(groups) : (s + 1) * len(groups)] for s in range(slots)]
         rest = refs[slots * len(groups) :]
-        chunk_kernel(named, slots, part, act_refs, rest[:slots], rest[slots + len(after) :])
+        starts = [sum(pieces[:s]) for s in range(slots)]
+        panel_refs = [by_kind(rest[a : a + n]) for a, n in zip(starts, pieces)]
+        chunk_kernel(named, slots, part, act_refs, panel_refs, rest[sum(pieces) + len(after) :])
 
     return pl.pallas_call(
         kernel,
         out_shape=tuple(jax.ShapeDtypeStruct((part, width), BF16) for _ in wanted),
-        in_specs=[whole_in_vmem()] * (slots * len(groups) + slots) + [untouched()] * len(after),
+        in_specs=[whole_in_vmem()] * (slots * len(groups) + sum(pieces)) + [untouched()] * len(after),
         out_specs=tuple(whole_in_vmem() for _ in wanted),
         compiler_params=pltpu.CompilerParams(vmem_limit_bytes=VMEM_LIMIT),
         cost_estimate=cost,
         name=f"chunks_{len(wanted)}",
-    )(*[act for slot_acts in acts for act in slot_acts], *panels, *after)
+    )(*[act for slot_acts in acts for act in slot_acts], *[piece for panel in panels for piece in panel], *after)
 
 
 def final_rows_kernel(*refs):
@@ -420,7 +453,7 @@
         )
 
     def make_grads(turn):
-        shape = read[turn].shape
+        shape = panels.shape[1:]
         grads[turn] = line.step(
             lambda after: grads_pass(
                 turn,
@@ -435,47 +468,48 @@
             back[turn] = [exchange(grad, turn, slots) if turn else grad for grad in grads[turn]]
 
     read = [None] * slots
-    first_turns = [late] + middle
-    picked = line.step(lambda after: pick_pass(first_turns, stride, fetch_pick, panels, after))
-    for turn, panel in zip(first_turns, picked):
-        read[turn] = exchange(panel, turn, slots)
-    read[last], read[0] = line.step(lambda after: pick_pass([last, 0], stride, fetch_pick, panels, after))
+    picked = line.step(lambda after: pick_pass([late], stride, fetch_pick, panels, False, after))
+    read[late] = [exchange(picked[0], late, slots)]
+    for turn in middle:
+        picked = line.step(lambda after: pick_pass([turn], stride, fetch_pick, panels, True, after))
+        read[turn] = [exchange(piece, turn, slots) for piece in picked]
+    picked = line.step(lambda after: pick_pass([last, 0], stride, fetch_pick, panels, False, after))
+    read[last], read[0] = [[piece] for piece in picked]
 
     chains = [(x_parts, 1, up_most), (dy_parts, -1, up_most), (x_parts, -1, down_most), (dy_parts, 1, down_most)]
     moving = [ring_step(parts[0], order, way) for parts, way, _ in chains]
     for turn in middle:
-        read[turn] = line.arrive(read[turn])
+        read[turn] = [line.arrive(piece) for piece in read[turn]]
     for hop in range(1, up_most + 1):
         for i, (parts, way, hops) in enumerate(chains):
             if hop > hops:
                 continue
             if hop == max(1, up_most // 2) and i == 2:
-                read[late] = line.arrive(read[late])
-                read[last] = exchange(line.arrive(read[last]), last, slots)
+                read[late] = [line.arrive(read[late][0])]
+                read[last] = [exchange(line.arrive(read[last][0]), last, slots)]
             arrived = line.arrive(moving[i])
             parts[-way * hop % size] = arrived
             if hop < hops:
                 moving[i] = ring_step(arrived, order, way)
             if hop == max(1, up_most // 2) and i == len(chains) - 1:
-                for turn in middle + [0]:
+                for turn in middle + [0, late]:
                     make_acts(turn, 0)
 
+    make_acts(late, 1)
+    make_grads(late)
     for turn in middle:
         make_acts(turn, 1)
         make_grads(turn)
-    make_acts(late, 0)
-    make_acts(late, 1)
-    make_grads(late)
     make_acts(0, 1)
+    read[last] = [line.arrive(read[last][0])]
+    make_acts(last, 1)
+    make_acts(last, 0)
     for turn in middle:
         back[turn] = [line.arrive(grad) for grad in back[turn]]
-    read[last] = line.arrive(read[last])
-    make_acts(last, 1)
-    make_acts(last, 0)
 
     kinds = ("mixed", "grad")
     early = [("mixed", up_most), ("grad", size - up_most), ("mixed", size - down_most), ("grad", down_most)]
-    early_cost = work_cost(6 * len(early) * slots * part * read[0].size // 6)
+    early_cost = work_cost(6 * len(early) * slots * part * read[0][0].size // 6)
     later = [(kind, d) for kind in kinds for d in range(size) if (kind, d) not in early]
     chunks = dict(zip(early, line.step(lambda after: chunk_pass(early, acts, read, groups, part, early_cost, after))))
     chains = [("mixed", 1, up_most), ("grad", -1, up_most), ("mixed", -1, down_most), ("grad", 1, down_most)]

time: 202 us -> 202 us (level)
  waiting for transfers between devices: 114 us -> 108 us
  starting transfers between devices: 35.6 us -> 38.5 us
  Pallas kernels: 50.4 us -> 52.9 us
    ppermute x8 -> x10, waiting for transfers between devices: 14.4 us -> 8.73 us  [exchange(): lax.ppermute(block, 'node', [(owner_of(node, turn, slots, stride), node)...]
    ppermute x28, starting transfers between devices: 29.3 us -> 33.3 us  [ring_step(): lax.ppermute(block, 'local', [(order[i], order[(i + distance) % size]) fo...]
    pallas_call x2 -> x3, Pallas kernels: 5.72 us -> 7.22 us  [pick_pass(): pl.pallas_call(lambda *refs: pick_kernel(turns, stride, apart, *refs), ou...]
    ppermute x8 -> x10, starting transfers between devices: 6.32 us -> 5.21 us  [exchange(): lax.ppermute(block, 'node', [(owner_of(node, turn, slots, stride), node)...]
  transfers between devices with their start and end apart: 36 -> 38, of which waited for: 18 -> 22; matrix products, arithmetic and copies ran while one was open for 0% -> 0% of each run, Pallas kernels for 22% -> 24%
where the time goes in v6:
time: 202 us; the launch traced here: 201 us
  waiting for transfers between devices  108 us (53%)
  Pallas kernels  52.9 us (26%)
  starting transfers between devices  38.5 us (19%)
    ppermute x28, waiting for transfers between devices, ring_step(): lax.ppermute(block, 'local', [(order[i], order[(i + distance) % size]) fo...  99.5 us
    ppermute x28, starting transfers between devices, ring_step(): lax.ppermute(block, 'local', [(order[i], order[(i + distance) % size]) fo...  33.3 us
    pallas_call x8, Pallas kernels, acts_pass(): pl.pallas_call(lambda *refs: acts_kernel(turn, slots, stride, routes.shap...  12.6 us
    pallas_call x2, Pallas kernels, chunk_pass(): pl.pallas_call(kernel, out_shape=tuple((jax.ShapeDtypeStruct((part, width...  12.1 us
    pallas_call x4, Pallas kernels, grads_pass(): pl.pallas_call(lambda *refs: grads_kernel(parts, len(acts), len(shapes),...  9.6 us
    ppermute x10, waiting for transfers between devices, exchange(): lax.ppermute(block, 'node', [(owner_of(node, turn, slots, stride), node)...  8.73 us
    pallas_call x3, Pallas kernels, pick_pass(): pl.pallas_call(lambda *refs: pick_kernel(turns, stride, apart, *refs), ou...  7.22 us
    ppermute x10, starting transfers between devices, exchange(): lax.ppermute(block, 'node', [(owner_of(node, turn, slots, stride), node)...  5.21 us
  transfers between devices with their start and end apart: 38, of which 22 were waited for; matrix products, arithmetic and copies ran while one was open for 0% of the time, Pallas kernels for 24%

profile of v6, /device:TPU:0, one launch (start us, length us, event | category | flops | bytes accessed | tf_op | source)
XLA Modules:
  0.0 201.5 jit_solution(15429444191377738604)
XLA Ops:
  0.6 0.7 copy-done.4
  1.3 2.2 %pick.3.refs_2_ = bf16[3,176,2048]{2,1,0:T(8,128)(2,1)S(1)} custom-call(s32[4,4]{1,0:T(4,128)S(1)} %copy-done.4, bf16[2,3,176,2048]{3,2,1,0:T(8,128)(2,1)} %refs_1_.5), custom_call_target="tpu_custom_call" | custom-call | flops 1 | bytes 1 | tf_op jit(solution)/shard_map/pick/pallas_call | solution.py:125
  3.5 3.0 %collective-permute-start.10 = (bf16[3,176,2048]{2,1,0:T(8,128)(2,1)S(1)}, bf16[3,176,2048]{2,1,0:T(8,128)(2,1)S(1)}, u32[]{:S(2)}, u32[]{:S(2)}) collective-permute-start(bf16[3,176,2048]{2,1,0:T(8,128)(2,1)S(1)} %pick.3.refs_2_), channel_id=1, source_target_pairs={{16,0},{24,8},{0,16},{8,24},{17,1},{25,9},{1,17},{9,25},{18,2},{26... | collective-permute-start | bytes 6488072 | tf_op jit(solution)/shard_map/ppermute | solution.py:89
  6.5 2.2 %pick.4 = (bf16[176,2048]{1,0:T(8,128)(2,1)S(1)}, bf16[176,2048]{1,0:T(8,128)(2,1)S(1)}, bf16[176,2048]{1,0:T(8,128)(2,1)S(1)}) custom-call(s32[4,4]{1,0:T(4,128)S(1)} %copy-done.5, bf16[2,3,176,2048]{3,2,1,0:T(8,128)(2,1)} %refs_1_.5, bf16[3,176,2048]{2,1,0:T(8,128)(2,1)S(1)} %pick.3.refs_2_), custom_call_target="tpu_custom_call" | custom-call | flops 1 | bytes 1 | tf_op jit(solution)/shard_map/pick/pallas_call | solution.py:125
  9.4 1.6 collective-permute-start.2
  11.0 1.5 collective-permute-start.1
  12.5 1.6 collective-permute-start
  14.1 0.6 collective-permute-start.7
  14.6 2.9 %pick.5 = (bf16[3,176,2048]{2,1,0:T(8,128)(2,1)S(1)}, bf16[3,176,2048]{2,1,0:T(8,128)(2,1)S(1)}) custom-call(s32[4,4]{1,0:T(4,128)S(1)} %copy-done.5, bf16[2,3,176,2048]{3,2,1,0:T(8,128)(2,1)} %refs_1_.5, bf16[176,2048]{1,0:T(8,128)(2,1)S(1)} %get-tuple-element.34.refs_2_), custom_call_target="tpu_custom_call" | custom-call | flops 1 | bytes 1 | tf_op jit(solution)/shard_map/pick/pallas_call | solution.py:125
  17.5 6.6 %collective-permute-done.2.refs_0_ = bf16[128,2048]{1,0:T(8,128)(2,1)S(1)} collective-permute-done((bf16[128,2048]{1,0:T(8,128)(2,1)S(1)}, bf16[128,2048]{1,0:T(8,128)(2,1)S(1)}, u32[]{:S(2)}, u32[]{:S(2)}) %collective-permute-start.2) | collective-permute-done | bytes 524320 | tf_op jit(solution)/shard_map/ppermute | solution.py:229
  24.1 1.6 collective-permute-start.6
  25.8 1.5 collective-permute-start.11
  27.2 9.7 %collective-permute-done.refs_0_ = bf16[128,2048]{1,0:T(8,128)(2,1)S(1)} collective-permute-done((bf16[128,2048]{1,0:T(8,128)(2,1)S(1)}, bf16[128,2048]{1,0:T(8,128)(2,1)S(1)}, u32[]{:S(2)}, u32[]{:S(2)}) %collective-permute-start) | collective-permute-done | bytes 524320 | tf_op jit(solution)/shard_map/ppermute | solution.py:229
  37.0 1.5 collective-permute-start.9
  38.5 0.5 collective-permute-start.8
  39.0 7.6 %collective-permute-done.6.refs_0_ = bf16[128,2048]{1,0:T(8,128)(2,1)S(1)} collective-permute-done((bf16[128,2048]{1,0:T(8,128)(2,1)S(1)}, bf16[128,2048]{1,0:T(8,128)(2,1)S(1)}, u32[]{:S(2)}, u32[]{:S(2)}) %collective-permute-start.6) | collective-permute-done | bytes 524320 | tf_op jit(solution)/shard_map/ppermute | solution.py:229
  46.6 1.6 collective-permute-start.14
  48.2 1.5 collective-permute-start.13
  49.7 3.9 %collective-permute-done.10.refs_0_ = bf16[3,176,2048]{2,1,0:T(8,128)(2,1)S(1)} collective-permute-done((bf16[3,176,2048]{2,1,0:T(8,128)(2,1)S(1)}, bf16[3,176,2048]{2,1,0:T(8,128)(2,1)S(1)}, u32[]{:S(2)}, u32[]{:S(2)}) %collective-permute-start.10) | collective-permute-done | bytes 2162720 | tf_op jit(solution)/shard_map/ppermute | solution.py:89
  53.9 5.6 %collective-permute-done.9.refs_0_ = bf16[128,2048]{1,0:T(8,128)(2,1)S(1)} collective-permute-done((bf16[128,2048]{1,0:T(8,128)(2,1)S(1)}, bf16[128,2048]{1,0:T(8,128)(2,1)S(1)}, u32[]{:S(2)}, u32[]{:S(2)}) %collective-permute-start.9) | collective-permute-done | bytes 524320 | tf_op jit(solution)/shard_map/ppermute | solution.py:229
  59.5 1.6 acts_1_n.1.refs_11_.refs_16_.refs_2_
  61.1 1.6 collective-permute-start.16
  62.7 1.6 acts_0_n.1.refs_11_.refs_0_.refs_16_
  64.3 0.5 collective-permute-start.12
  64.8 1.6 acts_2_n.1.refs_1_.refs_16_.refs_4_
  66.4 2.7 %collective-permute-done.14.refs_0_ = bf16[128,2048]{1,0:T(8,128)(2,1)S(1)} collective-permute-done((bf16[128,2048]{1,0:T(8,128)(2,1)S(1)}, bf16[128,2048]{1,0:T(8,128)(2,1)S(1)}, u32[]{:S(2)}, u32[]{:S(2)}) %collective-permute-start.14) | collective-permute-done | bytes 524320 | tf_op jit(solution)/shard_map/ppermute | solution.py:229
  69.0 1.6 collective-permute-start.15
  70.7 1.5 collective-permute-start.17
  72.2 9.7 %collective-permute-done.12.refs_0_ = bf16[128,2048]{1,0:T(8,128)(2,1)S(1)} collective-permute-done((bf16[128,2048]{1,0:T(8,128)(2,1)S(1)}, bf16[128,2048]{1,0:T(8,128)(2,1)S(1)}, u32[]{:S(2)}, u32[]{:S(2)}) %collective-permute-start.12) | collective-permute-done | bytes 524320 | tf_op jit(solution)/shard_map/ppermute | solution.py:229
  81.9 9.1 %collective-permute-done.15.refs_0_ = bf16[128,2048]{1,0:T(8,128)(2,1)S(1)} collective-permute-done((bf16[128,2048]{1,0:T(8,128)(2,1)S(1)}, bf16[128,2048]{1,0:T(8,128)(2,1)S(1)}, u32[]{:S(2)}, u32[]{:S(2)}) %collective-permute-start.15) | collective-permute-done | bytes 524320 | tf_op jit(solution)/shard_map/ppermute | solution.py:229
  91.1 1.3 collective-permute-done.17.refs_0_
  92.4 1.6 acts_2_f.1.refs_17_.refs_18_.refs_5_
  94.0 2.4 %grads_2.1.refs_13_ = bf16[3,176,2048]{2,1,0:T(8,128)(2,1)S(1)} custom-call(bf16[128,2048]{1,0:T(8,128)(2,1)S(1)} %copy-done, bf16[128,2048]{1,0:T(8,128)(2,1)S(1)} %gate.31.refs_1_, bf16[128,2048]{1,0:T(8,128)(2,1)S(1)} %gate.33.refs_1_.refs_2_, bf16[128,2048]{1,0:T(8,128)(2,1)S(1)} %gate.29.refs_1_.refs_3_, ...), custom_call_target="tpu_custom_call" | custom-call | flops 2214592512 | bytes 1 | tf_op jit(solution)/shard_map/grads_2/pallas_call | solution.py:324
  96.4 1.6 acts_1_f.1.refs_17_.refs_18_.refs_3_
  97.9 0.6 collective-permute-start.30
  98.5 2.4 %grads_1.1 = (bf16[176,2048]{1,0:T(8,128)(2,1)S(1)}, bf16[176,2048]{1,0:T(8,128)(2,1)S(1)}, bf16[176,2048]{1,0:T(8,128)(2,1)S(1)}) custom-call(bf16[128,2048]{1,0:T(8,128)(2,1)S(1)} %copy-done, bf16[128,2048]{1,0:T(8,128)(2,1)S(1)} %gate.31.refs_1_, bf16[128,2048]{1,0:T(8,128)(2,1)S(1)} %gate.33.refs_1_.refs_2_, bf16[128,2048]{1,0:T(8,128)(2,1)S(1)} %gate.29.refs_1_.refs_3_, ...), custom_call_target="tpu_custom_call" | custom-call | flops 2214592512 | bytes 1 | tf_op jit(solution)/shard_map/grads_1/pallas_call | solution.py:324
  101.6 1.6 acts_0_f.1.refs_1_.refs_17_
  103.2 1.6 acts_3_f.1.refs_11_.refs_7_.refs_17_
  104.8 1.6 acts_3_n.1.refs_1_.refs_6_.refs_16_
  106.4 4.0 %chunks_4.1 = (bf16[128,2048]{1,0:T(8,128)(2,1)S(1)}, bf16[128,2048]{1,0:T(8,128)(2,1)}, bf16[128,2048]{1,0:T(8,128)(2,1)}, bf16[128,2048]{1,0:T(8,128)(2,1)S(1)}) custom-call(bf16[528,512]{1,0:T(8,128)(2,1)S(1)} %acts_0_n.1.refs_11_.refs_0_.refs_16_, bf16[528,512]{1,0:T(8,128)(2,1)S(1)} %acts_0_f.1.refs_1_.refs_17_, ...), custom_call_target="tpu_custom_call" | custom-call | flops 2214592512 | bytes 1 | tf_op jit(solution)/shard_map/chunks_4/pallas_call | solution.py:373
  110.4 1.6 collective-permute-start.22
  112.4 8.1 %chunks_12.1 = (bf16[128,2048]{1,0:T(8,128)(2,1)S(1)}, bf16[128,2048]{1,0:T(8,128)(2,1)S(1)}, bf16[128,2048]{1,0:T(8,128)(2,1)S(1)}, bf16[128,2048]{1,0:T(8,128)...) custom-call(bf16[528,512]{1,0:T(8,128)(2,1)S(1)} %acts_0_n.1.refs_11, ...), custom_call_target="tpu_custom_call" | custom-call | flops 1 | bytes 1 | tf_op jit(solution)/shard_map/chunks_12/pallas_call | solution.py:373
  120.5 1.6 collective-permute-start.24
  122.6 2.4 %grads_3.1.refs_18_.refs_0_ = bf16[3,176,2048]{2,1,0:T(8,128)(2,1)S(1)} custom-call(bf16[128,2048]{1,0:T(8,128)(2,1)S(1)} %copy-done, bf16[128,2048]{1,0:T(8,128)(2,1)S(1)} %gate.31.refs_1_, bf16[128,2048]{1,0:T(8,128)(2,1)S(1)} %gate.33.refs_1_.refs_2_, bf16[128,2048]{1,0:T(8,128)(2,1)S(1)} %gate.29.refs_1_.refs_3_, ...), custom_call_target="tpu_custom_call" | custom-call | flops 2214592512 | bytes 1 | tf_op jit(solution)/shard_map/grads_3/pallas_call | solution.py:324
  125.0 2.4 %grads_0.1.refs_2_.refs_1_ = bf16[3,176,2048]{2,1,0:T(8,128)(2,1)S(1)} custom-call(bf16[128,2048]{1,0:T(8,128)(2,1)S(1)} %copy-done, bf16[128,2048]{1,0:T(8,128)(2,1)S(1)} %gate.31.refs_1_, bf16[128,2048]{1,0:T(8,128)(2,1)S(1)} %gate.33.refs_1_.refs_2_, bf16[128,2048]{1,0:T(8,128)(2,1)S(1)} %gate.29.refs_1_.refs_3_, ...), custom_call_target="tpu_custom_call" | custom-call | flops 2214592512 | bytes 1 | tf_op jit(solution)/shard_map/grads_0/pallas_call | solution.py:324
  127.6 1.6 collective-permute-start.23
  129.2 1.2 add_rows.13.refs_2_
  130.9 7.3 %collective-permute-done.25.refs_0_ = bf16[128,2048]{1,0:T(8,128)(2,1)S(1)} collective-permute-done((bf16[128,2048]{1,0:T(8,128)(2,1)}, bf16[128,2048]{1,0:T(8,128)(2,1)S(1)}, u32[]{:S(2)}, u32[]{:S(2)}) %collective-permute-start.25) | collective-permute-done | bytes 524320 | tf_op jit(solution)/shard_map/ppermute | solution.py:229
  138.3 0.5 collective-permute-start.29
  138.9 1.6 collective-permute-start.28
  140.5 7.0 %collective-permute-done.23.refs_0_ = bf16[128,2048]{1,0:T(8,128)(2,1)S(1)} collective-permute-done((bf16[128,2048]{1,0:T(8,128)(2,1)S(1)}, bf16[128,2048]{1,0:T(8,128)(2,1)S(1)}, u32[]{:S(2)}, u32[]{:S(2)}) %collective-permute-start.23) | collective-permute-done | bytes 524320 | tf_op jit(solution)/shard_map/ppermute | solution.py:229
  147.7 1.6 collective-permute-start.27
  150.0 10.6 %collective-permute-done.29.refs_0_ = bf16[128,2048]{1,0:T(8,128)(2,1)S(1)} collective-permute-done((bf16[128,2048]{1,0:T(8,128)(2,1)S(1)}, bf16[128,2048]{1,0:T(8,128)(2,1)S(1)}, u32[]{:S(2)}, u32[]{:S(2)}) %collective-permute-start.29) | collective-permute-done | bytes 524320 | tf_op jit(solution)/shard_map/ppermute | solution.py:229
  161.4 1.6 collective-permute-start.35
  163.0 7.0 %collective-permute-done.27.refs_0_ = bf16[128,2048]{1,0:T(8,128)(2,1)S(1)} collective-permute-done((bf16[128,2048]{1,0:T(8,128)(2,1)S(1)}, bf16[128,2048]{1,0:T(8,128)(2,1)S(1)}, u32[]{:S(2)}, u32[]{:S(2)}) %collective-permute-start.27) | collective-permute-done | bytes 524320 | tf_op jit(solution)/shard_map/ppermute | solution.py:229
  170.2 1.6 collective-permute-start.32
  172.5 10.6 %collective-permute-done.33.refs_0_ = bf16[128,2048]{1,0:T(8,128)(2,1)S(1)} collective-permute-done((bf16[128,2048]{1,0:T(8,128)(2,1)S(1)}, bf16[128,2048]{1,0:T(8,128)(2,1)S(1)}, u32[]{:S(2)}, u32[]{:S(2)}) %collective-permute-start.33) | collective-permute-done | bytes 524320 | tf_op jit(solution)/shard_map/ppermute | solution.py:229
  183.3 5.1 %total.1 = (bf16[2,3,176,2048]{3,2,1,0:T(8,128)(2,1)}, bf16[3,176,2048]{2,1,0:T(8,128)(2,1)S(1)}, f32[8,128]{1,0:T(8,128)S(1)}) custom-call(s32[4,4]{1,0:T(4,128)S(1)} %copy-done.5, bf16[3,176,2048]{2,1,0:T(8,128)(2,1)S(1)} %grads_0.1.refs_2_.refs_1_, bf16[176,2048]{1,0:T(8,128)(2,1)S(1)} %gate.46.refs_1_.refs_2_, ...), custom_call_target="tpu_custom_call" | custom-call | flops 1 | bytes 1 | tf_op jit(solution)/shard_map/total/pallas_call | solution.py:180
  188.4 3.6 %collective-permute-done.32.refs_0_ = bf16[128,2048]{1,0:T(8,128)(2,1)S(1)} collective-permute-done((bf16[128,2048]{1,0:T(8,128)(2,1)S(1)}, bf16[128,2048]{1,0:T(8,128)(2,1)S(1)}, u32[]{:S(2)}, u32[]{:S(2)}) %collective-permute-start.32) | collective-permute-done | bytes 524320 | tf_op jit(solution)/shard_map/ppermute | solution.py:229
  192.0 0.9 final_rows.2
  193.0 0.6 collective-permute-done.36.refs_0_
  193.6 0.9 final_rows.3
  194.5 4.8 %collective-permute-done.37.refs_0_ = bf16[3,176,2048]{2,1,0:T(8,128)(2,1)S(1)} collective-permute-done((bf16[3,176,2048]{2,1,0:T(8,128)(2,1)S(1)}, bf16[3,176,2048]{2,1,0:T(8,128)(2,1)S(1)}, u32[]{:S(2)}, u32[]{:S(2)}) %collective-permute-start.37) | collective-permute-done | bytes 2162720 | tf_op jit(solution)/shard_map/ppermute | solution.py:89
  199.3 2.0 %add.1 = bf16[2,3,176,2048]{3,2,1,0:T(8,128)(2,1)} custom-call(s32[4,4]{1,0:T(4,128)S(1)} %copy-done.5, bf16[2,3,176,2048]{3,2,1,0:T(8,128)(2,1)} %get-tuple-element.62.refs_1_, bf16[3,176,2048]{2,1,0:T(8,128)(2,1)S(1)} %get-tuple-element.63.refs_2_, bf16[3,176,2048]{2,1,0:T(8,128)(2,1)S(1)} %gate.51.refs_3_), custom_call_target="tpu_custom_call", output_to_operand_aliasing={{}: (1, {})} | custom-call | flops 1 | bytes 1 | tf_op jit(solution)/shard_map/add/pallas_call | solution.py:214
  (83 shorter events, 6.3 us)
Async XLA Ops:
  0.6 0.7 copy-start.4
  1.3 5.2 %copy-start.5 = (s32[4,4]{1,0:T(4,128)S(1)}, s32[4,4]{1,0:T(4,128)}, u32[]{:S(2)}) copy-start(s32[4,4]{1,0:T(4,128)} %refs_0_.25) | copy-start | bytes 196
  3.5 5.9 %copy-start = (bf16[128,2048]{1,0:T(8,128)(2,1)S(1)}, bf16[128,2048]{1,0:T(8,128)(2,1)}, u32[]{:S(2)}) copy-start(bf16[128,2048]{1,0:T(8,128)(2,1)} %refs_0_.23) | copy-start | bytes 1572868
  3.5 7.5 %copy-start.1 = (bf16[128,2048]{1,0:T(8,128)(2,1)S(1)}, bf16[128,2048]{1,0:T(8,128)(2,1)}, u32[]{:S(2)}) copy-start(bf16[128,2048]{1,0:T(8,128)(2,1)} %refs_8_.7) | copy-start | bytes 1572868
  3.5 50.1 %collective-permute-start.10 = (bf16[3,176,2048]{2,1,0:T(8,128)(2,1)S(1)}, bf16[3,176,2048]{2,1,0:T(8,128)(2,1)S(1)}, u32[]{:S(2)}, u32[]{:S(2)}) collective-permute-start(bf16[3,176,2048]{2,1,0:T(8,128)(2,1)S(1)} %pick.3.refs_2_), channel_id=1, source_target_pairs={{16,0},{24,8},{0,16},{8,24},{17,1},{25,9},{1,17},{9,25},{18,2},{26... | collective-permute-start | bytes 6488072 | tf_op jit(solution)/shard_map/ppermute | solution.py:89
  8.7 2.3 %collective-permute-start.4 = (bf16[176,2048]{1,0:T(8,128)(2,1)S(1)}, bf16[176,2048]{1,0:T(8,128)(2,1)S(1)}, u32[]{:S(2)}, u32[]{:S(2)}) collective-permute-start(bf16[176,2048]{1,0:T(8,128)(2,1)S(1)} %get-tuple-element.35), channel_id=1, source_target_pairs={{8,0},{0,8},{24,16},{16,24},{9,1},{1,9},{25,17},{17,25},{10,2},{2,... | collective-permute-start | bytes 2162696 | tf_op jit(solution)/shard_map/ppermute | solution.py:89
  8.8 3.7 %collective-permute-start.5 = (bf16[176,2048]{1,0:T(8,128)(2,1)S(1)}, bf16[176,2048]{1,0:T(8,128)(2,1)S(1)}, u32[]{:S(2)}, u32[]{:S(2)}) collective-permute-start(bf16[176,2048]{1,0:T(8,128)(2,1)S(1)} %get-tuple-element.36), channel_id=1, source_target_pairs={{8,0},{0,8},{24,16},{16,24},{9,1},{1,9},{25,17},{17,25},{10,2},{2,... | collective-permute-start | bytes 2162696 | tf_op jit(solution)/shard_map/ppermute | solution.py:89
  9.3 4.8 %collective-permute-start.3 = (bf16[176,2048]{1,0:T(8,128)(2,1)S(1)}, bf16[176,2048]{1,0:T(8,128)(2,1)S(1)}, u32[]{:S(2)}, u32[]{:S(2)}) collective-permute-start(bf16[176,2048]{1,0:T(8,128)(2,1)S(1)} %get-tuple-element.34.refs_2_), channel_id=1, source_target_pairs={{8,0},{0,8},{24,16},{16,24},{9,1},{1,9},{25,17},{17,25},{10,2},{2,... | collective-permute-start | bytes 2162696 | tf_op jit(solution)/shard_map/ppermute | solution.py:89
  9.4 14.7 %collective-permute-start.2 = (bf16[128,2048]{1,0:T(8,128)(2,1)S(1)}, bf16[128,2048]{1,0:T(8,128)(2,1)S(1)}, u32[]{:S(2)}, u32[]{:S(2)}) collective-permute-start(bf16[128,2048]{1,0:T(8,128)(2,1)S(1)} %copy-done), channel_id=1, source_target_pairs={{0,2},{2,4},{4,6},{6,7},{7,5},{5,3},{3,1},{1,0},{8,10},{10,12},{12... | collective-permute-start | bytes 1572872 | tf_op jit(solution)/shard_map/ppermute | solution.py:229
  11.0 14.8 %collective-permute-start.1 = (bf16[128,2048]{1,0:T(8,128)(2,1)S(1)}, bf16[128,2048]{1,0:T(8,128)(2,1)S(1)}, u32[]{:S(2)}, u32[]{:S(2)}) collective-permute-start(bf16[128,2048]{1,0:T(8,128)(2,1)S(1)} %copy-done.1), channel_id=1, source_target_pairs={{0,1},{2,0},{4,2},{6,4},{7,6},{5,7},{3,5},{1,3},{8,9},{10,8},{12,1... | collective-permute-start | bytes 1572872 | tf_op jit(solution)/shard_map/ppermute | solution.py:229
  12.5 24.5 %collective-permute-start = (bf16[128,2048]{1,0:T(8,128)(2,1)S(1)}, bf16[128,2048]{1,0:T(8,128)(2,1)S(1)}, u32[]{:S(2)}, u32[]{:S(2)}) collective-permute-start(bf16[128,2048]{1,0:T(8,128)(2,1)S(1)} %copy-done), channel_id=1, source_target_pairs={{0,1},{2,0},{4,2},{6,4},{7,6},{5,7},{3,5},{1,3},{8,9},{10,8},{12,1... | collective-permute-start | bytes 1572872 | tf_op jit(solution)/shard_map/ppermute | solution.py:229
  14.1 24.4 %collective-permute-start.7 = (bf16[128,2048]{1,0:T(8,128)(2,1)S(1)}, bf16[128,2048]{1,0:T(8,128)(2,1)S(1)}, u32[]{:S(2)}, u32[]{:S(2)}) collective-permute-start(bf16[128,2048]{1,0:T(8,128)(2,1)S(1)} %copy-done.1), channel_id=1, source_target_pairs={{0,2},{2,4},{4,6},{6,7},{7,5},{5,3},{3,1},{1,0},{8,10},{10,12},{12... | collective-permute-start | bytes 1572872 | tf_op jit(solution)/shard_map/ppermute | solution.py:229
  24.1 22.5 %collective-permute-start.6 = (bf16[128,2048]{1,0:T(8,128)(2,1)S(1)}, bf16[128,2048]{1,0:T(8,128)(2,1)S(1)}, u32[]{:S(2)}, u32[]{:S(2)}) collective-permute-start(bf16[128,2048]{1,0:T(8,128)(2,1)S(1)} %gate.29.refs_1_.refs_3_), channel_id=1, source_target_pairs={{0,2},{2,4},{4,6},{6,7},{7,5},{5,3},{3,1},{1,0},{8,10},{10,12},{12... | collective-permute-start | bytes 1572872 | tf_op jit(solution)/shard_map/ppermute | solution.py:229
  25.8 22.5 %collective-permute-start.11 = (bf16[128,2048]{1,0:T(8,128)(2,1)S(1)}, bf16[128,2048]{1,0:T(8,128)(2,1)S(1)}, u32[]{:S(2)}, u32[]{:S(2)}) collective-permute-start(bf16[128,2048]{1,0:T(8,128)(2,1)S(1)} %gate.30.refs_1_.refs_5_.refs_9_), channel_id=1, source_target_pairs={{0,1},{2,0},{4,2},{6,4},{7,6},{5,7},{3,5},{1,3},{8,9},{10,8},{12,1... | collective-permute-start | bytes 1572872 | tf_op jit(solution)/shard_map/ppermute | solution.py:229
  37.0 22.5 %collective-permute-start.9 = (bf16[128,2048]{1,0:T(8,128)(2,1)S(1)}, bf16[128,2048]{1,0:T(8,128)(2,1)S(1)}, u32[]{:S(2)}, u32[]{:S(2)}) collective-permute-start(bf16[128,2048]{1,0:T(8,128)(2,1)S(1)} %gate.31.refs_1_), channel_id=1, source_target_pairs={{0,1},{2,0},{4,2},{6,4},{7,6},{5,7},{3,5},{1,3},{8,9},{10,8},{12,1... | collective-permute-start | bytes 1572872 | tf_op jit(solution)/shard_map/ppermute | solution.py:229
  38.5 21.0 %collective-permute-start.8 = (bf16[128,2048]{1,0:T(8,128)(2,1)S(1)}, bf16[128,2048]{1,0:T(8,128)(2,1)S(1)}, u32[]{:S(2)}, u32[]{:S(2)}) collective-permute-start(bf16[128,2048]{1,0:T(8,128)(2,1)S(1)} %gate.32.refs_1_.refs_7_.refs_11_), channel_id=1, source_target_pairs={{0,2},{2,4},{4,6},{6,7},{7,5},{5,3},{3,1},{1,0},{8,10},{10,12},{12... | collective-permute-start | bytes 1572872 | tf_op jit(solution)/shard_map/ppermute | solution.py:229
  46.6 22.5 %collective-permute-start.14 = (bf16[128,2048]{1,0:T(8,128)(2,1)S(1)}, bf16[128,2048]{1,0:T(8,128)(2,1)S(1)}, u32[]{:S(2)}, u32[]{:S(2)}) collective-permute-start(bf16[128,2048]{1,0:T(8,128)(2,1)S(1)} %gate.33.refs_1_.refs_2_), channel_id=1, source_target_pairs={{0,2},{2,4},{4,6},{6,7},{7,5},{5,3},{3,1},{1,0},{8,10},{10,12},{12... | collective-permute-start | bytes 1572872 | tf_op jit(solution)/shard_map/ppermute | solution.py:229
  48.2 22.5 %collective-permute-start.13 = (bf16[128,2048]{1,0:T(8,128)(2,1)S(1)}, bf16[128,2048]{1,0:T(8,128)(2,1)S(1)}, u32[]{:S(2)}, u32[]{:S(2)}) collective-permute-start(bf16[128,2048]{1,0:T(8,128)(2,1)S(1)} %gate.34.refs_1_.refs_4_.refs_12_), channel_id=1, source_target_pairs={{0,1},{2,0},{4,2},{6,4},{7,6},{5,7},{3,5},{1,3},{8,9},{10,8},{12,1... | collective-permute-start | bytes 1572872 | tf_op jit(solution)/shard_map/ppermute | solution.py:229
  53.6 5.9 %copy-start.2 = (s32[1024,1]{0,1:T(1,128)S(1)}, s32[1024,1]{0,1:T(1,128)}, u32[]{:S(2)}) copy-start(s32[1024,1]{0,1:T(1,128)} %param.8) | copy-start | bytes 12292
  53.6 5.9 %copy-start.3 = (f32[1024,1]{0,1:T(1,128)S(1)}, f32[1024,1]{0,1:T(1,128)}, u32[]{:S(2)}) copy-start(f32[1024,1]{0,1:T(1,128)} %param.9) | copy-start | bytes 12292
  53.6 49.6 %collective-permute-start.18 = (bf16[3,176,2048]{2,1,0:T(8,128)(2,1)S(1)}, bf16[3,176,2048]{2,1,0:T(8,128)(2,1)S(1)}, u32[]{:S(2)}, u32[]{:S(2)}) collective-permute-start(bf16[3,176,2048]{2,1,0:T(8,128)(2,1)S(1)} %gate.36.refs_1_), channel_id=1, source_target_pairs={{24,0},{16,8},{8,16},{0,24},{25,1},{17,9},{9,17},{1,25},{26,2},{18... | collective-permute-start | bytes 6488072 | tf_op jit(solution)/shard_map/ppermute | solution.py:89
  61.1 20.9 %collective-permute-start.16 = (bf16[128,2048]{1,0:T(8,128)(2,1)S(1)}, bf16[128,2048]{1,0:T(8,128)(2,1)S(1)}, u32[]{:S(2)}, u32[]{:S(2)}) collective-permute-start(bf16[128,2048]{1,0:T(8,128)(2,1)S(1)} %gate.38.refs_6_.refs_13_.refs_10_), channel_id=1, source_target_pairs={{0,2},{2,4},{4,6},{6,7},{7,5},{5,3},{3,1},{1,0},{8,10},{10,12},{12... | collective-permute-start | bytes 1572872 | tf_op jit(solution)/shard_map/ppermute | solution.py:229
  64.3 17.7 %collective-permute-start.12 = (bf16[128,2048]{1,0:T(8,128)(2,1)S(1)}, bf16[128,2048]{1,0:T(8,128)(2,1)S(1)}, u32[]{:S(2)}, u32[]{:S(2)}) collective-permute-start(bf16[128,2048]{1,0:T(8,128)(2,1)S(1)} %gate.37.refs_1_.refs_0_.refs_4_), channel_id=1, source_target_pairs={{0,1},{2,0},{4,2},{6,4},{7,6},{5,7},{3,5},{1,3},{8,9},{10,8},{12,1... | collective-permute-start | bytes 1572872 | tf_op jit(solution)/shard_map/ppermute | solution.py:229
  69.0 22.0 %collective-permute-start.15 = (bf16[128,2048]{1,0:T(8,128)(2,1)S(1)}, bf16[128,2048]{1,0:T(8,128)(2,1)S(1)}, u32[]{:S(2)}, u32[]{:S(2)}) collective-permute-start(bf16[128,2048]{1,0:T(8,128)(2,1)S(1)} %gate.39.refs_1_.refs_3_.refs_7_), channel_id=1, source_target_pairs={{0,2},{2,4},{4,6},{6,7},{7,5},{5,3},{3,1},{1,0},{8,10},{10,12},{12... | collective-permute-start | bytes 1572872 | tf_op jit(solution)/shard_map/ppermute | solution.py:229
  70.7 21.7 %collective-permute-start.17 = (bf16[128,2048]{1,0:T(8,128)(2,1)S(1)}, bf16[128,2048]{1,0:T(8,128)(2,1)S(1)}, u32[]{:S(2)}, u32[]{:S(2)}) collective-permute-start(bf16[128,2048]{1,0:T(8,128)(2,1)S(1)} %gate.40.refs_1_.refs_5_.refs_13_), channel_id=1, source_target_pairs={{0,1},{2,0},{4,2},{6,4},{7,6},{5,7},{3,5},{1,3},{8,9},{10,8},{12,1... | collective-permute-start | bytes 1572872 | tf_op jit(solution)/shard_map/ppermute | solution.py:229
  97.9 52.1 %collective-permute-start.30 = (bf16[3,176,2048]{2,1,0:T(8,128)(2,1)S(1)}, bf16[3,176,2048]{2,1,0:T(8,128)(2,1)S(1)}, u32[]{:S(2)}, u32[]{:S(2)}) collective-permute-start(bf16[3,176,2048]{2,1,0:T(8,128)(2,1)S(1)} %grads_2.1.refs_13_), channel_id=1, source_target_pairs={{16,0},{24,8},{0,16},{8,24},{17,1},{25,9},{1,17},{9,25},{18,2},{26... | collective-permute-start | bytes 6488072 | tf_op jit(solution)/shard_map/ppermute | solution.py:89
  100.9 5.4 %collective-permute-start.21 = (bf16[176,2048]{1,0:T(8,128)(2,1)S(1)}, bf16[176,2048]{1,0:T(8,128)(2,1)S(1)}, u32[]{:S(2)}, u32[]{:S(2)}) collective-permute-start(bf16[176,2048]{1,0:T(8,128)(2,1)S(1)} %get-tuple-element.41), channel_id=1, source_target_pairs={{8,0},{0,8},{24,16},{16,24},{9,1},{1,9},{25,17},{17,25},{10,2},{2,... | collective-permute-start | bytes 2162696 | tf_op jit(solution)/shard_map/ppermute | solution.py:89
  101.0 5.4 %collective-permute-start.20 = (bf16[176,2048]{1,0:T(8,128)(2,1)S(1)}, bf16[176,2048]{1,0:T(8,128)(2,1)S(1)}, u32[]{:S(2)}, u32[]{:S(2)}) collective-permute-start(bf16[176,2048]{1,0:T(8,128)(2,1)S(1)} %get-tuple-element.40), channel_id=1, source_target_pairs={{8,0},{0,8},{24,16},{16,24},{9,1},{1,9},{25,17},{17,25},{10,2},{2,... | collective-permute-start | bytes 2162696 | tf_op jit(solution)/shard_map/ppermute | solution.py:89
  101.5 4.9 %collective-permute-start.19 = (bf16[176,2048]{1,0:T(8,128)(2,1)S(1)}, bf16[176,2048]{1,0:T(8,128)(2,1)S(1)}, u32[]{:S(2)}, u32[]{:S(2)}) collective-permute-start(bf16[176,2048]{1,0:T(8,128)(2,1)S(1)} %get-tuple-element.39.refs_11_), channel_id=1, source_target_pairs={{8,0},{0,8},{24,16},{16,24},{9,1},{1,9},{25,17},{17,25},{10,2},{2,... | collective-permute-start | bytes 2162696 | tf_op jit(solution)/shard_map/ppermute | solution.py:89
  110.4 17.1 %collective-permute-start.22 = (bf16[128,2048]{1,0:T(8,128)(2,1)S(1)}, bf16[128,2048]{1,0:T(8,128)(2,1)S(1)}, u32[]{:S(2)}, u32[]{:S(2)}) collective-permute-start(bf16[128,2048]{1,0:T(8,128)(2,1)S(1)} %get-tuple-element.42), channel_id=1, source_target_pairs={{0,2},{2,4},{4,6},{6,7},{7,5},{5,3},{3,1},{1,0},{8,10},{10,12},{12... | collective-permute-start | bytes 1572872 | tf_op jit(solution)/shard_map/ppermute | solution.py:229
  111.9 17.3 %collective-permute-start.26 = (bf16[128,2048]{1,0:T(8,128)(2,1)}, bf16[128,2048]{1,0:T(8,128)(2,1)}, u32[]{:S(2)}, u32[]{:S(2)}) collective-permute-start(bf16[128,2048]{1,0:T(8,128)(2,1)} %get-tuple-element.50), channel_id=1, source_target_pairs={{0,1},{2,0},{4,2},{6,4},{7,6},{5,7},{3,5},{1,3},{8,9},{10,8},{12,1... | collective-permute-start | bytes 1572872 | tf_op jit(solution)/shard_map/ppermute | solution.py:229
  120.5 18.2 %collective-permute-start.24 = (bf16[128,2048]{1,0:T(8,128)(2,1)S(1)}, bf16[128,2048]{1,0:T(8,128)(2,1)S(1)}, u32[]{:S(2)}, u32[]{:S(2)}) collective-permute-start(bf16[128,2048]{1,0:T(8,128)(2,1)S(1)} %get-tuple-element.43.refs_14_), channel_id=1, source_target_pairs={{0,2},{2,4},{4,6},{6,7},{7,5},{5,3},{3,1},{1,0},{8,10},{10,12},{12... | collective-permute-start | bytes 1572872 | tf_op jit(solution)/shard_map/ppermute | solution.py:229
  122.2 16.0 %collective-permute-start.25 = (bf16[128,2048]{1,0:T(8,128)(2,1)}, bf16[128,2048]{1,0:T(8,128)(2,1)S(1)}, u32[]{:S(2)}, u32[]{:S(2)}) collective-permute-start(bf16[128,2048]{1,0:T(8,128)(2,1)} %get-tuple-element.48), channel_id=1, source_target_pairs={{0,1},{2,0},{4,2},{6,4},{7,6},{5,7},{3,5},{1,3},{8,9},{10,8},{12,1... | collective-permute-start | bytes 1572872 | tf_op jit(solution)/shard_map/ppermute | solution.py:229
  127.6 20.0 %collective-permute-start.23 = (bf16[128,2048]{1,0:T(8,128)(2,1)S(1)}, bf16[128,2048]{1,0:T(8,128)(2,1)S(1)}, u32[]{:S(2)}, u32[]{:S(2)}) collective-permute-start(bf16[128,2048]{1,0:T(8,128)(2,1)S(1)} %add_rows.12.refs_2_), channel_id=1, source_target_pairs={{0,2},{2,4},{4,6},{6,7},{7,5},{5,3},{3,1},{1,0},{8,10},{10,12},{12... | collective-permute-start | bytes 1572872 | tf_op jit(solution)/shard_map/ppermute | solution.py:229
  130.4 19.0 %collective-permute-start.31 = (bf16[128,2048]{1,0:T(8,128)(2,1)S(1)}, bf16[128,2048]{1,0:T(8,128)(2,1)S(1)}, u32[]{:S(2)}, u32[]{:S(2)}) collective-permute-start(bf16[128,2048]{1,0:T(8,128)(2,1)S(1)} %add_rows.13.refs_2_), channel_id=1, source_target_pairs={{0,1},{2,0},{4,2},{6,4},{7,6},{5,7},{3,5},{1,3},{8,9},{10,8},{12,1... | collective-permute-start | bytes 1572872 | tf_op jit(solution)/shard_map/ppermute | solution.py:229
  138.3 22.3 %collective-permute-start.29 = (bf16[128,2048]{1,0:T(8,128)(2,1)S(1)}, bf16[128,2048]{1,0:T(8,128)(2,1)S(1)}, u32[]{:S(2)}, u32[]{:S(2)}) collective-permute-start(bf16[128,2048]{1,0:T(8,128)(2,1)S(1)} %add_rows.14.refs_2_), channel_id=1, source_target_pairs={{0,1},{2,0},{4,2},{6,4},{7,6},{5,7},{3,5},{1,3},{8,9},{10,8},{12,1... | collective-permute-start | bytes 1572872 | tf_op jit(solution)/shard_map/ppermute | solution.py:229
  138.9 22.3 %collective-permute-start.28 = (bf16[128,2048]{1,0:T(8,128)(2,1)S(1)}, bf16[128,2048]{1,0:T(8,128)(2,1)S(1)}, u32[]{:S(2)}, u32[]{:S(2)}) collective-permute-start(bf16[128,2048]{1,0:T(8,128)(2,1)S(1)} %add_rows.15.refs_2_), channel_id=1, source_target_pairs={{0,2},{2,4},{4,6},{6,7},{7,5},{5,3},{3,1},{1,0},{8,10},{10,12},{12... | collective-permute-start | bytes 1572872 | tf_op jit(solution)/shard_map/ppermute | solution.py:229
  147.7 22.3 %collective-permute-start.27 = (bf16[128,2048]{1,0:T(8,128)(2,1)S(1)}, bf16[128,2048]{1,0:T(8,128)(2,1)S(1)}, u32[]{:S(2)}, u32[]{:S(2)}) collective-permute-start(bf16[128,2048]{1,0:T(8,128)(2,1)S(1)} %add_rows.16.refs_2_), channel_id=1, source_target_pairs={{0,2},{2,4},{4,6},{6,7},{7,5},{5,3},{3,1},{1,0},{8,10},{10,12},{12... | collective-permute-start | bytes 1572872 | tf_op jit(solution)/shard_map/ppermute | solution.py:229
  149.5 22.3 %collective-permute-start.34 = (bf16[128,2048]{1,0:T(8,128)(2,1)S(1)}, bf16[128,2048]{1,0:T(8,128)(2,1)S(1)}, u32[]{:S(2)}, u32[]{:S(2)}) collective-permute-start(bf16[128,2048]{1,0:T(8,128)(2,1)S(1)} %add_rows.17.refs_1_), channel_id=1, source_target_pairs={{0,1},{2,0},{4,2},{6,4},{7,6},{5,7},{3,5},{1,3},{8,9},{10,8},{12,1... | collective-permute-start | bytes 1572872 | tf_op jit(solution)/shard_map/ppermute | solution.py:229
  150.0 49.3 %collective-permute-start.37 = (bf16[3,176,2048]{2,1,0:T(8,128)(2,1)S(1)}, bf16[3,176,2048]{2,1,0:T(8,128)(2,1)S(1)}, u32[]{:S(2)}, u32[]{:S(2)}) collective-permute-start(bf16[3,176,2048]{2,1,0:T(8,128)(2,1)S(1)} %gate.50.refs_2_), channel_id=1, source_target_pairs={{24,0},{16,8},{8,16},{0,24},{25,1},{17,9},{9,17},{1,25},{26,2},{18... | collective-permute-start | bytes 6488072 | tf_op jit(solution)/shard_map/ppermute | solution.py:89
  160.8 22.3 %collective-permute-start.33 = (bf16[128,2048]{1,0:T(8,128)(2,1)S(1)}, bf16[128,2048]{1,0:T(8,128)(2,1)S(1)}, u32[]{:S(2)}, u32[]{:S(2)}) collective-permute-start(bf16[128,2048]{1,0:T(8,128)(2,1)S(1)} %add_rows.18.refs_2_), channel_id=1, source_target_pairs={{0,1},{2,0},{4,2},{6,4},{7,6},{5,7},{3,5},{1,3},{8,9},{10,8},{12,1... | collective-permute-start | bytes 1572872 | tf_op jit(solution)/shard_map/ppermute | solution.py:229
  161.4 21.8 %collective-permute-start.35 = (bf16[128,2048]{1,0:T(8,128)(2,1)S(1)}, bf16[128,2048]{1,0:T(8,128)(2,1)S(1)}, u32[]{:S(2)}, u32[]{:S(2)}) collective-permute-start(bf16[128,2048]{1,0:T(8,128)(2,1)S(1)} %add_rows.19.refs_2_), channel_id=1, source_target_pairs={{0,2},{2,4},{4,6},{6,7},{7,5},{5,3},{3,1},{1,0},{8,10},{10,12},{12... | collective-permute-start | bytes 1572872 | tf_op jit(solution)/shard_map/ppermute | solution.py:229
  170.2 21.9 %collective-permute-start.32 = (bf16[128,2048]{1,0:T(8,128)(2,1)S(1)}, bf16[128,2048]{1,0:T(8,128)(2,1)S(1)}, u32[]{:S(2)}, u32[]{:S(2)}) collective-permute-start(bf16[128,2048]{1,0:T(8,128)(2,1)S(1)} %add_rows.20.refs_2_), channel_id=1, source_target_pairs={{0,2},{2,4},{4,6},{6,7},{7,5},{5,3},{3,1},{1,0},{8,10},{10,12},{12... | collective-permute-start | bytes 1572872 | tf_op jit(solution)/shard_map/ppermute | solution.py:229
  172.0 21.6 %collective-permute-start.36 = (bf16[128,2048]{1,0:T(8,128)(2,1)S(1)}, bf16[128,2048]{1,0:T(8,128)(2,1)S(1)}, u32[]{:S(2)}, u32[]{:S(2)}) collective-permute-start(bf16[128,2048]{1,0:T(8,128)(2,1)S(1)} %add_rows.21.refs_2_), channel_id=1, source_target_pairs={{0,1},{2,0},{4,2},{6,4},{7,6},{5,7},{3,5},{1,3},{8,9},{10,8},{12,1... | collective-permute-start | bytes 1572872 | tf_op jit(solution)/shard_map/ppermute | solution.py:229

commit v7 on v6

--- a/solution.py
+++ b/solution.py
@@ -414,6 +414,7 @@
 
 def body(tokens, cotangent, routes, route_weight, fetch_pick, panels):
     panels = pltpu.with_memory_space_constraint(panels, pltpu.HBM)
+    fetch_pick = pltpu.with_memory_space_constraint(fetch_pick, pltpu.HBM)
     slots = fetch_pick.shape[1]
     stride = lax.axis_size("node") // slots
     part, width = tokens.shape

time: 202 us -> 202 us (level)
  transfers between devices with their start and end apart: 38 -> 38, of which waited for: 22 -> 22; matrix products, arithmetic and copies ran while one was open for 0% -> 0% of each run, Pallas kernels for 24% -> 25%
where the time goes in v7:
time: 202 us; the launch traced here: 201 us
  waiting for transfers between devices  108 us (53%)
  Pallas kernels  53.8 us (27%)
  starting transfers between devices  38.5 us (19%)
    ppermute x28, waiting for transfers between devices, ring_step(): lax.ppermute(block, 'local', [(order[i], order[(i + distance) % size]) fo...  99.1 us
    ppermute x28, starting transfers between devices, ring_step(): lax.ppermute(block, 'local', [(order[i], order[(i + distance) % size]) fo...  33.3 us
    pallas_call x8, Pallas kernels, acts_pass(): pl.pallas_call(lambda *refs: acts_kernel(turn, slots, stride, routes.shap...  12.6 us
    pallas_call x2, Pallas kernels, chunk_pass(): pl.pallas_call(kernel, out_shape=tuple((jax.ShapeDtypeStruct((part, width...  12.3 us
    pallas_call x4, Pallas kernels, grads_pass(): pl.pallas_call(lambda *refs: grads_kernel(parts, len(acts), len(shapes),...  9.7 us
    ppermute x10, waiting for transfers between devices, exchange(): lax.ppermute(block, 'node', [(owner_of(node, turn, slots, stride), node)...  8.63 us
    pallas_call x3, Pallas kernels, pick_pass(): pl.pallas_call(lambda *refs: pick_kernel(turns, stride, apart, *refs), ou...  7.57 us
    ppermute x10, starting transfers between devices, exchange(): lax.ppermute(block, 'node', [(owner_of(node, turn, slots, stride), node)...  5.21 us
  transfers between devices with their start and end apart: 38, of which 22 were waited for; matrix products, arithmetic and copies ran while one was open for 0% of the time, Pallas kernels for 25%

profile of v7, /device:TPU:0, one launch (start us, length us, event | category | flops | bytes accessed | tf_op | source)
XLA Modules:
  0.0 201.2 jit_solution(3423780564881334903)
XLA Ops:
  0.6 2.3 %pick.3.refs_2_ = bf16[3,176,2048]{2,1,0:T(8,128)(2,1)S(1)} custom-call(s32[4,4]{1,0:T(4,128)} %refs_0_.25, bf16[2,3,176,2048]{3,2,1,0:T(8,128)(2,1)} %refs_1_.5), custom_call_target="tpu_custom_call" | custom-call | flops 1 | bytes 1 | tf_op jit(solution)/shard_map/pick/pallas_call | solution.py:125
  3.0 3.0 %collective-permute-start.10 = (bf16[3,176,2048]{2,1,0:T(8,128)(2,1)S(1)}, bf16[3,176,2048]{2,1,0:T(8,128)(2,1)S(1)}, u32[]{:S(2)}, u32[]{:S(2)}) collective-permute-start(bf16[3,176,2048]{2,1,0:T(8,128)(2,1)S(1)} %pick.3.refs_2_), channel_id=1, source_target_pairs={{16,0},{24,8},{0,16},{8,24},{17,1},{25,9},{1,17},{9,25},{18,2},{26... | collective-permute-start | bytes 6488072 | tf_op jit(solution)/shard_map/ppermute | solution.py:89
  6.0 2.3 %pick.4 = (bf16[176,2048]{1,0:T(8,128)(2,1)S(1)}, bf16[176,2048]{1,0:T(8,128)(2,1)S(1)}, bf16[176,2048]{1,0:T(8,128)(2,1)S(1)}) custom-call(s32[4,4]{1,0:T(4,128)} %refs_0_.25, bf16[2,3,176,2048]{3,2,1,0:T(8,128)(2,1)} %refs_1_.5, bf16[3,176,2048]{2,1,0:T(8,128)(2,1)S(1)} %pick.3.refs_2_), custom_call_target="tpu_custom_call" | custom-call | flops 1 | bytes 1 | tf_op jit(solution)/shard_map/pick/pallas_call | solution.py:125
  8.9 1.6 collective-permute-start.2
  10.5 1.5 collective-permute-start.1
  12.0 1.6 collective-permute-start
  13.6 0.6 collective-permute-start.7
  14.2 3.0 %pick.5 = (bf16[3,176,2048]{2,1,0:T(8,128)(2,1)S(1)}, bf16[3,176,2048]{2,1,0:T(8,128)(2,1)S(1)}) custom-call(s32[4,4]{1,0:T(4,128)} %refs_0_.25, bf16[2,3,176,2048]{3,2,1,0:T(8,128)(2,1)} %refs_1_.5, bf16[176,2048]{1,0:T(8,128)(2,1)S(1)} %get-tuple-element.34.refs_2_), custom_call_target="tpu_custom_call" | custom-call | flops 1 | bytes 1 | tf_op jit(solution)/shard_map/pick/pallas_call | solution.py:125
  17.2 6.5 %collective-permute-done.2.refs_0_ = bf16[128,2048]{1,0:T(8,128)(2,1)S(1)} collective-permute-done((bf16[128,2048]{1,0:T(8,128)(2,1)S(1)}, bf16[128,2048]{1,0:T(8,128)(2,1)S(1)}, u32[]{:S(2)}, u32[]{:S(2)}) %collective-permute-start.2) | collective-permute-done | bytes 524320 | tf_op jit(solution)/shard_map/ppermute | solution.py:229
  23.7 1.6 collective-permute-start.6
  25.3 1.5 collective-permute-start.11
  26.8 9.7 %collective-permute-done.refs_0_ = bf16[128,2048]{1,0:T(8,128)(2,1)S(1)} collective-permute-done((bf16[128,2048]{1,0:T(8,128)(2,1)S(1)}, bf16[128,2048]{1,0:T(8,128)(2,1)S(1)}, u32[]{:S(2)}, u32[]{:S(2)}) %collective-permute-start) | collective-permute-done | bytes 524320 | tf_op jit(solution)/shard_map/ppermute | solution.py:229
  36.6 1.5 collective-permute-start.9
  38.0 0.5 collective-permute-start.8
  38.6 7.6 %collective-permute-done.6.refs_0_ = bf16[128,2048]{1,0:T(8,128)(2,1)S(1)} collective-permute-done((bf16[128,2048]{1,0:T(8,128)(2,1)S(1)}, bf16[128,2048]{1,0:T(8,128)(2,1)S(1)}, u32[]{:S(2)}, u32[]{:S(2)}) %collective-permute-start.6) | collective-permute-done | bytes 524320 | tf_op jit(solution)/shard_map/ppermute | solution.py:229
  46.1 1.6 collective-permute-start.14
  47.8 1.5 collective-permute-start.13
  49.3 3.7 %collective-permute-done.10.refs_0_ = bf16[3,176,2048]{2,1,0:T(8,128)(2,1)S(1)} collective-permute-done((bf16[3,176,2048]{2,1,0:T(8,128)(2,1)S(1)}, bf16[3,176,2048]{2,1,0:T(8,128)(2,1)S(1)}, u32[]{:S(2)}, u32[]{:S(2)}) %collective-permute-start.10) | collective-permute-done | bytes 2162720 | tf_op jit(solution)/shard_map/ppermute | solution.py:89
  53.3 5.7 %collective-permute-done.9.refs_0_ = bf16[128,2048]{1,0:T(8,128)(2,1)S(1)} collective-permute-done((bf16[128,2048]{1,0:T(8,128)(2,1)S(1)}, bf16[128,2048]{1,0:T(8,128)(2,1)S(1)}, u32[]{:S(2)}, u32[]{:S(2)}) %collective-permute-start.9) | collective-permute-done | bytes 524320 | tf_op jit(solution)/shard_map/ppermute | solution.py:229
  59.0 1.6 acts_1_n.1.refs_11_.refs_16_.refs_2_
  60.6 1.6 collective-permute-start.16
  62.3 1.6 acts_0_n.1.refs_11_.refs_0_.refs_16_
  63.8 0.5 collective-permute-start.12
  64.3 1.6 acts_2_n.1.refs_1_.refs_16_.refs_4_
  65.9 2.7 %collective-permute-done.14.refs_0_ = bf16[128,2048]{1,0:T(8,128)(2,1)S(1)} collective-permute-done((bf16[128,2048]{1,0:T(8,128)(2,1)S(1)}, bf16[128,2048]{1,0:T(8,128)(2,1)S(1)}, u32[]{:S(2)}, u32[]{:S(2)}) %collective-permute-start.14) | collective-permute-done | bytes 524320 | tf_op jit(solution)/shard_map/ppermute | solution.py:229
  68.6 1.6 collective-permute-start.15
  70.3 1.5 collective-permute-start.17
  71.7 9.7 %collective-permute-done.12.refs_0_ = bf16[128,2048]{1,0:T(8,128)(2,1)S(1)} collective-permute-done((bf16[128,2048]{1,0:T(8,128)(2,1)S(1)}, bf16[128,2048]{1,0:T(8,128)(2,1)S(1)}, u32[]{:S(2)}, u32[]{:S(2)}) %collective-permute-start.12) | collective-permute-done | bytes 524320 | tf_op jit(solution)/shard_map/ppermute | solution.py:229
  81.5 9.1 %collective-permute-done.15.refs_0_ = bf16[128,2048]{1,0:T(8,128)(2,1)S(1)} collective-permute-done((bf16[128,2048]{1,0:T(8,128)(2,1)S(1)}, bf16[128,2048]{1,0:T(8,128)(2,1)S(1)}, u32[]{:S(2)}, u32[]{:S(2)}) %collective-permute-start.15) | collective-permute-done | bytes 524320 | tf_op jit(solution)/shard_map/ppermute | solution.py:229
  90.6 1.3 collective-permute-done.17.refs_0_
  91.9 1.6 acts_2_f.1.refs_17_.refs_18_.refs_5_
  93.5 2.4 %grads_2.1.refs_13_ = bf16[3,176,2048]{2,1,0:T(8,128)(2,1)S(1)} custom-call(bf16[128,2048]{1,0:T(8,128)(2,1)S(1)} %copy-done, bf16[128,2048]{1,0:T(8,128)(2,1)S(1)} %gate.31.refs_1_, bf16[128,2048]{1,0:T(8,128)(2,1)S(1)} %gate.33.refs_1_.refs_2_, bf16[128,2048]{1,0:T(8,128)(2,1)S(1)} %gate.29.refs_1_.refs_3_, ...), custom_call_target="tpu_custom_call" | custom-call | flops 2214592512 | bytes 1 | tf_op jit(solution)/shard_map/grads_2/pallas_call | solution.py:324
  95.9 1.6 acts_1_f.1.refs_17_.refs_18_.refs_3_
  97.5 0.6 collective-permute-start.30
  98.1 2.4 %grads_1.1 = (bf16[176,2048]{1,0:T(8,128)(2,1)S(1)}, bf16[176,2048]{1,0:T(8,128)(2,1)S(1)}, bf16[176,2048]{1,0:T(8,128)(2,1)S(1)}) custom-call(bf16[128,2048]{1,0:T(8,128)(2,1)S(1)} %copy-done, bf16[128,2048]{1,0:T(8,128)(2,1)S(1)} %gate.31.refs_1_, bf16[128,2048]{1,0:T(8,128)(2,1)S(1)} %gate.33.refs_1_.refs_2_, bf16[128,2048]{1,0:T(8,128)(2,1)S(1)} %gate.29.refs_1_.refs_3_, ...), custom_call_target="tpu_custom_call" | custom-call | flops 2214592512 | bytes 1 | tf_op jit(solution)/shard_map/grads_1/pallas_call | solution.py:324
  101.1 1.6 acts_0_f.1.refs_1_.refs_17_
  102.7 1.6 acts_3_f.1.refs_11_.refs_7_.refs_17_
  104.3 1.6 acts_3_n.1.refs_1_.refs_6_.refs_16_
  106.0 4.0 %chunks_4.1 = (bf16[128,2048]{1,0:T(8,128)(2,1)S(1)}, bf16[128,2048]{1,0:T(8,128)(2,1)}, bf16[128,2048]{1,0:T(8,128)(2,1)}, bf16[128,2048]{1,0:T(8,128)(2,1)S(1)}) custom-call(bf16[528,512]{1,0:T(8,128)(2,1)S(1)} %acts_0_n.1.refs_11_.refs_0_.refs_16_, bf16[528,512]{1,0:T(8,128)(2,1)S(1)} %acts_0_f.1.refs_1_.refs_17_, ...), custom_call_target="tpu_custom_call" | custom-call | flops 2214592512 | bytes 1 | tf_op jit(solution)/shard_map/chunks_4/pallas_call | solution.py:373
  109.9 1.6 collective-permute-start.22
  112.0 8.3 %chunks_12.1 = (bf16[128,2048]{1,0:T(8,128)(2,1)S(1)}, bf16[128,2048]{1,0:T(8,128)(2,1)S(1)}, bf16[128,2048]{1,0:T(8,128)(2,1)S(1)}, bf16[128,2048]{1,0:T(8,128)...) custom-call(bf16[528,512]{1,0:T(8,128)(2,1)S(1)} %acts_0_n.1.refs_11, ...), custom_call_target="tpu_custom_call" | custom-call | flops 1 | bytes 1 | tf_op jit(solution)/shard_map/chunks_12/pallas_call | solution.py:373
  120.3 1.6 collective-permute-start.24
  122.4 2.4 %grads_3.1.refs_18_.refs_0_ = bf16[3,176,2048]{2,1,0:T(8,128)(2,1)S(1)} custom-call(bf16[128,2048]{1,0:T(8,128)(2,1)S(1)} %copy-done, bf16[128,2048]{1,0:T(8,128)(2,1)S(1)} %gate.31.refs_1_, bf16[128,2048]{1,0:T(8,128)(2,1)S(1)} %gate.33.refs_1_.refs_2_, bf16[128,2048]{1,0:T(8,128)(2,1)S(1)} %gate.29.refs_1_.refs_3_, ...), custom_call_target="tpu_custom_call" | custom-call | flops 2214592512 | bytes 1 | tf_op jit(solution)/shard_map/grads_3/pallas_call | solution.py:324
  124.8 2.5 %grads_0.1.refs_2_.refs_1_ = bf16[3,176,2048]{2,1,0:T(8,128)(2,1)S(1)} custom-call(bf16[128,2048]{1,0:T(8,128)(2,1)S(1)} %copy-done, bf16[128,2048]{1,0:T(8,128)(2,1)S(1)} %gate.31.refs_1_, bf16[128,2048]{1,0:T(8,128)(2,1)S(1)} %gate.33.refs_1_.refs_2_, bf16[128,2048]{1,0:T(8,128)(2,1)S(1)} %gate.29.refs_1_.refs_3_, ...), custom_call_target="tpu_custom_call" | custom-call | flops 2214592512 | bytes 1 | tf_op jit(solution)/shard_map/grads_0/pallas_call | solution.py:324
  127.4 1.6 collective-permute-start.23
  129.1 1.2 add_rows.13.refs_2_
  130.2 0.5 collective-permute-start.31
  130.7 7.0 %collective-permute-done.25.refs_0_ = bf16[128,2048]{1,0:T(8,128)(2,1)S(1)} collective-permute-done((bf16[128,2048]{1,0:T(8,128)(2,1)}, bf16[128,2048]{1,0:T(8,128)(2,1)S(1)}, u32[]{:S(2)}, u32[]{:S(2)}) %collective-permute-start.25) | collective-permute-done | bytes 524320 | tf_op jit(solution)/shard_map/ppermute | solution.py:229
  138.5 1.6 collective-permute-start.28
  140.1 7.0 %collective-permute-done.23.refs_0_ = bf16[128,2048]{1,0:T(8,128)(2,1)S(1)} collective-permute-done((bf16[128,2048]{1,0:T(8,128)(2,1)S(1)}, bf16[128,2048]{1,0:T(8,128)(2,1)S(1)}, u32[]{:S(2)}, u32[]{:S(2)}) %collective-permute-start.23) | collective-permute-done | bytes 524320 | tf_op jit(solution)/shard_map/ppermute | solution.py:229
  147.3 1.6 collective-permute-start.27
  149.1 0.5 collective-permute-start.34
  149.6 10.6 %collective-permute-done.29.refs_0_ = bf16[128,2048]{1,0:T(8,128)(2,1)S(1)} collective-permute-done((bf16[128,2048]{1,0:T(8,128)(2,1)S(1)}, bf16[128,2048]{1,0:T(8,128)(2,1)S(1)}, u32[]{:S(2)}, u32[]{:S(2)}) %collective-permute-start.29) | collective-permute-done | bytes 524320 | tf_op jit(solution)/shard_map/ppermute | solution.py:229
  161.0 1.6 collective-permute-start.35
  162.6 7.0 %collective-permute-done.27.refs_0_ = bf16[128,2048]{1,0:T(8,128)(2,1)S(1)} collective-permute-done((bf16[128,2048]{1,0:T(8,128)(2,1)S(1)}, bf16[128,2048]{1,0:T(8,128)(2,1)S(1)}, u32[]{:S(2)}, u32[]{:S(2)}) %collective-permute-start.27) | collective-permute-done | bytes 524320 | tf_op jit(solution)/shard_map/ppermute | solution.py:229
  169.7 1.6 collective-permute-start.32
  172.1 10.6 %collective-permute-done.33.refs_0_ = bf16[128,2048]{1,0:T(8,128)(2,1)S(1)} collective-permute-done((bf16[128,2048]{1,0:T(8,128)(2,1)S(1)}, bf16[128,2048]{1,0:T(8,128)(2,1)S(1)}, u32[]{:S(2)}, u32[]{:S(2)}) %collective-permute-start.33) | collective-permute-done | bytes 524320 | tf_op jit(solution)/shard_map/ppermute | solution.py:229
  182.9 5.2 %total.1 = (bf16[2,3,176,2048]{3,2,1,0:T(8,128)(2,1)}, bf16[3,176,2048]{2,1,0:T(8,128)(2,1)S(1)}, f32[8,128]{1,0:T(8,128)S(1)}) custom-call(s32[4,4]{1,0:T(4,128)} %refs_0_.25, bf16[3,176,2048]{2,1,0:T(8,128)(2,1)S(1)} %grads_0.1.refs_2_.refs_1_, bf16[176,2048]{1,0:T(8,128)(2,1)S(1)} %gate.46.refs_1_.refs_2_, bf16[176,2048]{1,0:T(8,128)(2,1)S(1)} %gate.47.refs_1_.refs_3_, ...), custom_call_target="tpu_custom_call" | custom-call | flops 1 | bytes 1 | tf_op jit(solution)/shard_map/total/pallas_call | solution.py:180
  188.1 3.5 %collective-permute-done.32.refs_0_ = bf16[128,2048]{1,0:T(8,128)(2,1)S(1)} collective-permute-done((bf16[128,2048]{1,0:T(8,128)(2,1)S(1)}, bf16[128,2048]{1,0:T(8,128)(2,1)S(1)}, u32[]{:S(2)}, u32[]{:S(2)}) %collective-permute-start.32) | collective-permute-done | bytes 524320 | tf_op jit(solution)/shard_map/ppermute | solution.py:229
  191.6 0.9 final_rows.2
  192.6 0.6 collective-permute-done.36.refs_0_
  193.1 0.9 final_rows.3
  194.0 4.8 %collective-permute-done.37.refs_0_ = bf16[3,176,2048]{2,1,0:T(8,128)(2,1)S(1)} collective-permute-done((bf16[3,176,2048]{2,1,0:T(8,128)(2,1)S(1)}, bf16[3,176,2048]{2,1,0:T(8,128)(2,1)S(1)}, u32[]{:S(2)}, u32[]{:S(2)}) %collective-permute-start.37) | collective-permute-done | bytes 2162720 | tf_op jit(solution)/shard_map/ppermute | solution.py:89
  198.9 2.1 %add.1 = bf16[2,3,176,2048]{3,2,1,0:T(8,128)(2,1)} custom-call(s32[4,4]{1,0:T(4,128)} %refs_0_.25, bf16[2,3,176,2048]{3,2,1,0:T(8,128)(2,1)} %get-tuple-element.62.refs_1_, bf16[3,176,2048]{2,1,0:T(8,128)(2,1)S(1)} %get-tuple-element.63.refs_2_, bf16[3,176,2048]{2,1,0:T(8,128)(2,1)S(1)} %gate.51.refs_3_), custom_call_target="tpu_custom_call", output_to_operand_aliasing={{}: (1, {})} | custom-call | flops 1 | bytes 1 | tf_op jit(solution)/shard_map/add/pallas_call | solution.py:214
  (79 shorter events, 5.8 us)
Async XLA Ops:
  2.9 6.0 %copy-start = (bf16[128,2048]{1,0:T(8,128)(2,1)S(1)}, bf16[128,2048]{1,0:T(8,128)(2,1)}, u32[]{:S(2)}) copy-start(bf16[128,2048]{1,0:T(8,128)(2,1)} %refs_0_.23) | copy-start | bytes 1572868
  2.9 7.6 %copy-start.1 = (bf16[128,2048]{1,0:T(8,128)(2,1)S(1)}, bf16[128,2048]{1,0:T(8,128)(2,1)}, u32[]{:S(2)}) copy-start(bf16[128,2048]{1,0:T(8,128)(2,1)} %refs_8_.7) | copy-start | bytes 1572868
  3.0 50.1 %collective-permute-start.10 = (bf16[3,176,2048]{2,1,0:T(8,128)(2,1)S(1)}, bf16[3,176,2048]{2,1,0:T(8,128)(2,1)S(1)}, u32[]{:S(2)}, u32[]{:S(2)}) collective-permute-start(bf16[3,176,2048]{2,1,0:T(8,128)(2,1)S(1)} %pick.3.refs_2_), channel_id=1, source_target_pairs={{16,0},{24,8},{0,16},{8,24},{17,1},{25,9},{1,17},{9,25},{18,2},{26... | collective-permute-start | bytes 6488072 | tf_op jit(solution)/shard_map/ppermute | solution.py:89
  8.3 2.3 %collective-permute-start.4 = (bf16[176,2048]{1,0:T(8,128)(2,1)S(1)}, bf16[176,2048]{1,0:T(8,128)(2,1)S(1)}, u32[]{:S(2)}, u32[]{:S(2)}) collective-permute-start(bf16[176,2048]{1,0:T(8,128)(2,1)S(1)} %get-tuple-element.35), channel_id=1, source_target_pairs={{8,0},{0,8},{24,16},{16,24},{9,1},{1,9},{25,17},{17,25},{10,2},{2,... | collective-permute-start | bytes 2162696 | tf_op jit(solution)/shard_map/ppermute | solution.py:89
  8.4 3.7 %collective-permute-start.5 = (bf16[176,2048]{1,0:T(8,128)(2,1)S(1)}, bf16[176,2048]{1,0:T(8,128)(2,1)S(1)}, u32[]{:S(2)}, u32[]{:S(2)}) collective-permute-start(bf16[176,2048]{1,0:T(8,128)(2,1)S(1)} %get-tuple-element.36), channel_id=1, source_target_pairs={{8,0},{0,8},{24,16},{16,24},{9,1},{1,9},{25,17},{17,25},{10,2},{2,... | collective-permute-start | bytes 2162696 | tf_op jit(solution)/shard_map/ppermute | solution.py:89
  8.9 4.8 %collective-permute-start.3 = (bf16[176,2048]{1,0:T(8,128)(2,1)S(1)}, bf16[176,2048]{1,0:T(8,128)(2,1)S(1)}, u32[]{:S(2)}, u32[]{:S(2)}) collective-permute-start(bf16[176,2048]{1,0:T(8,128)(2,1)S(1)} %get-tuple-element.34.refs_2_), channel_id=1, source_target_pairs={{8,0},{0,8},{24,16},{16,24},{9,1},{1,9},{25,17},{17,25},{10,2},{2,... | collective-permute-start | bytes 2162696 | tf_op jit(solution)/shard_map/ppermute | solution.py:89
  8.9 14.7 %collective-permute-start.2 = (bf16[128,2048]{1,0:T(8,128)(2,1)S(1)}, bf16[128,2048]{1,0:T(8,128)(2,1)S(1)}, u32[]{:S(2)}, u32[]{:S(2)}) collective-permute-start(bf16[128,2048]{1,0:T(8,128)(2,1)S(1)} %copy-done), channel_id=1, source_target_pairs={{0,2},{2,4},{4,6},{6,7},{7,5},{5,3},{3,1},{1,0},{8,10},{10,12},{12... | collective-permute-start | bytes 1572872 | tf_op jit(solution)/shard_map/ppermute | solution.py:229
  10.5 14.8 %collective-permute-start.1 = (bf16[128,2048]{1,0:T(8,128)(2,1)S(1)}, bf16[128,2048]{1,0:T(8,128)(2,1)S(1)}, u32[]{:S(2)}, u32[]{:S(2)}) collective-permute-start(bf16[128,2048]{1,0:T(8,128)(2,1)S(1)} %copy-done.1), channel_id=1, source_target_pairs={{0,1},{2,0},{4,2},{6,4},{7,6},{5,7},{3,5},{1,3},{8,9},{10,8},{12,1... | collective-permute-start | bytes 1572872 | tf_op jit(solution)/shard_map/ppermute | solution.py:229
  12.0 24.5 %collective-permute-start = (bf16[128,2048]{1,0:T(8,128)(2,1)S(1)}, bf16[128,2048]{1,0:T(8,128)(2,1)S(1)}, u32[]{:S(2)}, u32[]{:S(2)}) collective-permute-start(bf16[128,2048]{1,0:T(8,128)(2,1)S(1)} %copy-done), channel_id=1, source_target_pairs={{0,1},{2,0},{4,2},{6,4},{7,6},{5,7},{3,5},{1,3},{8,9},{10,8},{12,1... | collective-permute-start | bytes 1572872 | tf_op jit(solution)/shard_map/ppermute | solution.py:229
  13.6 24.4 %collective-permute-start.7 = (bf16[128,2048]{1,0:T(8,128)(2,1)S(1)}, bf16[128,2048]{1,0:T(8,128)(2,1)S(1)}, u32[]{:S(2)}, u32[]{:S(2)}) collective-permute-start(bf16[128,2048]{1,0:T(8,128)(2,1)S(1)} %copy-done.1), channel_id=1, source_target_pairs={{0,2},{2,4},{4,6},{6,7},{7,5},{5,3},{3,1},{1,0},{8,10},{10,12},{12... | collective-permute-start | bytes 1572872 | tf_op jit(solution)/shard_map/ppermute | solution.py:229
  23.7 22.5 %collective-permute-start.6 = (bf16[128,2048]{1,0:T(8,128)(2,1)S(1)}, bf16[128,2048]{1,0:T(8,128)(2,1)S(1)}, u32[]{:S(2)}, u32[]{:S(2)}) collective-permute-start(bf16[128,2048]{1,0:T(8,128)(2,1)S(1)} %gate.29.refs_1_.refs_3_), channel_id=1, source_target_pairs={{0,2},{2,4},{4,6},{6,7},{7,5},{5,3},{3,1},{1,0},{8,10},{10,12},{12... | collective-permute-start | bytes 1572872 | tf_op jit(solution)/shard_map/ppermute | solution.py:229
  25.3 22.5 %collective-permute-start.11 = (bf16[128,2048]{1,0:T(8,128)(2,1)S(1)}, bf16[128,2048]{1,0:T(8,128)(2,1)S(1)}, u32[]{:S(2)}, u32[]{:S(2)}) collective-permute-start(bf16[128,2048]{1,0:T(8,128)(2,1)S(1)} %gate.30.refs_1_.refs_5_.refs_9_), channel_id=1, source_target_pairs={{0,1},{2,0},{4,2},{6,4},{7,6},{5,7},{3,5},{1,3},{8,9},{10,8},{12,1... | collective-permute-start | bytes 1572872 | tf_op jit(solution)/shard_map/ppermute | solution.py:229
  36.6 22.5 %collective-permute-start.9 = (bf16[128,2048]{1,0:T(8,128)(2,1)S(1)}, bf16[128,2048]{1,0:T(8,128)(2,1)S(1)}, u32[]{:S(2)}, u32[]{:S(2)}) collective-permute-start(bf16[128,2048]{1,0:T(8,128)(2,1)S(1)} %gate.31.refs_1_), channel_id=1, source_target_pairs={{0,1},{2,0},{4,2},{6,4},{7,6},{5,7},{3,5},{1,3},{8,9},{10,8},{12,1... | collective-permute-start | bytes 1572872 | tf_op jit(solution)/shard_map/ppermute | solution.py:229
  38.0 21.0 %collective-permute-start.8 = (bf16[128,2048]{1,0:T(8,128)(2,1)S(1)}, bf16[128,2048]{1,0:T(8,128)(2,1)S(1)}, u32[]{:S(2)}, u32[]{:S(2)}) collective-permute-start(bf16[128,2048]{1,0:T(8,128)(2,1)S(1)} %gate.32.refs_1_.refs_7_.refs_11_), channel_id=1, source_target_pairs={{0,2},{2,4},{4,6},{6,7},{7,5},{5,3},{3,1},{1,0},{8,10},{10,12},{12... | collective-permute-start | bytes 1572872 | tf_op jit(solution)/shard_map/ppermute | solution.py:229
  46.1 22.5 %collective-permute-start.14 = (bf16[128,2048]{1,0:T(8,128)(2,1)S(1)}, bf16[128,2048]{1,0:T(8,128)(2,1)S(1)}, u32[]{:S(2)}, u32[]{:S(2)}) collective-permute-start(bf16[128,2048]{1,0:T(8,128)(2,1)S(1)} %gate.33.refs_1_.refs_2_), channel_id=1, source_target_pairs={{0,2},{2,4},{4,6},{6,7},{7,5},{5,3},{3,1},{1,0},{8,10},{10,12},{12... | collective-permute-start | bytes 1572872 | tf_op jit(solution)/shard_map/ppermute | solution.py:229
  47.8 22.5 %collective-permute-start.13 = (bf16[128,2048]{1,0:T(8,128)(2,1)S(1)}, bf16[128,2048]{1,0:T(8,128)(2,1)S(1)}, u32[]{:S(2)}, u32[]{:S(2)}) collective-permute-start(bf16[128,2048]{1,0:T(8,128)(2,1)S(1)} %gate.34.refs_1_.refs_4_.refs_12_), channel_id=1, source_target_pairs={{0,1},{2,0},{4,2},{6,4},{7,6},{5,7},{3,5},{1,3},{8,9},{10,8},{12,1... | collective-permute-start | bytes 1572872 | tf_op jit(solution)/shard_map/ppermute | solution.py:229
  53.0 6.0 %copy-start.2 = (s32[1024,1]{0,1:T(1,128)S(1)}, s32[1024,1]{0,1:T(1,128)}, u32[]{:S(2)}) copy-start(s32[1024,1]{0,1:T(1,128)} %param.8) | copy-start | bytes 12292
  53.0 6.0 %copy-start.3 = (f32[1024,1]{0,1:T(1,128)S(1)}, f32[1024,1]{0,1:T(1,128)}, u32[]{:S(2)}) copy-start(f32[1024,1]{0,1:T(1,128)} %param.9) | copy-start | bytes 12292
  53.0 49.7 %collective-permute-start.18 = (bf16[3,176,2048]{2,1,0:T(8,128)(2,1)S(1)}, bf16[3,176,2048]{2,1,0:T(8,128)(2,1)S(1)}, u32[]{:S(2)}, u32[]{:S(2)}) collective-permute-start(bf16[3,176,2048]{2,1,0:T(8,128)(2,1)S(1)} %gate.36.refs_1_), channel_id=1, source_target_pairs={{24,0},{16,8},{8,16},{0,24},{25,1},{17,9},{9,17},{1,25},{26,2},{18... | collective-permute-start | bytes 6488072 | tf_op jit(solution)/shard_map/ppermute | solution.py:89
  60.6 20.9 %collective-permute-start.16 = (bf16[128,2048]{1,0:T(8,128)(2,1)S(1)}, bf16[128,2048]{1,0:T(8,128)(2,1)S(1)}, u32[]{:S(2)}, u32[]{:S(2)}) collective-permute-start(bf16[128,2048]{1,0:T(8,128)(2,1)S(1)} %gate.38.refs_6_.refs_13_.refs_10_), channel_id=1, source_target_pairs={{0,2},{2,4},{4,6},{6,7},{7,5},{5,3},{3,1},{1,0},{8,10},{10,12},{12... | collective-permute-start | bytes 1572872 | tf_op jit(solution)/shard_map/ppermute | solution.py:229
  63.8 17.7 %collective-permute-start.12 = (bf16[128,2048]{1,0:T(8,128)(2,1)S(1)}, bf16[128,2048]{1,0:T(8,128)(2,1)S(1)}, u32[]{:S(2)}, u32[]{:S(2)}) collective-permute-start(bf16[128,2048]{1,0:T(8,128)(2,1)S(1)} %gate.37.refs_1_.refs_0_.refs_4_), channel_id=1, source_target_pairs={{0,1},{2,0},{4,2},{6,4},{7,6},{5,7},{3,5},{1,3},{8,9},{10,8},{12,1... | collective-permute-start | bytes 1572872 | tf_op jit(solution)/shard_map/ppermute | solution.py:229
  68.6 22.0 %collective-permute-start.15 = (bf16[128,2048]{1,0:T(8,128)(2,1)S(1)}, bf16[128,2048]{1,0:T(8,128)(2,1)S(1)}, u32[]{:S(2)}, u32[]{:S(2)}) collective-permute-start(bf16[128,2048]{1,0:T(8,128)(2,1)S(1)} %gate.39.refs_1_.refs_3_.refs_7_), channel_id=1, source_target_pairs={{0,2},{2,4},{4,6},{6,7},{7,5},{5,3},{3,1},{1,0},{8,10},{10,12},{12... | collective-permute-start | bytes 1572872 | tf_op jit(solution)/shard_map/ppermute | solution.py:229
  70.3 21.7 %collective-permute-start.17 = (bf16[128,2048]{1,0:T(8,128)(2,1)S(1)}, bf16[128,2048]{1,0:T(8,128)(2,1)S(1)}, u32[]{:S(2)}, u32[]{:S(2)}) collective-permute-start(bf16[128,2048]{1,0:T(8,128)(2,1)S(1)} %gate.40.refs_1_.refs_5_.refs_13_), channel_id=1, source_target_pairs={{0,1},{2,0},{4,2},{6,4},{7,6},{5,7},{3,5},{1,3},{8,9},{10,8},{12,1... | collective-permute-start | bytes 1572872 | tf_op jit(solution)/shard_map/ppermute | solution.py:229
  97.5 52.1 %collective-permute-start.30 = (bf16[3,176,2048]{2,1,0:T(8,128)(2,1)S(1)}, bf16[3,176,2048]{2,1,0:T(8,128)(2,1)S(1)}, u32[]{:S(2)}, u32[]{:S(2)}) collective-permute-start(bf16[3,176,2048]{2,1,0:T(8,128)(2,1)S(1)} %grads_2.1.refs_13_), channel_id=1, source_target_pairs={{16,0},{24,8},{0,16},{8,24},{17,1},{25,9},{1,17},{9,25},{18,2},{26... | collective-permute-start | bytes 6488072 | tf_op jit(solution)/shard_map/ppermute | solution.py:89
  100.5 5.4 %collective-permute-start.21 = (bf16[176,2048]{1,0:T(8,128)(2,1)S(1)}, bf16[176,2048]{1,0:T(8,128)(2,1)S(1)}, u32[]{:S(2)}, u32[]{:S(2)}) collective-permute-start(bf16[176,2048]{1,0:T(8,128)(2,1)S(1)} %get-tuple-element.41), channel_id=1, source_target_pairs={{8,0},{0,8},{24,16},{16,24},{9,1},{1,9},{25,17},{17,25},{10,2},{2,... | collective-permute-start | bytes 2162696 | tf_op jit(solution)/shard_map/ppermute | solution.py:89
  100.6 5.4 %collective-permute-start.20 = (bf16[176,2048]{1,0:T(8,128)(2,1)S(1)}, bf16[176,2048]{1,0:T(8,128)(2,1)S(1)}, u32[]{:S(2)}, u32[]{:S(2)}) collective-permute-start(bf16[176,2048]{1,0:T(8,128)(2,1)S(1)} %get-tuple-element.40), channel_id=1, source_target_pairs={{8,0},{0,8},{24,16},{16,24},{9,1},{1,9},{25,17},{17,25},{10,2},{2,... | collective-permute-start | bytes 2162696 | tf_op jit(solution)/shard_map/ppermute | solution.py:89
  101.1 4.9 %collective-permute-start.19 = (bf16[176,2048]{1,0:T(8,128)(2,1)S(1)}, bf16[176,2048]{1,0:T(8,128)(2,1)S(1)}, u32[]{:S(2)}, u32[]{:S(2)}) collective-permute-start(bf16[176,2048]{1,0:T(8,128)(2,1)S(1)} %get-tuple-element.39.refs_11_), channel_id=1, source_target_pairs={{8,0},{0,8},{24,16},{16,24},{9,1},{1,9},{25,17},{17,25},{10,2},{2,... | collective-permute-start | bytes 2162696 | tf_op jit(solution)/shard_map/ppermute | solution.py:89
  109.9 17.3 %collective-permute-start.22 = (bf16[128,2048]{1,0:T(8,128)(2,1)S(1)}, bf16[128,2048]{1,0:T(8,128)(2,1)S(1)}, u32[]{:S(2)}, u32[]{:S(2)}) collective-permute-start(bf16[128,2048]{1,0:T(8,128)(2,1)S(1)} %get-tuple-element.42), channel_id=1, source_target_pairs={{0,2},{2,4},{4,6},{6,7},{7,5},{5,3},{3,1},{1,0},{8,10},{10,12},{12... | collective-permute-start | bytes 1572872 | tf_op jit(solution)/shard_map/ppermute | solution.py:229
  111.5 17.5 %collective-permute-start.26 = (bf16[128,2048]{1,0:T(8,128)(2,1)}, bf16[128,2048]{1,0:T(8,128)(2,1)}, u32[]{:S(2)}, u32[]{:S(2)}) collective-permute-start(bf16[128,2048]{1,0:T(8,128)(2,1)} %get-tuple-element.50), channel_id=1, source_target_pairs={{0,1},{2,0},{4,2},{6,4},{7,6},{5,7},{3,5},{1,3},{8,9},{10,8},{12,1... | collective-permute-start | bytes 1572872 | tf_op jit(solution)/shard_map/ppermute | solution.py:229
  120.3 18.1 %collective-permute-start.24 = (bf16[128,2048]{1,0:T(8,128)(2,1)S(1)}, bf16[128,2048]{1,0:T(8,128)(2,1)S(1)}, u32[]{:S(2)}, u32[]{:S(2)}) collective-permute-start(bf16[128,2048]{1,0:T(8,128)(2,1)S(1)} %get-tuple-element.43.refs_14_), channel_id=1, source_target_pairs={{0,2},{2,4},{4,6},{6,7},{7,5},{5,3},{3,1},{1,0},{8,10},{10,12},{12... | collective-permute-start | bytes 1572872 | tf_op jit(solution)/shard_map/ppermute | solution.py:229
  121.9 15.8 %collective-permute-start.25 = (bf16[128,2048]{1,0:T(8,128)(2,1)}, bf16[128,2048]{1,0:T(8,128)(2,1)S(1)}, u32[]{:S(2)}, u32[]{:S(2)}) collective-permute-start(bf16[128,2048]{1,0:T(8,128)(2,1)} %get-tuple-element.48), channel_id=1, source_target_pairs={{0,1},{2,0},{4,2},{6,4},{7,6},{5,7},{3,5},{1,3},{8,9},{10,8},{12,1... | collective-permute-start | bytes 1572872 | tf_op jit(solution)/shard_map/ppermute | solution.py:229
  127.4 19.7 %collective-permute-start.23 = (bf16[128,2048]{1,0:T(8,128)(2,1)S(1)}, bf16[128,2048]{1,0:T(8,128)(2,1)S(1)}, u32[]{:S(2)}, u32[]{:S(2)}) collective-permute-start(bf16[128,2048]{1,0:T(8,128)(2,1)S(1)} %add_rows.12.refs_2_), channel_id=1, source_target_pairs={{0,2},{2,4},{4,6},{6,7},{7,5},{5,3},{3,1},{1,0},{8,10},{10,12},{12... | collective-permute-start | bytes 1572872 | tf_op jit(solution)/shard_map/ppermute | solution.py:229
  130.2 18.7 %collective-permute-start.31 = (bf16[128,2048]{1,0:T(8,128)(2,1)S(1)}, bf16[128,2048]{1,0:T(8,128)(2,1)S(1)}, u32[]{:S(2)}, u32[]{:S(2)}) collective-permute-start(bf16[128,2048]{1,0:T(8,128)(2,1)S(1)} %add_rows.13.refs_2_), channel_id=1, source_target_pairs={{0,1},{2,0},{4,2},{6,4},{7,6},{5,7},{3,5},{1,3},{8,9},{10,8},{12,1... | collective-permute-start | bytes 1572872 | tf_op jit(solution)/shard_map/ppermute | solution.py:229
  137.9 22.3 %collective-permute-start.29 = (bf16[128,2048]{1,0:T(8,128)(2,1)S(1)}, bf16[128,2048]{1,0:T(8,128)(2,1)S(1)}, u32[]{:S(2)}, u32[]{:S(2)}) collective-permute-start(bf16[128,2048]{1,0:T(8,128)(2,1)S(1)} %add_rows.14.refs_2_), channel_id=1, source_target_pairs={{0,1},{2,0},{4,2},{6,4},{7,6},{5,7},{3,5},{1,3},{8,9},{10,8},{12,1... | collective-permute-start | bytes 1572872 | tf_op jit(solution)/shard_map/ppermute | solution.py:229
  138.5 22.3 %collective-permute-start.28 = (bf16[128,2048]{1,0:T(8,128)(2,1)S(1)}, bf16[128,2048]{1,0:T(8,128)(2,1)S(1)}, u32[]{:S(2)}, u32[]{:S(2)}) collective-permute-start(bf16[128,2048]{1,0:T(8,128)(2,1)S(1)} %add_rows.15.refs_2_), channel_id=1, source_target_pairs={{0,2},{2,4},{4,6},{6,7},{7,5},{5,3},{3,1},{1,0},{8,10},{10,12},{12... | collective-permute-start | bytes 1572872 | tf_op jit(solution)/shard_map/ppermute | solution.py:229
  147.3 22.3 %collective-permute-start.27 = (bf16[128,2048]{1,0:T(8,128)(2,1)S(1)}, bf16[128,2048]{1,0:T(8,128)(2,1)S(1)}, u32[]{:S(2)}, u32[]{:S(2)}) collective-permute-start(bf16[128,2048]{1,0:T(8,128)(2,1)S(1)} %add_rows.16.refs_2_), channel_id=1, source_target_pairs={{0,2},{2,4},{4,6},{6,7},{7,5},{5,3},{3,1},{1,0},{8,10},{10,12},{12... | collective-permute-start | bytes 1572872 | tf_op jit(solution)/shard_map/ppermute | solution.py:229
  149.1 22.3 %collective-permute-start.34 = (bf16[128,2048]{1,0:T(8,128)(2,1)S(1)}, bf16[128,2048]{1,0:T(8,128)(2,1)S(1)}, u32[]{:S(2)}, u32[]{:S(2)}) collective-permute-start(bf16[128,2048]{1,0:T(8,128)(2,1)S(1)} %add_rows.17.refs_1_), channel_id=1, source_target_pairs={{0,1},{2,0},{4,2},{6,4},{7,6},{5,7},{3,5},{1,3},{8,9},{10,8},{12,1... | collective-permute-start | bytes 1572872 | tf_op jit(solution)/shard_map/ppermute | solution.py:229
  149.6 49.3 %collective-permute-start.37 = (bf16[3,176,2048]{2,1,0:T(8,128)(2,1)S(1)}, bf16[3,176,2048]{2,1,0:T(8,128)(2,1)S(1)}, u32[]{:S(2)}, u32[]{:S(2)}) collective-permute-start(bf16[3,176,2048]{2,1,0:T(8,128)(2,1)S(1)} %gate.50.refs_2_), channel_id=1, source_target_pairs={{24,0},{16,8},{8,16},{0,24},{25,1},{17,9},{9,17},{1,25},{26,2},{18... | collective-permute-start | bytes 6488072 | tf_op jit(solution)/shard_map/ppermute | solution.py:89
  160.3 22.3 %collective-permute-start.33 = (bf16[128,2048]{1,0:T(8,128)(2,1)S(1)}, bf16[128,2048]{1,0:T(8,128)(2,1)S(1)}, u32[]{:S(2)}, u32[]{:S(2)}) collective-permute-start(bf16[128,2048]{1,0:T(8,128)(2,1)S(1)} %add_rows.18.refs_2_), channel_id=1, source_target_pairs={{0,1},{2,0},{4,2},{6,4},{7,6},{5,7},{3,5},{1,3},{8,9},{10,8},{12,1... | collective-permute-start | bytes 1572872 | tf_op jit(solution)/shard_map/ppermute | solution.py:229
  161.0 21.8 %collective-permute-start.35 = (bf16[128,2048]{1,0:T(8,128)(2,1)S(1)}, bf16[128,2048]{1,0:T(8,128)(2,1)S(1)}, u32[]{:S(2)}, u32[]{:S(2)}) collective-permute-start(bf16[128,2048]{1,0:T(8,128)(2,1)S(1)} %add_rows.19.refs_2_), channel_id=1, source_target_pairs={{0,2},{2,4},{4,6},{6,7},{7,5},{5,3},{3,1},{1,0},{8,10},{10,12},{12... | collective-permute-start | bytes 1572872 | tf_op jit(solution)/shard_map/ppermute | solution.py:229
  169.7 21.9 %collective-permute-start.32 = (bf16[128,2048]{1,0:T(8,128)(2,1)S(1)}, bf16[128,2048]{1,0:T(8,128)(2,1)S(1)}, u32[]{:S(2)}, u32[]{:S(2)}) collective-permute-start(bf16[128,2048]{1,0:T(8,128)(2,1)S(1)} %add_rows.20.refs_2_), channel_id=1, source_target_pairs={{0,2},{2,4},{4,6},{6,7},{7,5},{5,3},{3,1},{1,0},{8,10},{10,12},{12... | collective-permute-start | bytes 1572872 | tf_op jit(solution)/shard_map/ppermute | solution.py:229
  171.6 21.6 %collective-permute-start.36 = (bf16[128,2048]{1,0:T(8,128)(2,1)S(1)}, bf16[128,2048]{1,0:T(8,128)(2,1)S(1)}, u32[]{:S(2)}, u32[]{:S(2)}) collective-permute-start(bf16[128,2048]{1,0:T(8,128)(2,1)S(1)} %add_rows.21.refs_2_), channel_id=1, source_target_pairs={{0,1},{2,0},{4,2},{6,4},{7,6},{5,7},{3,5},{1,3},{8,9},{10,8},{12,1... | collective-permute-start | bytes 1572872 | tf_op jit(solution)/shard_map/ppermute | solution.py:229

commit v8 on v6

--- a/solution.py
+++ b/solution.py
@@ -414,6 +414,7 @@
 
 def body(tokens, cotangent, routes, route_weight, fetch_pick, panels):
     panels = pltpu.with_memory_space_constraint(panels, pltpu.HBM)
+    fetch_pick_far = pltpu.with_memory_space_constraint(fetch_pick, pltpu.HBM)
     slots = fetch_pick.shape[1]
     stride = lax.axis_size("node") // slots
     part, width = tokens.shape
@@ -468,7 +469,7 @@
             back[turn] = [exchange(grad, turn, slots) if turn else grad for grad in grads[turn]]
 
     read = [None] * slots
-    picked = line.step(lambda after: pick_pass([late], stride, fetch_pick, panels, False, after))
+    picked = line.step(lambda after: pick_pass([late], stride, fetch_pick_far, panels, False, after))
     read[late] = [exchange(picked[0], late, slots)]
     for turn in middle:
         picked = line.step(lambda after: pick_pass([turn], stride, fetch_pick, panels, True, after))

time: 202 us -> 201 us (level)
  no operation moved by 1% of the time
where the time goes in v8:
time: 201 us
  waiting for transfers between devices  108 us (54%)
  Pallas kernels  53.4 us (27%)
  starting transfers between devices  38.5 us (19%)
    ppermute x28, waiting for transfers between devices, ring_step(): lax.ppermute(block, 'local', [(order[i], order[(i + distance) % size]) fo...  99.2 us
    ppermute x28, starting transfers between devices, ring_step(): lax.ppermute(block, 'local', [(order[i], order[(i + distance) % size]) fo...  33.3 us
    pallas_call x8, Pallas kernels, acts_pass(): pl.pallas_call(lambda *refs: acts_kernel(turn, slots, stride, routes.shap...  12.6 us
    pallas_call x2, Pallas kernels, chunk_pass(): pl.pallas_call(kernel, out_shape=tuple((jax.ShapeDtypeStruct((part, width...  12.1 us
    pallas_call x4, Pallas kernels, grads_pass(): pl.pallas_call(lambda *refs: grads_kernel(parts, len(acts), len(shapes),...  9.6 us
    ppermute x10, waiting for transfers between devices, exchange(): lax.ppermute(block, 'node', [(owner_of(node, turn, slots, stride), node)...  8.73 us
    pallas_call x3, Pallas kernels, pick_pass(): pl.pallas_call(lambda *refs: pick_kernel(turns, stride, apart, *refs), ou...  7.46 us
    pallas_call x1, Pallas kernels, total_pass(): pl.pallas_call(lambda *refs: total_kernel(turns, last, stride, counts, *r...  5.31 us
  transfers between devices with their start and end apart: 38, of which 22 were waited for; matrix products, arithmetic and copies ran while one was open for 0% of the time, Pallas kernels for 24%

profile of v8, /device:TPU:0, one launch (start us, length us, event | category | flops | bytes accessed | tf_op | source)
XLA Modules:
  0.0 201.1 jit_solution(9638162640306248951)
XLA Ops:
  0.6 2.4 %pick.3.refs_2_ = bf16[3,176,2048]{2,1,0:T(8,128)(2,1)S(1)} custom-call(s32[4,4]{1,0:T(4,128)} %refs_0_.25, bf16[2,3,176,2048]{3,2,1,0:T(8,128)(2,1)} %refs_1_.5), custom_call_target="tpu_custom_call" | custom-call | flops 1 | bytes 1 | tf_op jit(solution)/shard_map/pick/pallas_call | solution.py:125
  3.1 3.0 %collective-permute-start.10 = (bf16[3,176,2048]{2,1,0:T(8,128)(2,1)S(1)}, bf16[3,176,2048]{2,1,0:T(8,128)(2,1)S(1)}, u32[]{:S(2)}, u32[]{:S(2)}) collective-permute-start(bf16[3,176,2048]{2,1,0:T(8,128)(2,1)S(1)} %pick.3.refs_2_), channel_id=1, source_target_pairs={{16,0},{24,8},{0,16},{8,24},{17,1},{25,9},{1,17},{9,25},{18,2},{26... | collective-permute-start | bytes 6488072 | tf_op jit(solution)/shard_map/ppermute | solution.py:89
  6.1 2.2 %pick.4 = (bf16[176,2048]{1,0:T(8,128)(2,1)S(1)}, bf16[176,2048]{1,0:T(8,128)(2,1)S(1)}, bf16[176,2048]{1,0:T(8,128)(2,1)S(1)}) custom-call(s32[4,4]{1,0:T(4,128)S(1)} %copy-done.4, bf16[2,3,176,2048]{3,2,1,0:T(8,128)(2,1)} %refs_1_.5, bf16[3,176,2048]{2,1,0:T(8,128)(2,1)S(1)} %pick.3.refs_2_), custom_call_target="tpu_custom_call" | custom-call | flops 1 | bytes 1 | tf_op jit(solution)/shard_map/pick/pallas_call | solution.py:125
  9.0 1.6 collective-permute-start.2
  10.6 1.5 collective-permute-start.1
  12.1 1.6 collective-permute-start
  13.6 0.6 collective-permute-start.7
  14.2 2.9 %pick.5 = (bf16[3,176,2048]{2,1,0:T(8,128)(2,1)S(1)}, bf16[3,176,2048]{2,1,0:T(8,128)(2,1)S(1)}) custom-call(s32[4,4]{1,0:T(4,128)S(1)} %copy-done.4, bf16[2,3,176,2048]{3,2,1,0:T(8,128)(2,1)} %refs_1_.5, bf16[176,2048]{1,0:T(8,128)(2,1)S(1)} %get-tuple-element.34.refs_2_), custom_call_target="tpu_custom_call" | custom-call | flops 1 | bytes 1 | tf_op jit(solution)/shard_map/pick/pallas_call | solution.py:125
  17.1 6.6 %collective-permute-done.2.refs_0_ = bf16[128,2048]{1,0:T(8,128)(2,1)S(1)} collective-permute-done((bf16[128,2048]{1,0:T(8,128)(2,1)S(1)}, bf16[128,2048]{1,0:T(8,128)(2,1)S(1)}, u32[]{:S(2)}, u32[]{:S(2)}) %collective-permute-start.2) | collective-permute-done | bytes 524320 | tf_op jit(solution)/shard_map/ppermute | solution.py:229
  23.7 1.6 collective-permute-start.6
  25.3 1.5 collective-permute-start.11
  26.8 9.7 %collective-permute-done.refs_0_ = bf16[128,2048]{1,0:T(8,128)(2,1)S(1)} collective-permute-done((bf16[128,2048]{1,0:T(8,128)(2,1)S(1)}, bf16[128,2048]{1,0:T(8,128)(2,1)S(1)}, u32[]{:S(2)}, u32[]{:S(2)}) %collective-permute-start) | collective-permute-done | bytes 524320 | tf_op jit(solution)/shard_map/ppermute | solution.py:229
  36.6 1.5 collective-permute-start.9
  38.1 0.5 collective-permute-start.8
  38.6 7.6 %collective-permute-done.6.refs_0_ = bf16[128,2048]{1,0:T(8,128)(2,1)S(1)} collective-permute-done((bf16[128,2048]{1,0:T(8,128)(2,1)S(1)}, bf16[128,2048]{1,0:T(8,128)(2,1)S(1)}, u32[]{:S(2)}, u32[]{:S(2)}) %collective-permute-start.6) | collective-permute-done | bytes 524320 | tf_op jit(solution)/shard_map/ppermute | solution.py:229
  46.2 1.6 collective-permute-start.14
  47.8 1.5 collective-permute-start.13
  49.3 3.9 %collective-permute-done.10.refs_0_ = bf16[3,176,2048]{2,1,0:T(8,128)(2,1)S(1)} collective-permute-done((bf16[3,176,2048]{2,1,0:T(8,128)(2,1)S(1)}, bf16[3,176,2048]{2,1,0:T(8,128)(2,1)S(1)}, u32[]{:S(2)}, u32[]{:S(2)}) %collective-permute-start.10) | collective-permute-done | bytes 2162720 | tf_op jit(solution)/shard_map/ppermute | solution.py:89
  53.5 5.6 %collective-permute-done.9.refs_0_ = bf16[128,2048]{1,0:T(8,128)(2,1)S(1)} collective-permute-done((bf16[128,2048]{1,0:T(8,128)(2,1)S(1)}, bf16[128,2048]{1,0:T(8,128)(2,1)S(1)}, u32[]{:S(2)}, u32[]{:S(2)}) %collective-permute-start.9) | collective-permute-done | bytes 524320 | tf_op jit(solution)/shard_map/ppermute | solution.py:229
  59.1 1.6 acts_1_n.1.refs_11_.refs_16_.refs_2_
  60.6 1.6 collective-permute-start.16
  62.3 1.6 acts_0_n.1.refs_11_.refs_0_.refs_16_
  63.9 0.5 collective-permute-start.12
  64.4 1.6 acts_2_n.1.refs_1_.refs_16_.refs_4_
  65.9 2.7 %collective-permute-done.14.refs_0_ = bf16[128,2048]{1,0:T(8,128)(2,1)S(1)} collective-permute-done((bf16[128,2048]{1,0:T(8,128)(2,1)S(1)}, bf16[128,2048]{1,0:T(8,128)(2,1)S(1)}, u32[]{:S(2)}, u32[]{:S(2)}) %collective-permute-start.14) | collective-permute-done | bytes 524320 | tf_op jit(solution)/shard_map/ppermute | solution.py:229
  68.6 1.6 collective-permute-start.15
  70.3 1.5 collective-permute-start.17
  71.8 9.7 %collective-permute-done.12.refs_0_ = bf16[128,2048]{1,0:T(8,128)(2,1)S(1)} collective-permute-done((bf16[128,2048]{1,0:T(8,128)(2,1)S(1)}, bf16[128,2048]{1,0:T(8,128)(2,1)S(1)}, u32[]{:S(2)}, u32[]{:S(2)}) %collective-permute-start.12) | collective-permute-done | bytes 524320 | tf_op jit(solution)/shard_map/ppermute | solution.py:229
  81.5 9.1 %collective-permute-done.15.refs_0_ = bf16[128,2048]{1,0:T(8,128)(2,1)S(1)} collective-permute-done((bf16[128,2048]{1,0:T(8,128)(2,1)S(1)}, bf16[128,2048]{1,0:T(8,128)(2,1)S(1)}, u32[]{:S(2)}, u32[]{:S(2)}) %collective-permute-start.15) | collective-permute-done | bytes 524320 | tf_op jit(solution)/shard_map/ppermute | solution.py:229
  90.6 1.3 collective-permute-done.17.refs_0_
  92.0 1.6 acts_2_f.1.refs_17_.refs_18_.refs_5_
  93.5 2.4 %grads_2.1.refs_13_ = bf16[3,176,2048]{2,1,0:T(8,128)(2,1)S(1)} custom-call(bf16[128,2048]{1,0:T(8,128)(2,1)S(1)} %copy-done, bf16[128,2048]{1,0:T(8,128)(2,1)S(1)} %gate.31.refs_1_, bf16[128,2048]{1,0:T(8,128)(2,1)S(1)} %gate.33.refs_1_.refs_2_, bf16[128,2048]{1,0:T(8,128)(2,1)S(1)} %gate.29.refs_1_.refs_3_, ...), custom_call_target="tpu_custom_call" | custom-call | flops 2214592512 | bytes 1 | tf_op jit(solution)/shard_map/grads_2/pallas_call | solution.py:324
  95.9 1.6 acts_1_f.1.refs_17_.refs_18_.refs_3_
  97.5 0.6 collective-permute-start.30
  98.1 2.4 %grads_1.1 = (bf16[176,2048]{1,0:T(8,128)(2,1)S(1)}, bf16[176,2048]{1,0:T(8,128)(2,1)S(1)}, bf16[176,2048]{1,0:T(8,128)(2,1)S(1)}) custom-call(bf16[128,2048]{1,0:T(8,128)(2,1)S(1)} %copy-done, bf16[128,2048]{1,0:T(8,128)(2,1)S(1)} %gate.31.refs_1_, bf16[128,2048]{1,0:T(8,128)(2,1)S(1)} %gate.33.refs_1_.refs_2_, bf16[128,2048]{1,0:T(8,128)(2,1)S(1)} %gate.29.refs_1_.refs_3_, ...), custom_call_target="tpu_custom_call" | custom-call | flops 2214592512 | bytes 1 | tf_op jit(solution)/shard_map/grads_1/pallas_call | solution.py:324
  101.2 1.6 acts_0_f.1.refs_1_.refs_17_
  102.8 1.6 acts_3_f.1.refs_11_.refs_7_.refs_17_
  104.3 1.6 acts_3_n.1.refs_1_.refs_6_.refs_16_
  106.0 4.0 %chunks_4.1 = (bf16[128,2048]{1,0:T(8,128)(2,1)S(1)}, bf16[128,2048]{1,0:T(8,128)(2,1)}, bf16[128,2048]{1,0:T(8,128)(2,1)}, bf16[128,2048]{1,0:T(8,128)(2,1)S(1)}) custom-call(bf16[528,512]{1,0:T(8,128)(2,1)S(1)} %acts_0_n.1.refs_11_.refs_0_.refs_16_, bf16[528,512]{1,0:T(8,128)(2,1)S(1)} %acts_0_f.1.refs_1_.refs_17_, ...), custom_call_target="tpu_custom_call" | custom-call | flops 2214592512 | bytes 1 | tf_op jit(solution)/shard_map/chunks_4/pallas_call | solution.py:373
  109.9 1.6 collective-permute-start.22
  112.0 8.1 %chunks_12.1 = (bf16[128,2048]{1,0:T(8,128)(2,1)S(1)}, bf16[128,2048]{1,0:T(8,128)(2,1)S(1)}, bf16[128,2048]{1,0:T(8,128)(2,1)S(1)}, bf16[128,2048]{1,0:T(8,128)...) custom-call(bf16[528,512]{1,0:T(8,128)(2,1)S(1)} %acts_0_n.1.refs_11, ...), custom_call_target="tpu_custom_call" | custom-call | flops 1 | bytes 1 | tf_op jit(solution)/shard_map/chunks_12/pallas_call | solution.py:373
  120.1 1.6 collective-permute-start.24
  122.2 2.4 %grads_3.1.refs_18_.refs_0_ = bf16[3,176,2048]{2,1,0:T(8,128)(2,1)S(1)} custom-call(bf16[128,2048]{1,0:T(8,128)(2,1)S(1)} %copy-done, bf16[128,2048]{1,0:T(8,128)(2,1)S(1)} %gate.31.refs_1_, bf16[128,2048]{1,0:T(8,128)(2,1)S(1)} %gate.33.refs_1_.refs_2_, bf16[128,2048]{1,0:T(8,128)(2,1)S(1)} %gate.29.refs_1_.refs_3_, ...), custom_call_target="tpu_custom_call" | custom-call | flops 2214592512 | bytes 1 | tf_op jit(solution)/shard_map/grads_3/pallas_call | solution.py:324
  124.6 2.4 %grads_0.1.refs_2_.refs_1_ = bf16[3,176,2048]{2,1,0:T(8,128)(2,1)S(1)} custom-call(bf16[128,2048]{1,0:T(8,128)(2,1)S(1)} %copy-done, bf16[128,2048]{1,0:T(8,128)(2,1)S(1)} %gate.31.refs_1_, bf16[128,2048]{1,0:T(8,128)(2,1)S(1)} %gate.33.refs_1_.refs_2_, bf16[128,2048]{1,0:T(8,128)(2,1)S(1)} %gate.29.refs_1_.refs_3_, ...), custom_call_target="tpu_custom_call" | custom-call | flops 2214592512 | bytes 1 | tf_op jit(solution)/shard_map/grads_0/pallas_call | solution.py:324
  127.2 1.6 collective-permute-start.23
  128.8 1.2 add_rows.13.refs_2_
  130.5 7.3 %collective-permute-done.25.refs_0_ = bf16[128,2048]{1,0:T(8,128)(2,1)S(1)} collective-permute-done((bf16[128,2048]{1,0:T(8,128)(2,1)}, bf16[128,2048]{1,0:T(8,128)(2,1)S(1)}, u32[]{:S(2)}, u32[]{:S(2)}) %collective-permute-start.25) | collective-permute-done | bytes 524320 | tf_op jit(solution)/shard_map/ppermute | solution.py:229
  138.5 1.6 collective-permute-start.28
  140.1 7.0 %collective-permute-done.23.refs_0_ = bf16[128,2048]{1,0:T(8,128)(2,1)S(1)} collective-permute-done((bf16[128,2048]{1,0:T(8,128)(2,1)S(1)}, bf16[128,2048]{1,0:T(8,128)(2,1)S(1)}, u32[]{:S(2)}, u32[]{:S(2)}) %collective-permute-start.23) | collective-permute-done | bytes 524320 | tf_op jit(solution)/shard_map/ppermute | solution.py:229
  147.3 1.6 collective-permute-start.27
  149.1 0.5 collective-permute-start.34
  149.6 10.6 %collective-permute-done.29.refs_0_ = bf16[128,2048]{1,0:T(8,128)(2,1)S(1)} collective-permute-done((bf16[128,2048]{1,0:T(8,128)(2,1)S(1)}, bf16[128,2048]{1,0:T(8,128)(2,1)S(1)}, u32[]{:S(2)}, u32[]{:S(2)}) %collective-permute-start.29) | collective-permute-done | bytes 524320 | tf_op jit(solution)/shard_map/ppermute | solution.py:229
  160.3 0.5 collective-permute-start.33
  161.0 1.6 collective-permute-start.35
  162.6 7.0 %collective-permute-done.27.refs_0_ = bf16[128,2048]{1,0:T(8,128)(2,1)S(1)} collective-permute-done((bf16[128,2048]{1,0:T(8,128)(2,1)S(1)}, bf16[128,2048]{1,0:T(8,128)(2,1)S(1)}, u32[]{:S(2)}, u32[]{:S(2)}) %collective-permute-start.27) | collective-permute-done | bytes 524320 | tf_op jit(solution)/shard_map/ppermute | solution.py:229
  169.7 1.6 collective-permute-start.32
  172.1 10.6 %collective-permute-done.33.refs_0_ = bf16[128,2048]{1,0:T(8,128)(2,1)S(1)} collective-permute-done((bf16[128,2048]{1,0:T(8,128)(2,1)S(1)}, bf16[128,2048]{1,0:T(8,128)(2,1)S(1)}, u32[]{:S(2)}, u32[]{:S(2)}) %collective-permute-start.33) | collective-permute-done | bytes 524320 | tf_op jit(solution)/shard_map/ppermute | solution.py:229
  182.9 5.3 %total.1 = (bf16[2,3,176,2048]{3,2,1,0:T(8,128)(2,1)}, bf16[3,176,2048]{2,1,0:T(8,128)(2,1)S(1)}, f32[8,128]{1,0:T(8,128)S(1)}) custom-call(s32[4,4]{1,0:T(4,128)S(1)} %copy-done.4, bf16[3,176,2048]{2,1,0:T(8,128)(2,1)S(1)} %grads_0.1.refs_2_.refs_1_, bf16[176,2048]{1,0:T(8,128)(2,1)S(1)} %gate.46.refs_1_.refs_2_, ...), custom_call_target="tpu_custom_call" | custom-call | flops 1 | bytes 1 | tf_op jit(solution)/shard_map/total/pallas_call | solution.py:180
  188.2 3.4 %collective-permute-done.32.refs_0_ = bf16[128,2048]{1,0:T(8,128)(2,1)S(1)} collective-permute-done((bf16[128,2048]{1,0:T(8,128)(2,1)S(1)}, bf16[128,2048]{1,0:T(8,128)(2,1)S(1)}, u32[]{:S(2)}, u32[]{:S(2)}) %collective-permute-start.32) | collective-permute-done | bytes 524320 | tf_op jit(solution)/shard_map/ppermute | solution.py:229
  191.6 0.9 final_rows.2
  192.5 0.6 collective-permute-done.36.refs_0_
  193.1 0.9 final_rows.3
  194.1 4.8 %collective-permute-done.37.refs_0_ = bf16[3,176,2048]{2,1,0:T(8,128)(2,1)S(1)} collective-permute-done((bf16[3,176,2048]{2,1,0:T(8,128)(2,1)S(1)}, bf16[3,176,2048]{2,1,0:T(8,128)(2,1)S(1)}, u32[]{:S(2)}, u32[]{:S(2)}) %collective-permute-start.37) | collective-permute-done | bytes 2162720 | tf_op jit(solution)/shard_map/ppermute | solution.py:89
  198.9 2.0 %add.1 = bf16[2,3,176,2048]{3,2,1,0:T(8,128)(2,1)} custom-call(s32[4,4]{1,0:T(4,128)S(1)} %copy-done.4, bf16[2,3,176,2048]{3,2,1,0:T(8,128)(2,1)} %get-tuple-element.62.refs_1_, bf16[3,176,2048]{2,1,0:T(8,128)(2,1)S(1)} %get-tuple-element.63.refs_2_, bf16[3,176,2048]{2,1,0:T(8,128)(2,1)S(1)} %gate.51.refs_3_), custom_call_target="tpu_custom_call", output_to_operand_aliasing={{}: (1, {})} | custom-call | flops 1 | bytes 1 | tf_op jit(solution)/shard_map/add/pallas_call | solution.py:214
  (81 shorter events, 5.8 us)
Async XLA Ops:
  0.6 5.5 %copy-start.4 = (s32[4,4]{1,0:T(4,128)S(1)}, s32[4,4]{1,0:T(4,128)}, u32[]{:S(2)}) copy-start(s32[4,4]{1,0:T(4,128)} %refs_0_.25) | copy-start | bytes 196
  3.1 5.9 %copy-start = (bf16[128,2048]{1,0:T(8,128)(2,1)S(1)}, bf16[128,2048]{1,0:T(8,128)(2,1)}, u32[]{:S(2)}) copy-start(bf16[128,2048]{1,0:T(8,128)(2,1)} %refs_0_.23) | copy-start | bytes 1572868
  3.1 7.5 %copy-start.1 = (bf16[128,2048]{1,0:T(8,128)(2,1)S(1)}, bf16[128,2048]{1,0:T(8,128)(2,1)}, u32[]{:S(2)}) copy-start(bf16[128,2048]{1,0:T(8,128)(2,1)} %refs_8_.7) | copy-start | bytes 1572868
  3.1 50.1 %collective-permute-start.10 = (bf16[3,176,2048]{2,1,0:T(8,128)(2,1)S(1)}, bf16[3,176,2048]{2,1,0:T(8,128)(2,1)S(1)}, u32[]{:S(2)}, u32[]{:S(2)}) collective-permute-start(bf16[3,176,2048]{2,1,0:T(8,128)(2,1)S(1)} %pick.3.refs_2_), channel_id=1, source_target_pairs={{16,0},{24,8},{0,16},{8,24},{17,1},{25,9},{1,17},{9,25},{18,2},{26... | collective-permute-start | bytes 6488072 | tf_op jit(solution)/shard_map/ppermute | solution.py:89
  8.3 2.3 %collective-permute-start.4 = (bf16[176,2048]{1,0:T(8,128)(2,1)S(1)}, bf16[176,2048]{1,0:T(8,128)(2,1)S(1)}, u32[]{:S(2)}, u32[]{:S(2)}) collective-permute-start(bf16[176,2048]{1,0:T(8,128)(2,1)S(1)} %get-tuple-element.35), channel_id=1, source_target_pairs={{8,0},{0,8},{24,16},{16,24},{9,1},{1,9},{25,17},{17,25},{10,2},{2,... | collective-permute-start | bytes 2162696 | tf_op jit(solution)/shard_map/ppermute | solution.py:89
  8.4 3.7 %collective-permute-start.5 = (bf16[176,2048]{1,0:T(8,128)(2,1)S(1)}, bf16[176,2048]{1,0:T(8,128)(2,1)S(1)}, u32[]{:S(2)}, u32[]{:S(2)}) collective-permute-start(bf16[176,2048]{1,0:T(8,128)(2,1)S(1)} %get-tuple-element.36), channel_id=1, source_target_pairs={{8,0},{0,8},{24,16},{16,24},{9,1},{1,9},{25,17},{17,25},{10,2},{2,... | collective-permute-start | bytes 2162696 | tf_op jit(solution)/shard_map/ppermute | solution.py:89
  8.9 4.8 %collective-permute-start.3 = (bf16[176,2048]{1,0:T(8,128)(2,1)S(1)}, bf16[176,2048]{1,0:T(8,128)(2,1)S(1)}, u32[]{:S(2)}, u32[]{:S(2)}) collective-permute-start(bf16[176,2048]{1,0:T(8,128)(2,1)S(1)} %get-tuple-element.34.refs_2_), channel_id=1, source_target_pairs={{8,0},{0,8},{24,16},{16,24},{9,1},{1,9},{25,17},{17,25},{10,2},{2,... | collective-permute-start | bytes 2162696 | tf_op jit(solution)/shard_map/ppermute | solution.py:89
  9.0 14.7 %collective-permute-start.2 = (bf16[128,2048]{1,0:T(8,128)(2,1)S(1)}, bf16[128,2048]{1,0:T(8,128)(2,1)S(1)}, u32[]{:S(2)}, u32[]{:S(2)}) collective-permute-start(bf16[128,2048]{1,0:T(8,128)(2,1)S(1)} %copy-done), channel_id=1, source_target_pairs={{0,2},{2,4},{4,6},{6,7},{7,5},{5,3},{3,1},{1,0},{8,10},{10,12},{12... | collective-permute-start | bytes 1572872 | tf_op jit(solution)/shard_map/ppermute | solution.py:229
  10.6 14.8 %collective-permute-start.1 = (bf16[128,2048]{1,0:T(8,128)(2,1)S(1)}, bf16[128,2048]{1,0:T(8,128)(2,1)S(1)}, u32[]{:S(2)}, u32[]{:S(2)}) collective-permute-start(bf16[128,2048]{1,0:T(8,128)(2,1)S(1)} %copy-done.1), channel_id=1, source_target_pairs={{0,1},{2,0},{4,2},{6,4},{7,6},{5,7},{3,5},{1,3},{8,9},{10,8},{12,1... | collective-permute-start | bytes 1572872 | tf_op jit(solution)/shard_map/ppermute | solution.py:229
  12.1 24.5 %collective-permute-start = (bf16[128,2048]{1,0:T(8,128)(2,1)S(1)}, bf16[128,2048]{1,0:T(8,128)(2,1)S(1)}, u32[]{:S(2)}, u32[]{:S(2)}) collective-permute-start(bf16[128,2048]{1,0:T(8,128)(2,1)S(1)} %copy-done), channel_id=1, source_target_pairs={{0,1},{2,0},{4,2},{6,4},{7,6},{5,7},{3,5},{1,3},{8,9},{10,8},{12,1... | collective-permute-start | bytes 1572872 | tf_op jit(solution)/shard_map/ppermute | solution.py:229
  13.6 24.4 %collective-permute-start.7 = (bf16[128,2048]{1,0:T(8,128)(2,1)S(1)}, bf16[128,2048]{1,0:T(8,128)(2,1)S(1)}, u32[]{:S(2)}, u32[]{:S(2)}) collective-permute-start(bf16[128,2048]{1,0:T(8,128)(2,1)S(1)} %copy-done.1), channel_id=1, source_target_pairs={{0,2},{2,4},{4,6},{6,7},{7,5},{5,3},{3,1},{1,0},{8,10},{10,12},{12... | collective-permute-start | bytes 1572872 | tf_op jit(solution)/shard_map/ppermute | solution.py:229
  23.7 22.5 %collective-permute-start.6 = (bf16[128,2048]{1,0:T(8,128)(2,1)S(1)}, bf16[128,2048]{1,0:T(8,128)(2,1)S(1)}, u32[]{:S(2)}, u32[]{:S(2)}) collective-permute-start(bf16[128,2048]{1,0:T(8,128)(2,1)S(1)} %gate.29.refs_1_.refs_3_), channel_id=1, source_target_pairs={{0,2},{2,4},{4,6},{6,7},{7,5},{5,3},{3,1},{1,0},{8,10},{10,12},{12... | collective-permute-start | bytes 1572872 | tf_op jit(solution)/shard_map/ppermute | solution.py:229
  25.3 22.5 %collective-permute-start.11 = (bf16[128,2048]{1,0:T(8,128)(2,1)S(1)}, bf16[128,2048]{1,0:T(8,128)(2,1)S(1)}, u32[]{:S(2)}, u32[]{:S(2)}) collective-permute-start(bf16[128,2048]{1,0:T(8,128)(2,1)S(1)} %gate.30.refs_1_.refs_5_.refs_9_), channel_id=1, source_target_pairs={{0,1},{2,0},{4,2},{6,4},{7,6},{5,7},{3,5},{1,3},{8,9},{10,8},{12,1... | collective-permute-start | bytes 1572872 | tf_op jit(solution)/shard_map/ppermute | solution.py:229
  36.6 22.5 %collective-permute-start.9 = (bf16[128,2048]{1,0:T(8,128)(2,1)S(1)}, bf16[128,2048]{1,0:T(8,128)(2,1)S(1)}, u32[]{:S(2)}, u32[]{:S(2)}) collective-permute-start(bf16[128,2048]{1,0:T(8,128)(2,1)S(1)} %gate.31.refs_1_), channel_id=1, source_target_pairs={{0,1},{2,0},{4,2},{6,4},{7,6},{5,7},{3,5},{1,3},{8,9},{10,8},{12,1... | collective-permute-start | bytes 1572872 | tf_op jit(solution)/shard_map/ppermute | solution.py:229
  38.1 21.0 %collective-permute-start.8 = (bf16[128,2048]{1,0:T(8,128)(2,1)S(1)}, bf16[128,2048]{1,0:T(8,128)(2,1)S(1)}, u32[]{:S(2)}, u32[]{:S(2)}) collective-permute-start(bf16[128,2048]{1,0:T(8,128)(2,1)S(1)} %gate.32.refs_1_.refs_7_.refs_11_), channel_id=1, source_target_pairs={{0,2},{2,4},{4,6},{6,7},{7,5},{5,3},{3,1},{1,0},{8,10},{10,12},{12... | collective-permute-start | bytes 1572872 | tf_op jit(solution)/shard_map/ppermute | solution.py:229
  46.2 22.5 %collective-permute-start.14 = (bf16[128,2048]{1,0:T(8,128)(2,1)S(1)}, bf16[128,2048]{1,0:T(8,128)(2,1)S(1)}, u32[]{:S(2)}, u32[]{:S(2)}) collective-permute-start(bf16[128,2048]{1,0:T(8,128)(2,1)S(1)} %gate.33.refs_1_.refs_2_), channel_id=1, source_target_pairs={{0,2},{2,4},{4,6},{6,7},{7,5},{5,3},{3,1},{1,0},{8,10},{10,12},{12... | collective-permute-start | bytes 1572872 | tf_op jit(solution)/shard_map/ppermute | solution.py:229
  47.8 22.5 %collective-permute-start.13 = (bf16[128,2048]{1,0:T(8,128)(2,1)S(1)}, bf16[128,2048]{1,0:T(8,128)(2,1)S(1)}, u32[]{:S(2)}, u32[]{:S(2)}) collective-permute-start(bf16[128,2048]{1,0:T(8,128)(2,1)S(1)} %gate.34.refs_1_.refs_4_.refs_12_), channel_id=1, source_target_pairs={{0,1},{2,0},{4,2},{6,4},{7,6},{5,7},{3,5},{1,3},{8,9},{10,8},{12,1... | collective-permute-start | bytes 1572872 | tf_op jit(solution)/shard_map/ppermute | solution.py:229
  53.2 5.9 %copy-start.2 = (s32[1024,1]{0,1:T(1,128)S(1)}, s32[1024,1]{0,1:T(1,128)}, u32[]{:S(2)}) copy-start(s32[1024,1]{0,1:T(1,128)} %param.8) | copy-start | bytes 12292
  53.2 5.9 %copy-start.3 = (f32[1024,1]{0,1:T(1,128)S(1)}, f32[1024,1]{0,1:T(1,128)}, u32[]{:S(2)}) copy-start(f32[1024,1]{0,1:T(1,128)} %param.9) | copy-start | bytes 12292
  53.2 49.6 %collective-permute-start.18 = (bf16[3,176,2048]{2,1,0:T(8,128)(2,1)S(1)}, bf16[3,176,2048]{2,1,0:T(8,128)(2,1)S(1)}, u32[]{:S(2)}, u32[]{:S(2)}) collective-permute-start(bf16[3,176,2048]{2,1,0:T(8,128)(2,1)S(1)} %gate.36.refs_1_), channel_id=1, source_target_pairs={{24,0},{16,8},{8,16},{0,24},{25,1},{17,9},{9,17},{1,25},{26,2},{18... | collective-permute-start | bytes 6488072 | tf_op jit(solution)/shard_map/ppermute | solution.py:89
  60.6 20.9 %collective-permute-start.16 = (bf16[128,2048]{1,0:T(8,128)(2,1)S(1)}, bf16[128,2048]{1,0:T(8,128)(2,1)S(1)}, u32[]{:S(2)}, u32[]{:S(2)}) collective-permute-start(bf16[128,2048]{1,0:T(8,128)(2,1)S(1)} %gate.38.refs_6_.refs_13_.refs_10_), channel_id=1, source_target_pairs={{0,2},{2,4},{4,6},{6,7},{7,5},{5,3},{3,1},{1,0},{8,10},{10,12},{12... | collective-permute-start | bytes 1572872 | tf_op jit(solution)/shard_map/ppermute | solution.py:229
  63.9 17.7 %collective-permute-start.12 = (bf16[128,2048]{1,0:T(8,128)(2,1)S(1)}, bf16[128,2048]{1,0:T(8,128)(2,1)S(1)}, u32[]{:S(2)}, u32[]{:S(2)}) collective-permute-start(bf16[128,2048]{1,0:T(8,128)(2,1)S(1)} %gate.37.refs_1_.refs_0_.refs_4_), channel_id=1, source_target_pairs={{0,1},{2,0},{4,2},{6,4},{7,6},{5,7},{3,5},{1,3},{8,9},{10,8},{12,1... | collective-permute-start | bytes 1572872 | tf_op jit(solution)/shard_map/ppermute | solution.py:229
  68.6 22.0 %collective-permute-start.15 = (bf16[128,2048]{1,0:T(8,128)(2,1)S(1)}, bf16[128,2048]{1,0:T(8,128)(2,1)S(1)}, u32[]{:S(2)}, u32[]{:S(2)}) collective-permute-start(bf16[128,2048]{1,0:T(8,128)(2,1)S(1)} %gate.39.refs_1_.refs_3_.refs_7_), channel_id=1, source_target_pairs={{0,2},{2,4},{4,6},{6,7},{7,5},{5,3},{3,1},{1,0},{8,10},{10,12},{12... | collective-permute-start | bytes 1572872 | tf_op jit(solution)/shard_map/ppermute | solution.py:229
  70.3 21.7 %collective-permute-start.17 = (bf16[128,2048]{1,0:T(8,128)(2,1)S(1)}, bf16[128,2048]{1,0:T(8,128)(2,1)S(1)}, u32[]{:S(2)}, u32[]{:S(2)}) collective-permute-start(bf16[128,2048]{1,0:T(8,128)(2,1)S(1)} %gate.40.refs_1_.refs_5_.refs_13_), channel_id=1, source_target_pairs={{0,1},{2,0},{4,2},{6,4},{7,6},{5,7},{3,5},{1,3},{8,9},{10,8},{12,1... | collective-permute-start | bytes 1572872 | tf_op jit(solution)/shard_map/ppermute | solution.py:229
  97.5 52.1 %collective-permute-start.30 = (bf16[3,176,2048]{2,1,0:T(8,128)(2,1)S(1)}, bf16[3,176,2048]{2,1,0:T(8,128)(2,1)S(1)}, u32[]{:S(2)}, u32[]{:S(2)}) collective-permute-start(bf16[3,176,2048]{2,1,0:T(8,128)(2,1)S(1)} %grads_2.1.refs_13_), channel_id=1, source_target_pairs={{16,0},{24,8},{0,16},{8,24},{17,1},{25,9},{1,17},{9,25},{18,2},{26... | collective-permute-start | bytes 6488072 | tf_op jit(solution)/shard_map/ppermute | solution.py:89
  100.5 5.4 %collective-permute-start.21 = (bf16[176,2048]{1,0:T(8,128)(2,1)S(1)}, bf16[176,2048]{1,0:T(8,128)(2,1)S(1)}, u32[]{:S(2)}, u32[]{:S(2)}) collective-permute-start(bf16[176,2048]{1,0:T(8,128)(2,1)S(1)} %get-tuple-element.41), channel_id=1, source_target_pairs={{8,0},{0,8},{24,16},{16,24},{9,1},{1,9},{25,17},{17,25},{10,2},{2,... | collective-permute-start | bytes 2162696 | tf_op jit(solution)/shard_map/ppermute | solution.py:89
  100.6 5.4 %collective-permute-start.20 = (bf16[176,2048]{1,0:T(8,128)(2,1)S(1)}, bf16[176,2048]{1,0:T(8,128)(2,1)S(1)}, u32[]{:S(2)}, u32[]{:S(2)}) collective-permute-start(bf16[176,2048]{1,0:T(8,128)(2,1)S(1)} %get-tuple-element.40), channel_id=1, source_target_pairs={{8,0},{0,8},{24,16},{16,24},{9,1},{1,9},{25,17},{17,25},{10,2},{2,... | collective-permute-start | bytes 2162696 | tf_op jit(solution)/shard_map/ppermute | solution.py:89
  101.1 4.9 %collective-permute-start.19 = (bf16[176,2048]{1,0:T(8,128)(2,1)S(1)}, bf16[176,2048]{1,0:T(8,128)(2,1)S(1)}, u32[]{:S(2)}, u32[]{:S(2)}) collective-permute-start(bf16[176,2048]{1,0:T(8,128)(2,1)S(1)} %get-tuple-element.39.refs_11_), channel_id=1, source_target_pairs={{8,0},{0,8},{24,16},{16,24},{9,1},{1,9},{25,17},{17,25},{10,2},{2,... | collective-permute-start | bytes 2162696 | tf_op jit(solution)/shard_map/ppermute | solution.py:89
  109.9 17.1 %collective-permute-start.22 = (bf16[128,2048]{1,0:T(8,128)(2,1)S(1)}, bf16[128,2048]{1,0:T(8,128)(2,1)S(1)}, u32[]{:S(2)}, u32[]{:S(2)}) collective-permute-start(bf16[128,2048]{1,0:T(8,128)(2,1)S(1)} %get-tuple-element.42), channel_id=1, source_target_pairs={{0,2},{2,4},{4,6},{6,7},{7,5},{5,3},{3,1},{1,0},{8,10},{10,12},{12... | collective-permute-start | bytes 1572872 | tf_op jit(solution)/shard_map/ppermute | solution.py:229
  111.5 17.3 %collective-permute-start.26 = (bf16[128,2048]{1,0:T(8,128)(2,1)}, bf16[128,2048]{1,0:T(8,128)(2,1)}, u32[]{:S(2)}, u32[]{:S(2)}) collective-permute-start(bf16[128,2048]{1,0:T(8,128)(2,1)} %get-tuple-element.50), channel_id=1, source_target_pairs={{0,1},{2,0},{4,2},{6,4},{7,6},{5,7},{3,5},{1,3},{8,9},{10,8},{12,1... | collective-permute-start | bytes 1572872 | tf_op jit(solution)/shard_map/ppermute | solution.py:229
  120.1 18.2 %collective-permute-start.24 = (bf16[128,2048]{1,0:T(8,128)(2,1)S(1)}, bf16[128,2048]{1,0:T(8,128)(2,1)S(1)}, u32[]{:S(2)}, u32[]{:S(2)}) collective-permute-start(bf16[128,2048]{1,0:T(8,128)(2,1)S(1)} %get-tuple-element.43.refs_14_), channel_id=1, source_target_pairs={{0,2},{2,4},{4,6},{6,7},{7,5},{5,3},{3,1},{1,0},{8,10},{10,12},{12... | collective-permute-start | bytes 1572872 | tf_op jit(solution)/shard_map/ppermute | solution.py:229
  121.8 16.0 %collective-permute-start.25 = (bf16[128,2048]{1,0:T(8,128)(2,1)}, bf16[128,2048]{1,0:T(8,128)(2,1)S(1)}, u32[]{:S(2)}, u32[]{:S(2)}) collective-permute-start(bf16[128,2048]{1,0:T(8,128)(2,1)} %get-tuple-element.48), channel_id=1, source_target_pairs={{0,1},{2,0},{4,2},{6,4},{7,6},{5,7},{3,5},{1,3},{8,9},{10,8},{12,1... | collective-permute-start | bytes 1572872 | tf_op jit(solution)/shard_map/ppermute | solution.py:229
  127.2 20.0 %collective-permute-start.23 = (bf16[128,2048]{1,0:T(8,128)(2,1)S(1)}, bf16[128,2048]{1,0:T(8,128)(2,1)S(1)}, u32[]{:S(2)}, u32[]{:S(2)}) collective-permute-start(bf16[128,2048]{1,0:T(8,128)(2,1)S(1)} %add_rows.12.refs_2_), channel_id=1, source_target_pairs={{0,2},{2,4},{4,6},{6,7},{7,5},{5,3},{3,1},{1,0},{8,10},{10,12},{12... | collective-permute-start | bytes 1572872 | tf_op jit(solution)/shard_map/ppermute | solution.py:229
  130.0 19.0 %collective-permute-start.31 = (bf16[128,2048]{1,0:T(8,128)(2,1)S(1)}, bf16[128,2048]{1,0:T(8,128)(2,1)S(1)}, u32[]{:S(2)}, u32[]{:S(2)}) collective-permute-start(bf16[128,2048]{1,0:T(8,128)(2,1)S(1)} %add_rows.13.refs_2_), channel_id=1, source_target_pairs={{0,1},{2,0},{4,2},{6,4},{7,6},{5,7},{3,5},{1,3},{8,9},{10,8},{12,1... | collective-permute-start | bytes 1572872 | tf_op jit(solution)/shard_map/ppermute | solution.py:229
  137.9 22.3 %collective-permute-start.29 = (bf16[128,2048]{1,0:T(8,128)(2,1)S(1)}, bf16[128,2048]{1,0:T(8,128)(2,1)S(1)}, u32[]{:S(2)}, u32[]{:S(2)}) collective-permute-start(bf16[128,2048]{1,0:T(8,128)(2,1)S(1)} %add_rows.14.refs_2_), channel_id=1, source_target_pairs={{0,1},{2,0},{4,2},{6,4},{7,6},{5,7},{3,5},{1,3},{8,9},{10,8},{12,1... | collective-permute-start | bytes 1572872 | tf_op jit(solution)/shard_map/ppermute | solution.py:229
  138.5 22.3 %collective-permute-start.28 = (bf16[128,2048]{1,0:T(8,128)(2,1)S(1)}, bf16[128,2048]{1,0:T(8,128)(2,1)S(1)}, u32[]{:S(2)}, u32[]{:S(2)}) collective-permute-start(bf16[128,2048]{1,0:T(8,128)(2,1)S(1)} %add_rows.15.refs_2_), channel_id=1, source_target_pairs={{0,2},{2,4},{4,6},{6,7},{7,5},{5,3},{3,1},{1,0},{8,10},{10,12},{12... | collective-permute-start | bytes 1572872 | tf_op jit(solution)/shard_map/ppermute | solution.py:229
  147.3 22.3 %collective-permute-start.27 = (bf16[128,2048]{1,0:T(8,128)(2,1)S(1)}, bf16[128,2048]{1,0:T(8,128)(2,1)S(1)}, u32[]{:S(2)}, u32[]{:S(2)}) collective-permute-start(bf16[128,2048]{1,0:T(8,128)(2,1)S(1)} %add_rows.16.refs_2_), channel_id=1, source_target_pairs={{0,2},{2,4},{4,6},{6,7},{7,5},{5,3},{3,1},{1,0},{8,10},{10,12},{12... | collective-permute-start | bytes 1572872 | tf_op jit(solution)/shard_map/ppermute | solution.py:229
  149.1 22.3 %collective-permute-start.34 = (bf16[128,2048]{1,0:T(8,128)(2,1)S(1)}, bf16[128,2048]{1,0:T(8,128)(2,1)S(1)}, u32[]{:S(2)}, u32[]{:S(2)}) collective-permute-start(bf16[128,2048]{1,0:T(8,128)(2,1)S(1)} %add_rows.17.refs_1_), channel_id=1, source_target_pairs={{0,1},{2,0},{4,2},{6,4},{7,6},{5,7},{3,5},{1,3},{8,9},{10,8},{12,1... | collective-permute-start | bytes 1572872 | tf_op jit(solution)/shard_map/ppermute | solution.py:229
  149.6 49.3 %collective-permute-start.37 = (bf16[3,176,2048]{2,1,0:T(8,128)(2,1)S(1)}, bf16[3,176,2048]{2,1,0:T(8,128)(2,1)S(1)}, u32[]{:S(2)}, u32[]{:S(2)}) collective-permute-start(bf16[3,176,2048]{2,1,0:T(8,128)(2,1)S(1)} %gate.50.refs_2_), channel_id=1, source_target_pairs={{24,0},{16,8},{8,16},{0,24},{25,1},{17,9},{9,17},{1,25},{26,2},{18... | collective-permute-start | bytes 6488072 | tf_op jit(solution)/shard_map/ppermute | solution.py:89
  160.3 22.3 %collective-permute-start.33 = (bf16[128,2048]{1,0:T(8,128)(2,1)S(1)}, bf16[128,2048]{1,0:T(8,128)(2,1)S(1)}, u32[]{:S(2)}, u32[]{:S(2)}) collective-permute-start(bf16[128,2048]{1,0:T(8,128)(2,1)S(1)} %add_rows.18.refs_2_), channel_id=1, source_target_pairs={{0,1},{2,0},{4,2},{6,4},{7,6},{5,7},{3,5},{1,3},{8,9},{10,8},{12,1... | collective-permute-start | bytes 1572872 | tf_op jit(solution)/shard_map/ppermute | solution.py:229
  161.0 21.8 %collective-permute-start.35 = (bf16[128,2048]{1,0:T(8,128)(2,1)S(1)}, bf16[128,2048]{1,0:T(8,128)(2,1)S(1)}, u32[]{:S(2)}, u32[]{:S(2)}) collective-permute-start(bf16[128,2048]{1,0:T(8,128)(2,1)S(1)} %add_rows.19.refs_2_), channel_id=1, source_target_pairs={{0,2},{2,4},{4,6},{6,7},{7,5},{5,3},{3,1},{1,0},{8,10},{10,12},{12... | collective-permute-start | bytes 1572872 | tf_op jit(solution)/shard_map/ppermute | solution.py:229
  169.7 21.9 %collective-permute-start.32 = (bf16[128,2048]{1,0:T(8,128)(2,1)S(1)}, bf16[128,2048]{1,0:T(8,128)(2,1)S(1)}, u32[]{:S(2)}, u32[]{:S(2)}) collective-permute-start(bf16[128,2048]{1,0:T(8,128)(2,1)S(1)} %add_rows.20.refs_2_), channel_id=1, source_target_pairs={{0,2},{2,4},{4,6},{6,7},{7,5},{5,3},{3,1},{1,0},{8,10},{10,12},{12... | collective-permute-start | bytes 1572872 | tf_op jit(solution)/shard_map/ppermute | solution.py:229
  171.6 21.6 %collective-permute-start.36 = (bf16[128,2048]{1,0:T(8,128)(2,1)S(1)}, bf16[128,2048]{1,0:T(8,128)(2,1)S(1)}, u32[]{:S(2)}, u32[]{:S(2)}) collective-permute-start(bf16[128,2048]{1,0:T(8,128)(2,1)S(1)} %add_rows.21.refs_2_), channel_id=1, source_target_pairs={{0,1},{2,0},{4,2},{6,4},{7,6},{5,7},{3,5},{1,3},{8,9},{10,8},{12,1... | collective-permute-start | bytes 1572872 | tf_op jit(solution)/shard_map/ppermute | solution.py:229

commit v9 on v8

--- a/solution.py
+++ b/solution.py
@@ -91,14 +91,16 @@
     )
 
 
-def halves(units):
-    middle = max(16, units // 32 * 16) if units > 16 else units
-    return [(0, middle), (middle, units)] if middle < units else [(0, units)]
+def spans_of(units, most=4):
+    tiles = max(1, units // 16)
+    count = min(most, tiles)
+    cuts = [tiles * i // count * 16 for i in range(count)] + [units]
+    return list(zip(cuts[:-1], cuts[1:]))
 
 
 def pick_kernel(turns, stride, apart, fetch_pick, panels, *refs):
     kinds, units = panels.shape[1:3]
-    spans = halves(units)
+    spans = spans_of(units)
     outs, sems = refs[-len(turns) * (kinds if apart else 1) - 1 : -1], refs[-1]
     copies = []
     for i, turn in enumerate(turns):
@@ -127,7 +129,7 @@
         out_shape=tuple(jax.ShapeDtypeStruct(shape, BF16) for shape in shapes),
         in_specs=[pl.BlockSpec(memory_space=pltpu.SMEM), in_hbm()] + [untouched()] * len(after),
         out_specs=tuple(untouched() for _ in shapes),
-        scratch_shapes=[pltpu.SemaphoreType.DMA((len(turns), kinds, 2))],
+        scratch_shapes=[pltpu.SemaphoreType.DMA((len(turns), kinds, 4))],
         compiler_params=pltpu.CompilerParams(vmem_limit_bytes=1024 * 1024),
         cost_estimate=NO_COST,
         name="pick",
@@ -198,7 +200,7 @@
     pick = turn_pick(fetch_pick, turn, stride)
     writes = []
     for kind in range(grad.shape[0]):
-        for j, (low, high) in enumerate(halves(grad.shape[1])):
+        for j, (low, high) in enumerate(spans_of(grad.shape[1])):
             here = pl.ds(low, high - low)
             sums[kind, here] = (base[kind, here].astype(F32) + grad[kind, here].astype(F32)).astype(BF16)
             write = pltpu.make_async_copy(
@@ -217,7 +219,7 @@
         in_specs=[pl.BlockSpec(memory_space=pltpu.SMEM), in_hbm(), whole_in_vmem(), whole_in_vmem()],
         out_specs=in_hbm(),
         input_output_aliases={1: 0},
-        scratch_shapes=[pltpu.VMEM(grad.shape, BF16), pltpu.SemaphoreType.DMA((grad.shape[0], 2))],
+        scratch_shapes=[pltpu.VMEM(grad.shape, BF16), pltpu.SemaphoreType.DMA((grad.shape[0], 4))],
         compiler_params=pltpu.CompilerParams(vmem_limit_bytes=12 * 1024 * 1024),
         cost_estimate=NO_COST,
         name="add",

time: 201 us -> 202 us (level)
  no operation moved by 1% of the time
where the time goes in v9:
time: 202 us; the launch traced here: 201 us
  waiting for transfers between devices  108 us (53%)
  Pallas kernels  53.9 us (27%)
  starting transfers between devices  38.5 us (19%)
    ppermute x28, waiting for transfers between devices, ring_step(): lax.ppermute(block, 'local', [(order[i], order[(i + distance) % size]) fo...  99.2 us
    ppermute x28, starting transfers between devices, ring_step(): lax.ppermute(block, 'local', [(order[i], order[(i + distance) % size]) fo...  33.3 us
    pallas_call x8, Pallas kernels, acts_pass(): pl.pallas_call(lambda *refs: acts_kernel(turn, slots, stride, routes.shap...  12.6 us
    pallas_call x2, Pallas kernels, chunk_pass(): pl.pallas_call(kernel, out_shape=tuple((jax.ShapeDtypeStruct((part, width...  12.1 us
    pallas_call x4, Pallas kernels, grads_pass(): pl.pallas_call(lambda *refs: grads_kernel(parts, len(acts), len(shapes),...  9.6 us
    ppermute x10, waiting for transfers between devices, exchange(): lax.ppermute(block, 'node', [(owner_of(node, turn, slots, stride), node)...  8.59 us
    pallas_call x3, Pallas kernels, pick_pass(): pl.pallas_call(lambda *refs: pick_kernel(turns, stride, apart, *refs), ou...  7.94 us
    pallas_call x1, Pallas kernels, total_pass(): pl.pallas_call(lambda *refs: total_kernel(turns, last, stride, counts, *r...  5.31 us
  transfers between devices with their start and end apart: 38, of which 22 were waited for; matrix products, arithmetic and copies ran while one was open for 0% of the time, Pallas kernels for 24%

profile of v9, /device:TPU:0, one launch (start us, length us, event | category | flops | bytes accessed | tf_op | source)
XLA Modules:
  0.0 201.4 jit_solution(16852016066094309912)
XLA Ops:
  0.6 2.6 %pick.3.refs_2_ = bf16[3,176,2048]{2,1,0:T(8,128)(2,1)S(1)} custom-call(s32[4,4]{1,0:T(4,128)} %refs_0_.25, bf16[2,3,176,2048]{3,2,1,0:T(8,128)(2,1)} %refs_1_.5), custom_call_target="tpu_custom_call" | custom-call | flops 1 | bytes 1 | tf_op jit(solution)/shard_map/pick/pallas_call | solution.py:127
  3.2 3.0 %collective-permute-start.10 = (bf16[3,176,2048]{2,1,0:T(8,128)(2,1)S(1)}, bf16[3,176,2048]{2,1,0:T(8,128)(2,1)S(1)}, u32[]{:S(2)}, u32[]{:S(2)}) collective-permute-start(bf16[3,176,2048]{2,1,0:T(8,128)(2,1)S(1)} %pick.3.refs_2_), channel_id=1, source_target_pairs={{16,0},{24,8},{0,16},{8,24},{17,1},{25,9},{1,17},{9,25},{18,2},{26... | collective-permute-start | bytes 6488072 | tf_op jit(solution)/shard_map/ppermute | solution.py:89
  6.3 2.3 %pick.4 = (bf16[176,2048]{1,0:T(8,128)(2,1)S(1)}, bf16[176,2048]{1,0:T(8,128)(2,1)S(1)}, bf16[176,2048]{1,0:T(8,128)(2,1)S(1)}) custom-call(s32[4,4]{1,0:T(4,128)S(1)} %copy-done.4, bf16[2,3,176,2048]{3,2,1,0:T(8,128)(2,1)} %refs_1_.5, bf16[3,176,2048]{2,1,0:T(8,128)(2,1)S(1)} %pick.3.refs_2_), custom_call_target="tpu_custom_call" | custom-call | flops 1 | bytes 1 | tf_op jit(solution)/shard_map/pick/pallas_call | solution.py:127
  9.2 1.6 collective-permute-start.2
  10.8 1.5 collective-permute-start.1
  12.3 1.6 collective-permute-start
  13.9 0.6 collective-permute-start.7
  14.5 3.1 %pick.5 = (bf16[3,176,2048]{2,1,0:T(8,128)(2,1)S(1)}, bf16[3,176,2048]{2,1,0:T(8,128)(2,1)S(1)}) custom-call(s32[4,4]{1,0:T(4,128)S(1)} %copy-done.4, bf16[2,3,176,2048]{3,2,1,0:T(8,128)(2,1)} %refs_1_.5, bf16[176,2048]{1,0:T(8,128)(2,1)S(1)} %get-tuple-element.34.refs_2_), custom_call_target="tpu_custom_call" | custom-call | flops 1 | bytes 1 | tf_op jit(solution)/shard_map/pick/pallas_call | solution.py:127
  17.6 6.4 %collective-permute-done.2.refs_0_ = bf16[128,2048]{1,0:T(8,128)(2,1)S(1)} collective-permute-done((bf16[128,2048]{1,0:T(8,128)(2,1)S(1)}, bf16[128,2048]{1,0:T(8,128)(2,1)S(1)}, u32[]{:S(2)}, u32[]{:S(2)}) %collective-permute-start.2) | collective-permute-done | bytes 524320 | tf_op jit(solution)/shard_map/ppermute | solution.py:231
  24.0 1.6 collective-permute-start.6
  25.6 1.5 collective-permute-start.11
  27.1 9.7 %collective-permute-done.refs_0_ = bf16[128,2048]{1,0:T(8,128)(2,1)S(1)} collective-permute-done((bf16[128,2048]{1,0:T(8,128)(2,1)S(1)}, bf16[128,2048]{1,0:T(8,128)(2,1)S(1)}, u32[]{:S(2)}, u32[]{:S(2)}) %collective-permute-start) | collective-permute-done | bytes 524320 | tf_op jit(solution)/shard_map/ppermute | solution.py:231
  36.9 1.5 collective-permute-start.9
  38.3 0.5 collective-permute-start.8
  38.9 7.6 %collective-permute-done.6.refs_0_ = bf16[128,2048]{1,0:T(8,128)(2,1)S(1)} collective-permute-done((bf16[128,2048]{1,0:T(8,128)(2,1)S(1)}, bf16[128,2048]{1,0:T(8,128)(2,1)S(1)}, u32[]{:S(2)}, u32[]{:S(2)}) %collective-permute-start.6) | collective-permute-done | bytes 524320 | tf_op jit(solution)/shard_map/ppermute | solution.py:231
  46.4 1.6 collective-permute-start.14
  48.1 1.5 collective-permute-start.13
  49.6 3.7 %collective-permute-done.10.refs_0_ = bf16[3,176,2048]{2,1,0:T(8,128)(2,1)S(1)} collective-permute-done((bf16[3,176,2048]{2,1,0:T(8,128)(2,1)S(1)}, bf16[3,176,2048]{2,1,0:T(8,128)(2,1)S(1)}, u32[]{:S(2)}, u32[]{:S(2)}) %collective-permute-start.10) | collective-permute-done | bytes 2162720 | tf_op jit(solution)/shard_map/ppermute | solution.py:89
  53.6 5.7 %collective-permute-done.9.refs_0_ = bf16[128,2048]{1,0:T(8,128)(2,1)S(1)} collective-permute-done((bf16[128,2048]{1,0:T(8,128)(2,1)S(1)}, bf16[128,2048]{1,0:T(8,128)(2,1)S(1)}, u32[]{:S(2)}, u32[]{:S(2)}) %collective-permute-start.9) | collective-permute-done | bytes 524320 | tf_op jit(solution)/shard_map/ppermute | solution.py:231
  59.3 1.6 acts_1_n.1.refs_11_.refs_16_.refs_2_
  60.9 1.6 collective-permute-start.16
  62.6 1.6 acts_0_n.1.refs_11_.refs_0_.refs_16_
  64.1 0.5 collective-permute-start.12
  64.6 1.6 acts_2_n.1.refs_1_.refs_16_.refs_4_
  66.2 2.7 %collective-permute-done.14.refs_0_ = bf16[128,2048]{1,0:T(8,128)(2,1)S(1)} collective-permute-done((bf16[128,2048]{1,0:T(8,128)(2,1)S(1)}, bf16[128,2048]{1,0:T(8,128)(2,1)S(1)}, u32[]{:S(2)}, u32[]{:S(2)}) %collective-permute-start.14) | collective-permute-done | bytes 524320 | tf_op jit(solution)/shard_map/ppermute | solution.py:231
  68.9 1.6 collective-permute-start.15
  70.6 1.5 collective-permute-start.17
  72.0 9.7 %collective-permute-done.12.refs_0_ = bf16[128,2048]{1,0:T(8,128)(2,1)S(1)} collective-permute-done((bf16[128,2048]{1,0:T(8,128)(2,1)S(1)}, bf16[128,2048]{1,0:T(8,128)(2,1)S(1)}, u32[]{:S(2)}, u32[]{:S(2)}) %collective-permute-start.12) | collective-permute-done | bytes 524320 | tf_op jit(solution)/shard_map/ppermute | solution.py:231
  81.8 9.1 %collective-permute-done.15.refs_0_ = bf16[128,2048]{1,0:T(8,128)(2,1)S(1)} collective-permute-done((bf16[128,2048]{1,0:T(8,128)(2,1)S(1)}, bf16[128,2048]{1,0:T(8,128)(2,1)S(1)}, u32[]{:S(2)}, u32[]{:S(2)}) %collective-permute-start.15) | collective-permute-done | bytes 524320 | tf_op jit(solution)/shard_map/ppermute | solution.py:231
  90.9 1.3 collective-permute-done.17.refs_0_
  92.2 1.6 acts_2_f.1.refs_17_.refs_18_.refs_5_
  93.8 2.4 %grads_2.1.refs_13_ = bf16[3,176,2048]{2,1,0:T(8,128)(2,1)S(1)} custom-call(bf16[128,2048]{1,0:T(8,128)(2,1)S(1)} %copy-done, bf16[128,2048]{1,0:T(8,128)(2,1)S(1)} %gate.31.refs_1_, bf16[128,2048]{1,0:T(8,128)(2,1)S(1)} %gate.33.refs_1_.refs_2_, bf16[128,2048]{1,0:T(8,128)(2,1)S(1)} %gate.29.refs_1_.refs_3_, ...), custom_call_target="tpu_custom_call" | custom-call | flops 2214592512 | bytes 1 | tf_op jit(solution)/shard_map/grads_2/pallas_call | solution.py:326
  96.2 1.6 acts_1_f.1.refs_17_.refs_18_.refs_3_
  97.8 0.6 collective-permute-start.30
  98.4 2.4 %grads_1.1 = (bf16[176,2048]{1,0:T(8,128)(2,1)S(1)}, bf16[176,2048]{1,0:T(8,128)(2,1)S(1)}, bf16[176,2048]{1,0:T(8,128)(2,1)S(1)}) custom-call(bf16[128,2048]{1,0:T(8,128)(2,1)S(1)} %copy-done, bf16[128,2048]{1,0:T(8,128)(2,1)S(1)} %gate.31.refs_1_, bf16[128,2048]{1,0:T(8,128)(2,1)S(1)} %gate.33.refs_1_.refs_2_, bf16[128,2048]{1,0:T(8,128)(2,1)S(1)} %gate.29.refs_1_.refs_3_, ...), custom_call_target="tpu_custom_call" | custom-call | flops 2214592512 | bytes 1 | tf_op jit(solution)/shard_map/grads_1/pallas_call | solution.py:326
  101.4 1.6 acts_0_f.1.refs_1_.refs_17_
  103.0 1.6 acts_3_f.1.refs_11_.refs_7_.refs_17_
  104.6 1.6 acts_3_n.1.refs_1_.refs_6_.refs_16_
  106.3 4.0 %chunks_4.1 = (bf16[128,2048]{1,0:T(8,128)(2,1)S(1)}, bf16[128,2048]{1,0:T(8,128)(2,1)}, bf16[128,2048]{1,0:T(8,128)(2,1)}, bf16[128,2048]{1,0:T(8,128)(2,1)S(1)}) custom-call(bf16[528,512]{1,0:T(8,128)(2,1)S(1)} %acts_0_n.1.refs_11_.refs_0_.refs_16_, bf16[528,512]{1,0:T(8,128)(2,1)S(1)} %acts_0_f.1.refs_1_.refs_17_, ...), custom_call_target="tpu_custom_call" | custom-call | flops 2214592512 | bytes 1 | tf_op jit(solution)/shard_map/chunks_4/pallas_call | solution.py:375
  110.2 1.6 collective-permute-start.22
  112.3 8.1 %chunks_12.1 = (bf16[128,2048]{1,0:T(8,128)(2,1)S(1)}, bf16[128,2048]{1,0:T(8,128)(2,1)S(1)}, bf16[128,2048]{1,0:T(8,128)(2,1)S(1)}, bf16[128,2048]{1,0:T(8,128)...) custom-call(bf16[528,512]{1,0:T(8,128)(2,1)S(1)} %acts_0_n.1.refs_11, ...), custom_call_target="tpu_custom_call" | custom-call | flops 1 | bytes 1 | tf_op jit(solution)/shard_map/chunks_12/pallas_call | solution.py:375
  120.4 1.6 collective-permute-start.24
  122.5 2.4 %grads_3.1.refs_18_.refs_0_ = bf16[3,176,2048]{2,1,0:T(8,128)(2,1)S(1)} custom-call(bf16[128,2048]{1,0:T(8,128)(2,1)S(1)} %copy-done, bf16[128,2048]{1,0:T(8,128)(2,1)S(1)} %gate.31.refs_1_, bf16[128,2048]{1,0:T(8,128)(2,1)S(1)} %gate.33.refs_1_.refs_2_, bf16[128,2048]{1,0:T(8,128)(2,1)S(1)} %gate.29.refs_1_.refs_3_, ...), custom_call_target="tpu_custom_call" | custom-call | flops 2214592512 | bytes 1 | tf_op jit(solution)/shard_map/grads_3/pallas_call | solution.py:326
  124.9 2.4 %grads_0.1.refs_2_.refs_1_ = bf16[3,176,2048]{2,1,0:T(8,128)(2,1)S(1)} custom-call(bf16[128,2048]{1,0:T(8,128)(2,1)S(1)} %copy-done, bf16[128,2048]{1,0:T(8,128)(2,1)S(1)} %gate.31.refs_1_, bf16[128,2048]{1,0:T(8,128)(2,1)S(1)} %gate.33.refs_1_.refs_2_, bf16[128,2048]{1,0:T(8,128)(2,1)S(1)} %gate.29.refs_1_.refs_3_, ...), custom_call_target="tpu_custom_call" | custom-call | flops 2214592512 | bytes 1 | tf_op jit(solution)/shard_map/grads_0/pallas_call | solution.py:326
  127.4 1.6 collective-permute-start.23
  129.1 1.2 add_rows.13.refs_2_
  130.2 0.5 collective-permute-start.31
  130.7 7.3 %collective-permute-done.25.refs_0_ = bf16[128,2048]{1,0:T(8,128)(2,1)S(1)} collective-permute-done((bf16[128,2048]{1,0:T(8,128)(2,1)}, bf16[128,2048]{1,0:T(8,128)(2,1)S(1)}, u32[]{:S(2)}, u32[]{:S(2)}) %collective-permute-start.25) | collective-permute-done | bytes 524320 | tf_op jit(solution)/shard_map/ppermute | solution.py:231
  138.1 0.5 collective-permute-start.29
  138.8 1.6 collective-permute-start.28
  140.4 7.0 %collective-permute-done.23.refs_0_ = bf16[128,2048]{1,0:T(8,128)(2,1)S(1)} collective-permute-done((bf16[128,2048]{1,0:T(8,128)(2,1)S(1)}, bf16[128,2048]{1,0:T(8,128)(2,1)S(1)}, u32[]{:S(2)}, u32[]{:S(2)}) %collective-permute-start.23) | collective-permute-done | bytes 524320 | tf_op jit(solution)/shard_map/ppermute | solution.py:231
  147.6 1.6 collective-permute-start.27
  149.9 10.6 %collective-permute-done.29.refs_0_ = bf16[128,2048]{1,0:T(8,128)(2,1)S(1)} collective-permute-done((bf16[128,2048]{1,0:T(8,128)(2,1)S(1)}, bf16[128,2048]{1,0:T(8,128)(2,1)S(1)}, u32[]{:S(2)}, u32[]{:S(2)}) %collective-permute-start.29) | collective-permute-done | bytes 524320 | tf_op jit(solution)/shard_map/ppermute | solution.py:231
  161.2 1.6 collective-permute-start.35
  162.9 7.0 %collective-permute-done.27.refs_0_ = bf16[128,2048]{1,0:T(8,128)(2,1)S(1)} collective-permute-done((bf16[128,2048]{1,0:T(8,128)(2,1)S(1)}, bf16[128,2048]{1,0:T(8,128)(2,1)S(1)}, u32[]{:S(2)}, u32[]{:S(2)}) %collective-permute-start.27) | collective-permute-done | bytes 524320 | tf_op jit(solution)/shard_map/ppermute | solution.py:231
  170.0 1.6 collective-permute-start.32
  172.4 10.6 %collective-permute-done.33.refs_0_ = bf16[128,2048]{1,0:T(8,128)(2,1)S(1)} collective-permute-done((bf16[128,2048]{1,0:T(8,128)(2,1)S(1)}, bf16[128,2048]{1,0:T(8,128)(2,1)S(1)}, u32[]{:S(2)}, u32[]{:S(2)}) %collective-permute-start.33) | collective-permute-done | bytes 524320 | tf_op jit(solution)/shard_map/ppermute | solution.py:231
  183.2 5.3 %total.1 = (bf16[2,3,176,2048]{3,2,1,0:T(8,128)(2,1)}, bf16[3,176,2048]{2,1,0:T(8,128)(2,1)S(1)}, f32[8,128]{1,0:T(8,128)S(1)}) custom-call(s32[4,4]{1,0:T(4,128)S(1)} %copy-done.4, bf16[3,176,2048]{2,1,0:T(8,128)(2,1)S(1)} %grads_0.1.refs_2_.refs_1_, bf16[176,2048]{1,0:T(8,128)(2,1)S(1)} %gate.46.refs_1_.refs_2_, ...), custom_call_target="tpu_custom_call" | custom-call | flops 1 | bytes 1 | tf_op jit(solution)/shard_map/total/pallas_call | solution.py:182
  188.5 3.4 %collective-permute-done.32.refs_0_ = bf16[128,2048]{1,0:T(8,128)(2,1)S(1)} collective-permute-done((bf16[128,2048]{1,0:T(8,128)(2,1)S(1)}, bf16[128,2048]{1,0:T(8,128)(2,1)S(1)}, u32[]{:S(2)}, u32[]{:S(2)}) %collective-permute-start.32) | collective-permute-done | bytes 524320 | tf_op jit(solution)/shard_map/ppermute | solution.py:231
  191.9 0.9 final_rows.2
  192.8 0.6 collective-permute-done.36.refs_0_
  193.4 0.9 final_rows.3
  194.3 4.8 %collective-permute-done.37.refs_0_ = bf16[3,176,2048]{2,1,0:T(8,128)(2,1)S(1)} collective-permute-done((bf16[3,176,2048]{2,1,0:T(8,128)(2,1)S(1)}, bf16[3,176,2048]{2,1,0:T(8,128)(2,1)S(1)}, u32[]{:S(2)}, u32[]{:S(2)}) %collective-permute-start.37) | collective-permute-done | bytes 2162720 | tf_op jit(solution)/shard_map/ppermute | solution.py:89
  199.1 2.0 %add.1 = bf16[2,3,176,2048]{3,2,1,0:T(8,128)(2,1)} custom-call(s32[4,4]{1,0:T(4,128)S(1)} %copy-done.4, bf16[2,3,176,2048]{3,2,1,0:T(8,128)(2,1)} %get-tuple-element.62.refs_1_, bf16[3,176,2048]{2,1,0:T(8,128)(2,1)S(1)} %get-tuple-element.63.refs_2_, bf16[3,176,2048]{2,1,0:T(8,128)(2,1)S(1)} %gate.51.refs_3_), custom_call_target="tpu_custom_call", output_to_operand_aliasing={{}: (1, {})} | custom-call | flops 1 | bytes 1 | tf_op jit(solution)/shard_map/add/pallas_call | solution.py:216
  (81 shorter events, 5.8 us)
Async XLA Ops:
  0.6 5.6 %copy-start.4 = (s32[4,4]{1,0:T(4,128)S(1)}, s32[4,4]{1,0:T(4,128)}, u32[]{:S(2)}) copy-start(s32[4,4]{1,0:T(4,128)} %refs_0_.25) | copy-start | bytes 196
  3.2 6.0 %copy-start = (bf16[128,2048]{1,0:T(8,128)(2,1)S(1)}, bf16[128,2048]{1,0:T(8,128)(2,1)}, u32[]{:S(2)}) copy-start(bf16[128,2048]{1,0:T(8,128)(2,1)} %refs_0_.23) | copy-start | bytes 1572868
  3.2 7.6 %copy-start.1 = (bf16[128,2048]{1,0:T(8,128)(2,1)S(1)}, bf16[128,2048]{1,0:T(8,128)(2,1)}, u32[]{:S(2)}) copy-start(bf16[128,2048]{1,0:T(8,128)(2,1)} %refs_8_.7) | copy-start | bytes 1572868
  3.2 50.1 %collective-permute-start.10 = (bf16[3,176,2048]{2,1,0:T(8,128)(2,1)S(1)}, bf16[3,176,2048]{2,1,0:T(8,128)(2,1)S(1)}, u32[]{:S(2)}, u32[]{:S(2)}) collective-permute-start(bf16[3,176,2048]{2,1,0:T(8,128)(2,1)S(1)} %pick.3.refs_2_), channel_id=1, source_target_pairs={{16,0},{24,8},{0,16},{8,24},{17,1},{25,9},{1,17},{9,25},{18,2},{26... | collective-permute-start | bytes 6488072 | tf_op jit(solution)/shard_map/ppermute | solution.py:89
  8.6 2.3 %collective-permute-start.4 = (bf16[176,2048]{1,0:T(8,128)(2,1)S(1)}, bf16[176,2048]{1,0:T(8,128)(2,1)S(1)}, u32[]{:S(2)}, u32[]{:S(2)}) collective-permute-start(bf16[176,2048]{1,0:T(8,128)(2,1)S(1)} %get-tuple-element.35), channel_id=1, source_target_pairs={{8,0},{0,8},{24,16},{16,24},{9,1},{1,9},{25,17},{17,25},{10,2},{2,... | collective-permute-start | bytes 2162696 | tf_op jit(solution)/shard_map/ppermute | solution.py:89
  8.7 3.7 %collective-permute-start.5 = (bf16[176,2048]{1,0:T(8,128)(2,1)S(1)}, bf16[176,2048]{1,0:T(8,128)(2,1)S(1)}, u32[]{:S(2)}, u32[]{:S(2)}) collective-permute-start(bf16[176,2048]{1,0:T(8,128)(2,1)S(1)} %get-tuple-element.36), channel_id=1, source_target_pairs={{8,0},{0,8},{24,16},{16,24},{9,1},{1,9},{25,17},{17,25},{10,2},{2,... | collective-permute-start | bytes 2162696 | tf_op jit(solution)/shard_map/ppermute | solution.py:89
  9.2 4.8 %collective-permute-start.3 = (bf16[176,2048]{1,0:T(8,128)(2,1)S(1)}, bf16[176,2048]{1,0:T(8,128)(2,1)S(1)}, u32[]{:S(2)}, u32[]{:S(2)}) collective-permute-start(bf16[176,2048]{1,0:T(8,128)(2,1)S(1)} %get-tuple-element.34.refs_2_), channel_id=1, source_target_pairs={{8,0},{0,8},{24,16},{16,24},{9,1},{1,9},{25,17},{17,25},{10,2},{2,... | collective-permute-start | bytes 2162696 | tf_op jit(solution)/shard_map/ppermute | solution.py:89
  9.2 14.7 %collective-permute-start.2 = (bf16[128,2048]{1,0:T(8,128)(2,1)S(1)}, bf16[128,2048]{1,0:T(8,128)(2,1)S(1)}, u32[]{:S(2)}, u32[]{:S(2)}) collective-permute-start(bf16[128,2048]{1,0:T(8,128)(2,1)S(1)} %copy-done), channel_id=1, source_target_pairs={{0,2},{2,4},{4,6},{6,7},{7,5},{5,3},{3,1},{1,0},{8,10},{10,12},{12... | collective-permute-start | bytes 1572872 | tf_op jit(solution)/shard_map/ppermute | solution.py:231
  10.8 14.8 %collective-permute-start.1 = (bf16[128,2048]{1,0:T(8,128)(2,1)S(1)}, bf16[128,2048]{1,0:T(8,128)(2,1)S(1)}, u32[]{:S(2)}, u32[]{:S(2)}) collective-permute-start(bf16[128,2048]{1,0:T(8,128)(2,1)S(1)} %copy-done.1), channel_id=1, source_target_pairs={{0,1},{2,0},{4,2},{6,4},{7,6},{5,7},{3,5},{1,3},{8,9},{10,8},{12,1... | collective-permute-start | bytes 1572872 | tf_op jit(solution)/shard_map/ppermute | solution.py:231
  12.3 24.5 %collective-permute-start = (bf16[128,2048]{1,0:T(8,128)(2,1)S(1)}, bf16[128,2048]{1,0:T(8,128)(2,1)S(1)}, u32[]{:S(2)}, u32[]{:S(2)}) collective-permute-start(bf16[128,2048]{1,0:T(8,128)(2,1)S(1)} %copy-done), channel_id=1, source_target_pairs={{0,1},{2,0},{4,2},{6,4},{7,6},{5,7},{3,5},{1,3},{8,9},{10,8},{12,1... | collective-permute-start | bytes 1572872 | tf_op jit(solution)/shard_map/ppermute | solution.py:231
  13.9 24.4 %collective-permute-start.7 = (bf16[128,2048]{1,0:T(8,128)(2,1)S(1)}, bf16[128,2048]{1,0:T(8,128)(2,1)S(1)}, u32[]{:S(2)}, u32[]{:S(2)}) collective-permute-start(bf16[128,2048]{1,0:T(8,128)(2,1)S(1)} %copy-done.1), channel_id=1, source_target_pairs={{0,2},{2,4},{4,6},{6,7},{7,5},{5,3},{3,1},{1,0},{8,10},{10,12},{12... | collective-permute-start | bytes 1572872 | tf_op jit(solution)/shard_map/ppermute | solution.py:231
  24.0 22.5 %collective-permute-start.6 = (bf16[128,2048]{1,0:T(8,128)(2,1)S(1)}, bf16[128,2048]{1,0:T(8,128)(2,1)S(1)}, u32[]{:S(2)}, u32[]{:S(2)}) collective-permute-start(bf16[128,2048]{1,0:T(8,128)(2,1)S(1)} %gate.29.refs_1_.refs_3_), channel_id=1, source_target_pairs={{0,2},{2,4},{4,6},{6,7},{7,5},{5,3},{3,1},{1,0},{8,10},{10,12},{12... | collective-permute-start | bytes 1572872 | tf_op jit(solution)/shard_map/ppermute | solution.py:231
  25.6 22.5 %collective-permute-start.11 = (bf16[128,2048]{1,0:T(8,128)(2,1)S(1)}, bf16[128,2048]{1,0:T(8,128)(2,1)S(1)}, u32[]{:S(2)}, u32[]{:S(2)}) collective-permute-start(bf16[128,2048]{1,0:T(8,128)(2,1)S(1)} %gate.30.refs_1_.refs_5_.refs_9_), channel_id=1, source_target_pairs={{0,1},{2,0},{4,2},{6,4},{7,6},{5,7},{3,5},{1,3},{8,9},{10,8},{12,1... | collective-permute-start | bytes 1572872 | tf_op jit(solution)/shard_map/ppermute | solution.py:231
  36.9 22.5 %collective-permute-start.9 = (bf16[128,2048]{1,0:T(8,128)(2,1)S(1)}, bf16[128,2048]{1,0:T(8,128)(2,1)S(1)}, u32[]{:S(2)}, u32[]{:S(2)}) collective-permute-start(bf16[128,2048]{1,0:T(8,128)(2,1)S(1)} %gate.31.refs_1_), channel_id=1, source_target_pairs={{0,1},{2,0},{4,2},{6,4},{7,6},{5,7},{3,5},{1,3},{8,9},{10,8},{12,1... | collective-permute-start | bytes 1572872 | tf_op jit(solution)/shard_map/ppermute | solution.py:231
  38.3 21.0 %collective-permute-start.8 = (bf16[128,2048]{1,0:T(8,128)(2,1)S(1)}, bf16[128,2048]{1,0:T(8,128)(2,1)S(1)}, u32[]{:S(2)}, u32[]{:S(2)}) collective-permute-start(bf16[128,2048]{1,0:T(8,128)(2,1)S(1)} %gate.32.refs_1_.refs_7_.refs_11_), channel_id=1, source_target_pairs={{0,2},{2,4},{4,6},{6,7},{7,5},{5,3},{3,1},{1,0},{8,10},{10,12},{12... | collective-permute-start | bytes 1572872 | tf_op jit(solution)/shard_map/ppermute | solution.py:231
  46.4 22.5 %collective-permute-start.14 = (bf16[128,2048]{1,0:T(8,128)(2,1)S(1)}, bf16[128,2048]{1,0:T(8,128)(2,1)S(1)}, u32[]{:S(2)}, u32[]{:S(2)}) collective-permute-start(bf16[128,2048]{1,0:T(8,128)(2,1)S(1)} %gate.33.refs_1_.refs_2_), channel_id=1, source_target_pairs={{0,2},{2,4},{4,6},{6,7},{7,5},{5,3},{3,1},{1,0},{8,10},{10,12},{12... | collective-permute-start | bytes 1572872 | tf_op jit(solution)/shard_map/ppermute | solution.py:231
  48.1 22.5 %collective-permute-start.13 = (bf16[128,2048]{1,0:T(8,128)(2,1)S(1)}, bf16[128,2048]{1,0:T(8,128)(2,1)S(1)}, u32[]{:S(2)}, u32[]{:S(2)}) collective-permute-start(bf16[128,2048]{1,0:T(8,128)(2,1)S(1)} %gate.34.refs_1_.refs_4_.refs_12_), channel_id=1, source_target_pairs={{0,1},{2,0},{4,2},{6,4},{7,6},{5,7},{3,5},{1,3},{8,9},{10,8},{12,1... | collective-permute-start | bytes 1572872 | tf_op jit(solution)/shard_map/ppermute | solution.py:231
  53.3 6.0 %copy-start.2 = (s32[1024,1]{0,1:T(1,128)S(1)}, s32[1024,1]{0,1:T(1,128)}, u32[]{:S(2)}) copy-start(s32[1024,1]{0,1:T(1,128)} %param.8) | copy-start | bytes 12292
  53.3 6.0 %copy-start.3 = (f32[1024,1]{0,1:T(1,128)S(1)}, f32[1024,1]{0,1:T(1,128)}, u32[]{:S(2)}) copy-start(f32[1024,1]{0,1:T(1,128)} %param.9) | copy-start | bytes 12292
  53.3 49.7 %collective-permute-start.18 = (bf16[3,176,2048]{2,1,0:T(8,128)(2,1)S(1)}, bf16[3,176,2048]{2,1,0:T(8,128)(2,1)S(1)}, u32[]{:S(2)}, u32[]{:S(2)}) collective-permute-start(bf16[3,176,2048]{2,1,0:T(8,128)(2,1)S(1)} %gate.36.refs_1_), channel_id=1, source_target_pairs={{24,0},{16,8},{8,16},{0,24},{25,1},{17,9},{9,17},{1,25},{26,2},{18... | collective-permute-start | bytes 6488072 | tf_op jit(solution)/shard_map/ppermute | solution.py:89
  60.9 20.9 %collective-permute-start.16 = (bf16[128,2048]{1,0:T(8,128)(2,1)S(1)}, bf16[128,2048]{1,0:T(8,128)(2,1)S(1)}, u32[]{:S(2)}, u32[]{:S(2)}) collective-permute-start(bf16[128,2048]{1,0:T(8,128)(2,1)S(1)} %gate.38.refs_6_.refs_13_.refs_10_), channel_id=1, source_target_pairs={{0,2},{2,4},{4,6},{6,7},{7,5},{5,3},{3,1},{1,0},{8,10},{10,12},{12... | collective-permute-start | bytes 1572872 | tf_op jit(solution)/shard_map/ppermute | solution.py:231
  64.1 17.7 %collective-permute-start.12 = (bf16[128,2048]{1,0:T(8,128)(2,1)S(1)}, bf16[128,2048]{1,0:T(8,128)(2,1)S(1)}, u32[]{:S(2)}, u32[]{:S(2)}) collective-permute-start(bf16[128,2048]{1,0:T(8,128)(2,1)S(1)} %gate.37.refs_1_.refs_0_.refs_4_), channel_id=1, source_target_pairs={{0,1},{2,0},{4,2},{6,4},{7,6},{5,7},{3,5},{1,3},{8,9},{10,8},{12,1... | collective-permute-start | bytes 1572872 | tf_op jit(solution)/shard_map/ppermute | solution.py:231
  68.9 22.0 %collective-permute-start.15 = (bf16[128,2048]{1,0:T(8,128)(2,1)S(1)}, bf16[128,2048]{1,0:T(8,128)(2,1)S(1)}, u32[]{:S(2)}, u32[]{:S(2)}) collective-permute-start(bf16[128,2048]{1,0:T(8,128)(2,1)S(1)} %gate.39.refs_1_.refs_3_.refs_7_), channel_id=1, source_target_pairs={{0,2},{2,4},{4,6},{6,7},{7,5},{5,3},{3,1},{1,0},{8,10},{10,12},{12... | collective-permute-start | bytes 1572872 | tf_op jit(solution)/shard_map/ppermute | solution.py:231
  70.6 21.7 %collective-permute-start.17 = (bf16[128,2048]{1,0:T(8,128)(2,1)S(1)}, bf16[128,2048]{1,0:T(8,128)(2,1)S(1)}, u32[]{:S(2)}, u32[]{:S(2)}) collective-permute-start(bf16[128,2048]{1,0:T(8,128)(2,1)S(1)} %gate.40.refs_1_.refs_5_.refs_13_), channel_id=1, source_target_pairs={{0,1},{2,0},{4,2},{6,4},{7,6},{5,7},{3,5},{1,3},{8,9},{10,8},{12,1... | collective-permute-start | bytes 1572872 | tf_op jit(solution)/shard_map/ppermute | solution.py:231
  97.8 52.1 %collective-permute-start.30 = (bf16[3,176,2048]{2,1,0:T(8,128)(2,1)S(1)}, bf16[3,176,2048]{2,1,0:T(8,128)(2,1)S(1)}, u32[]{:S(2)}, u32[]{:S(2)}) collective-permute-start(bf16[3,176,2048]{2,1,0:T(8,128)(2,1)S(1)} %grads_2.1.refs_13_), channel_id=1, source_target_pairs={{16,0},{24,8},{0,16},{8,24},{17,1},{25,9},{1,17},{9,25},{18,2},{26... | collective-permute-start | bytes 6488072 | tf_op jit(solution)/shard_map/ppermute | solution.py:89
  100.8 5.4 %collective-permute-start.21 = (bf16[176,2048]{1,0:T(8,128)(2,1)S(1)}, bf16[176,2048]{1,0:T(8,128)(2,1)S(1)}, u32[]{:S(2)}, u32[]{:S(2)}) collective-permute-start(bf16[176,2048]{1,0:T(8,128)(2,1)S(1)} %get-tuple-element.41), channel_id=1, source_target_pairs={{8,0},{0,8},{24,16},{16,24},{9,1},{1,9},{25,17},{17,25},{10,2},{2,... | collective-permute-start | bytes 2162696 | tf_op jit(solution)/shard_map/ppermute | solution.py:89
  100.9 5.4 %collective-permute-start.20 = (bf16[176,2048]{1,0:T(8,128)(2,1)S(1)}, bf16[176,2048]{1,0:T(8,128)(2,1)S(1)}, u32[]{:S(2)}, u32[]{:S(2)}) collective-permute-start(bf16[176,2048]{1,0:T(8,128)(2,1)S(1)} %get-tuple-element.40), channel_id=1, source_target_pairs={{8,0},{0,8},{24,16},{16,24},{9,1},{1,9},{25,17},{17,25},{10,2},{2,... | collective-permute-start | bytes 2162696 | tf_op jit(solution)/shard_map/ppermute | solution.py:89
  101.4 4.9 %collective-permute-start.19 = (bf16[176,2048]{1,0:T(8,128)(2,1)S(1)}, bf16[176,2048]{1,0:T(8,128)(2,1)S(1)}, u32[]{:S(2)}, u32[]{:S(2)}) collective-permute-start(bf16[176,2048]{1,0:T(8,128)(2,1)S(1)} %get-tuple-element.39.refs_11_), channel_id=1, source_target_pairs={{8,0},{0,8},{24,16},{16,24},{9,1},{1,9},{25,17},{17,25},{10,2},{2,... | collective-permute-start | bytes 2162696 | tf_op jit(solution)/shard_map/ppermute | solution.py:89
  110.2 17.1 %collective-permute-start.22 = (bf16[128,2048]{1,0:T(8,128)(2,1)S(1)}, bf16[128,2048]{1,0:T(8,128)(2,1)S(1)}, u32[]{:S(2)}, u32[]{:S(2)}) collective-permute-start(bf16[128,2048]{1,0:T(8,128)(2,1)S(1)} %get-tuple-element.42), channel_id=1, source_target_pairs={{0,2},{2,4},{4,6},{6,7},{7,5},{5,3},{3,1},{1,0},{8,10},{10,12},{12... | collective-permute-start | bytes 1572872 | tf_op jit(solution)/shard_map/ppermute | solution.py:231
  111.8 17.3 %collective-permute-start.26 = (bf16[128,2048]{1,0:T(8,128)(2,1)}, bf16[128,2048]{1,0:T(8,128)(2,1)}, u32[]{:S(2)}, u32[]{:S(2)}) collective-permute-start(bf16[128,2048]{1,0:T(8,128)(2,1)} %get-tuple-element.50), channel_id=1, source_target_pairs={{0,1},{2,0},{4,2},{6,4},{7,6},{5,7},{3,5},{1,3},{8,9},{10,8},{12,1... | collective-permute-start | bytes 1572872 | tf_op jit(solution)/shard_map/ppermute | solution.py:231
  120.4 18.2 %collective-permute-start.24 = (bf16[128,2048]{1,0:T(8,128)(2,1)S(1)}, bf16[128,2048]{1,0:T(8,128)(2,1)S(1)}, u32[]{:S(2)}, u32[]{:S(2)}) collective-permute-start(bf16[128,2048]{1,0:T(8,128)(2,1)S(1)} %get-tuple-element.43.refs_14_), channel_id=1, source_target_pairs={{0,2},{2,4},{4,6},{6,7},{7,5},{5,3},{3,1},{1,0},{8,10},{10,12},{12... | collective-permute-start | bytes 1572872 | tf_op jit(solution)/shard_map/ppermute | solution.py:231
  122.0 16.0 %collective-permute-start.25 = (bf16[128,2048]{1,0:T(8,128)(2,1)}, bf16[128,2048]{1,0:T(8,128)(2,1)S(1)}, u32[]{:S(2)}, u32[]{:S(2)}) collective-permute-start(bf16[128,2048]{1,0:T(8,128)(2,1)} %get-tuple-element.48), channel_id=1, source_target_pairs={{0,1},{2,0},{4,2},{6,4},{7,6},{5,7},{3,5},{1,3},{8,9},{10,8},{12,1... | collective-permute-start | bytes 1572872 | tf_op jit(solution)/shard_map/ppermute | solution.py:231
  127.4 20.0 %collective-permute-start.23 = (bf16[128,2048]{1,0:T(8,128)(2,1)S(1)}, bf16[128,2048]{1,0:T(8,128)(2,1)S(1)}, u32[]{:S(2)}, u32[]{:S(2)}) collective-permute-start(bf16[128,2048]{1,0:T(8,128)(2,1)S(1)} %add_rows.12.refs_2_), channel_id=1, source_target_pairs={{0,2},{2,4},{4,6},{6,7},{7,5},{5,3},{3,1},{1,0},{8,10},{10,12},{12... | collective-permute-start | bytes 1572872 | tf_op jit(solution)/shard_map/ppermute | solution.py:231
  130.2 19.0 %collective-permute-start.31 = (bf16[128,2048]{1,0:T(8,128)(2,1)S(1)}, bf16[128,2048]{1,0:T(8,128)(2,1)S(1)}, u32[]{:S(2)}, u32[]{:S(2)}) collective-permute-start(bf16[128,2048]{1,0:T(8,128)(2,1)S(1)} %add_rows.13.refs_2_), channel_id=1, source_target_pairs={{0,1},{2,0},{4,2},{6,4},{7,6},{5,7},{3,5},{1,3},{8,9},{10,8},{12,1... | collective-permute-start | bytes 1572872 | tf_op jit(solution)/shard_map/ppermute | solution.py:231
  138.1 22.3 %collective-permute-start.29 = (bf16[128,2048]{1,0:T(8,128)(2,1)S(1)}, bf16[128,2048]{1,0:T(8,128)(2,1)S(1)}, u32[]{:S(2)}, u32[]{:S(2)}) collective-permute-start(bf16[128,2048]{1,0:T(8,128)(2,1)S(1)} %add_rows.14.refs_2_), channel_id=1, source_target_pairs={{0,1},{2,0},{4,2},{6,4},{7,6},{5,7},{3,5},{1,3},{8,9},{10,8},{12,1... | collective-permute-start | bytes 1572872 | tf_op jit(solution)/shard_map/ppermute | solution.py:231
  138.8 22.3 %collective-permute-start.28 = (bf16[128,2048]{1,0:T(8,128)(2,1)S(1)}, bf16[128,2048]{1,0:T(8,128)(2,1)S(1)}, u32[]{:S(2)}, u32[]{:S(2)}) collective-permute-start(bf16[128,2048]{1,0:T(8,128)(2,1)S(1)} %add_rows.15.refs_2_), channel_id=1, source_target_pairs={{0,2},{2,4},{4,6},{6,7},{7,5},{5,3},{3,1},{1,0},{8,10},{10,12},{12... | collective-permute-start | bytes 1572872 | tf_op jit(solution)/shard_map/ppermute | solution.py:231
  147.6 22.3 %collective-permute-start.27 = (bf16[128,2048]{1,0:T(8,128)(2,1)S(1)}, bf16[128,2048]{1,0:T(8,128)(2,1)S(1)}, u32[]{:S(2)}, u32[]{:S(2)}) collective-permute-start(bf16[128,2048]{1,0:T(8,128)(2,1)S(1)} %add_rows.16.refs_2_), channel_id=1, source_target_pairs={{0,2},{2,4},{4,6},{6,7},{7,5},{5,3},{3,1},{1,0},{8,10},{10,12},{12... | collective-permute-start | bytes 1572872 | tf_op jit(solution)/shard_map/ppermute | solution.py:231
  149.4 22.3 %collective-permute-start.34 = (bf16[128,2048]{1,0:T(8,128)(2,1)S(1)}, bf16[128,2048]{1,0:T(8,128)(2,1)S(1)}, u32[]{:S(2)}, u32[]{:S(2)}) collective-permute-start(bf16[128,2048]{1,0:T(8,128)(2,1)S(1)} %add_rows.17.refs_1_), channel_id=1, source_target_pairs={{0,1},{2,0},{4,2},{6,4},{7,6},{5,7},{3,5},{1,3},{8,9},{10,8},{12,1... | collective-permute-start | bytes 1572872 | tf_op jit(solution)/shard_map/ppermute | solution.py:231
  149.9 49.3 %collective-permute-start.37 = (bf16[3,176,2048]{2,1,0:T(8,128)(2,1)S(1)}, bf16[3,176,2048]{2,1,0:T(8,128)(2,1)S(1)}, u32[]{:S(2)}, u32[]{:S(2)}) collective-permute-start(bf16[3,176,2048]{2,1,0:T(8,128)(2,1)S(1)} %gate.50.refs_2_), channel_id=1, source_target_pairs={{24,0},{16,8},{8,16},{0,24},{25,1},{17,9},{9,17},{1,25},{26,2},{18... | collective-permute-start | bytes 6488072 | tf_op jit(solution)/shard_map/ppermute | solution.py:89
  160.6 22.3 %collective-permute-start.33 = (bf16[128,2048]{1,0:T(8,128)(2,1)S(1)}, bf16[128,2048]{1,0:T(8,128)(2,1)S(1)}, u32[]{:S(2)}, u32[]{:S(2)}) collective-permute-start(bf16[128,2048]{1,0:T(8,128)(2,1)S(1)} %add_rows.18.refs_2_), channel_id=1, source_target_pairs={{0,1},{2,0},{4,2},{6,4},{7,6},{5,7},{3,5},{1,3},{8,9},{10,8},{12,1... | collective-permute-start | bytes 1572872 | tf_op jit(solution)/shard_map/ppermute | solution.py:231
  161.2 21.8 %collective-permute-start.35 = (bf16[128,2048]{1,0:T(8,128)(2,1)S(1)}, bf16[128,2048]{1,0:T(8,128)(2,1)S(1)}, u32[]{:S(2)}, u32[]{:S(2)}) collective-permute-start(bf16[128,2048]{1,0:T(8,128)(2,1)S(1)} %add_rows.19.refs_2_), channel_id=1, source_target_pairs={{0,2},{2,4},{4,6},{6,7},{7,5},{5,3},{3,1},{1,0},{8,10},{10,12},{12... | collective-permute-start | bytes 1572872 | tf_op jit(solution)/shard_map/ppermute | solution.py:231
  170.0 21.9 %collective-permute-start.32 = (bf16[128,2048]{1,0:T(8,128)(2,1)S(1)}, bf16[128,2048]{1,0:T(8,128)(2,1)S(1)}, u32[]{:S(2)}, u32[]{:S(2)}) collective-permute-start(bf16[128,2048]{1,0:T(8,128)(2,1)S(1)} %add_rows.20.refs_2_), channel_id=1, source_target_pairs={{0,2},{2,4},{4,6},{6,7},{7,5},{5,3},{3,1},{1,0},{8,10},{10,12},{12... | collective-permute-start | bytes 1572872 | tf_op jit(solution)/shard_map/ppermute | solution.py:231
  171.9 21.6 %collective-permute-start.36 = (bf16[128,2048]{1,0:T(8,128)(2,1)S(1)}, bf16[128,2048]{1,0:T(8,128)(2,1)S(1)}, u32[]{:S(2)}, u32[]{:S(2)}) collective-permute-start(bf16[128,2048]{1,0:T(8,128)(2,1)S(1)} %add_rows.21.refs_2_), channel_id=1, source_target_pairs={{0,1},{2,0},{4,2},{6,4},{7,6},{5,7},{3,5},{1,3},{8,9},{10,8},{12,1... | collective-permute-start | bytes 1572872 | tf_op jit(solution)/shard_map/ppermute | solution.py:231
